TPU v7x, 32 devices: a whole 2x2x4 slice. The times are simulated.
32 devices in a mesh: parts: 2 (over y), tensor: 8 (over z, x), dp: 2 (over core).
Axes of the slice: x: 2, y: 2, z: 4, core: 2. Of those that a mesh axis runs over, the one named last changes fastest.
Arguments:
- hidden: bfloat16 [512, 28672], P(('parts', 'dp'), 'tensor'), parts along dimension 0, may hold values from -6 to 6
- frozen_down_weight: bfloat16 [28672, 8192], P('tensor'), may hold values from -8 to 8
- adapter_down_weight: bfloat16 [57344, 64], P(('parts', 'tensor')), parts along dimension 0, may hold values from -0.03125 to 0.03125
- adapter_up_weight: bfloat16 [128, 8192], P('parts'), parts along dimension 0, may hold values from -0.75 to 0.75
- magnitude: float32 [16384], P(('parts', 'tensor')), parts along dimension 0, may hold values from 0.5 to 2
- cotangent: bfloat16 [512, 8192], P(('parts', 'dp'), 'tensor'), parts along dimension 0, may hold values from -6 to 6
Outputs:
- mixed: bfloat16 [512, 8192], P(('parts', 'dp'), 'tensor'), parts along dimension 0
- hidden_gradient: bfloat16 [512, 28672], P(('parts', 'dp'), 'tensor'), parts along dimension 0
- down_weight_gradient: float32 [57344, 64], P(('parts', 'tensor')), parts along dimension 0
- up_weight_gradient: float32 [128, 8192], P('parts', 'tensor'), parts along dimension 0
- grad_magnitude: float32 [16384], P(('parts', 'tensor')), parts along dimension 0
There are 2 independent parts, one for each index of `parts`. A program takes and returns all parts, laid end to end along the dimension named above; an argument that names none is the same for every part. Nothing has to cross between parts.
All inputs are finite; a program needn't handle non-finite values.
Results may differ from a plain program's by a relative error of at most 0.0075.
Values may be sent and summed in bfloat16 or wider, within the bound.
No kernel may reach another device: no remote copies, remote signals or barrier semaphores. Data moves between devices by JAX's collectives and lax.ppermute only.
A program may use at most 192 MiB of HBM per device.

v0:
```python
import jax
import jax.numpy as jnp
from jax import lax
from jax.sharding import PartitionSpec as P

adapter_scale = 2.0
stability_floor = 1e-06


def local(hidden, frozen_down_weight, adapter_down_weight, adapter_up_weight, magnitude, cotangent):
    column_slice = magnitude.shape[0]
    block_offset = lax.axis_index("tensor") * column_slice
    combined_weight = frozen_down_weight.astype(jnp.float32) + adapter_scale * jnp.dot(
        adapter_down_weight, adapter_up_weight, preferred_element_type=jnp.float32
    )
    squares_part = jnp.sum(combined_weight * combined_weight, axis=0)
    reduced_rank_piece = jnp.dot(hidden, adapter_down_weight, preferred_element_type=jnp.float32)
    squares, reduced_rank_product = lax.psum((squares_part, reduced_rank_piece), "tensor")
    norm_all = jnp.sqrt(squares + stability_floor)
    column_length_norm = lax.dynamic_slice_in_dim(norm_all, block_offset, column_slice)
    up_weight_columns = lax.dynamic_slice_in_dim(adapter_up_weight, block_offset, column_slice, 1)
    contract_first = (((0,), (0,)), ((), ()))
    partial_terms = jnp.dot(hidden, frozen_down_weight, preferred_element_type=jnp.float32)
    summed_output = lax.psum_scatter(partial_terms, "tensor", scatter_dimension=1, tiled=True)
    unscaled_output = summed_output + adapter_scale * jnp.dot(
        reduced_rank_product, up_weight_columns.astype(jnp.float32), precision=lax.Precision.HIGHEST
    )
    rescale = magnitude / column_length_norm
    mixed = (unscaled_output * rescale).astype(jnp.bfloat16)
    upstream = cotangent.astype(jnp.float32)
    scaled_output = (upstream * rescale).astype(jnp.bfloat16)
    magnitude_part = jnp.sum(upstream * unscaled_output, axis=0) / column_length_norm
    contract_trailing = (((1,), (1,)), ((), ()))
    block_input = lax.all_gather(scaled_output, "tensor", axis=1, tiled=True)
    projected_output = lax.dot_general(
        block_input, adapter_up_weight, contract_trailing, preferred_element_type=jnp.float32
    ).astype(jnp.bfloat16)
    hidden_gradient = lax.dot_general(
        block_input, frozen_down_weight, contract_trailing, preferred_element_type=jnp.float32
    ) + adapter_scale * lax.dot_general(
        projected_output, adapter_down_weight, contract_trailing, preferred_element_type=jnp.float32
    )
    hidden_gradient = hidden_gradient.astype(jnp.bfloat16)
    down_gradient_piece = adapter_scale * lax.dot_general(
        hidden, projected_output, contract_first, preferred_element_type=jnp.float32
    )
    up_gradient_piece = adapter_scale * lax.dot_general(
        reduced_rank_product,
        scaled_output.astype(jnp.float32),
        contract_first,
        precision=lax.Precision.HIGHEST,
    )
    down_weight_gradient, up_weight_gradient, grad_magnitude = (
        lax.psum(down_gradient_piece.astype(jnp.bfloat16), "dp").astype(jnp.float32),
        lax.psum(up_gradient_piece.astype(jnp.bfloat16), "dp").astype(jnp.float32),
        lax.psum(magnitude_part.astype(jnp.bfloat16), "dp").astype(jnp.float32),
    )
    return (mixed, hidden_gradient, down_weight_gradient, up_weight_gradient, grad_magnitude)


def solution(mesh):
    in_specs = (
        P(("parts", "dp"), "tensor"),
        P("tensor", None),
        P(("parts", "tensor"), None),
        P("parts", None),
        P(("parts", "tensor")),
        P(("parts", "dp"), "tensor"),
    )
    out_specs = (
        P(("parts", "dp"), "tensor"),
        P(("parts", "dp"), "tensor"),
        P(("parts", "tensor"), None),
        P("parts", "tensor"),
        P(("parts", "tensor")),
    )
    return jax.shard_map(local, mesh=mesh, in_specs=in_specs, out_specs=out_specs, check_vma=False)
```

profile of v0, /device:TPU:0, one launch (start us, length us, event | category | flops | bytes accessed | tf_op | source)
XLA Modules:
  0.0 296.0 jit_solution(17417159659305427193)
XLA Ops:
  7.2 0.0 copy-start
  7.2 0.0 all-reduce.5.cloned.1.call-start
  7.2 2.4 fusion.13
  9.6 0.0 copy-done
  9.6 0.0 copy-start.2
  9.6 26.0 %multiply_reduce_fusion = f32[8192]{0:T(1024)} fusion(bf16[3584,8192]{1,0:T(8,128)(2,1)} %param.7, bf16[3584,64]{0,1:T(8,128)(2,1)} %param.8, bf16[64,8192]{1,0:T(8,128)(2,1)S(1)} %copy-done), kind=kOutput, calls=%fused_computation | convolution fusion | flops 3904888832 | bytes 60260352 | tf_op jit(solution)/shard_map/dot_general | solution.py:13
  35.6 0.0 all-reduce.5.cloned.1.call-update
  35.7 0.0 reduce-scatter.2.cloned.1.call-start
  35.7 0.0 copy-done.2
  35.7 22.5 %fusion.12 = f32[128,8192]{1,0:T(8,128)} fusion(bf16[128,3584]{1,0:T(8,128)(2,1)S(1)} %copy-done.2, bf16[3584,8192]{1,0:T(8,128)(2,1)} %param.7), kind=kOutput, calls=%fused_computation.23 | convolution fusion | flops 7516192768 | bytes 63832064 | tf_op jit(solution)/shard_map/dot_general | solution.py:23
  58.3 0.0 copy-start.4
  58.3 0.0 copy-start.3
  58.3 0.0 reduce-scatter.2.cloned.1.call-update
  58.3 0.0 all-gather.2.cloned.1.call-start
  58.3 48.9 %all-reduce.5.cloned.1.call-done = (f32[128,64]{0,1:T(8,128)}, f32[8192]{0:T(1024)}) async-done(((f32[128,64]{0,1:T(8,128)}, f32[8192]{0:T(1024)}), (f32[128,64]{0,1:T(8,128)}, f32[8192]{0:T(1024)})) %all-reduce.5.cloned.1.call-update) | async-done | bytes 65552 | tf_op jit(solution)/shard_map/psum | solution.py:18
  107.2 0.0 copy-done.4
  107.2 0.7 fusion.10
  107.9 91.2 %reduce-scatter.2.cloned.1.call-done = f32[128,1024]{1,0:T(8,128)} async-done(((f32[128,8192]{1,0:T(8,128)}), f32[128,1024]{1,0:T(8,128)}) %reduce-scatter.2.cloned.1.call-update) | async-done | bytes 524304 | tf_op jit(solution)/shard_map/reduce_scatter | solution.py:24
  199.2 0.0 copy-done.3
  199.2 2.3 fusion.7
  201.5 0.0 all-gather.2.cloned.1.call-update
  201.5 0.0 all-reduce.7.cloned.1.call-start
  201.6 0.7 divide_convert_fusion
  202.3 2.6 psum.39
  204.9 0.6 convert_element_type.53
  205.5 1.9 fusion.5
  207.4 43.8 %all-gather.2.cloned.1.call-done = bf16[128,8192]{1,0:T(8,128)(2,1)} async-done(((bf16[128,1024]{1,0:T(8,128)(2,1)}), bf16[128,8192]{1,0:T(8,128)(2,1)}) %all-gather.2.cloned.1.call-update) | async-done | bytes 2097168 | tf_op jit(solution)/shard_map/all_gather | solution.py:34
  251.2 0.0 copy-start.1
  251.2 2.6 convolution_convert_fusion
  253.8 2.2 fusion.3
  256.0 0.0 all-reduce.7.cloned.1.call-update
  256.0 0.0 copy-done.1
  256.0 26.8 %fusion.14 = f32[128,3584]{1,0:T(8,128)} fusion(bf16[128,8192]{1,0:T(8,128)(2,1)S(1)} %copy-done.1, bf16[3584,8192]{1,0:T(8,128)(2,1)} %param.7), kind=kOutput, calls=%fused_computation.25 | convolution fusion | flops 7516192768 | bytes 62652416 | tf_op jit(solution)/shard_map/dot_general | solution.py:38
  282.9 3.0 %fusion.1 = bf16[128,3584]{1,0:T(8,128)(2,1)} fusion(f32[128,3584]{1,0:T(8,128)} %fusion.14, bf16[128,64]{0,1:T(8,128)(2,1)S(1)} %convolution_convert_fusion, bf16[3584,64]{0,1:T(8,128)(2,1)} %param.8), kind=kOutput, calls=%fused_computation.3 | convolution fusion | flops 60096512 | bytes 3227648 | tf_op jit(solution)/shard_map/dot_general | solution.py:40
  285.9 0.0 all-reduce.7.cloned.1.call-done
  285.9 1.6 convert_element_type.51
  287.5 2.0 convert_element_type.49
Async XLA Ops:
  7.2 2.5 copy-start
  7.2 100.0 %all-reduce.5.cloned.1.call-start = ((), (), s32[]{:S(2)}) async-start(), calls=%async_computation.3 | async-start | bytes 131072 | tf_op jit(solution)/shard_map/psum | solution.py:18
  9.6 26.1 %copy-start.2 = (bf16[128,3584]{1,0:T(8,128)(2,1)S(1)}, bf16[128,3584]{1,0:T(8,128)(2,1)}, u32[]{:S(2)}) copy-start(bf16[128,3584]{1,0:T(8,128)(2,1)} %param.6) | copy-start | bytes 2752516
  35.7 163.5 %reduce-scatter.2.cloned.1.call-start = ((), (), s32[]{:S(2)}) async-start(), calls=%async_computation.1 | async-start | bytes 4718592 | tf_op jit(solution)/shard_map/reduce_scatter | solution.py:24
  58.3 49.0 %copy-start.4 = (f32[1024]{0:T(1024)S(1)}, f32[1024]{0:T(1024)}, u32[]{:S(2)}) copy-start(f32[1024]{0:T(1024)} %param.10) | copy-start | bytes 12292
  58.3 140.9 %copy-start.3 = (bf16[128,1024]{1,0:T(8,128)(2,1)S(1)}, bf16[128,1024]{1,0:T(8,128)(2,1)}, u32[]{:S(2)}) copy-start(bf16[128,1024]{1,0:T(8,128)(2,1)} %param.11) | copy-start | bytes 786436
  58.3 192.9 %all-gather.2.cloned.1.call-start = ((), (), s32[]{:S(2)}) async-start(), calls=%async_computation.2 | async-start | bytes 2359296 | tf_op jit(solution)/shard_map/all_gather | solution.py:34
  201.5 84.3 %all-reduce.7.cloned.1.call-start = ((), (), s32[]{:S(2)}) async-start(), calls=%async_computation.4 | async-start | bytes 1179648 | tf_op jit(solution)/shard_map/psum | solution.py:54
  251.2 4.8 %copy-start.1 = (bf16[128,8192]{1,0:T(8,128)(2,1)S(1)}, bf16[128,8192]{1,0:T(8,128)(2,1)}, u32[]{:S(2)}) copy-start(bf16[128,8192]{1,0:T(8,128)(2,1)} %all-gather.2.cloned.1.call-done) | copy-start | bytes 6291460
Sparse Core Ops, SparseCore 0:
  35.8 71.4 all-reduce.4
  110.9 88.2 reduce-scatter.1
  202.2 48.9 all-gather.1
  256.1 17.3 all-reduce.6
where the time goes:
time: 297 us; the launch traced here: 296 us
  waiting for transfers between devices  184 us (62%)
  matrix products  89.8 us (30%)
  between operations  13.8 us (5%)
  other arithmetic  5.61 us (2%)
    reduce_scatter x1, waiting for transfers between devices, local(): lax.psum_scatter(partial_terms, 'tensor', scatter_dimension=1, tiled=True)  91.2 us
    psum x1, waiting for transfers between devices, local(): lax.psum((squares_part, reduced_rank_piece), 'tensor')  48.9 us
    all_gather x1, waiting for transfers between devices, local(): block_input = lax.all_gather(scaled_output, 'tensor', axis=1, tiled=True)  43.8 us
    dot_general x1, matrix products, local(): lax.dot_general(block_input, frozen_down_weight, contract_trailing, prefe...  26.8 us
    dot_general x1, matrix products, local(): jnp.dot(adapter_down_weight, adapter_up_weight, preferred_element_type=jn...  26 us
    dot_general x1, matrix products, local(): jnp.dot(hidden, frozen_down_weight, preferred_element_type=jnp.float32)  22.5 us
  transfers between devices with their start and end apart: 4, of which 3 were waited for; matrix products, arithmetic and copies ran while one was open for 19% of the time, Pallas kernels for 0%

commit v1 on v0

v1 whole, which is shorter than its diff:
```python
import functools

import jax
import jax.numpy as jnp
from jax import lax
from jax.experimental import pallas as pl
from jax.experimental.pallas import tpu as pltpu
from jax.sharding import PartitionSpec as P

adapter_scale = 2.0
stability_floor = 1e-06
pad_rows = 16
vmem_bytes = 50 * 1024 * 1024
f32, bf16 = jnp.float32, jnp.bfloat16
contract_trailing = (((1,), (1,)), ((), ()))
contract_first = (((0,), (0,)), ((), ()))


def dot(a, b, dims=(((1,), (0,)), ((), ()))):
    return lax.dot_general(a, b, dims, preferred_element_type=f32)


def split_pair(x):
    high = x.astype(bf16)
    return high, (x - high.astype(f32)).astype(bf16)


def sum_of_squares(w_ref):
    rows, width = w_ref.shape
    totals = [jnp.zeros((8, width), f32) for _ in range(2)]
    for i in range(rows // 16):
        w = w_ref[i * 16 : (i + 1) * 16, :].astype(f32)
        w = w * w
        totals[0] = totals[0] + w[:8]
        totals[1] = totals[1] + w[8:]
    return jnp.sum(totals[0] + totals[1], axis=0, keepdims=True)


def forward_kernel(tokens, rank, steps, place_ref, own_ref, other_ref, at_ref, w_ref, b_ref, *rest):
    outs, squares_ref, lowrank_ref, lhs_ref, adapter_ref = rest[:steps], *rest[steps:]
    step = pl.program_id(0)
    both = 2 * tokens

    @pl.when(step == 0)
    def _():
        lhs_ref[:tokens, :] = own_ref[...]
        lhs_ref[tokens:both, :] = other_ref[...]
        lhs_ref[both:, :] = at_ref[...]
        lowrank = dot(lhs_ref[...], at_ref[...], contract_trailing)
        high, low = split_pair(lowrank)
        adapter_ref[:, :rank] = high
        adapter_ref[:, rank:] = low
        lowrank_ref[...] = lowrank[:tokens]

    up = b_ref[...]
    product = dot(lhs_ref[...], w_ref[...])
    through = dot(adapter_ref[...], jnp.concatenate([up, up], axis=0))
    result = (product[:both] + adapter_scale * through[:both]).astype(bf16)
    for k in range(steps):

        @pl.when(step == k)
        def _():
            outs[k][...] = result

    cross = jnp.sum(up.astype(f32) * (product[both:] + through[both:]), axis=0, keepdims=True)
    squares_ref[0] = sum_of_squares(w_ref) + (adapter_scale * adapter_scale) * cross


def forward(place, own, other, at, weight, up, half):
    tokens, rows = own.shape
    rank = at.shape[0]
    steps = place.shape[0] // 2
    whole = lambda *shape: pl.BlockSpec(shape, lambda i, p: (0,) * len(shape))
    column = lambda n: pl.BlockSpec((n, half), lambda i, p: (0, p[i]))
    out_shape = [jax.ShapeDtypeStruct((2 * tokens, half), bf16)] * steps + [
        jax.ShapeDtypeStruct((steps, 1, half), f32),
        jax.ShapeDtypeStruct((tokens, rank), f32),
    ]
    return pl.pallas_call(
        functools.partial(forward_kernel, tokens, rank, steps),
        grid_spec=pltpu.PrefetchScalarGridSpec(
            num_scalar_prefetch=1,
            grid=(steps,),
            in_specs=[whole(tokens, rows), whole(tokens, rows), whole(rank, rows), column(rows), column(rank)],
            out_specs=[whole(2 * tokens, half)] * steps
            + [pl.BlockSpec((1, 1, half), lambda i, p: (i, 0, 0)), whole(tokens, rank)],
            scratch_shapes=[
                pltpu.VMEM((2 * tokens + rank, rows), bf16),
                pltpu.VMEM((2 * tokens + rank, 2 * rank), bf16),
            ],
        ),
        out_shape=out_shape,
        compiler_params=pltpu.CompilerParams(vmem_limit_bytes=vmem_bytes),
        cost_estimate=pl.CostEstimate(
            flops=2 * steps * (2 * tokens + rank) * rows * half,
            bytes_accessed=2 * steps * rows * half + 8 * tokens * rows,
            transcendentals=0,
        ),
        name="forward",
    )(place, own, other, at, weight, up)


def backward_kernel(tokens, rank, steps, place_ref, *refs):
    cots, (squares_ref, at_ref, w_ref, b_ref) = refs[:steps], refs[steps : steps + 4]
    own_out, other_out, proj_own, proj_other, cot_ref, acc_ref, proj_ref = refs[steps + 4 :]
    step = pl.program_id(0)
    both = 2 * tokens
    for k in range(steps):

        @pl.when(step == k)
        def _():
            cot_ref[...] = cots[k][...]

    magnitude = jnp.sum(cot_ref[both:, :].astype(f32), axis=0, keepdims=True)
    rescale = magnitude / jnp.sqrt(squares_ref[0] + stability_floor)
    scaled = (cot_ref[:both, :].astype(f32) * rescale).astype(bf16)
    projected = dot(scaled, b_ref[...], contract_trailing)

    @pl.when(step == 0)
    def _():
        proj_ref[...] = projected
        acc_ref[...] = dot(scaled, w_ref[...], contract_trailing)

    @pl.when(step > 0)
    def _():
        proj_ref[...] += projected
        acc_ref[...] += dot(scaled, w_ref[...], contract_trailing)

    @pl.when(step == steps - 1)
    def _():
        proj = proj_ref[...]
        total = acc_ref[...] + adapter_scale * dot(proj.astype(bf16), at_ref[...])
        own_out[...] = total[:tokens]
        other_out[...] = total[tokens:].astype(bf16)
        proj_own[...] = proj[:tokens]
        proj_other[...] = proj[tokens:]


def backward(place, cots, squares, at, weight, up, half):
    steps = len(cots)
    both = cots[0].shape[0] - pad_rows
    tokens = both // 2
    rank, rows = at.shape
    whole = lambda *shape: pl.BlockSpec(shape, lambda i, p: (0,) * len(shape))
    column = lambda n: pl.BlockSpec((n, half), lambda i, p: (0, p[i]))
    out_shape = [
        jax.ShapeDtypeStruct((tokens, rows), f32),
        jax.ShapeDtypeStruct((tokens, rows), bf16),
        jax.ShapeDtypeStruct((tokens, rank), f32),
        jax.ShapeDtypeStruct((tokens, rank), f32),
    ]
    return pl.pallas_call(
        functools.partial(backward_kernel, tokens, rank, steps),
        grid_spec=pltpu.PrefetchScalarGridSpec(
            num_scalar_prefetch=1,
            grid=(steps,),
            in_specs=[whole(both + pad_rows, half)] * steps
            + [
                pl.BlockSpec((1, 1, half), lambda i, p: (p[steps + i], 0, 0)),
                whole(rank, rows),
                column(rows),
                column(rank),
            ],
            out_specs=[whole(*o.shape) for o in out_shape],
            scratch_shapes=[
                pltpu.VMEM((both + pad_rows, half), bf16),
                pltpu.VMEM((both, rows), f32),
                pltpu.VMEM((both, rank), f32),
            ],
        ),
        out_shape=out_shape,
        compiler_params=pltpu.CompilerParams(vmem_limit_bytes=vmem_bytes),
        cost_estimate=pl.CostEstimate(
            flops=2 * steps * both * rows * half,
            bytes_accessed=2 * steps * rows * half,
            transcendentals=0,
        ),
        name="backward",
    )(place, *cots, squares, at, weight, up)


def split_columns(n, hidden, weight, down, up, magnitude, cotangent):
    tokens = hidden.shape[0]
    half = magnitude.shape[0] // 2
    me, core = lax.axis_index("tensor"), lax.axis_index("dp")
    swap = lambda x: lax.ppermute(x, "dp", [(0, 1), (1, 0)])
    send = lambda x, r: lax.ppermute(x, "tensor", [(t, t ^ r) for t in range(n)])
    mine = lambda x, axis: lax.dynamic_slice_in_dim(x, core * half, half, axis)
    theirs = lambda x, axis: lax.dynamic_slice_in_dim(x, (1 - core) * half, half, axis)
    place = lambda rs: jnp.stack([2 * (me ^ r) + core for r in rs] + [me ^ r for r in rs]).astype(jnp.int32)
    at = down.T
    odds, evens = list(range(3, n, 2)) + [1], list(range(2, n, 2)) + [0]

    hidden_other = swap(hidden)
    cot_own, cot_other = mine(cotangent, 1), swap(theirs(cotangent, 1))
    own_magnitude = mine(magnitude, 0)
    first = lax.reduce_precision(own_magnitude, 8, 7)
    second = lax.reduce_precision(own_magnitude - first, 8, 7)
    third = own_magnitude - first - second
    magnitude_rows = jnp.concatenate(
        [jnp.stack([first, second, third]), jnp.zeros((pad_rows - 3, half), f32)]
    ).astype(bf16)
    own_block = jnp.concatenate([cot_own, cot_other, magnitude_rows])

    cots = {0: own_block}
    for r in range(2, n, 2):
        cots[r] = send(own_block, r)
    for r in range(0, n, 2):
        cots[r + 1] = send(cots[r], 1)

    *parts_odd, squares_odd, lowrank = forward(place(odds), hidden, hidden_other, at, weight, up, half)
    arrived = {r - 1: send(p, 1) for r, p in zip(odds, parts_odd)}
    *parts_even, squares_even, _ = forward(place(evens), hidden, hidden_other, at, weight, up, half)
    partial = dict(zip(evens, parts_even))
    total = {r: partial[r].astype(f32) + arrived[r].astype(f32) for r in evens}
    along = [send(total[r].astype(bf16), r) for r in evens if r]

    sq_even, sq_odd = squares_even[:, 0], squares_odd[:, 0]
    got_even, got_odd = send((sq_even, sq_odd), 1)
    sq_even, sq_odd = sq_even + got_odd, sq_odd + got_even
    squares_mine = jnp.stack([sq_even, sq_odd])
    index_of = {r: i for i, r in enumerate(evens)}
    squares = squares_mine
    for r in evens:
        if r:
            order = jnp.array([index_of[e ^ r] for e in evens])
            squares = squares + send(squares_mine, r)[:, order]
    squares_own = squares[0, index_of[0]]
    squares_rows = squares.reshape(n, 1, half)

    lowrank_sum = lowrank + send(lowrank, 1)
    lowrank_own = lowrank_sum
    for r in evens:
        if r:
            lowrank_own = lowrank_own + send(lowrank_sum, r)
    lowrank_all = jnp.concatenate([lowrank_own, swap(lowrank_own)])

    rs = evens + odds
    order_place = jnp.concatenate(
        [jnp.stack([2 * (me ^ r) + core for r in rs]).astype(jnp.int32),
         jnp.array([index_of[r - r % 2] + (r % 2) * len(evens) for r in rs], jnp.int32)]
    )
    grad_own, grad_other, proj_own, proj_other = backward(
        order_place, [cots[r] for r in rs], squares_rows, at, weight, up, half
    )
    hidden_gradient = (grad_own + swap(grad_other).astype(f32)).astype(bf16)
    from_own, from_other = swap((proj_own, proj_other))
    proj_own = (proj_own + from_other).astype(bf16)
    proj_other = (proj_other + from_own).astype(bf16)
    down_weight_gradient = adapter_scale * (
        dot(proj_own, hidden, contract_first) + dot(proj_other, hidden_other, contract_first)
    ).T

    norm = jnp.sqrt(squares_own + stability_floor)
    rescale = own_magnitude / norm
    upstream = own_block[: 2 * tokens].astype(f32)
    scaled = (upstream * rescale).astype(bf16)
    up_half = adapter_scale * lax.dot_general(
        lowrank_all, scaled.astype(f32), contract_first, precision=lax.Precision.HIGHEST
    )
    unscaled = total[0]
    for part in along:
        unscaled = unscaled + part.astype(f32)
    mixed = (unscaled * rescale).astype(bf16)
    magnitude_half = jnp.sum(upstream * unscaled, axis=0) / norm

    def join(own, other, axis):
        pair = jnp.concatenate([own, other, own], axis)
        return lax.dynamic_slice_in_dim(pair, core * half, 2 * half, axis)

    mixed = join(mixed[:tokens], swap(mixed[tokens:]), 1)
    up_weight_gradient = join(up_half, swap(up_half), 1)
    grad_magnitude = join(magnitude_half, swap(magnitude_half), 0)
    return (mixed, hidden_gradient, down_weight_gradient, up_weight_gradient, grad_magnitude)


def by_tokens(hidden, frozen_down_weight, adapter_down_weight, adapter_up_weight, magnitude, cotangent):
    column_slice = magnitude.shape[0]
    block_offset = lax.axis_index("tensor") * column_slice
    combined_weight = frozen_down_weight.astype(f32) + adapter_scale * dot(adapter_down_weight, adapter_up_weight)
    squares_part = jnp.sum(combined_weight * combined_weight, axis=0)
    squares, reduced_rank_product = lax.psum((squares_part, dot(hidden, adapter_down_weight)), "tensor")
    norm_all = jnp.sqrt(squares + stability_floor)
    column_length_norm = lax.dynamic_slice_in_dim(norm_all, block_offset, column_slice)
    up_weight_columns = lax.dynamic_slice_in_dim(adapter_up_weight, block_offset, column_slice, 1)
    summed_output = lax.psum_scatter(dot(hidden, frozen_down_weight), "tensor", scatter_dimension=1, tiled=True)
    unscaled_output = summed_output + adapter_scale * jnp.dot(
        reduced_rank_product, up_weight_columns.astype(f32), precision=lax.Precision.HIGHEST
    )
    rescale = magnitude / column_length_norm
    mixed = (unscaled_output * rescale).astype(bf16)
    upstream = cotangent.astype(f32)
    scaled_output = (upstream * rescale).astype(bf16)
    magnitude_part = jnp.sum(upstream * unscaled_output, axis=0) / column_length_norm
    block_input = lax.all_gather(scaled_output, "tensor", axis=1, tiled=True)
    projected_output = dot(block_input, adapter_up_weight, contract_trailing).astype(bf16)
    hidden_gradient = dot(block_input, frozen_down_weight, contract_trailing)
    hidden_gradient = hidden_gradient + adapter_scale * dot(projected_output, adapter_down_weight, contract_trailing)
    hidden_gradient = hidden_gradient.astype(bf16)
    down_gradient_piece = adapter_scale * dot(hidden, projected_output, contract_first)
    up_gradient_piece = adapter_scale * lax.dot_general(
        reduced_rank_product, scaled_output.astype(f32), contract_first, precision=lax.Precision.HIGHEST
    )
    pieces = (down_gradient_piece, up_gradient_piece, magnitude_part)
    pieces = [lax.psum(p.astype(bf16), "dp").astype(f32) for p in pieces]
    return (mixed, hidden_gradient, *pieces)


def solution(mesh):
    n = mesh.shape["tensor"]

    def local(hidden, weight, down, up, magnitude, cotangent):
        aligned = magnitude.shape[0] % 256 == 0 and weight.shape[0] % 256 == 0 and hidden.shape[0] % 16 == 0
        if aligned and mesh.shape["dp"] == 2 and n in (4, 8, 16) and down.shape[1] == 64:
            return split_columns(n, hidden, weight, down, up, magnitude, cotangent)
        return by_tokens(hidden, weight, down, up, magnitude, cotangent)

    in_specs = (
        P(("parts", "dp"), "tensor"),
        P("tensor", None),
        P(("parts", "tensor"), None),
        P("parts", None),
        P(("parts", "tensor")),
        P(("parts", "dp"), "tensor"),
    )
    out_specs = (
        P(("parts", "dp"), "tensor"),
        P(("parts", "dp"), "tensor"),
        P(("parts", "tensor"), None),
        P("parts", "tensor"),
        P(("parts", "tensor")),
    )
    return jax.shard_map(local, mesh=mesh, in_specs=in_specs, out_specs=out_specs, check_vma=False)
```

time: 297 us -> 141 us (0.47)
  waiting for transfers between devices: 184 us -> 45.7 us
  matrix products: 89.8 us -> 2.73 us
  Pallas kernels: 0 us -> 40.7 us
  starting transfers between devices: 0.16 us -> 30.9 us
  between operations: 13.8 us -> 0.9 us
  other arithmetic: 5.61 us -> 12.7 us
  local copies, waits for them, and re-layouts: 0.02 us -> 6.91 us
    reduce_scatter x1 -> x0, waiting for transfers between devices: 91.2 us -> none  [local(): lax.psum_scatter(partial_terms, 'tensor', scatter_dimension=1, tiled=True)]
    dot_general x9 -> x3, matrix products: 89.8 us -> 2.73 us  [the longest x2 1.55 us: dot(): return lax.dot_general(a, b, dims, preferred_element_type=f32)]
    psum x2 -> x0, waiting for transfers between devices: 48.9 us -> none  [the longest x1 48.9 us: local(): lax.psum((squares_part, reduced_rank_piece), 'tensor')]
    ppermute x0 -> x32, waiting for transfers between devices: none -> 45.7 us  [the longest x23 44.7 us: split_columns(): lax.ppermute(x, 'tensor', [(t, t ^ r) for t in range(n)])]
    all_gather x1 -> x0, waiting for transfers between devices: 43.8 us -> none  [local(): block_input = lax.all_gather(scaled_output, 'tensor', axis=1, tiled=True)]
    pallas_call x0 -> x3, Pallas kernels: none -> 40.7 us  [the longest x2 22.5 us: forward(): pl.pallas_call(functools.partial(forward_kernel, tokens, rank, steps), gr...]
    ppermute x0 -> x32, starting transfers between devices: none -> 30.9 us  [the longest x23 29 us: split_columns(): lax.ppermute(x, 'tensor', [(t, t ^ r) for t in range(n)])]
    unnamed x10 -> x28, local copies, waits for them, and re-layouts: 0.02 us -> 3.66 us
  transfers between devices with their start and end apart: 4 -> 32, of which waited for: 3 -> 11; matrix products, arithmetic and copies ran while one was open for 19% -> 13% of each run, Pallas kernels for 0% -> 29%
where the time goes in v1:
time: 141 us; the launch traced here: 140 us
  waiting for transfers between devices  45.7 us (32%)
  Pallas kernels  40.7 us (29%)
  starting transfers between devices  30.9 us (22%)
  other arithmetic  12.7 us (9%)
  local copies, waits for them, and re-layouts  6.91 us (5%)
  matrix products  2.73 us (2%)
    ppermute x23, waiting for transfers between devices, split_columns(): lax.ppermute(x, 'tensor', [(t, t ^ r) for t in range(n)])  44.7 us
    ppermute x23, starting transfers between devices, split_columns(): lax.ppermute(x, 'tensor', [(t, t ^ r) for t in range(n)])  29 us
    pallas_call x2, Pallas kernels, forward(): pl.pallas_call(functools.partial(forward_kernel, tokens, rank, steps), gr...  22.5 us
    pallas_call x1, Pallas kernels, backward(): pl.pallas_call(functools.partial(backward_kernel, tokens, rank, steps), g...  18.2 us
    convert_element_type x3, other arithmetic, split_columns(): along = [send(total[r].astype(bf16), r) for r in evens if r]  5.32 us
    unnamed x28, local copies, waits for them, and re-layouts  3.66 us
    concatenate x3, other arithmetic, join(): pair = jnp.concatenate([own, other, own], axis)  3.23 us
  transfers between devices with their start and end apart: 32, of which 11 were waited for; matrix products, arithmetic and copies ran while one was open for 13% of the time, Pallas kernels for 29%

profile of v1, /device:TPU:0, one launch (start us, length us, event | category | flops | bytes accessed | tf_op | source)
XLA Modules:
  0.0 140.5 jit_solution(1199716234494129395)
XLA Ops:
  0.6 0.5 collective-permute-start
  1.1 1.0 constant_dynamic-slice_fusion
  2.1 0.1 collective-permute-start.14
  2.3 0.1 stack.91.place_ref
  2.4 0.1 stack.100.place_ref
  2.4 0.7 pad_clamp_fusion.2
  3.1 0.7 pad_clamp_fusion.1
  3.8 1.2 copy-done
  5.0 1.0 copy-done.2
  6.0 11.4 %forward.3 = (bf16[256,512]{1,0:T(8,128)(2,1)}, bf16[256,512]{1,0:T(8,128)(2,1)S(1)}, bf16[256,512]{1,0:T(8,128)(2,1)}, bf16[256,512]{1,0:T(8,128)(2,1)}, f32[4,...) custom-call(s32[8]{0:T(128)S(1)} %stack.100.place_ref, bf16[128,3584]{1,0:T(8,128)(2,1)S(1)} %copy-done, ...), custom_call_target="tpu_custom_call" | custom-call | flops 4697620480 | bytes 18350080 | tf_op jit(solution)/shard_map/forward/pallas_call | solution.py:79
  17.4 3.0 %collective-permute-start.8 = (f32[4,512]{1,0:T(4,128)S(1)}, f32[4,512]{1,0:T(4,128)S(1)}, u32[]{:S(2)}, u32[]{:S(2)}) collective-permute-start(f32[4,512]{1,0:T(4,128)S(1)} %bitcast.51), channel_id=1, source_target_pairs={{0,2},{2,0},{4,6},{6,4},{8,10},{10,8},{12,14},{14,12},{1,3},{3,1},... | collective-permute-start | bytes 24584 | tf_op jit(solution)/shard_map/ppermute | solution.py:187
  20.4 11.1 %forward.2 = (bf16[256,512]{1,0:T(8,128)(2,1)S(1)}, bf16[256,512]{1,0:T(8,128)(2,1)S(1)}, bf16[256,512]{1,0:T(8,128)(2,1)S(1)}, bf16[256,512]{1,0:T(8,128)(2,1)S...) custom-call(s32[8]{0:T(128)S(1)} %stack.91.place_ref, bf16[128,3584]{1,0:T(8,128)(2,1)S(1)} %copy-done.1, ...), custom_call_target="tpu_custom_call" | custom-call | flops 4697620480 | bytes 18350080 | tf_op jit(solution)/shard_map/forward/pallas_call | solution.py:79
  31.5 0.7 copy-done.4
  32.2 0.7 copy-done.5
  33.0 3.6 %collective-permute-done.9 = f32[4,512]{1,0:T(4,128)S(1)} collective-permute-done((f32[4,512]{1,0:T(4,128)S(1)}, f32[4,512]{1,0:T(4,128)S(1)}, u32[]{:S(2)}, u32[]{:S(2)}) %collective-permute-start.9) | collective-permute-done | bytes 8224 | tf_op jit(solution)/shard_map/ppermute | solution.py:187
  36.6 2.7 %collective-permute-start.11 = (f32[2,4,512]{2,1,0:T(4,128)S(1)}, f32[2,4,512]{2,1,0:T(4,128)S(1)}, u32[]{:S(2)}, u32[]{:S(2)}) collective-permute-start(f32[2,4,512]{2,1,0:T(4,128)S(1)} %pad_maximum_fusion.2), channel_id=1, source_target_pairs={{0,8},{2,10},{4,12},{6,14},{8,0},{10,2},{12,4},{14,6},{1,9},{3,11}... | collective-permute-start | bytes 49160 | tf_op jit(solution)/shard_map/ppermute | solution.py:187
  39.3 1.3 collective-permute-start.12
  40.6 0.2 collective-permute-start.10
  40.8 0.6 collective-permute-start.25
  41.5 1.5 %collective-permute-start.1 = (bf16[256,512]{1,0:T(8,128)(2,1)}, bf16[256,512]{1,0:T(8,128)(2,1)}, u32[]{:S(2)}, u32[]{:S(2)}) collective-permute-start(bf16[256,512]{1,0:T(8,128)(2,1)} %get-tuple-element.21), channel_id=1, source_target_pairs={{0,2},{2,0},{4,6},{6,4},{8,10},{10,8},{12,14},{14,12},{1,3},{3,1},... | collective-permute-start | bytes 786440 | tf_op jit(solution)/shard_map/ppermute | solution.py:187
  43.0 0.6 gather_fusion.1
  43.5 1.3 collective-permute-done.12
  44.8 0.6 gather_fusion.2
  45.4 0.6 gather_fusion
  46.0 2.8 %collective-permute-start.28 = (f32[128,64]{1,0:T(8,128)S(1)}, f32[128,64]{1,0:T(8,128)S(1)}, u32[]{:S(2)}, u32[]{:S(2)}) collective-permute-start(f32[128,64]{1,0:T(8,128)S(1)} %add.181), channel_id=1, source_target_pairs={{0,12},{2,14},{4,8},{6,10},{8,4},{10,6},{12,0},{14,2},{1,13},{3,15... | collective-permute-start | bytes 98312 | tf_op jit(solution)/shard_map/ppermute | solution.py:187
  48.8 1.6 %collective-permute-start.26 = (f32[128,64]{1,0:T(8,128)S(1)}, f32[128,64]{1,0:T(8,128)S(1)}, u32[]{:S(2)}, u32[]{:S(2)}) collective-permute-start(f32[128,64]{1,0:T(8,128)S(1)} %add.181), channel_id=1, source_target_pairs={{0,4},{2,6},{4,0},{6,2},{8,12},{10,14},{12,8},{14,10},{1,5},{3,7},... | collective-permute-start | bytes 98312 | tf_op jit(solution)/shard_map/ppermute | solution.py:187
  50.5 1.7 %collective-permute-done.28 = f32[128,64]{1,0:T(8,128)S(1)} collective-permute-done((f32[128,64]{1,0:T(8,128)S(1)}, f32[128,64]{1,0:T(8,128)S(1)}, u32[]{:S(2)}, u32[]{:S(2)}) %collective-permute-start.28) | collective-permute-done | bytes 32800 | tf_op jit(solution)/shard_map/ppermute | solution.py:187
  52.2 0.6 collective-permute-start.2
  52.8 1.5 %collective-permute-done.27 = f32[128,64]{1,0:T(8,128)S(1)} collective-permute-done((f32[128,64]{1,0:T(8,128)S(1)}, f32[128,64]{1,0:T(8,128)S(1)}, u32[]{:S(2)}, u32[]{:S(2)}) %collective-permute-start.27) | collective-permute-done | bytes 32800 | tf_op jit(solution)/shard_map/ppermute | solution.py:187
  54.2 1.0 collective-permute-start.4
  55.3 0.1 fusion.16
  55.5 1.1 collective-permute-start.6
  56.6 0.2 concatenate.26.refs_3_
  56.8 2.1 %collective-permute-start.17 = (bf16[272,512]{1,0:T(8,128)(2,1)S(1)}, bf16[272,512]{1,0:T(8,128)(2,1)S(1)}, u32[]{:S(2)}, u32[]{:S(2)}) collective-permute-start(bf16[272,512]{1,0:T(8,128)(2,1)S(1)} %concatenate.26.refs_3_), channel_id=1, source_target_pairs={{0,12},{2,14},{4,8},{6,10},{8,4},{10,6},{12,0},{14,2},{1,13},{3,15... | collective-permute-start | bytes 835592 | tf_op jit(solution)/shard_map/ppermute | solution.py:187
  58.9 1.2 convolution_multiply_fusion
  60.1 5.1 %collective-permute-done.4 = bf16[256,512]{1,0:T(8,128)(2,1)} collective-permute-done((bf16[256,512]{1,0:T(8,128)(2,1)S(1)}, bf16[256,512]{1,0:T(8,128)(2,1)}, u32[]{:S(2)}, u32[]{:S(2)}) %collective-permute-start.4) | collective-permute-done | bytes 262176 | tf_op jit(solution)/shard_map/ppermute | solution.py:187
  65.2 1.7 %add_convert_fusion.2 = bf16[256,512]{1,0:T(8,128)(2,1)} fusion(bf16[256,512]{1,0:T(8,128)(2,1)} %collective-permute-done.4, bf16[256,512]{1,0:T(8,128)(2,1)S(1)} %get-tuple-element.24), kind=kLoop, calls=%fused_computation.15 | loop fusion | flops 524288 | bytes 786432 | tf_op jit(solution)/shard_map/convert_element_type | solution.py:216
  67.0 1.8 %add_convert_fusion.3 = bf16[256,512]{1,0:T(8,128)(2,1)} fusion(bf16[256,512]{1,0:T(8,128)(2,1)} %collective-permute-done.2, bf16[256,512]{1,0:T(8,128)(2,1)S(1)} %get-tuple-element.22), kind=kLoop, calls=%fused_computation.16 | loop fusion | flops 524288 | bytes 786432 | tf_op jit(solution)/shard_map/convert_element_type | solution.py:216
  68.8 2.6 %collective-permute-start.15 = (bf16[272,512]{1,0:T(8,128)(2,1)S(1)}, bf16[272,512]{1,0:T(8,128)(2,1)S(1)}, u32[]{:S(2)}, u32[]{:S(2)}) collective-permute-start(bf16[272,512]{1,0:T(8,128)(2,1)S(1)} %concatenate.26.refs_3_), channel_id=1, source_target_pairs={{0,4},{2,6},{4,0},{6,2},{8,12},{10,14},{12,8},{14,10},{1,5},{3,7},... | collective-permute-start | bytes 835592 | tf_op jit(solution)/shard_map/ppermute | solution.py:187
  71.4 2.3 %collective-permute-start.5 = (bf16[256,512]{1,0:T(8,128)(2,1)}, bf16[256,512]{1,0:T(8,128)(2,1)}, u32[]{:S(2)}, u32[]{:S(2)}) collective-permute-start(bf16[256,512]{1,0:T(8,128)(2,1)} %add_convert_fusion.2), channel_id=1, source_target_pairs={{0,8},{2,10},{4,12},{6,14},{8,0},{10,2},{12,4},{14,6},{1,9},{3,11}... | collective-permute-start | bytes 786440 | tf_op jit(solution)/shard_map/ppermute | solution.py:187
  73.7 1.8 %add_convert_fusion.1 = bf16[256,512]{1,0:T(8,128)(2,1)} fusion(bf16[256,512]{1,0:T(8,128)(2,1)} %collective-permute-done.6, bf16[256,512]{1,0:T(8,128)(2,1)} %copy-done.5), kind=kLoop, calls=%fused_computation.14 | loop fusion | flops 524288 | bytes 786432 | tf_op jit(solution)/shard_map/convert_element_type | solution.py:216
  75.5 2.1 %collective-permute-start.7 = (bf16[256,512]{1,0:T(8,128)(2,1)}, bf16[256,512]{1,0:T(8,128)(2,1)}, u32[]{:S(2)}, u32[]{:S(2)}) collective-permute-start(bf16[256,512]{1,0:T(8,128)(2,1)} %add_convert_fusion.1), channel_id=1, source_target_pairs={{0,12},{2,14},{4,8},{6,10},{8,4},{10,6},{12,0},{14,2},{1,13},{3,15... | collective-permute-start | bytes 786440 | tf_op jit(solution)/shard_map/ppermute | solution.py:187
  77.6 0.1 concatenate.25.place_ref
  77.7 5.9 %collective-permute-done.16.refs_1_ = bf16[272,512]{1,0:T(8,128)(2,1)S(1)} collective-permute-done((bf16[272,512]{1,0:T(8,128)(2,1)S(1)}, bf16[272,512]{1,0:T(8,128)(2,1)S(1)}, u32[]{:S(2)}, u32[]{:S(2)}) %collective-permute-start.16) | collective-permute-done | bytes 278560 | tf_op jit(solution)/shard_map/ppermute | solution.py:187
  83.7 1.0 collective-permute-start.21
  84.7 3.1 %collective-permute-done.15.refs_0_ = bf16[272,512]{1,0:T(8,128)(2,1)S(1)} collective-permute-done((bf16[272,512]{1,0:T(8,128)(2,1)S(1)}, bf16[272,512]{1,0:T(8,128)(2,1)S(1)}, u32[]{:S(2)}, u32[]{:S(2)}) %collective-permute-start.15) | collective-permute-done | bytes 278560 | tf_op jit(solution)/shard_map/ppermute | solution.py:187
  87.8 0.3 collective-permute-start.20
  88.1 13.5 %collective-permute-done.3 = bf16[256,512]{1,0:T(8,128)(2,1)} collective-permute-done((bf16[256,512]{1,0:T(8,128)(2,1)}, bf16[256,512]{1,0:T(8,128)(2,1)}, u32[]{:S(2)}, u32[]{:S(2)}) %collective-permute-start.3) | collective-permute-done | bytes 262176 | tf_op jit(solution)/shard_map/ppermute | solution.py:187
  101.6 0.8 collective-permute-start.19
  102.4 1.2 collective-permute-start.18
  103.6 1.7 %fusion.5 = f32[64,1024]{1,0:T(8,128)} fusion(s32[]{:T(128)S(6)} %select_n.25, f32[64,512]{1,0:T(8,128)} %copy-done.9, f32[64,512]{1,0:T(8,128)} %copy-done.10), kind=kLoop, calls=%fused_computation.24 | loop fusion | flops 131072 | bytes 524292 | tf_op jit(solution)/shard_map/concatenate | solution.py:268
  105.3 1.6 %fusion.3 = (f32[512]{0:T(512)S(1)}, bf16[256,512]{1,0:T(8,128)(2,1)S(1)}) fusion(bf16[128,512]{1,0:T(8,128)(2,1)} %copy-done.8, bf16[128,512]{1,0:T(8,128)(2,1)} %copy-done.7, bf16[256,512]{1,0:T(8,128)(2,1)} %collective-permute-done.7, bf16[256,512]{1,0:T(8,128)(2,1)} %collective-permute-done.5, bf16[256,512]{1,0:T(8,128)(2,1)} %collective-permute-done.3, ...), kind=kLoop, calls=%fused_computation.11 | loop fusion | flops 2227712 | bytes 1839104 | tf_op jit(solution)/shard_map/reduce_sum | solution.py:265
  107.1 4.1 %collective-permute-done.19.refs_5_ = bf16[272,512]{1,0:T(8,128)(2,1)S(1)} collective-permute-done((bf16[272,512]{1,0:T(8,128)(2,1)S(1)}, bf16[272,512]{1,0:T(8,128)(2,1)S(1)}, u32[]{:S(2)}, u32[]{:S(2)}) %collective-permute-start.19) | collective-permute-done | bytes 278560 | tf_op jit(solution)/shard_map/ppermute | solution.py:187
  111.1 4.9 %collective-permute-done.18.refs_4_ = bf16[272,512]{1,0:T(8,128)(2,1)S(1)} collective-permute-done((bf16[272,512]{1,0:T(8,128)(2,1)S(1)}, bf16[272,512]{1,0:T(8,128)(2,1)S(1)}, u32[]{:S(2)}, u32[]{:S(2)}) %collective-permute-start.18) | collective-permute-done | bytes 278560 | tf_op jit(solution)/shard_map/ppermute | solution.py:187
  116.1 18.2 %backward.1 = (f32[128,3584]{1,0:T(8,128)}, bf16[128,3584]{1,0:T(8,128)(2,1)S(1)}, f32[128,64]{1,0:T(8,128)S(1)}, f32[128,64]{1,0:T(8,128)S(1)}) custom-call(s32[16]{0:T(128)S(1)} %concatenate.25.place_ref, bf16[272,512]{1,0:T(8,128)(2,1)S(1)} %collective-permute-done.15.refs_0_, bf16[272,512]{1,0:T(8,128)(2,1)S(1)} %collective-permute-done.16.refs_1_, ...), custom_call_target="tpu_custom_call" | custom-call | flops 7516192768 | bytes 29360128 | tf_op jit(solution)/shard_map/backward/pallas_call | solution.py:152
  134.3 0.6 collective-permute-start.13
  134.8 0.1 collective-permute-start.24
  134.9 0.7 fusion.15
  135.6 0.4 collective-permute-start.23
  136.0 1.0 collective-permute-done.24
  137.0 0.3 fusion.13
  137.3 1.2 fusion.1
  138.6 0.8 fusion.7
  139.4 1.1 add_convert_fusion
  (72 shorter events, 0.6 us)
Async XLA Ops:
  0.6 3.1 %collective-permute-start = (bf16[128,3584]{1,0:T(8,128)(2,1)}, bf16[128,3584]{1,0:T(8,128)(2,1)S(1)}, u32[]{:S(2)}, u32[]{:S(2)}) collective-permute-start(bf16[128,3584]{1,0:T(8,128)(2,1)} %own_ref.3), channel_id=1, source_target_pairs={{0,1},{1,0},{2,3},{3,2},{4,5},{5,4},{6,7},{7,6},{8,9},{9,8},{10,11... | collective-permute-start | bytes 2752520 | tf_op jit(solution)/shard_map/ppermute | solution.py:186
  2.1 56.8 %copy-start.7 = (bf16[128,512]{1,0:T(8,128)(2,1)}, bf16[128,512]{1,0:T(8,128)(2,1)S(1)}, u32[]{:S(2)}) copy-start(bf16[128,512]{1,0:T(8,128)(2,1)S(1)} %get-tuple-element.38) | copy-start | bytes 393220
  2.1 53.3 %collective-permute-start.14 = (bf16[128,512]{1,0:T(8,128)(2,1)S(1)}, bf16[128,512]{1,0:T(8,128)(2,1)S(1)}, u32[]{:S(2)}, u32[]{:S(2)}) collective-permute-start(bf16[128,512]{1,0:T(8,128)(2,1)S(1)} %get-tuple-element.37), channel_id=1, source_target_pairs={{0,1},{1,0},{2,3},{3,2},{4,5},{5,4},{6,7},{7,6},{8,9},{9,8},{10,11... | collective-permute-start | bytes 393224 | tf_op jit(solution)/shard_map/ppermute | solution.py:186
  3.8 1.2 copy-start
  4.9 1.0 copy-start.2
  6.0 14.4 %copy-start.1 = (bf16[128,3584]{1,0:T(8,128)(2,1)S(1)}, bf16[128,3584]{1,0:T(8,128)(2,1)}, u32[]{:S(2)}) copy-start(bf16[128,3584]{1,0:T(8,128)(2,1)} %own_ref.3) | copy-start | bytes 2752516
  17.4 23.5 %copy-start.12 = (s32[4]{0:T(128)S(1)}, s32[4]{0:T(128)}, u32[]{:S(2)}) copy-start(s32[4]{0:T(128)} %constant.67) | copy-start | bytes 52
  17.4 38.0 %copy-start.11 = (f32[1024]{0:T(1024)S(1)}, f32[1024]{0:T(1024)}, u32[]{:S(2)}) copy-start(f32[1024]{0:T(1024)} %param.14) | copy-start | bytes 12292
  17.4 15.6 %collective-permute-start.8 = (f32[4,512]{1,0:T(4,128)S(1)}, f32[4,512]{1,0:T(4,128)S(1)}, u32[]{:S(2)}, u32[]{:S(2)}) collective-permute-start(f32[4,512]{1,0:T(4,128)S(1)} %bitcast.51), channel_id=1, source_target_pairs={{0,2},{2,0},{4,6},{6,4},{8,10},{10,8},{12,14},{14,12},{1,3},{3,1},... | collective-permute-start | bytes 24584 | tf_op jit(solution)/shard_map/ppermute | solution.py:187
  31.5 0.7 copy-start.4
  32.2 0.7 copy-start.5
  32.9 3.7 %collective-permute-start.9 = (f32[4,512]{1,0:T(4,128)S(1)}, f32[4,512]{1,0:T(4,128)S(1)}, u32[]{:S(2)}, u32[]{:S(2)}) collective-permute-start(f32[4,512]{1,0:T(4,128)S(1)} %bitcast.52), channel_id=1, source_target_pairs={{0,2},{2,0},{4,6},{6,4},{8,10},{10,8},{12,14},{14,12},{1,3},{3,1},... | collective-permute-start | bytes 24584 | tf_op jit(solution)/shard_map/ppermute | solution.py:187
  36.6 4.9 %collective-permute-start.11 = (f32[2,4,512]{2,1,0:T(4,128)S(1)}, f32[2,4,512]{2,1,0:T(4,128)S(1)}, u32[]{:S(2)}, u32[]{:S(2)}) collective-permute-start(f32[2,4,512]{2,1,0:T(4,128)S(1)} %pad_maximum_fusion.2), channel_id=1, source_target_pairs={{0,8},{2,10},{4,12},{6,14},{8,0},{10,2},{12,4},{14,6},{1,9},{3,11}... | collective-permute-start | bytes 49160 | tf_op jit(solution)/shard_map/ppermute | solution.py:187
  39.3 5.5 %collective-permute-start.12 = (f32[2,4,512]{2,1,0:T(4,128)S(1)}, f32[2,4,512]{2,1,0:T(4,128)S(1)}, u32[]{:S(2)}, u32[]{:S(2)}) collective-permute-start(f32[2,4,512]{2,1,0:T(4,128)S(1)} %pad_maximum_fusion.2), channel_id=1, source_target_pairs={{0,12},{2,14},{4,8},{6,10},{8,4},{10,6},{12,0},{14,2},{1,13},{3,15... | collective-permute-start | bytes 49160 | tf_op jit(solution)/shard_map/ppermute | solution.py:187
  40.6 4.8 %collective-permute-start.10 = (f32[2,4,512]{2,1,0:T(4,128)S(1)}, f32[2,4,512]{2,1,0:T(4,128)S(1)}, u32[]{:S(2)}, u32[]{:S(2)}) collective-permute-start(f32[2,4,512]{2,1,0:T(4,128)S(1)} %pad_maximum_fusion.2), channel_id=1, source_target_pairs={{0,4},{2,6},{4,0},{6,2},{8,12},{10,14},{12,8},{14,10},{1,5},{3,7},... | collective-permute-start | bytes 49160 | tf_op jit(solution)/shard_map/ppermute | solution.py:187
  40.8 5.2 %collective-permute-start.25 = (f32[128,64]{1,0:T(8,128)S(1)}, f32[128,64]{1,0:T(8,128)S(1)}, u32[]{:S(2)}, u32[]{:S(2)}) collective-permute-start(f32[128,64]{1,0:T(8,128)S(1)} %get-tuple-element.34), channel_id=1, source_target_pairs={{0,2},{2,0},{4,6},{6,4},{8,10},{10,8},{12,14},{14,12},{1,3},{3,1},... | collective-permute-start | bytes 98312 | tf_op jit(solution)/shard_map/ppermute | solution.py:187
  41.5 29.9 %collective-permute-start.1 = (bf16[256,512]{1,0:T(8,128)(2,1)}, bf16[256,512]{1,0:T(8,128)(2,1)}, u32[]{:S(2)}, u32[]{:S(2)}) collective-permute-start(bf16[256,512]{1,0:T(8,128)(2,1)} %get-tuple-element.21), channel_id=1, source_target_pairs={{0,2},{2,0},{4,6},{6,4},{8,10},{10,8},{12,14},{14,12},{1,3},{3,1},... | collective-permute-start | bytes 786440 | tf_op jit(solution)/shard_map/ppermute | solution.py:187
  46.0 6.1 %collective-permute-start.28 = (f32[128,64]{1,0:T(8,128)S(1)}, f32[128,64]{1,0:T(8,128)S(1)}, u32[]{:S(2)}, u32[]{:S(2)}) collective-permute-start(f32[128,64]{1,0:T(8,128)S(1)} %add.181), channel_id=1, source_target_pairs={{0,12},{2,14},{4,8},{6,10},{8,4},{10,6},{12,0},{14,2},{1,13},{3,15... | collective-permute-start | bytes 98312 | tf_op jit(solution)/shard_map/ppermute | solution.py:187
  48.8 5.4 %collective-permute-start.27 = (f32[128,64]{1,0:T(8,128)S(1)}, f32[128,64]{1,0:T(8,128)S(1)}, u32[]{:S(2)}, u32[]{:S(2)}) collective-permute-start(f32[128,64]{1,0:T(8,128)S(1)} %add.181), channel_id=1, source_target_pairs={{0,8},{2,10},{4,12},{6,14},{8,0},{10,2},{12,4},{14,6},{1,9},{3,11}... | collective-permute-start | bytes 98312 | tf_op jit(solution)/shard_map/ppermute | solution.py:187
  48.8 6.4 %collective-permute-start.26 = (f32[128,64]{1,0:T(8,128)S(1)}, f32[128,64]{1,0:T(8,128)S(1)}, u32[]{:S(2)}, u32[]{:S(2)}) collective-permute-start(f32[128,64]{1,0:T(8,128)S(1)} %add.181), channel_id=1, source_target_pairs={{0,4},{2,6},{4,0},{6,2},{8,12},{10,14},{12,8},{14,10},{1,5},{3,7},... | collective-permute-start | bytes 98312 | tf_op jit(solution)/shard_map/ppermute | solution.py:187
  52.2 14.8 %collective-permute-start.2 = (bf16[256,512]{1,0:T(8,128)(2,1)}, bf16[256,512]{1,0:T(8,128)(2,1)}, u32[]{:S(2)}, u32[]{:S(2)}) collective-permute-start(bf16[256,512]{1,0:T(8,128)(2,1)} %get-tuple-element.23), channel_id=1, source_target_pairs={{0,2},{2,0},{4,6},{6,4},{8,10},{10,8},{12,14},{14,12},{1,3},{3,1},... | collective-permute-start | bytes 786440 | tf_op jit(solution)/shard_map/ppermute | solution.py:187
  54.2 11.0 %collective-permute-start.4 = (bf16[256,512]{1,0:T(8,128)(2,1)S(1)}, bf16[256,512]{1,0:T(8,128)(2,1)}, u32[]{:S(2)}, u32[]{:S(2)}) collective-permute-start(bf16[256,512]{1,0:T(8,128)(2,1)S(1)} %get-tuple-element.25), channel_id=1, source_target_pairs={{0,2},{2,0},{4,6},{6,4},{8,10},{10,8},{12,14},{14,12},{1,3},{3,1},... | collective-permute-start | bytes 786440 | tf_op jit(solution)/shard_map/ppermute | solution.py:187
  55.3 1.5 %collective-permute-start.29 = (f32[128,64]{1,0:T(8,128)S(1)}, f32[128,64]{1,0:T(8,128)S(1)}, u32[]{:S(2)}, u32[]{:S(2)}) collective-permute-start(f32[128,64]{1,0:T(8,128)S(1)} %add_add_fusion), channel_id=1, source_target_pairs={{0,1},{1,0},{2,3},{3,2},{4,5},{5,4},{6,7},{7,6},{8,9},{9,8},{10,11... | collective-permute-start | bytes 98312 | tf_op jit(solution)/shard_map/ppermute | solution.py:186
  55.5 1.3 copy-start.8
  55.5 16.0 %collective-permute-start.6 = (bf16[256,512]{1,0:T(8,128)(2,1)}, bf16[256,512]{1,0:T(8,128)(2,1)}, u32[]{:S(2)}, u32[]{:S(2)}) collective-permute-start(bf16[256,512]{1,0:T(8,128)(2,1)} %get-tuple-element.27), channel_id=1, source_target_pairs={{0,2},{2,0},{4,6},{6,4},{8,10},{10,8},{12,14},{14,12},{1,3},{3,1},... | collective-permute-start | bytes 786440 | tf_op jit(solution)/shard_map/ppermute | solution.py:187
  56.8 18.7 %collective-permute-start.17 = (bf16[272,512]{1,0:T(8,128)(2,1)S(1)}, bf16[272,512]{1,0:T(8,128)(2,1)S(1)}, u32[]{:S(2)}, u32[]{:S(2)}) collective-permute-start(bf16[272,512]{1,0:T(8,128)(2,1)S(1)} %concatenate.26.refs_3_), channel_id=1, source_target_pairs={{0,12},{2,14},{4,8},{6,10},{8,4},{10,6},{12,0},{14,2},{1,13},{3,15... | collective-permute-start | bytes 835592 | tf_op jit(solution)/shard_map/ppermute | solution.py:187
  60.1 15.4 %copy-start.9 = (f32[64,512]{1,0:T(8,128)}, f32[64,512]{1,0:T(8,128)S(1)}, u32[]{:S(2)}) copy-start(f32[64,512]{1,0:T(8,128)S(1)} %convolution_multiply_fusion) | copy-start | bytes 393220
  65.2 18.5 %collective-permute-start.16 = (bf16[272,512]{1,0:T(8,128)(2,1)S(1)}, bf16[272,512]{1,0:T(8,128)(2,1)S(1)}, u32[]{:S(2)}, u32[]{:S(2)}) collective-permute-start(bf16[272,512]{1,0:T(8,128)(2,1)S(1)} %concatenate.26.refs_3_), channel_id=1, source_target_pairs={{0,8},{2,10},{4,12},{6,14},{8,0},{10,2},{12,4},{14,6},{1,9},{3,11}... | collective-permute-start | bytes 835592 | tf_op jit(solution)/shard_map/ppermute | solution.py:187
  67.0 1.8 %collective-permute-start.30 = (f32[64,512]{1,0:T(8,128)S(1)}, f32[64,512]{1,0:T(8,128)S(1)}, u32[]{:S(2)}, u32[]{:S(2)}) collective-permute-start(f32[64,512]{1,0:T(8,128)S(1)} %convolution_multiply_fusion), channel_id=1, source_target_pairs={{0,1},{1,0},{2,3},{3,2},{4,5},{5,4},{6,7},{7,6},{8,9},{9,8},{10,11... | collective-permute-start | bytes 393224 | tf_op jit(solution)/shard_map/ppermute | solution.py:186
  67.0 49.1 %copy-start.3 = (bf16[3584,64]{0,1:T(8,128)(2,1)S(1)}, bf16[3584,64]{0,1:T(8,128)(2,1)}, u32[]{:S(2)}) copy-start(bf16[3584,64]{0,1:T(8,128)(2,1)} %param.12) | copy-start | bytes 1376260
  68.8 6.8 %copy-start.10 = (f32[64,512]{1,0:T(8,128)}, f32[64,512]{1,0:T(8,128)S(1)}, u32[]{:S(2)}) copy-start(f32[64,512]{1,0:T(8,128)S(1)} %collective-permute-done.30) | copy-start | bytes 393220
  68.8 19.1 %collective-permute-start.15 = (bf16[272,512]{1,0:T(8,128)(2,1)S(1)}, bf16[272,512]{1,0:T(8,128)(2,1)S(1)}, u32[]{:S(2)}, u32[]{:S(2)}) collective-permute-start(bf16[272,512]{1,0:T(8,128)(2,1)S(1)} %concatenate.26.refs_3_), channel_id=1, source_target_pairs={{0,4},{2,6},{4,0},{6,2},{8,12},{10,14},{12,8},{14,10},{1,5},{3,7},... | collective-permute-start | bytes 835592 | tf_op jit(solution)/shard_map/ppermute | solution.py:187
  71.4 30.2 %collective-permute-start.3 = (bf16[256,512]{1,0:T(8,128)(2,1)}, bf16[256,512]{1,0:T(8,128)(2,1)}, u32[]{:S(2)}, u32[]{:S(2)}) collective-permute-start(bf16[256,512]{1,0:T(8,128)(2,1)} %add_convert_fusion.3), channel_id=1, source_target_pairs={{0,4},{2,6},{4,0},{6,2},{8,12},{10,14},{12,8},{14,10},{1,5},{3,7},... | collective-permute-start | bytes 786440 | tf_op jit(solution)/shard_map/ppermute | solution.py:187
  71.4 31.0 %collective-permute-start.5 = (bf16[256,512]{1,0:T(8,128)(2,1)}, bf16[256,512]{1,0:T(8,128)(2,1)}, u32[]{:S(2)}, u32[]{:S(2)}) collective-permute-start(bf16[256,512]{1,0:T(8,128)(2,1)} %add_convert_fusion.2), channel_id=1, source_target_pairs={{0,8},{2,10},{4,12},{6,14},{8,0},{10,2},{12,4},{14,6},{1,9},{3,11}... | collective-permute-start | bytes 786440 | tf_op jit(solution)/shard_map/ppermute | solution.py:187
  75.5 29.8 %collective-permute-start.7 = (bf16[256,512]{1,0:T(8,128)(2,1)}, bf16[256,512]{1,0:T(8,128)(2,1)}, u32[]{:S(2)}, u32[]{:S(2)}) collective-permute-start(bf16[256,512]{1,0:T(8,128)(2,1)} %add_convert_fusion.1), channel_id=1, source_target_pairs={{0,12},{2,14},{4,8},{6,10},{8,4},{10,6},{12,0},{14,2},{1,13},{3,15... | collective-permute-start | bytes 786440 | tf_op jit(solution)/shard_map/ppermute | solution.py:187
  83.7 23.4 %collective-permute-start.21 = (bf16[272,512]{1,0:T(8,128)(2,1)S(1)}, bf16[272,512]{1,0:T(8,128)(2,1)S(1)}, u32[]{:S(2)}, u32[]{:S(2)}) collective-permute-start(bf16[272,512]{1,0:T(8,128)(2,1)S(1)} %concatenate.26.refs_3_), channel_id=1, source_target_pairs={{0,2},{2,0},{4,6},{6,4},{8,10},{10,8},{12,14},{14,12},{1,3},{3,1},... | collective-permute-start | bytes 835592 | tf_op jit(solution)/shard_map/ppermute | solution.py:187
  87.8 19.2 %collective-permute-start.20 = (bf16[272,512]{1,0:T(8,128)(2,1)S(1)}, bf16[272,512]{1,0:T(8,128)(2,1)S(1)}, u32[]{:S(2)}, u32[]{:S(2)}) collective-permute-start(bf16[272,512]{1,0:T(8,128)(2,1)S(1)} %collective-permute-done.17.refs_2_), channel_id=1, source_target_pairs={{0,2},{2,0},{4,6},{6,4},{8,10},{10,8},{12,14},{14,12},{1,3},{3,1},... | collective-permute-start | bytes 835592 | tf_op jit(solution)/shard_map/ppermute | solution.py:187
  101.6 9.5 %collective-permute-start.19 = (bf16[272,512]{1,0:T(8,128)(2,1)S(1)}, bf16[272,512]{1,0:T(8,128)(2,1)S(1)}, u32[]{:S(2)}, u32[]{:S(2)}) collective-permute-start(bf16[272,512]{1,0:T(8,128)(2,1)S(1)} %collective-permute-done.16.refs_1_), channel_id=1, source_target_pairs={{0,2},{2,0},{4,6},{6,4},{8,10},{10,8},{12,14},{14,12},{1,3},{3,1},... | collective-permute-start | bytes 835592 | tf_op jit(solution)/shard_map/ppermute | solution.py:187
  102.4 13.7 %collective-permute-start.18 = (bf16[272,512]{1,0:T(8,128)(2,1)S(1)}, bf16[272,512]{1,0:T(8,128)(2,1)S(1)}, u32[]{:S(2)}, u32[]{:S(2)}) collective-permute-start(bf16[272,512]{1,0:T(8,128)(2,1)S(1)} %collective-permute-done.15.refs_0_), channel_id=1, source_target_pairs={{0,2},{2,0},{4,6},{6,4},{8,10},{10,8},{12,14},{14,12},{1,3},{3,1},... | collective-permute-start | bytes 835592 | tf_op jit(solution)/shard_map/ppermute | solution.py:187
  107.0 28.0 %collective-permute-start.31 = (f32[512]{0:T(512)S(1)}, f32[512]{0:T(512)S(1)}, u32[]{:S(2)}, u32[]{:S(2)}) collective-permute-start(f32[512]{0:T(512)S(1)} %div.7), channel_id=1, source_target_pairs={{0,1},{1,0},{2,3},{3,2},{4,5},{5,4},{6,7},{7,6},{8,9},{9,8},{10,11... | collective-permute-start | bytes 6152 | tf_op jit(solution)/shard_map/ppermute | solution.py:186
  134.3 5.2 %collective-permute-start.22 = (bf16[128,3584]{1,0:T(8,128)(2,1)S(1)}, bf16[128,3584]{1,0:T(8,128)(2,1)S(1)}, u32[]{:S(2)}, u32[]{:S(2)}) collective-permute-start(bf16[128,3584]{1,0:T(8,128)(2,1)S(1)} %get-tuple-element.31), channel_id=1, source_target_pairs={{0,1},{1,0},{2,3},{3,2},{4,5},{5,4},{6,7},{7,6},{8,9},{9,8},{10,11... | collective-permute-start | bytes 2752520 | tf_op jit(solution)/shard_map/ppermute | solution.py:186
  134.3 4.3 %collective-permute-start.13 = (bf16[128,512]{1,0:T(8,128)(2,1)S(1)}, bf16[128,512]{1,0:T(8,128)(2,1)S(1)}, u32[]{:S(2)}, u32[]{:S(2)}) collective-permute-start(bf16[128,512]{1,0:T(8,128)(2,1)S(1)} %get-tuple-element.39), channel_id=1, source_target_pairs={{0,1},{1,0},{2,3},{3,2},{4,5},{5,4},{6,7},{7,6},{8,9},{9,8},{10,11... | collective-permute-start | bytes 393224 | tf_op jit(solution)/shard_map/ppermute | solution.py:186
  134.8 2.2 %collective-permute-start.24 = (f32[128,64]{1,0:T(8,128)S(1)}, f32[128,64]{1,0:T(8,128)S(1)}, u32[]{:S(2)}, u32[]{:S(2)}) collective-permute-start(f32[128,64]{1,0:T(8,128)S(1)} %get-tuple-element.32), channel_id=1, source_target_pairs={{0,1},{1,0},{2,3},{3,2},{4,5},{5,4},{6,7},{7,6},{8,9},{9,8},{10,11... | collective-permute-start | bytes 98312 | tf_op jit(solution)/shard_map/ppermute | solution.py:186
  135.6 1.7 %collective-permute-start.23 = (f32[128,64]{1,0:T(8,128)S(1)}, f32[128,64]{1,0:T(8,128)S(1)}, u32[]{:S(2)}, u32[]{:S(2)}) collective-permute-start(f32[128,64]{1,0:T(8,128)S(1)} %get-tuple-element.33), channel_id=1, source_target_pairs={{0,1},{1,0},{2,3},{3,2},{4,5},{5,4},{6,7},{7,6},{8,9},{9,8},{10,11... | collective-permute-start | bytes 98312 | tf_op jit(solution)/shard_map/ppermute | solution.py:186
  137.3 2.1 %copy-start.6 = (f32[128,3584]{1,0:T(8,128)S(1)}, f32[128,3584]{1,0:T(8,128)}, u32[]{:S(2)}) copy-start(f32[128,3584]{1,0:T(8,128)} %get-tuple-element.30) | copy-start | bytes 5505028

commit v2 on v0

v2 whole, which is shorter than its diff:
```python
import functools

import jax
import jax.numpy as jnp
from jax import lax
from jax.experimental import pallas as pl
from jax.experimental.pallas import tpu as pltpu
from jax.sharding import PartitionSpec as P

adapter_scale = 2.0
stability_floor = 1e-06
pad_rows = 16
vmem_bytes = 28 * 1024 * 1024
f32, bf16 = jnp.float32, jnp.bfloat16
small_cost = pl.CostEstimate(flops=1 << 20, bytes_accessed=1 << 20, transcendentals=0)
contract_trailing = (((1,), (1,)), ((), ()))
contract_first = (((0,), (0,)), ((), ()))


def dot(a, b, dims=(((1,), (0,)), ((), ()))):
    return lax.dot_general(a, b, dims, preferred_element_type=f32)


def split_pair(x):
    high = x.astype(bf16)
    return high, (x - high.astype(f32)).astype(bf16)


def sum_of_squares(w_ref):
    rows, width = w_ref.shape
    totals = [jnp.zeros((8, width), f32) for _ in range(2)]
    for i in range(rows // 16):
        w = w_ref[i * 16 : (i + 1) * 16, :].astype(f32)
        w = w * w
        totals[0] = totals[0] + w[:8]
        totals[1] = totals[1] + w[8:]
    return jnp.sum(totals[0] + totals[1], axis=0, keepdims=True)


def vmem():
    return pl.BlockSpec(memory_space=pltpu.VMEM)


def params():
    return pltpu.CompilerParams(vmem_limit_bytes=vmem_bytes)


def block_kernel(tokens, core_ref, own_ref, other_ref, magnitude_ref, out_ref):
    out_ref[:tokens, :] = own_ref[...]
    out_ref[tokens : 2 * tokens, :] = other_ref[...]
    out_ref[2 * tokens :, :] = magnitude_ref[...]


def own_block(core, cotangent, other, magnitude_rows):
    tokens, columns = cotangent.shape
    half = columns // 2
    padded = 2 * tokens + pad_rows
    return pl.pallas_call(
        functools.partial(block_kernel, tokens),
        grid_spec=pltpu.PrefetchScalarGridSpec(
            num_scalar_prefetch=1,
            grid=(1,),
            in_specs=[
                pl.BlockSpec((tokens, half), lambda i, c: (0, c[0])),
                pl.BlockSpec((tokens, half), lambda i, c: (0, c[0])),
                pl.BlockSpec((pad_rows, half), lambda i, c: (0, c[0])),
            ],
            out_specs=pl.BlockSpec((padded, half), lambda i, c: (0, 0)),
        ),
        out_shape=jax.ShapeDtypeStruct((padded, half), bf16),
        cost_estimate=small_cost,
        name="own_block",
    )(core, cotangent, other, magnitude_rows)


def forward_kernel(tokens, rank, n, first, place_ref, *refs):
    if first:
        own_ref, other_ref, at_ref, b_ref, w_ref, out_ref, stats_ref, lhs_ref, adapter_ref = refs[:-3]
    else:
        lhs_ref, adapter_ref, before_ref, b_ref, w_ref, out_ref, stats_ref = refs[:-3]
    acc_ref, squares_ref, sem = refs[-3:]
    block, step = pl.program_id(0), pl.program_id(1)
    blocks, steps = pl.num_programs(0), pl.num_programs(1)
    both = 2 * tokens
    half = acc_ref.shape[1]
    depth = w_ref.shape[0]

    @pl.when((block == 0) & (step == 0))
    def _():
        if first:
            spans = [(own_ref, 0, tokens), (other_ref, tokens, tokens), (at_ref, both, rank)]
            copies = [
                pltpu.make_async_copy(ref, lhs_ref.at[start : start + size], sem.at[i])
                for i, (ref, start, size) in enumerate(spans)
            ]
            for copy in copies:
                copy.start()
            for copy in copies:
                copy.wait()
            lowrank = dot(lhs_ref[...], lhs_ref[both:, :], contract_trailing)
            high, low = split_pair(lowrank)
            adapter_ref[:, :rank] = high
            adapter_ref[:, rank:] = low
            turned = lowrank[:tokens].T
            lanes = half // tokens
            span = rank // lanes
            stats_ref[:n, :] = jnp.zeros((n, half), f32)
            for j in range(lanes):
                stats_ref[n:, j * tokens : (j + 1) * tokens] = turned[j * span : (j + 1) * span]
        else:
            stats_ref[...] = before_ref[...]

    columns = pl.ds(pl.multiple_of(step * depth, depth), depth)
    product = dot(lhs_ref[:, columns], w_ref[...])
    squares = sum_of_squares(w_ref)

    @pl.when(step == 0)
    def _():
        acc_ref[...] = product
        squares_ref[...] = squares

    @pl.when((step > 0) & (step < steps - 1))
    def _():
        acc_ref[...] += product
        squares_ref[...] += squares

    @pl.when(step == steps - 1)
    def _():
        up = b_ref[:, pl.ds(pl.multiple_of(place_ref[block] * half, half), half)]
        through = dot(adapter_ref[...], jnp.concatenate([up, up], axis=0))
        total = acc_ref[...] + product
        out_ref[0] = (total[:both] + adapter_scale * through[:both]).astype(bf16)
        cross = up.astype(f32) * (2 * adapter_scale * total[both:] + adapter_scale * adapter_scale * through[both:])
        stats_ref[pl.ds(place_ref[blocks + block], 1), :] = (
            squares_ref[...] + squares + jnp.sum(cross, axis=0, keepdims=True)
        )


def forward(n, place, weight, up, half, first=None, later=None):
    blocks = place.shape[0] // 2
    rows = weight.shape[0]
    steps = 2
    if later is None:
        own, other, at = first
        tokens, rank = own.shape[0], at.shape[0]
        operands = [own, other, at]
        specs = [pl.BlockSpec(memory_space=m) for m in (pltpu.HBM, pl.ANY, pltpu.HBM)]
    else:
        lhs, adapter, before = operands = later
        rank = adapter.shape[1] // 2
        tokens = (lhs.shape[0] - rank) // 2
        specs = [vmem()] * 3
    stats = (n + rank * tokens // half, half)
    extra = [((2 * tokens + rank, rows), bf16), ((2 * tokens + rank, 2 * rank), bf16)] if first else []
    return pl.pallas_call(
        functools.partial(forward_kernel, tokens, rank, n, later is None),
        grid_spec=pltpu.PrefetchScalarGridSpec(
            num_scalar_prefetch=1,
            grid=(blocks, steps),
            in_specs=specs
            + [
                vmem(),
                pl.BlockSpec((rows // steps, half), lambda i, j, p: (j, p[i])),
            ],
            out_specs=[pl.BlockSpec((1, 2 * tokens, half), lambda i, j, p: (i, 0, 0)), vmem()] + [vmem()] * len(extra),
            scratch_shapes=[
                pltpu.VMEM((2 * tokens + rank, half), f32),
                pltpu.VMEM((1, half), f32),
                pltpu.SemaphoreType.DMA((3,)),
            ],
        ),
        out_shape=[jax.ShapeDtypeStruct((blocks, 2 * tokens, half), bf16), jax.ShapeDtypeStruct(stats, f32)]
        + [jax.ShapeDtypeStruct(*e) for e in extra],
        compiler_params=params(),
        cost_estimate=small_cost,
        name="forward",
    )(place, *operands, up, weight)


def backward_kernel(tokens, n, first, place_ref, *refs):
    if first:
        cots, (stats_ref, b_ref) = refs[:n], refs[n : n + 2]
        at_ref, *w_refs = refs[n + 2 : 2 * n + 3]
        own_out, other_out, scaled_ref, proj_ref = refs[2 * n + 3 :]
    else:
        scaled_ref, proj_ref, at_ref, *w_refs = refs[: n + 3]
        own_out, other_out = refs[n + 3 :]
    both = 2 * tokens
    half = w_refs[0].shape[1]
    spans = [slice(k * half, (k + 1) * half) for k in range(n)]

    if first:

        @pl.when(pl.program_id(0) == 0)
        def _():
            projected = jnp.zeros(proj_ref.shape, f32)
            for k in range(n):
                magnitude = jnp.sum(cots[k][both:, :].astype(f32), axis=0, keepdims=True)
                squares = stats_ref[pl.ds(place_ref[n + k], 1), :]
                rescale = magnitude / jnp.sqrt(squares + stability_floor)
                scaled = (cots[k][:both, :].astype(f32) * rescale).astype(bf16)
                scaled_ref[:, spans[k]] = scaled
                up = b_ref[:, pl.ds(pl.multiple_of(place_ref[k] * half, half), half)]
                projected = projected + dot(scaled, up, contract_trailing)
            proj_ref[...] = projected

    total = adapter_scale * dot(proj_ref[...].astype(bf16), at_ref[...])
    for k in range(n):
        total = total + dot(scaled_ref[:, spans[k]], w_refs[k][...], contract_trailing)
    own_out[...] = total[:tokens]
    other_out[...] = total[tokens:].astype(bf16)


def backward(place, start, bands, band, at, weight, half, first=None, later=None):
    n = place.shape[0] // 2
    rank, rows = at.shape
    if later is None:
        cots, stats, up = first
        both = cots[0].shape[0] - pad_rows
        operands, specs = [*cots, stats, up], [vmem()] * (n + 2)
        extra = [((both, n * half), bf16), ((both, rank), f32)]
    else:
        operands, specs, extra = later, [vmem()] * 2, []
        both = later[0].shape[0]
    tokens = both // 2
    part = lambda k: pl.BlockSpec((band, half), lambda i, p: (start + i, p[k]))
    return pl.pallas_call(
        functools.partial(backward_kernel, tokens, n, later is None),
        grid_spec=pltpu.PrefetchScalarGridSpec(
            num_scalar_prefetch=1,
            grid=(bands,),
            in_specs=specs
            + [pl.BlockSpec((rank, band), lambda i, p: (0, start + i))]
            + [part(k) for k in range(n)],
            out_specs=[pl.BlockSpec((tokens, band), lambda i, p: (0, i))] * 2 + [vmem()] * len(extra),
        ),
        out_shape=[
            jax.ShapeDtypeStruct((tokens, bands * band), f32),
            jax.ShapeDtypeStruct((tokens, bands * band), bf16),
        ]
        + [jax.ShapeDtypeStruct(*e) for e in extra],
        compiler_params=params(),
        cost_estimate=small_cost,
        name="backward",
    )(place, *operands, at, *[weight] * n)


def split_columns(hidden, weight, down, up, magnitude, cotangent):
    n, bits = 8, 3
    tokens = hidden.shape[0]
    half = magnitude.shape[0] // 2
    rows = weight.shape[0]
    me, core = lax.axis_index("tensor"), lax.axis_index("dp")
    swap = lambda x: lax.ppermute(x, "dp", [(0, 1), (1, 0)])
    orders = [[1, 2, 4], [2, 1, 4]]

    def send(x, k):
        pairs = [(2 * t + c, 2 * (t ^ orders[c][k]) + c) for t in range(n) for c in range(2)]
        return lax.ppermute(x, ("tensor", "dp"), pairs)

    def reach(v, c):
        return sum(orders[c][k] for k in range(bits) if v >> (bits - 1 - k) & 1)

    def place(*vs):
        shard = [me ^ jnp.where(core == 0, reach(v, 0), reach(v, 1)) for v in vs]
        return jnp.stack([2 * s + core for s in shard] + shard).astype(jnp.int32)

    mine = lambda x, axis: lax.dynamic_slice_in_dim(x, core * half, half, axis)
    at = down.T
    tie = lax.optimization_barrier

    cot_other = swap(cotangent)
    hidden_other = swap(hidden)
    first = lax.reduce_precision(magnitude, 8, 7)
    second = lax.reduce_precision(magnitude - first, 8, 7)
    third = magnitude - first - second
    magnitude_rows = jnp.concatenate(
        [jnp.stack([first, second, third]), jnp.zeros((pad_rows - 3, 2 * half), f32)]
    ).astype(bf16)
    block = own_block(core.astype(jnp.int32).reshape(1), cotangent, cot_other, magnitude_rows)

    cots = {0b000: block, 0b001: send(block, 2), 0b010: send(block, 1), 0b100: send(block, 0)}
    run = functools.partial(forward, n, weight=weight, up=up, half=half)

    far1, stats, lhs, adapter = run(place(0b110, 0b111), first=(hidden, hidden_other, at))
    from1 = send(far1, 0)
    far0, stats = run(place(0b100, 0b101), later=(lhs, adapter, stats))
    from0 = send(far0, 0)
    *got, stats = tie((*(cots[v] for v in (0b001, 0b010, 0b100)), stats))
    cots[0b001], cots[0b010], cots[0b100] = got
    cots[0b011], cots[0b101], cots[0b110] = send(cots[0b001], 1), send(cots[0b001], 0), send(cots[0b010], 0)
    near1, stats = run(place(0b010, 0b011), later=(lhs, adapter, stats))
    cots[0b011], from1, stats = tie((cots[0b011], from1, stats))
    cots[0b111] = send(cots[0b011], 0)
    sent = (near1.astype(f32) + from1.astype(f32)).astype(bf16)
    arrived = send(sent, 1)
    near0, stats = run(place(0b000, 0b001), later=(lhs, adapter, stats))
    cots[0b101], cots[0b110], from0, stats = tie((cots[0b101], cots[0b110], from0, stats))

    stats = stats + send(stats, 0)
    stats = stats + send(stats, 1)
    arrived, cots[0b111], stats = tie((arrived, cots[0b111], stats))
    kept = near0.astype(f32) + from0.astype(f32) + arrived.astype(f32)
    last = send(kept[1].astype(bf16), 2)
    stats = stats + send(stats, 2)
    lowrank_rows = stats[n:]
    lowrank_other = swap(lowrank_rows)

    band = 256
    bands = rows // band
    many = (bands + 2) // 2
    order = place(*range(n))
    grad_a, other_a, scaled, proj = backward(
        order, 0, many, band, at, weight, half, first=([cots[v] for v in range(n)], stats, up)
    )
    got_a = swap(other_a)
    last, proj = tie((last, proj))
    unscaled = kept[0] + last.astype(f32)
    grad_b, other_b = backward(order, many, bands - many, band, at, weight, half, later=(scaled, proj))
    got_b = swap(other_b)
    hidden_gradient = jnp.concatenate(
        [(own + got.astype(f32)).astype(bf16) for own, got in ((grad_a, got_a), (grad_b, got_b))], axis=1
    )
    from_sibling = swap(proj)
    proj_own = (proj[:tokens] + from_sibling[tokens:]).astype(bf16)
    proj_other = (proj[tokens:] + from_sibling[:tokens]).astype(bf16)
    down_weight_gradient = adapter_scale * (
        dot(proj_own, hidden, contract_first) + dot(proj_other, hidden_other, contract_first)
    ).T

    norm = jnp.sqrt(lax.dynamic_slice_in_dim(stats, me, 1, 0)[0] + stability_floor)
    rescale = mine(magnitude, 0) / norm
    upstream = block[: 2 * tokens].astype(f32)
    scaled_own = (upstream * rescale).astype(bf16).astype(f32)

    def turned(part):
        lanes = half // tokens
        return jnp.concatenate([part[:, j * tokens : (j + 1) * tokens] for j in range(lanes)])

    up_half = adapter_scale * (
        jnp.dot(turned(lowrank_rows), scaled_own[:tokens], precision=lax.Precision.HIGHEST)
        + jnp.dot(turned(lowrank_other), scaled_own[tokens:], precision=lax.Precision.HIGHEST)
    )
    mixed = (unscaled * rescale).astype(bf16)
    magnitude_half = jnp.sum(upstream * unscaled, axis=0) / norm

    def join(own, other, axis):
        pair = jnp.concatenate([own, other, own], axis)
        return lax.dynamic_slice_in_dim(pair, core * half, 2 * half, axis)

    mixed = join(mixed[:tokens], swap(mixed[tokens:]), 1)
    up_weight_gradient = join(up_half, swap(up_half), 1)
    grad_magnitude = join(magnitude_half, swap(magnitude_half), 0)
    return (mixed, hidden_gradient, down_weight_gradient, up_weight_gradient, grad_magnitude)


def by_tokens(hidden, frozen_down_weight, adapter_down_weight, adapter_up_weight, magnitude, cotangent):
    column_slice = magnitude.shape[0]
    block_offset = lax.axis_index("tensor") * column_slice
    combined_weight = frozen_down_weight.astype(f32) + adapter_scale * dot(adapter_down_weight, adapter_up_weight)
    squares_part = jnp.sum(combined_weight * combined_weight, axis=0)
    squares, reduced_rank_product = lax.psum((squares_part, dot(hidden, adapter_down_weight)), "tensor")
    norm_all = jnp.sqrt(squares + stability_floor)
    column_length_norm = lax.dynamic_slice_in_dim(norm_all, block_offset, column_slice)
    up_weight_columns = lax.dynamic_slice_in_dim(adapter_up_weight, block_offset, column_slice, 1)
    summed_output = lax.psum_scatter(dot(hidden, frozen_down_weight), "tensor", scatter_dimension=1, tiled=True)
    unscaled_output = summed_output + adapter_scale * jnp.dot(
        reduced_rank_product, up_weight_columns.astype(f32), precision=lax.Precision.HIGHEST
    )
    rescale = magnitude / column_length_norm
    mixed = (unscaled_output * rescale).astype(bf16)
    upstream = cotangent.astype(f32)
    scaled_output = (upstream * rescale).astype(bf16)
    magnitude_part = jnp.sum(upstream * unscaled_output, axis=0) / column_length_norm
    block_input = lax.all_gather(scaled_output, "tensor", axis=1, tiled=True)
    projected_output = dot(block_input, adapter_up_weight, contract_trailing).astype(bf16)
    hidden_gradient = dot(block_input, frozen_down_weight, contract_trailing)
    hidden_gradient = hidden_gradient + adapter_scale * dot(projected_output, adapter_down_weight, contract_trailing)
    hidden_gradient = hidden_gradient.astype(bf16)
    down_gradient_piece = adapter_scale * dot(hidden, projected_output, contract_first)
    up_gradient_piece = adapter_scale * lax.dot_general(
        reduced_rank_product, scaled_output.astype(f32), contract_first, precision=lax.Precision.HIGHEST
    )
    pieces = (down_gradient_piece, up_gradient_piece, magnitude_part)
    pieces = [lax.psum(p.astype(bf16), "dp").astype(f32) for p in pieces]
    return (mixed, hidden_gradient, *pieces)


def solution(mesh):
    n = mesh.shape["tensor"]

    def local(hidden, weight, down, up, magnitude, cotangent):
        aligned = magnitude.shape[0] % 256 == 0 and weight.shape[0] % 256 == 0 and hidden.shape[0] % 128 == 0
        if aligned and mesh.shape["dp"] == 2 and n == 8 and down.shape[1] * hidden.shape[0] % (magnitude.shape[0] // 2 * 8) == 0:
            return split_columns(hidden, weight, down, up, magnitude, cotangent)
        return by_tokens(hidden, weight, down, up, magnitude, cotangent)

    in_specs = (
        P(("parts", "dp"), "tensor"),
        P("tensor", None),
        P(("parts", "tensor"), None),
        P("parts", None),
        P(("parts", "tensor")),
        P(("parts", "dp"), "tensor"),
    )
    out_specs = (
        P(("parts", "dp"), "tensor"),
        P(("parts", "dp"), "tensor"),
        P(("parts", "tensor"), None),
        P("parts", "tensor"),
        P(("parts", "tensor")),
    )
    return jax.shard_map(local, mesh=mesh, in_specs=in_specs, out_specs=out_specs, check_vma=False)
```

time: 297 us -> 109 us (0.37)
  waiting for transfers between devices: 184 us -> 13 us
  matrix products: 89.8 us -> 1.95 us
  Pallas kernels: 0 us -> 51.6 us
  starting transfers between devices: 0.16 us -> 21.9 us
  between operations: 13.8 us -> 1.02 us
  local copies, waits for them, and re-layouts: 0.02 us -> 9.33 us
  other arithmetic: 5.61 us -> 8.77 us
    reduce_scatter x1 -> x0, waiting for transfers between devices: 91.2 us -> none  [local(): lax.psum_scatter(partial_terms, 'tensor', scatter_dimension=1, tiled=True)]
    dot_general x9 -> x4, matrix products: 89.8 us -> 1.95 us  [the longest x2 1.56 us: dot(): return lax.dot_general(a, b, dims, preferred_element_type=f32)]
    pallas_call x0 -> x7, Pallas kernels: none -> 51.6 us  [the longest x4 28.7 us: forward(): pl.pallas_call(functools.partial(forward_kernel, tokens, rank, n, later i...]
    psum x2 -> x0, waiting for transfers between devices: 48.9 us -> none  [the longest x1 48.9 us: local(): lax.psum((squares_part, reduced_rank_piece), 'tensor')]
    all_gather x1 -> x0, waiting for transfers between devices: 43.8 us -> none  [local(): block_input = lax.all_gather(scaled_output, 'tensor', axis=1, tiled=True)]
    ppermute x0 -> x23, starting transfers between devices: none -> 21.9 us  [the longest x14 19.5 us: send(): return lax.ppermute(x, ('tensor', 'dp'), pairs)]
    ppermute x0 -> x23, waiting for transfers between devices: none -> 13 us  [the longest x14 9.81 us: send(): return lax.ppermute(x, ('tensor', 'dp'), pairs)]
    unnamed x10 -> x44, local copies, waits for them, and re-layouts: 0.02 us -> 8.48 us
  transfers between devices with their start and end apart: 4 -> 23, of which waited for: 3 -> 7; matrix products, arithmetic and copies ran while one was open for 19% -> 10% of each run, Pallas kernels for 0% -> 48%
where the time goes in v2:
time: 109 us; the launch traced here: 108 us
  Pallas kernels  51.6 us (47%)
  starting transfers between devices  21.9 us (20%)
  waiting for transfers between devices  13 us (12%)
  local copies, waits for them, and re-layouts  9.33 us (9%)
  other arithmetic  8.77 us (8%)
  matrix products  1.95 us (2%)
    pallas_call x4, Pallas kernels, forward(): pl.pallas_call(functools.partial(forward_kernel, tokens, rank, n, later i...  28.7 us
    pallas_call x2, Pallas kernels, backward(): pl.pallas_call(functools.partial(backward_kernel, tokens, n, later is Non...  21.2 us
    ppermute x14, starting transfers between devices, send(): return lax.ppermute(x, ('tensor', 'dp'), pairs)  19.5 us
    ppermute x14, waiting for transfers between devices, send(): return lax.ppermute(x, ('tensor', 'dp'), pairs)  9.81 us
    unnamed x44, local copies, waits for them, and re-layouts  8.48 us
    ppermute x9, waiting for transfers between devices, split_columns(): swap = lambda x: lax.ppermute(x, 'dp', [(0, 1), (1, 0)])  3.22 us
    ppermute x9, starting transfers between devices, split_columns(): swap = lambda x: lax.ppermute(x, 'dp', [(0, 1), (1, 0)])  2.46 us
    concatenate x3, other arithmetic, join(): pair = jnp.concatenate([own, other, own], axis)  2.27 us
  transfers between devices with their start and end apart: 23, of which 7 were waited for; matrix products, arithmetic and copies ran while one was open for 10% of the time, Pallas kernels for 48%

profile of v2, /device:TPU:0, one launch (start us, length us, event | category | flops | bytes accessed | tf_op | source)
XLA Modules:
  0.0 107.7 jit_solution(12045175826525230328)
XLA Ops:
  0.6 0.5 collective-permute-start
  1.1 0.1 collective-permute-start.1
  1.2 0.7 reduce-precision_convert_fusion.1
  2.0 0.1 pad.30.clone
  2.1 0.7 maximum_maximum_fusion.magnitude_ref
  2.8 1.1 %collective-permute-done.1.other_ref = bf16[128,1024]{1,0:T(8,128)(2,1)S(1)} collective-permute-done((bf16[128,1024]{1,0:T(8,128)(2,1)}, bf16[128,1024]{1,0:T(8,128)(2,1)S(1)}, u32[]{:S(2)}, u32[]{:S(2)}) %collective-permute-start.1) | collective-permute-done | bytes 262176 | tf_op jit(solution)/shard_map/ppermute | solution.py:254
  3.8 0.7 copy-done.16
  4.5 1.7 %own_block.1.refs_0_ = bf16[272,512]{1,0:T(8,128)(2,1)} custom-call(s32[1]{0:T(128)} %bitcast.9.core_ref, bf16[128,1024]{1,0:T(8,128)(2,1)} %own_ref.1, bf16[128,1024]{1,0:T(8,128)(2,1)} %copy-done.16, bf16[16,1024]{1,0:T(8,128)(2,1)} %maximum_maximum_fusion.magnitude_ref), custom_call_target="tpu_custom_call" | custom-call | flops 1048576 | bytes 1048576 | tf_op jit(solution)/shard_map/own_block/pallas_call | solution.py:58
  6.2 4.0 %collective-permute-start.2 = (bf16[272,512]{1,0:T(8,128)(2,1)}, bf16[272,512]{1,0:T(8,128)(2,1)}, u32[]{:S(2)}, u32[]{:S(2)}) collective-permute-start(bf16[272,512]{1,0:T(8,128)(2,1)} %own_block.1.refs_0_), channel_id=1, source_target_pairs={{0,8},{1,9},{2,10},{3,11},{4,12},{5,13},{6,14},{7,15},{8,0},{9,1},... | collective-permute-start | bytes 835592 | tf_op jit(solution)/shard_map/ppermute | solution.py:259
  10.2 1.6 %collective-permute-start.3 = (bf16[272,512]{1,0:T(8,128)(2,1)}, bf16[272,512]{1,0:T(8,128)(2,1)}, u32[]{:S(2)}, u32[]{:S(2)}) collective-permute-start(bf16[272,512]{1,0:T(8,128)(2,1)} %own_block.1.refs_0_), channel_id=1, source_target_pairs={{0,4},{1,3},{2,6},{3,1},{4,0},{5,7},{6,2},{7,5},{8,12},{9,11},{10,... | collective-permute-start | bytes 835592 | tf_op jit(solution)/shard_map/ppermute | solution.py:259
  11.8 1.5 %collective-permute-start.4 = (bf16[272,512]{1,0:T(8,128)(2,1)}, bf16[272,512]{1,0:T(8,128)(2,1)}, u32[]{:S(2)}, u32[]{:S(2)}) collective-permute-start(bf16[272,512]{1,0:T(8,128)(2,1)} %own_block.1.refs_0_), channel_id=1, source_target_pairs={{0,2},{1,5},{2,0},{3,7},{4,6},{5,1},{6,4},{7,3},{8,10},{9,13},{10,... | collective-permute-start | bytes 835592 | tf_op jit(solution)/shard_map/ppermute | solution.py:259
  13.3 0.1 pad_add_fusion
  13.4 0.9 copy-done.6
  14.3 1.2 %copy-done = bf16[64,8192]{1,0:T(8,128)(2,1)S(1)} copy-done((bf16[64,8192]{1,0:T(8,128)(2,1)S(1)}, bf16[64,8192]{1,0:T(8,128)(2,1)}, u32[]{:S(2)}) %copy-start) | copy-done | bytes 1048600
  15.5 1.0 copy-done.2
  16.5 1.2 %copy-done.4 = bf16[128,3584]{1,0:T(8,128)(2,1)S(1)} copy-done((bf16[128,3584]{1,0:T(8,128)(2,1)S(1)}, bf16[128,3584]{1,0:T(8,128)(2,1)}, u32[]{:S(2)}) %copy-start.4) | copy-done | bytes 917528
  17.7 1.2 %copy-done.7 = bf16[128,3584]{1,0:T(8,128)(2,1)S(1)} copy-done((bf16[128,3584]{1,0:T(8,128)(2,1)S(1)}, bf16[128,3584]{1,0:T(8,128)(2,1)}, u32[]{:S(2)}) %copy-start.7) | copy-done | bytes 917528
  18.9 8.9 %forward.4 = (bf16[2,256,512]{2,1,0:T(8,128)(2,1)}, f32[24,512]{1,0:T(8,128)S(1)}, bf16[320,3584]{1,0:T(8,128)(2,1)S(1)}, bf16[320,128]{1,0:T(8,128)(2,1)S(1)}) custom-call(s32[4]{0:T(128)S(1)} %get-tuple-element.86.place_ref, bf16[128,3584]{1,0:T(8,128)(2,1)S(1)} %copy-done.4, bf16[128,3584]{1,0:T(8,128)(2,1)S(1)} %copy-done.7, ...), custom_call_target="tpu_custom_call" | custom-call | flops 1048576 | bytes 1048576 | tf_op jit(solution)/shard_map/forward/pallas_call | solution.py:155
  27.8 0.6 collective-permute-start.6
  28.4 0.1 pad_add_fusion.2
  28.5 6.6 %forward.5 = (bf16[2,256,512]{2,1,0:T(8,128)(2,1)S(1)}, f32[24,512]{1,0:T(8,128)S(1)}) custom-call(s32[4]{0:T(128)S(1)} %get-tuple-element.87.place_ref, bf16[320,3584]{1,0:T(8,128)(2,1)S(1)} %get-tuple-element.37.refs_0_, bf16[320,128]{1,0:T(8,128)(2,1)S(1)} %get-tuple-element.38.refs_1_, f32[24,512]{1,0:T(8,128)S(1)} %get-tuple-element.39.refs_2_, ...), custom_call_target="tpu_custom_call" | custom-call | flops 1048576 | bytes 1048576 | tf_op jit(solution)/shard_map/forward/pallas_call | solution.py:155
  35.1 0.5 collective-permute-start.5
  35.6 1.5 %collective-permute-start.9 = (bf16[2,256,512]{2,1,0:T(8,128)(2,1)S(1)}, bf16[2,256,512]{2,1,0:T(8,128)(2,1)S(1)}, u32[]{:S(2)}, u32[]{:S(2)}) collective-permute-start(bf16[2,256,512]{2,1,0:T(8,128)(2,1)S(1)} %get-tuple-element.48), channel_id=1, source_target_pairs={{0,2},{1,5},{2,0},{3,7},{4,6},{5,1},{6,4},{7,3},{8,10},{9,13},{10,... | collective-permute-start | bytes 1572872 | tf_op jit(solution)/shard_map/ppermute | solution.py:259
  37.1 6.6 %forward.6 = (bf16[2,256,512]{2,1,0:T(8,128)(2,1)S(1)}, f32[24,512]{1,0:T(8,128)S(1)}) custom-call(s32[4]{0:T(128)S(1)} %get-tuple-element.88.place_ref, bf16[320,3584]{1,0:T(8,128)(2,1)S(1)} %get-tuple-element.37.refs_0_, bf16[320,128]{1,0:T(8,128)(2,1)S(1)} %get-tuple-element.38.refs_1_, f32[24,512]{1,0:T(8,128)S(1)} %get-tuple-element.43.refs_2_, ...), custom_call_target="tpu_custom_call" | custom-call | flops 1048576 | bytes 1048576 | tf_op jit(solution)/shard_map/forward/pallas_call | solution.py:155
  43.7 1.4 %collective-permute-done.5.refs_3_ = bf16[272,512]{1,0:T(8,128)(2,1)} collective-permute-done((bf16[272,512]{1,0:T(8,128)(2,1)}, bf16[272,512]{1,0:T(8,128)(2,1)}, u32[]{:S(2)}, u32[]{:S(2)}) %collective-permute-start.5) | collective-permute-done | bytes 278560 | tf_op jit(solution)/shard_map/ppermute | solution.py:259
  45.1 2.0 %add_convert_fusion.1 = bf16[2,256,512]{2,1,0:T(8,128)(2,1)} fusion(bf16[2,256,512]{2,1,0:T(8,128)(2,1)} %collective-permute-done.6, bf16[2,256,512]{2,1,0:T(8,128)(2,1)S(1)} %get-tuple-element.51), kind=kLoop, calls=%fused_computation.7 | loop fusion | flops 1048576 | bytes 1572864 | tf_op jit(solution)/shard_map/convert_element_type | solution.py:295
  47.1 0.4 collective-permute-start.10
  47.4 1.5 %collective-permute-start.7 = (bf16[272,512]{1,0:T(8,128)(2,1)}, bf16[272,512]{1,0:T(8,128)(2,1)S(1)}, u32[]{:S(2)}, u32[]{:S(2)}) collective-permute-start(bf16[272,512]{1,0:T(8,128)(2,1)} %collective-permute-done.2.refs_1_), channel_id=1, source_target_pairs={{0,2},{1,5},{2,0},{3,7},{4,6},{5,1},{6,4},{7,3},{8,10},{9,13},{10,... | collective-permute-start | bytes 835592 | tf_op jit(solution)/shard_map/ppermute | solution.py:259
  48.9 0.5 collective-permute-start.8
  49.5 1.5 %collective-permute-start.11 = (bf16[272,512]{1,0:T(8,128)(2,1)}, bf16[272,512]{1,0:T(8,128)(2,1)}, u32[]{:S(2)}, u32[]{:S(2)}) collective-permute-start(bf16[272,512]{1,0:T(8,128)(2,1)} %collective-permute-done.5.refs_3_), channel_id=1, source_target_pairs={{0,2},{1,5},{2,0},{3,7},{4,6},{5,1},{6,4},{7,3},{8,10},{9,13},{10,... | collective-permute-start | bytes 835592 | tf_op jit(solution)/shard_map/ppermute | solution.py:259
  51.0 6.6 %forward.7 = (bf16[2,256,512]{2,1,0:T(8,128)(2,1)S(1)}, f32[24,512]{1,0:T(8,128)S(1)}) custom-call(s32[4]{0:T(128)S(1)} %get-tuple-element.85.place_ref, bf16[320,3584]{1,0:T(8,128)(2,1)S(1)} %get-tuple-element.37.refs_0_, bf16[320,128]{1,0:T(8,128)(2,1)S(1)} %get-tuple-element.38.refs_1_, f32[24,512]{1,0:T(8,128)S(1)} %get-tuple-element.45.refs_2_, ...), custom_call_target="tpu_custom_call" | custom-call | flops 1048576 | bytes 1048576 | tf_op jit(solution)/shard_map/forward/pallas_call | solution.py:155
  57.6 0.8 copy-done.10
  58.4 0.7 copy-done.11
  59.1 0.7 copy-done.13
  59.8 1.2 %collective-permute-start.12 = (f32[24,512]{1,0:T(8,128)S(1)}, f32[24,512]{1,0:T(8,128)S(1)}, u32[]{:S(2)}, u32[]{:S(2)}) collective-permute-start(f32[24,512]{1,0:T(8,128)S(1)} %get-tuple-element.54), channel_id=1, source_target_pairs={{0,2},{1,5},{2,0},{3,7},{4,6},{5,1},{6,4},{7,3},{8,10},{9,13},{10,... | collective-permute-start | bytes 147464 | tf_op jit(solution)/shard_map/ppermute | solution.py:259
  61.0 3.0 %collective-permute-done.12 = f32[24,512]{1,0:T(8,128)S(1)} collective-permute-done((f32[24,512]{1,0:T(8,128)S(1)}, f32[24,512]{1,0:T(8,128)S(1)}, u32[]{:S(2)}, u32[]{:S(2)}) %collective-permute-start.12) | collective-permute-done | bytes 49184 | tf_op jit(solution)/shard_map/ppermute | solution.py:259
  64.0 1.7 %collective-permute-start.13 = (f32[24,512]{1,0:T(8,128)S(1)}, f32[24,512]{1,0:T(8,128)S(1)}, u32[]{:S(2)}, u32[]{:S(2)}) collective-permute-start(f32[24,512]{1,0:T(8,128)S(1)} %add.101), channel_id=1, source_target_pairs={{0,4},{1,3},{2,6},{3,1},{4,0},{5,7},{6,2},{7,5},{8,12},{9,11},{10,... | collective-permute-start | bytes 147464 | tf_op jit(solution)/shard_map/ppermute | solution.py:259
  65.7 0.1 stack.114.place_ref
  65.8 2.3 %collective-permute-done.13 = f32[24,512]{1,0:T(8,128)S(1)} collective-permute-done((f32[24,512]{1,0:T(8,128)S(1)}, f32[24,512]{1,0:T(8,128)S(1)}, u32[]{:S(2)}, u32[]{:S(2)}) %collective-permute-start.13) | collective-permute-done | bytes 49184 | tf_op jit(solution)/shard_map/ppermute | solution.py:259
  68.2 0.4 collective-permute-start.15
  68.6 1.6 %convert_add_fusion = f32[2,256,512]{2,1,0:T(8,128)S(1)} fusion(bf16[2,256,512]{2,1,0:T(8,128)(2,1)} %collective-permute-done.10, bf16[2,256,512]{2,1,0:T(8,128)(2,1)} %copy-done.15, bf16[2,256,512]{2,1,0:T(8,128)(2,1)} %copy-done.10), kind=kLoop, calls=%fused_computation.6 | loop fusion | flops 1310720 | bytes 2621440 | tf_op jit(solution)/shard_map/add | solution.py:303
  70.2 2.7 %collective-permute-start.14 = (bf16[256,512]{1,0:T(8,128)(2,1)S(1)}, bf16[256,512]{1,0:T(8,128)(2,1)S(1)}, u32[]{:S(2)}, u32[]{:S(2)}) collective-permute-start(bf16[256,512]{1,0:T(8,128)(2,1)S(1)} %fusion.10), channel_id=1, source_target_pairs={{0,8},{1,9},{2,10},{3,11},{4,12},{5,13},{6,14},{7,15},{8,0},{9,1},... | collective-permute-start | bytes 786440 | tf_op jit(solution)/shard_map/ppermute | solution.py:259
  72.8 3.1 %collective-permute-done.15 = f32[24,512]{1,0:T(8,128)S(1)} collective-permute-done((f32[24,512]{1,0:T(8,128)S(1)}, f32[24,512]{1,0:T(8,128)S(1)}, u32[]{:S(2)}, u32[]{:S(2)}) %collective-permute-start.15) | collective-permute-done | bytes 49184 | tf_op jit(solution)/shard_map/ppermute | solution.py:259
  75.9 0.6 fusion.39
  76.6 12.5 %backward.2 = (f32[128,2048]{1,0:T(8,128)S(1)}, bf16[128,2048]{1,0:T(8,128)(2,1)S(1)}, bf16[256,4096]{1,0:T(8,128)(2,1)S(1)}, f32[256,64]{1,0:T(8,128)S(1)}) custom-call(s32[16]{0:T(128)S(1)} %stack.114.place_ref, bf16[272,512]{1,0:T(8,128)(2,1)S(1)} %copy-done.9, bf16[272,512]{1,0:T(8,128)(2,1)} %collective-permute-done.2.refs_1_, ...), custom_call_target="tpu_custom_call" | custom-call | flops 1048576 | bytes 1048576 | tf_op jit(solution)/shard_map/backward/pallas_call | solution.py:227
  89.2 0.5 collective-permute-start.20
  89.8 1.4 %collective-permute-done.20 = f32[16,512]{1,0:T(8,128)S(1)} collective-permute-done((f32[16,512]{1,0:T(8,128)S(1)}, f32[16,512]{1,0:T(8,128)S(1)}, u32[]{:S(2)}, u32[]{:S(2)}) %collective-permute-start.20) | collective-permute-done | bytes 32800 | tf_op jit(solution)/shard_map/ppermute | solution.py:254
  91.1 0.2 fusion.4
  91.3 0.2 collective-permute-start.16
  91.5 0.4 collective-permute-start.19
  91.9 8.8 %backward.3 = (f32[128,1536]{1,0:T(8,128)S(1)}, bf16[128,1536]{1,0:T(8,128)(2,1)S(1)}) custom-call(s32[16]{0:T(128)S(1)} %stack.114.place_ref, bf16[256,4096]{1,0:T(8,128)(2,1)S(1)} %get-tuple-element.65.refs_0_, f32[256,64]{1,0:T(8,128)S(1)} %get-tuple-element.66.refs_1_, bf16[64,3584]{1,0:T(8,128)(2,1)S(1)} %bitcast.35, bf16[3584,8192]{1,0:T(8,128)(2,1)} %refs_10_.1, ...), custom_call_target="tpu_custom_call" | custom-call | flops 1048576 | bytes 1048576 | tf_op jit(solution)/shard_map/backward/pallas_call | solution.py:227
  100.7 0.2 collective-permute-start.18
  100.9 0.4 collective-permute-start.22
  101.3 0.2 fusion.11
  101.5 0.2 fusion.2
  101.7 0.8 collective-permute-done.22
  102.5 0.1 collective-permute-start.21
  102.6 0.7 fusion.35
  103.3 0.3 fusion.17
  103.6 1.2 %fusion.1 = f32[3584,64]{0,1:T(8,128)} fusion(f32[64,3584]{1,0:T(8,128)S(1)} %fusion.17, bf16[128,3584]{1,0:T(8,128)(2,1)S(1)} %copy-done.5, f32[256,64]{1,0:T(8,128)S(1)} %collective-permute-done.19, f32[256,64]{1,0:T(8,128)S(1)} %get-tuple-element.66.refs_1_), kind=kOutput, calls=%fused_computation.2 | convolution fusion | flops 59195392 | bytes 2883584 | tf_op jit(solution)/shard_map/dot_general | solution.py:21
  104.9 0.8 fusion.7
  105.6 0.8 fusion.9
  106.5 0.1 add_convert_fusion
  106.7 1.0 pad_maximum_fusion
  (67 shorter events, 0.5 us)
Async XLA Ops:
  0.6 12.7 %collective-permute-start = (bf16[128,3584]{1,0:T(8,128)(2,1)}, bf16[128,3584]{1,0:T(8,128)(2,1)S(1)}, u32[]{:S(2)}, u32[]{:S(2)}) collective-permute-start(bf16[128,3584]{1,0:T(8,128)(2,1)} %refs_0_.1), channel_id=1, source_target_pairs={{0,1},{1,0},{2,3},{3,2},{4,5},{5,4},{6,7},{7,6},{8,9},{9,8},{10,11... | collective-permute-start | bytes 2752520 | tf_op jit(solution)/shard_map/ppermute | solution.py:254
  1.1 2.7 %collective-permute-start.1 = (bf16[128,1024]{1,0:T(8,128)(2,1)}, bf16[128,1024]{1,0:T(8,128)(2,1)S(1)}, u32[]{:S(2)}, u32[]{:S(2)}) collective-permute-start(bf16[128,1024]{1,0:T(8,128)(2,1)} %own_ref.1), channel_id=1, source_target_pairs={{0,1},{1,0},{2,3},{3,2},{4,5},{5,4},{6,7},{7,6},{8,9},{9,8},{10,11... | collective-permute-start | bytes 786440 | tf_op jit(solution)/shard_map/ppermute | solution.py:254
  3.8 0.7 copy-start.16
  6.2 28.9 %collective-permute-start.2 = (bf16[272,512]{1,0:T(8,128)(2,1)}, bf16[272,512]{1,0:T(8,128)(2,1)}, u32[]{:S(2)}, u32[]{:S(2)}) collective-permute-start(bf16[272,512]{1,0:T(8,128)(2,1)} %own_block.1.refs_0_), channel_id=1, source_target_pairs={{0,8},{1,9},{2,10},{3,11},{4,12},{5,13},{6,14},{7,15},{8,0},{9,1},... | collective-permute-start | bytes 835592 | tf_op jit(solution)/shard_map/ppermute | solution.py:259
  10.2 24.9 %collective-permute-start.3 = (bf16[272,512]{1,0:T(8,128)(2,1)}, bf16[272,512]{1,0:T(8,128)(2,1)}, u32[]{:S(2)}, u32[]{:S(2)}) collective-permute-start(bf16[272,512]{1,0:T(8,128)(2,1)} %own_block.1.refs_0_), channel_id=1, source_target_pairs={{0,4},{1,3},{2,6},{3,1},{4,0},{5,7},{6,2},{7,5},{8,12},{9,11},{10,... | collective-permute-start | bytes 835592 | tf_op jit(solution)/shard_map/ppermute | solution.py:259
  11.8 23.3 %collective-permute-start.4 = (bf16[272,512]{1,0:T(8,128)(2,1)}, bf16[272,512]{1,0:T(8,128)(2,1)}, u32[]{:S(2)}, u32[]{:S(2)}) collective-permute-start(bf16[272,512]{1,0:T(8,128)(2,1)} %own_block.1.refs_0_), channel_id=1, source_target_pairs={{0,2},{1,5},{2,0},{3,7},{4,6},{5,1},{6,4},{7,3},{8,10},{9,13},{10,... | collective-permute-start | bytes 835592 | tf_op jit(solution)/shard_map/ppermute | solution.py:259
  13.3 0.9 copy-start.6
  14.3 1.2 %copy-start = (bf16[64,8192]{1,0:T(8,128)(2,1)S(1)}, bf16[64,8192]{1,0:T(8,128)(2,1)}, u32[]{:S(2)}) copy-start(bf16[64,8192]{1,0:T(8,128)(2,1)} %refs_9_.2) | copy-start | bytes 3145732
  15.5 1.0 copy-start.2
  16.5 1.2 %copy-start.4 = (bf16[128,3584]{1,0:T(8,128)(2,1)S(1)}, bf16[128,3584]{1,0:T(8,128)(2,1)}, u32[]{:S(2)}) copy-start(bf16[128,3584]{1,0:T(8,128)(2,1)} %refs_0_.1) | copy-start | bytes 2752516
  17.7 1.2 %copy-start.7 = (bf16[128,3584]{1,0:T(8,128)(2,1)S(1)}, bf16[128,3584]{1,0:T(8,128)(2,1)}, u32[]{:S(2)}) copy-start(bf16[128,3584]{1,0:T(8,128)(2,1)} %copy-done.6) | copy-start | bytes 2752516
  18.9 9.6 %copy-start.1 = (bf16[64,8192]{1,0:T(8,128)(2,1)S(1)}, bf16[64,8192]{1,0:T(8,128)(2,1)}, u32[]{:S(2)}) copy-start(bf16[64,8192]{1,0:T(8,128)(2,1)} %refs_9_.2) | copy-start | bytes 3145732
  27.8 17.3 %collective-permute-start.6 = (bf16[2,256,512]{2,1,0:T(8,128)(2,1)}, bf16[2,256,512]{2,1,0:T(8,128)(2,1)}, u32[]{:S(2)}, u32[]{:S(2)}) collective-permute-start(bf16[2,256,512]{2,1,0:T(8,128)(2,1)} %get-tuple-element.42), channel_id=1, source_target_pairs={{0,2},{1,5},{2,0},{3,7},{4,6},{5,1},{6,4},{7,3},{8,10},{9,13},{10,... | collective-permute-start | bytes 1572872 | tf_op jit(solution)/shard_map/ppermute | solution.py:259
  35.1 10.0 %collective-permute-start.5 = (bf16[272,512]{1,0:T(8,128)(2,1)}, bf16[272,512]{1,0:T(8,128)(2,1)}, u32[]{:S(2)}, u32[]{:S(2)}) collective-permute-start(bf16[272,512]{1,0:T(8,128)(2,1)} %collective-permute-done.2.refs_1_), channel_id=1, source_target_pairs={{0,4},{1,3},{2,6},{3,1},{4,0},{5,7},{6,2},{7,5},{8,12},{9,11},{10,... | collective-permute-start | bytes 835592 | tf_op jit(solution)/shard_map/ppermute | solution.py:259
  35.6 24.1 %collective-permute-start.9 = (bf16[2,256,512]{2,1,0:T(8,128)(2,1)S(1)}, bf16[2,256,512]{2,1,0:T(8,128)(2,1)S(1)}, u32[]{:S(2)}, u32[]{:S(2)}) collective-permute-start(bf16[2,256,512]{2,1,0:T(8,128)(2,1)S(1)} %get-tuple-element.48), channel_id=1, source_target_pairs={{0,2},{1,5},{2,0},{3,7},{4,6},{5,1},{6,4},{7,3},{8,10},{9,13},{10,... | collective-permute-start | bytes 1572872 | tf_op jit(solution)/shard_map/ppermute | solution.py:259
  47.1 21.1 %collective-permute-start.10 = (bf16[2,256,512]{2,1,0:T(8,128)(2,1)}, bf16[2,256,512]{2,1,0:T(8,128)(2,1)}, u32[]{:S(2)}, u32[]{:S(2)}) collective-permute-start(bf16[2,256,512]{2,1,0:T(8,128)(2,1)} %add_convert_fusion.1), channel_id=1, source_target_pairs={{0,4},{1,3},{2,6},{3,1},{4,0},{5,7},{6,2},{7,5},{8,12},{9,11},{10,... | collective-permute-start | bytes 1572872 | tf_op jit(solution)/shard_map/ppermute | solution.py:259
  47.4 10.9 %collective-permute-start.7 = (bf16[272,512]{1,0:T(8,128)(2,1)}, bf16[272,512]{1,0:T(8,128)(2,1)S(1)}, u32[]{:S(2)}, u32[]{:S(2)}) collective-permute-start(bf16[272,512]{1,0:T(8,128)(2,1)} %collective-permute-done.2.refs_1_), channel_id=1, source_target_pairs={{0,2},{1,5},{2,0},{3,7},{4,6},{5,1},{6,4},{7,3},{8,10},{9,13},{10,... | collective-permute-start | bytes 835592 | tf_op jit(solution)/shard_map/ppermute | solution.py:259
  48.9 10.1 %collective-permute-start.8 = (bf16[272,512]{1,0:T(8,128)(2,1)}, bf16[272,512]{1,0:T(8,128)(2,1)S(1)}, u32[]{:S(2)}, u32[]{:S(2)}) collective-permute-start(bf16[272,512]{1,0:T(8,128)(2,1)} %collective-permute-done.3.refs_2_), channel_id=1, source_target_pairs={{0,2},{1,5},{2,0},{3,7},{4,6},{5,1},{6,4},{7,3},{8,10},{9,13},{10,... | collective-permute-start | bytes 835592 | tf_op jit(solution)/shard_map/ppermute | solution.py:259
  49.5 18.7 %collective-permute-start.11 = (bf16[272,512]{1,0:T(8,128)(2,1)}, bf16[272,512]{1,0:T(8,128)(2,1)}, u32[]{:S(2)}, u32[]{:S(2)}) collective-permute-start(bf16[272,512]{1,0:T(8,128)(2,1)} %collective-permute-done.5.refs_3_), channel_id=1, source_target_pairs={{0,2},{1,5},{2,0},{3,7},{4,6},{5,1},{6,4},{7,3},{8,10},{9,13},{10,... | collective-permute-start | bytes 835592 | tf_op jit(solution)/shard_map/ppermute | solution.py:259
  57.6 0.8 copy-start.10
  58.4 18.2 %copy-start.3 = (bf16[3584,64]{0,1:T(8,128)(2,1)S(1)}, bf16[3584,64]{0,1:T(8,128)(2,1)}, u32[]{:S(2)}) copy-start(bf16[3584,64]{0,1:T(8,128)(2,1)} %param.8) | copy-start | bytes 1376260
  58.4 18.2 %copy-start.9 = (bf16[272,512]{1,0:T(8,128)(2,1)S(1)}, bf16[272,512]{1,0:T(8,128)(2,1)}, u32[]{:S(2)}) copy-start(bf16[272,512]{1,0:T(8,128)(2,1)} %own_block.1.refs_0_) | copy-start | bytes 835588
  58.4 0.7 copy-start.11
  59.1 0.7 copy-start.13
  59.8 16.8 %copy-start.12 = (bf16[272,512]{1,0:T(8,128)(2,1)S(1)}, bf16[272,512]{1,0:T(8,128)(2,1)}, u32[]{:S(2)}) copy-start(bf16[272,512]{1,0:T(8,128)(2,1)} %copy-done.11) | copy-start | bytes 835588
  59.8 4.2 %copy-start.15 = (bf16[2,256,512]{2,1,0:T(8,128)(2,1)}, bf16[2,256,512]{2,1,0:T(8,128)(2,1)S(1)}, u32[]{:S(2)}) copy-start(bf16[2,256,512]{2,1,0:T(8,128)(2,1)S(1)} %collective-permute-done.9) | copy-start | bytes 1572868
  59.8 16.8 %copy-start.14 = (bf16[272,512]{1,0:T(8,128)(2,1)S(1)}, bf16[272,512]{1,0:T(8,128)(2,1)}, u32[]{:S(2)}) copy-start(bf16[272,512]{1,0:T(8,128)(2,1)} %copy-done.13) | copy-start | bytes 835588
  59.8 4.2 %collective-permute-start.12 = (f32[24,512]{1,0:T(8,128)S(1)}, f32[24,512]{1,0:T(8,128)S(1)}, u32[]{:S(2)}, u32[]{:S(2)}) collective-permute-start(f32[24,512]{1,0:T(8,128)S(1)} %get-tuple-element.54), channel_id=1, source_target_pairs={{0,2},{1,5},{2,0},{3,7},{4,6},{5,1},{6,4},{7,3},{8,10},{9,13},{10,... | collective-permute-start | bytes 147464 | tf_op jit(solution)/shard_map/ppermute | solution.py:259
  64.0 4.2 %collective-permute-start.13 = (f32[24,512]{1,0:T(8,128)S(1)}, f32[24,512]{1,0:T(8,128)S(1)}, u32[]{:S(2)}, u32[]{:S(2)}) collective-permute-start(f32[24,512]{1,0:T(8,128)S(1)} %add.101), channel_id=1, source_target_pairs={{0,4},{1,3},{2,6},{3,1},{4,0},{5,7},{6,2},{7,5},{8,12},{9,11},{10,... | collective-permute-start | bytes 147464 | tf_op jit(solution)/shard_map/ppermute | solution.py:259
  68.2 7.8 %collective-permute-start.15 = (f32[24,512]{1,0:T(8,128)S(1)}, f32[24,512]{1,0:T(8,128)S(1)}, u32[]{:S(2)}, u32[]{:S(2)}) collective-permute-start(f32[24,512]{1,0:T(8,128)S(1)} %add.102), channel_id=1, source_target_pairs={{0,8},{1,9},{2,10},{3,11},{4,12},{5,13},{6,14},{7,15},{8,0},{9,1},... | collective-permute-start | bytes 147464 | tf_op jit(solution)/shard_map/ppermute | solution.py:259
  70.2 21.0 %collective-permute-start.14 = (bf16[256,512]{1,0:T(8,128)(2,1)S(1)}, bf16[256,512]{1,0:T(8,128)(2,1)S(1)}, u32[]{:S(2)}, u32[]{:S(2)}) collective-permute-start(bf16[256,512]{1,0:T(8,128)(2,1)S(1)} %fusion.10), channel_id=1, source_target_pairs={{0,8},{1,9},{2,10},{3,11},{4,12},{5,13},{6,14},{7,15},{8,0},{9,1},... | collective-permute-start | bytes 786440 | tf_op jit(solution)/shard_map/ppermute | solution.py:259
  76.6 13.1 %copy-start.21 = (f32[1024]{0:T(1024)S(1)}, f32[1024]{0:T(1024)}, u32[]{:S(2)}) copy-start(f32[1024]{0:T(1024)} %param.10) | copy-start | bytes 12292
  89.1 17.4 %collective-permute-start.17 = (bf16[128,2048]{1,0:T(8,128)(2,1)S(1)}, bf16[128,2048]{1,0:T(8,128)(2,1)S(1)}, u32[]{:S(2)}, u32[]{:S(2)}) collective-permute-start(bf16[128,2048]{1,0:T(8,128)(2,1)S(1)} %get-tuple-element.64), channel_id=1, source_target_pairs={{0,1},{1,0},{2,3},{3,2},{4,5},{5,4},{6,7},{7,6},{8,9},{9,8},{10,11... | collective-permute-start | bytes 1572872 | tf_op jit(solution)/shard_map/ppermute | solution.py:254
  89.2 1.9 %collective-permute-start.20 = (f32[16,512]{1,0:T(8,128)S(1)}, f32[16,512]{1,0:T(8,128)S(1)}, u32[]{:S(2)}, u32[]{:S(2)}) collective-permute-start(f32[16,512]{1,0:T(8,128)S(1)} %slice.97), channel_id=1, source_target_pairs={{0,1},{1,0},{2,3},{3,2},{4,5},{5,4},{6,7},{7,6},{8,9},{9,8},{10,11... | collective-permute-start | bytes 98312 | tf_op jit(solution)/shard_map/ppermute | solution.py:254
  91.3 14.3 %collective-permute-start.16 = (bf16[128,512]{1,0:T(8,128)(2,1)S(1)}, bf16[128,512]{1,0:T(8,128)(2,1)S(1)}, u32[]{:S(2)}, u32[]{:S(2)}) collective-permute-start(bf16[128,512]{1,0:T(8,128)(2,1)S(1)} %get-tuple-element.72), channel_id=1, source_target_pairs={{0,1},{1,0},{2,3},{3,2},{4,5},{5,4},{6,7},{7,6},{8,9},{9,8},{10,11... | collective-permute-start | bytes 393224 | tf_op jit(solution)/shard_map/ppermute | solution.py:254
  91.5 11.8 %collective-permute-start.19 = (f32[256,64]{1,0:T(8,128)S(1)}, f32[256,64]{1,0:T(8,128)S(1)}, u32[]{:S(2)}, u32[]{:S(2)}) collective-permute-start(f32[256,64]{1,0:T(8,128)S(1)} %get-tuple-element.66.refs_1_), channel_id=1, source_target_pairs={{0,1},{1,0},{2,3},{3,2},{4,5},{5,4},{6,7},{7,6},{8,9},{9,8},{10,11... | collective-permute-start | bytes 196616 | tf_op jit(solution)/shard_map/ppermute | solution.py:254
  91.9 9.6 %copy-start.17 = (f32[16,128]{1,0:T(8,128)S(1)}, f32[16,128]{1,0:T(8,128)}, u32[]{:S(2)}) copy-start(f32[16,128]{1,0:T(8,128)} %get-tuple-element.74) | copy-start | bytes 24580
  91.9 9.6 %copy-start.18 = (f32[16,128]{1,0:T(8,128)S(1)}, f32[16,128]{1,0:T(8,128)}, u32[]{:S(2)}) copy-start(f32[16,128]{1,0:T(8,128)} %get-tuple-element.75) | copy-start | bytes 24580
  91.9 9.6 %copy-start.19 = (f32[16,128]{1,0:T(8,128)S(1)}, f32[16,128]{1,0:T(8,128)}, u32[]{:S(2)}) copy-start(f32[16,128]{1,0:T(8,128)} %get-tuple-element.76) | copy-start | bytes 24580
  91.9 9.6 %copy-start.20 = (f32[16,128]{1,0:T(8,128)S(1)}, f32[16,128]{1,0:T(8,128)}, u32[]{:S(2)}) copy-start(f32[16,128]{1,0:T(8,128)} %get-tuple-element.77) | copy-start | bytes 24580
  91.9 11.4 %copy-start.8 = (bf16[128,3584]{1,0:T(8,128)(2,1)S(1)}, bf16[128,3584]{1,0:T(8,128)(2,1)}, u32[]{:S(2)}) copy-start(bf16[128,3584]{1,0:T(8,128)(2,1)} %copy-done.6) | copy-start | bytes 2752516
  100.7 2.9 %copy-start.5 = (bf16[128,3584]{1,0:T(8,128)(2,1)S(1)}, bf16[128,3584]{1,0:T(8,128)(2,1)}, u32[]{:S(2)}) copy-start(bf16[128,3584]{1,0:T(8,128)(2,1)} %refs_0_.1) | copy-start | bytes 2752516
  100.7 5.9 %collective-permute-start.18 = (bf16[128,1536]{1,0:T(8,128)(2,1)S(1)}, bf16[128,1536]{1,0:T(8,128)(2,1)S(1)}, u32[]{:S(2)}, u32[]{:S(2)}) collective-permute-start(bf16[128,1536]{1,0:T(8,128)(2,1)S(1)} %get-tuple-element.68), channel_id=1, source_target_pairs={{0,1},{1,0},{2,3},{3,2},{4,5},{5,4},{6,7},{7,6},{8,9},{9,8},{10,11... | collective-permute-start | bytes 1179656 | tf_op jit(solution)/shard_map/ppermute | solution.py:254
  100.9 1.6 %collective-permute-start.22 = (f32[512]{0:T(512)S(1)}, f32[512]{0:T(512)S(1)}, u32[]{:S(2)}, u32[]{:S(2)}) collective-permute-start(f32[512]{0:T(512)S(1)} %div.7), channel_id=1, source_target_pairs={{0,1},{1,0},{2,3},{3,2},{4,5},{5,4},{6,7},{7,6},{8,9},{9,8},{10,11... | collective-permute-start | bytes 6152 | tf_op jit(solution)/shard_map/ppermute | solution.py:254
  102.5 2.4 %collective-permute-start.21 = (f32[64,512]{1,0:T(8,128)S(1)}, f32[64,512]{1,0:T(8,128)S(1)}, u32[]{:S(2)}, u32[]{:S(2)}) collective-permute-start(f32[64,512]{1,0:T(8,128)S(1)} %fusion.2), channel_id=1, source_target_pairs={{0,1},{1,0},{2,3},{3,2},{4,5},{5,4},{6,7},{7,6},{8,9},{9,8},{10,11... | collective-permute-start | bytes 393224 | tf_op jit(solution)/shard_map/ppermute | solution.py:254

commit v3 on v2

--- a/solution.py
+++ b/solution.py
@@ -10,7 +10,7 @@
 adapter_scale = 2.0
 stability_floor = 1e-06
 pad_rows = 16
-vmem_bytes = 28 * 1024 * 1024
+vmem_bytes = 5 * 1024 * 1024
 f32, bf16 = jnp.float32, jnp.bfloat16
 small_cost = pl.CostEstimate(flops=1 << 20, bytes_accessed=1 << 20, transcendentals=0)
 contract_trailing = (((1,), (1,)), ((), ()))
@@ -73,120 +73,117 @@
     )(core, cotangent, other, magnitude_rows)
 
 
-def forward_kernel(tokens, rank, n, first, place_ref, *refs):
-    if first:
-        own_ref, other_ref, at_ref, b_ref, w_ref, out_ref, stats_ref, lhs_ref, adapter_ref = refs[:-3]
-    else:
-        lhs_ref, adapter_ref, before_ref, b_ref, w_ref, out_ref, stats_ref = refs[:-3]
-    acc_ref, squares_ref, sem = refs[-3:]
-    block, step = pl.program_id(0), pl.program_id(1)
-    blocks, steps = pl.num_programs(0), pl.num_programs(1)
-    both = 2 * tokens
-    half = acc_ref.shape[1]
-    depth = w_ref.shape[0]
-
-    @pl.when((block == 0) & (step == 0))
-    def _():
-        if first:
-            spans = [(own_ref, 0, tokens), (other_ref, tokens, tokens), (at_ref, both, rank)]
-            copies = [
-                pltpu.make_async_copy(ref, lhs_ref.at[start : start + size], sem.at[i])
-                for i, (ref, start, size) in enumerate(spans)
-            ]
-            for copy in copies:
-                copy.start()
-            for copy in copies:
-                copy.wait()
-            lowrank = dot(lhs_ref[...], lhs_ref[both:, :], contract_trailing)
-            high, low = split_pair(lowrank)
-            adapter_ref[:, :rank] = high
-            adapter_ref[:, rank:] = low
-            turned = lowrank[:tokens].T
-            lanes = half // tokens
-            span = rank // lanes
-            stats_ref[:n, :] = jnp.zeros((n, half), f32)
-            for j in range(lanes):
-                stats_ref[n:, j * tokens : (j + 1) * tokens] = turned[j * span : (j + 1) * span]
-        else:
-            stats_ref[...] = before_ref[...]
-
-    columns = pl.ds(pl.multiple_of(step * depth, depth), depth)
-    product = dot(lhs_ref[:, columns], w_ref[...])
-    squares = sum_of_squares(w_ref)
-
-    @pl.when(step == 0)
-    def _():
-        acc_ref[...] = product
-        squares_ref[...] = squares
-
-    @pl.when((step > 0) & (step < steps - 1))
-    def _():
-        acc_ref[...] += product
-        squares_ref[...] += squares
-
-    @pl.when(step == steps - 1)
-    def _():
-        up = b_ref[:, pl.ds(pl.multiple_of(place_ref[block] * half, half), half)]
-        through = dot(adapter_ref[...], jnp.concatenate([up, up], axis=0))
-        total = acc_ref[...] + product
-        out_ref[0] = (total[:both] + adapter_scale * through[:both]).astype(bf16)
-        cross = up.astype(f32) * (2 * adapter_scale * total[both:] + adapter_scale * adapter_scale * through[both:])
-        stats_ref[pl.ds(place_ref[blocks + block], 1), :] = (
-            squares_ref[...] + squares + jnp.sum(cross, axis=0, keepdims=True)
-        )
-
-
-def forward(n, place, weight, up, half, first=None, later=None):
+def load_kernel(tokens, rank, n, first, place_ref, *refs):
+    if first:
+        own_ref, at_ref, up_ref, w_hbm, *held, stats_ref, own_out, sem, own_sem = refs
+    else:
+        before_ref, at_ref, up_ref, w_hbm, *held, stats_ref, sem = refs
+    blocks, half = len(held), held[0].shape[1]
+    column = lambda k: pl.ds(pl.multiple_of(place_ref[k] * half, half), half)
+    copy = lambda k: pltpu.make_async_copy(w_hbm.at[:, column(k)], held[k], sem.at[k])
+    if first:
+        own_copy = pltpu.make_async_copy(own_ref, own_out, own_sem)
+        own_copy.start()
+    for k in range(blocks):
+        copy(k).start()
+
+    down = at_ref[...]
+    high, low = split_pair(dot(down, down, contract_trailing))
+    if first:
+        own_copy.wait()
+        turned = dot(down, own_out[...], contract_trailing)
+        lanes = half // tokens
+        span = rank // lanes
+        stats_ref[:n, :] = jnp.zeros((n, half), f32)
+        for j in range(lanes):
+            stats_ref[n:, j * tokens : (j + 1) * tokens] = turned[j * span : (j + 1) * span]
+    else:
+        stats_ref[...] = before_ref[...]
+
+    for k in range(blocks):
+        copy(k).wait()
+        up = up_ref[:, column(k)]
+        cross = 2 * dot(down, held[k][...]) + adapter_scale * (dot(high, up) + dot(low, up))
+        cross = jnp.sum(up.astype(f32) * cross, axis=0, keepdims=True)
+        stats_ref[pl.ds(place_ref[blocks + k], 1), :] = sum_of_squares(held[k]) + adapter_scale * cross
+
+
+def load(n, place, weight, at, up, half, own=None, before=None):
     blocks = place.shape[0] // 2
     rows = weight.shape[0]
-    steps = 2
+    rank = at.shape[0]
+    any_ = pl.BlockSpec(memory_space=pl.ANY)
+    first = before is None
+    if first:
+        tokens = own.shape[0]
+        stats = (n + rank * tokens // half, half)
+    else:
+        tokens, stats = None, before.shape
+    return pl.pallas_call(
+        functools.partial(load_kernel, tokens, rank, n, first),
+        in_specs=[pl.BlockSpec(memory_space=pltpu.SMEM), any_ if first else vmem(), vmem(), vmem(), any_],
+        out_specs=[vmem()] * (blocks + (2 if first else 1)),
+        out_shape=[jax.ShapeDtypeStruct((rows, half), bf16)] * blocks
+        + [jax.ShapeDtypeStruct(stats, f32)]
+        + ([jax.ShapeDtypeStruct(own.shape, bf16)] if first else []),
+        scratch_shapes=[pltpu.SemaphoreType.DMA((blocks,))] + ([pltpu.SemaphoreType.DMA] if first else []),
+        compiler_params=params(),
+        cost_estimate=small_cost,
+        name="load",
+    )(place, own if first else before, at, up, weight)
+
+
+def forward_kernel(tokens, rank, blocks, first, place_ref, *refs):
+    if first:
+        own_ref, other_ref, at_ref, up_ref, *held, out_ref, lhs_ref, adapter_ref, sem = refs
+        copy = pltpu.make_async_copy(other_ref, lhs_ref.at[tokens:], sem)
+        copy.start()
+        lhs_ref[:tokens, :] = own_ref[...]
+        copy.wait()
+        high, low = split_pair(dot(lhs_ref[...], at_ref[...], contract_trailing))
+        adapter_ref[:, :rank] = high
+        adapter_ref[:, rank:] = low
+    else:
+        lhs_ref, adapter_ref, up_ref, *held, out_ref = refs
+    half = out_ref.shape[2]
+    for i in range(blocks):
+        up = up_ref[:, pl.ds(pl.multiple_of(place_ref[i] * half, half), half)]
+        through = dot(adapter_ref[...], jnp.concatenate([up, up], axis=0))
+        out_ref[i] = (dot(lhs_ref[...], held[i][...]) + adapter_scale * through).astype(bf16)
+
+
+def forward(place, held, up, first=None, later=None):
+    rows, half = held[0].shape
     if later is None:
-        own, other, at = first
+        own, other, at = operands = first
         tokens, rank = own.shape[0], at.shape[0]
-        operands = [own, other, at]
-        specs = [pl.BlockSpec(memory_space=m) for m in (pltpu.HBM, pl.ANY, pltpu.HBM)]
-    else:
-        lhs, adapter, before = operands = later
-        rank = adapter.shape[1] // 2
-        tokens = (lhs.shape[0] - rank) // 2
-        specs = [vmem()] * 3
-    stats = (n + rank * tokens // half, half)
-    extra = [((2 * tokens + rank, rows), bf16), ((2 * tokens + rank, 2 * rank), bf16)] if first else []
+        specs = [vmem(), pl.BlockSpec(memory_space=pl.ANY), vmem()]
+    else:
+        lhs, adapter = operands = later
+        rank, tokens = adapter.shape[1] // 2, lhs.shape[0] // 2
+        specs = [vmem()] * 2
+    extra = [((2 * tokens, rows), bf16), ((2 * tokens, 2 * rank), bf16)] if first else []
     return pl.pallas_call(
-        functools.partial(forward_kernel, tokens, rank, n, later is None),
-        grid_spec=pltpu.PrefetchScalarGridSpec(
-            num_scalar_prefetch=1,
-            grid=(blocks, steps),
-            in_specs=specs
-            + [
-                vmem(),
-                pl.BlockSpec((rows // steps, half), lambda i, j, p: (j, p[i])),
-            ],
-            out_specs=[pl.BlockSpec((1, 2 * tokens, half), lambda i, j, p: (i, 0, 0)), vmem()] + [vmem()] * len(extra),
-            scratch_shapes=[
-                pltpu.VMEM((2 * tokens + rank, half), f32),
-                pltpu.VMEM((1, half), f32),
-                pltpu.SemaphoreType.DMA((3,)),
-            ],
-        ),
-        out_shape=[jax.ShapeDtypeStruct((blocks, 2 * tokens, half), bf16), jax.ShapeDtypeStruct(stats, f32)]
+        functools.partial(forward_kernel, tokens, rank, len(held), later is None),
+        in_specs=[pl.BlockSpec(memory_space=pltpu.SMEM), *specs] + [vmem()] * (1 + len(held)),
+        out_specs=[vmem()] * (1 + len(extra)),
+        out_shape=[jax.ShapeDtypeStruct((len(held), 2 * tokens, half), bf16)]
         + [jax.ShapeDtypeStruct(*e) for e in extra],
+        scratch_shapes=[pltpu.SemaphoreType.DMA] if first else [],
         compiler_params=params(),
         cost_estimate=small_cost,
         name="forward",
-    )(place, *operands, up, weight)
-
-
-def backward_kernel(tokens, n, first, place_ref, *refs):
-    if first:
-        cots, (stats_ref, b_ref) = refs[:n], refs[n : n + 2]
-        at_ref, *w_refs = refs[n + 2 : 2 * n + 3]
+    )(place, *operands, up, *held)
+
+
+def backward_kernel(tokens, n, start, band, first, place_ref, *refs):
+    if first:
+        cots, (stats_ref, up_ref, at_ref, *held) = refs[:n], refs[n : 2 * n + 3]
         own_out, other_out, scaled_ref, proj_ref = refs[2 * n + 3 :]
     else:
-        scaled_ref, proj_ref, at_ref, *w_refs = refs[: n + 3]
-        own_out, other_out = refs[n + 3 :]
+        scaled_ref, proj_ref, at_ref, *held, own_out, other_out = refs
     both = 2 * tokens
-    half = w_refs[0].shape[1]
+    half = held[0].shape[1]
     spans = [slice(k * half, (k + 1) * half) for k in range(n)]
 
     if first:
@@ -200,40 +197,36 @@
                 rescale = magnitude / jnp.sqrt(squares + stability_floor)
                 scaled = (cots[k][:both, :].astype(f32) * rescale).astype(bf16)
                 scaled_ref[:, spans[k]] = scaled
-                up = b_ref[:, pl.ds(pl.multiple_of(place_ref[k] * half, half), half)]
+                up = up_ref[:, pl.ds(pl.multiple_of(place_ref[k] * half, half), half)]
                 projected = projected + dot(scaled, up, contract_trailing)
             proj_ref[...] = projected
 
-    total = adapter_scale * dot(proj_ref[...].astype(bf16), at_ref[...])
+    row = pl.ds(pl.multiple_of((start + pl.program_id(0)) * band, band), band)
+    total = adapter_scale * dot(proj_ref[...].astype(bf16), at_ref[:, row])
     for k in range(n):
-        total = total + dot(scaled_ref[:, spans[k]], w_refs[k][...], contract_trailing)
+        total = total + dot(scaled_ref[:, spans[k]], held[k][row, :], contract_trailing)
     own_out[...] = total[:tokens]
     other_out[...] = total[tokens:].astype(bf16)
 
 
-def backward(place, start, bands, band, at, weight, half, first=None, later=None):
+def backward(place, start, bands, band, at, held, first=None, later=None):
     n = place.shape[0] // 2
-    rank, rows = at.shape
+    half = held[0].shape[1]
+    rank = at.shape[0]
     if later is None:
         cots, stats, up = first
         both = cots[0].shape[0] - pad_rows
-        operands, specs = [*cots, stats, up], [vmem()] * (n + 2)
+        operands = [*cots, stats, up]
         extra = [((both, n * half), bf16), ((both, rank), f32)]
     else:
-        operands, specs, extra = later, [vmem()] * 2, []
+        operands, extra = later, []
         both = later[0].shape[0]
     tokens = both // 2
-    part = lambda k: pl.BlockSpec((band, half), lambda i, p: (start + i, p[k]))
     return pl.pallas_call(
-        functools.partial(backward_kernel, tokens, n, later is None),
-        grid_spec=pltpu.PrefetchScalarGridSpec(
-            num_scalar_prefetch=1,
-            grid=(bands,),
-            in_specs=specs
-            + [pl.BlockSpec((rank, band), lambda i, p: (0, start + i))]
-            + [part(k) for k in range(n)],
-            out_specs=[pl.BlockSpec((tokens, band), lambda i, p: (0, i))] * 2 + [vmem()] * len(extra),
-        ),
+        functools.partial(backward_kernel, tokens, n, start, band, later is None),
+        grid=(bands,),
+        in_specs=[pl.BlockSpec(memory_space=pltpu.SMEM)] + [vmem()] * (len(operands) + 1 + n),
+        out_specs=[pl.BlockSpec((tokens, band), lambda i: (0, i))] * 2 + [vmem()] * len(extra),
         out_shape=[
             jax.ShapeDtypeStruct((tokens, bands * band), f32),
             jax.ShapeDtypeStruct((tokens, bands * band), bf16),
@@ -242,7 +235,7 @@
         compiler_params=params(),
         cost_estimate=small_cost,
         name="backward",
-    )(place, *operands, at, *[weight] * n)
+    )(place, *operands, at, *held)
 
 
 def split_columns(hidden, weight, down, up, magnitude, cotangent):
@@ -271,6 +264,9 @@
 
     cot_other = swap(cotangent)
     hidden_other = swap(hidden)
+    run_load = functools.partial(load, n, weight=weight, at=at, up=up, half=half)
+    *far, stats, own = run_load(place(0b100, 0b101, 0b110, 0b111), own=hidden)
+    cot_other, stats = tie((cot_other, stats))
     first = lax.reduce_precision(magnitude, 8, 7)
     second = lax.reduce_precision(magnitude - first, 8, 7)
     third = magnitude - first - second
@@ -280,29 +276,33 @@
     block = own_block(core.astype(jnp.int32).reshape(1), cotangent, cot_other, magnitude_rows)
 
     cots = {0b000: block, 0b001: send(block, 2), 0b010: send(block, 1), 0b100: send(block, 0)}
-    run = functools.partial(forward, n, weight=weight, up=up, half=half)
-
-    far1, stats, lhs, adapter = run(place(0b110, 0b111), first=(hidden, hidden_other, at))
+    *near, stats = run_load(place(0b000, 0b001, 0b010, 0b011), before=stats)
+
+    got = send(stats, 0)
+    far1, lhs, adapter = forward(place(0b110, 0b111), far[2:], up, first=(own, hidden_other, at))
+    run = functools.partial(forward, up=up, later=(lhs, adapter))
+    got, far1 = tie((got, far1))
+    stats = stats + got
+    got = send(stats, 1)
     from1 = send(far1, 0)
-    far0, stats = run(place(0b100, 0b101), later=(lhs, adapter, stats))
+    far0 = run(place(0b100, 0b101), far[:2])[0]
+    *arrived, got, far0 = tie((*(cots[v] for v in (0b001, 0b010, 0b100)), got, far0))
+    cots[0b001], cots[0b010], cots[0b100] = arrived
+    stats = stats + got
+    got = send(stats, 2)
     from0 = send(far0, 0)
-    *got, stats = tie((*(cots[v] for v in (0b001, 0b010, 0b100)), stats))
-    cots[0b001], cots[0b010], cots[0b100] = got
     cots[0b011], cots[0b101], cots[0b110] = send(cots[0b001], 1), send(cots[0b001], 0), send(cots[0b010], 0)
-    near1, stats = run(place(0b010, 0b011), later=(lhs, adapter, stats))
-    cots[0b011], from1, stats = tie((cots[0b011], from1, stats))
+    near1 = run(place(0b010, 0b011), near[2:])[0]
+    cots[0b011], from1, got, near1 = tie((cots[0b011], from1, got, near1))
+    stats = stats + got
     cots[0b111] = send(cots[0b011], 0)
-    sent = (near1.astype(f32) + from1.astype(f32)).astype(bf16)
-    arrived = send(sent, 1)
-    near0, stats = run(place(0b000, 0b001), later=(lhs, adapter, stats))
-    cots[0b101], cots[0b110], from0, stats = tie((cots[0b101], cots[0b110], from0, stats))
-
-    stats = stats + send(stats, 0)
-    stats = stats + send(stats, 1)
-    arrived, cots[0b111], stats = tie((arrived, cots[0b111], stats))
+    arrived = send((near1.astype(f32) + from1.astype(f32)).astype(bf16), 1)
+    near0 = run(place(0b000, 0b001), near[:2])[0]
+    cots[0b101], cots[0b110], cots[0b111], from0, near0, arrived, stats = tie(
+        (cots[0b101], cots[0b110], cots[0b111], from0, near0, arrived, stats)
+    )
     kept = near0.astype(f32) + from0.astype(f32) + arrived.astype(f32)
     last = send(kept[1].astype(bf16), 2)
-    stats = stats + send(stats, 2)
     lowrank_rows = stats[n:]
     lowrank_other = swap(lowrank_rows)
 
@@ -310,13 +310,12 @@
     bands = rows // band
     many = (bands + 2) // 2
     order = place(*range(n))
-    grad_a, other_a, scaled, proj = backward(
-        order, 0, many, band, at, weight, half, first=([cots[v] for v in range(n)], stats, up)
-    )
+    run = functools.partial(backward, order, band=band, at=at, held=near + far)
+    grad_a, other_a, scaled, proj = run(0, many, first=([cots[v] for v in range(n)], stats, up))
     got_a = swap(other_a)
     last, proj = tie((last, proj))
     unscaled = kept[0] + last.astype(f32)
-    grad_b, other_b = backward(order, many, bands - many, band, at, weight, half, later=(scaled, proj))
+    grad_b, other_b = run(many, bands - many, later=(scaled, proj))
     got_b = swap(other_b)
     hidden_gradient = jnp.concatenate(
         [(own + got.astype(f32)).astype(bf16) for own, got in ((grad_a, got_a), (grad_b, got_b))], axis=1

time: 109 us -> 122 us (1.12)
  local copies, waits for them, and re-layouts: 9.33 us -> 34.2 us
  Pallas kernels: 51.6 us -> 42.7 us
    unnamed x44 -> x76, local copies, waits for them, and re-layouts: 8.48 us -> 33.8 us
    pallas_call x6 -> x8, Pallas kernels: 49.9 us -> 41 us  [the longest x2 14.1 us: load(): pl.pallas_call(functools.partial(load_kernel, tokens, rank, n, first), in...]
  transfers between devices with their start and end apart: 23 -> 23, of which waited for: 7 -> 6; matrix products, arithmetic and copies ran while one was open for 10% -> 6% of each run, Pallas kernels for 48% -> 35%
where the time goes in v3:
time: 122 us
  Pallas kernels  42.7 us (35%)
  local copies, waits for them, and re-layouts  34.2 us (28%)
  starting transfers between devices  21.6 us (18%)
  waiting for transfers between devices  12.3 us (10%)
  other arithmetic  7.82 us (6%)
  matrix products  1.94 us (2%)
    unnamed x76, local copies, waits for them, and re-layouts  33.8 us
    ppermute x14, starting transfers between devices, send(): return lax.ppermute(x, ('tensor', 'dp'), pairs)  19.2 us
    pallas_call x2, Pallas kernels, load(): pl.pallas_call(functools.partial(load_kernel, tokens, rank, n, first), in...  14.1 us
    pallas_call x2, Pallas kernels, backward(): pl.pallas_call(functools.partial(backward_kernel, tokens, n, start, band,...  13.7 us
    pallas_call x4, Pallas kernels, forward(): pl.pallas_call(functools.partial(forward_kernel, tokens, rank, len(held),...  13.2 us
    ppermute x14, waiting for transfers between devices, send(): return lax.ppermute(x, ('tensor', 'dp'), pairs)  10.2 us
    ppermute x9, starting transfers between devices, split_columns(): swap = lambda x: lax.ppermute(x, 'dp', [(0, 1), (1, 0)])  2.46 us
  transfers between devices with their start and end apart: 23, of which 6 were waited for; matrix products, arithmetic and copies ran while one was open for 6% of the time, Pallas kernels for 35%

profile of v3, /device:TPU:0, one launch (start us, length us, event | category | flops | bytes accessed | tf_op | source)
XLA Modules:
  0.0 121.7 jit_solution(6818548157617999997)
XLA Ops:
  0.6 0.5 collective-permute-start.5
  1.2 0.7 reduce-precision_convert_fusion.1
  2.2 1.2 %copy-done = bf16[64,8192]{1,0:T(8,128)(2,1)S(1)} copy-done((bf16[64,8192]{1,0:T(8,128)(2,1)S(1)}, bf16[64,8192]{1,0:T(8,128)(2,1)}, u32[]{:S(2)}) %copy-start) | copy-done | bytes 1048600
  3.5 1.0 copy-done.25
  4.5 1.2 copy-done.27
  5.7 7.2 %load.2 = (bf16[3584,512]{1,0:T(8,128)(2,1)S(1)}, bf16[3584,512]{1,0:T(8,128)(2,1)S(1)}, bf16[3584,512]{1,0:T(8,128)(2,1)S(1)}, bf16[3584,512]{1,0:T(8,128)(2,1)...) custom-call(s32[8]{0:T(128)S(1)} %stack.121.place_ref, bf16[128,3584]{1,0:T(8,128)(2,1)S(1)} %copy-done.27, ...), custom_call_target="tpu_custom_call" | custom-call | flops 1048576 | bytes 1048576 | tf_op jit(solution)/shard_map/load/pallas_call | solution.py:122
  12.9 1.8 %copy-done.2 = bf16[3584,512]{1,0:T(8,128)(2,1)} copy-done((bf16[3584,512]{1,0:T(8,128)(2,1)}, bf16[3584,512]{1,0:T(8,128)(2,1)S(1)}, u32[]{:S(2)}) %copy-start.2) | copy-done | bytes 3670040
  14.7 1.8 %copy-done.5 = bf16[3584,512]{1,0:T(8,128)(2,1)} copy-done((bf16[3584,512]{1,0:T(8,128)(2,1)}, bf16[3584,512]{1,0:T(8,128)(2,1)S(1)}, u32[]{:S(2)}) %copy-start.5) | copy-done | bytes 3670040
  16.5 1.8 %copy-done.8 = bf16[3584,512]{1,0:T(8,128)(2,1)} copy-done((bf16[3584,512]{1,0:T(8,128)(2,1)}, bf16[3584,512]{1,0:T(8,128)(2,1)S(1)}, u32[]{:S(2)}) %copy-start.8) | copy-done | bytes 3670040
  18.3 1.8 %copy-done.11 = bf16[3584,512]{1,0:T(8,128)(2,1)} copy-done((bf16[3584,512]{1,0:T(8,128)(2,1)}, bf16[3584,512]{1,0:T(8,128)(2,1)S(1)}, u32[]{:S(2)}) %copy-start.11) | copy-done | bytes 3670040
  20.1 0.8 maximum_maximum_fusion.magnitude_ref
  20.9 1.7 %own_block.1.refs_0_ = bf16[272,512]{1,0:T(8,128)(2,1)} custom-call(s32[1]{0:T(128)} %bitcast.core_ref, bf16[128,1024]{1,0:T(8,128)(2,1)} %own_ref.1, bf16[128,1024]{1,0:T(8,128)(2,1)} %collective-permute-done.other_ref, bf16[16,1024]{1,0:T(8,128)(2,1)} %maximum_maximum_fusion.magnitude_ref), custom_call_target="tpu_custom_call" | custom-call | flops 1048576 | bytes 1048576 | tf_op jit(solution)/shard_map/own_block/pallas_call | solution.py:58
  22.6 4.0 %collective-permute-start.1 = (bf16[272,512]{1,0:T(8,128)(2,1)}, bf16[272,512]{1,0:T(8,128)(2,1)}, u32[]{:S(2)}, u32[]{:S(2)}) collective-permute-start(bf16[272,512]{1,0:T(8,128)(2,1)} %own_block.1.refs_0_), channel_id=1, source_target_pairs={{0,8},{1,9},{2,10},{3,11},{4,12},{5,13},{6,14},{7,15},{8,0},{9,1},... | collective-permute-start | bytes 835592 | tf_op jit(solution)/shard_map/ppermute | solution.py:252
  26.6 1.6 %collective-permute-start.2 = (bf16[272,512]{1,0:T(8,128)(2,1)}, bf16[272,512]{1,0:T(8,128)(2,1)}, u32[]{:S(2)}, u32[]{:S(2)}) collective-permute-start(bf16[272,512]{1,0:T(8,128)(2,1)} %own_block.1.refs_0_), channel_id=1, source_target_pairs={{0,4},{1,3},{2,6},{3,1},{4,0},{5,7},{6,2},{7,5},{8,12},{9,11},{10,... | collective-permute-start | bytes 835592 | tf_op jit(solution)/shard_map/ppermute | solution.py:252
  28.2 1.5 %collective-permute-start.3 = (bf16[272,512]{1,0:T(8,128)(2,1)}, bf16[272,512]{1,0:T(8,128)(2,1)S(1)}, u32[]{:S(2)}, u32[]{:S(2)}) collective-permute-start(bf16[272,512]{1,0:T(8,128)(2,1)} %own_block.1.refs_0_), channel_id=1, source_target_pairs={{0,2},{1,5},{2,0},{3,7},{4,6},{5,1},{6,4},{7,3},{8,10},{9,13},{10,... | collective-permute-start | bytes 835592 | tf_op jit(solution)/shard_map/ppermute | solution.py:252
  29.7 6.9 %load.3 = (bf16[3584,512]{1,0:T(8,128)(2,1)S(1)}, bf16[3584,512]{1,0:T(8,128)(2,1)S(1)}, bf16[3584,512]{1,0:T(8,128)(2,1)S(1)}, bf16[3584,512]{1,0:T(8,128)(2,1)S(1)}, f32[24,512]{1,0:T(8,128)S(1)}) custom-call(s32[8]{0:T(128)S(1)} %stack.133.place_ref, f32[24,512]{1,0:T(8,128)S(1)} %get-tuple-element.49.refs_0_, bf16[64,3584]{1,0:T(8,128)(2,1)S(1)} %bitcast.34, ...), custom_call_target="tpu_custom_call" | custom-call | flops 1048576 | bytes 1048576 | tf_op jit(solution)/shard_map/load/pallas_call | solution.py:122
  36.7 1.8 %copy-done.15 = bf16[3584,512]{1,0:T(8,128)(2,1)} copy-done((bf16[3584,512]{1,0:T(8,128)(2,1)}, bf16[3584,512]{1,0:T(8,128)(2,1)S(1)}, u32[]{:S(2)}) %copy-start.15) | copy-done | bytes 3670040
  38.5 1.9 %copy-done.18 = bf16[3584,512]{1,0:T(8,128)(2,1)} copy-done((bf16[3584,512]{1,0:T(8,128)(2,1)}, bf16[3584,512]{1,0:T(8,128)(2,1)S(1)}, u32[]{:S(2)}) %copy-start.18) | copy-done | bytes 3670040
  40.3 0.5 collective-permute-start.4
  41.0 1.4 %copy-done.29 = bf16[128,3584]{1,0:T(8,128)(2,1)} copy-done((bf16[128,3584]{1,0:T(8,128)(2,1)}, bf16[128,3584]{1,0:T(8,128)(2,1)S(1)}, u32[]{:S(2)}) %copy-start.29) | copy-done | bytes 917528
  42.4 1.9 %copy-done.30 = bf16[128,3584]{1,0:T(8,128)(2,1)S(1)} copy-done((bf16[128,3584]{1,0:T(8,128)(2,1)S(1)}, bf16[128,3584]{1,0:T(8,128)(2,1)}, u32[]{:S(2)}) %copy-start.30) | copy-done | bytes 917528
  44.2 1.2 copy-done.34
  45.4 4.2 %forward.4 = (bf16[2,256,512]{2,1,0:T(8,128)(2,1)S(1)}, bf16[256,3584]{1,0:T(8,128)(2,1)S(1)}, bf16[256,128]{1,0:T(8,128)(2,1)S(1)}) custom-call(s32[4]{0:T(128)S(1)} %pad_add_fusion.place_ref, bf16[128,3584]{1,0:T(8,128)(2,1)S(1)} %copy-done.34, bf16[128,3584]{1,0:T(8,128)(2,1)S(1)} %copy-done.30, bf16[64,3584]{1,0:T(8,128)(2,1)S(1)} %bitcast.35, ...), custom_call_target="tpu_custom_call" | custom-call | flops 1048576 | bytes 1048576 | tf_op jit(solution)/shard_map/forward/pallas_call | solution.py:166
  49.6 0.9 collective-permute-start.10
  50.5 0.5 collective-permute-start.6
  51.1 3.6 %forward.5 = bf16[2,256,512]{2,1,0:T(8,128)(2,1)} custom-call(s32[4]{0:T(128)S(1)} %pad_add_fusion.1.place_ref, bf16[256,3584]{1,0:T(8,128)(2,1)S(1)} %get-tuple-element.56.refs_0_, bf16[256,128]{1,0:T(8,128)(2,1)S(1)} %get-tuple-element.57.refs_1_, bf16[64,8192]{1,0:T(8,128)(2,1)S(1)} %copy-done.1, bf16[3584,512]{1,0:T(8,128)(2,1)S(1)} %copy-done.9, ...), custom_call_target="tpu_custom_call" | custom-call | flops 1048576 | bytes 1048576 | tf_op jit(solution)/shard_map/forward/pallas_call | solution.py:166
  54.7 0.7 copy-done.35
  55.4 1.6 %collective-permute-start.9 = (bf16[272,512]{1,0:T(8,128)(2,1)}, bf16[272,512]{1,0:T(8,128)(2,1)}, u32[]{:S(2)}, u32[]{:S(2)}) collective-permute-start(bf16[272,512]{1,0:T(8,128)(2,1)} %collective-permute-done.1.refs_1_), channel_id=1, source_target_pairs={{0,4},{1,3},{2,6},{3,1},{4,0},{5,7},{6,2},{7,5},{8,12},{9,11},{10,... | collective-permute-start | bytes 835592 | tf_op jit(solution)/shard_map/ppermute | solution.py:252
  57.0 0.4 collective-permute-start.11
  57.4 2.8 %forward.6 = bf16[2,256,512]{2,1,0:T(8,128)(2,1)S(1)} custom-call(s32[4]{0:T(128)S(1)} %pad_add_fusion.2.place_ref, bf16[256,3584]{1,0:T(8,128)(2,1)S(1)} %get-tuple-element.56.refs_0_, bf16[256,128]{1,0:T(8,128)(2,1)S(1)} %get-tuple-element.57.refs_1_, bf16[64,8192]{1,0:T(8,128)(2,1)S(1)} %copy-done.1, ...), custom_call_target="tpu_custom_call" | custom-call | flops 1048576 | bytes 1048576 | tf_op jit(solution)/shard_map/forward/pallas_call | solution.py:166
  60.2 1.3 %collective-permute-start.13 = (bf16[2,256,512]{2,1,0:T(8,128)(2,1)}, bf16[2,256,512]{2,1,0:T(8,128)(2,1)}, u32[]{:S(2)}, u32[]{:S(2)}) collective-permute-start(bf16[2,256,512]{2,1,0:T(8,128)(2,1)} %forward.5), channel_id=1, source_target_pairs={{0,2},{1,5},{2,0},{3,7},{4,6},{5,1},{6,4},{7,3},{8,10},{9,13},{10,... | collective-permute-start | bytes 1572872 | tf_op jit(solution)/shard_map/ppermute | solution.py:252
  61.5 2.7 %collective-permute-done.11 = f32[24,512]{1,0:T(8,128)S(1)} collective-permute-done((f32[24,512]{1,0:T(8,128)S(1)}, f32[24,512]{1,0:T(8,128)S(1)}, u32[]{:S(2)}, u32[]{:S(2)}) %collective-permute-start.11) | collective-permute-done | bytes 49184 | tf_op jit(solution)/shard_map/ppermute | solution.py:252
  64.2 0.9 add_convert_fusion.1
  65.1 1.5 %collective-permute-start.14 = (bf16[2,256,512]{2,1,0:T(8,128)(2,1)}, bf16[2,256,512]{2,1,0:T(8,128)(2,1)}, u32[]{:S(2)}, u32[]{:S(2)}) collective-permute-start(bf16[2,256,512]{2,1,0:T(8,128)(2,1)} %add_convert_fusion.1), channel_id=1, source_target_pairs={{0,4},{1,3},{2,6},{3,1},{4,0},{5,7},{6,2},{7,5},{8,12},{9,11},{10,... | collective-permute-start | bytes 1572872 | tf_op jit(solution)/shard_map/ppermute | solution.py:252
  66.6 1.2 collective-permute-start.7
  67.8 0.8 collective-permute-start.8
  68.6 1.2 collective-permute-start.12
  70.0 2.0 %copy-done.16 = bf16[3584,512]{1,0:T(8,128)(2,1)S(1)} copy-done((bf16[3584,512]{1,0:T(8,128)(2,1)S(1)}, bf16[3584,512]{1,0:T(8,128)(2,1)}, u32[]{:S(2)}) %copy-start.16) | copy-done | bytes 3670040
  72.1 2.0 %copy-done.19 = bf16[3584,512]{1,0:T(8,128)(2,1)S(1)} copy-done((bf16[3584,512]{1,0:T(8,128)(2,1)S(1)}, bf16[3584,512]{1,0:T(8,128)(2,1)}, u32[]{:S(2)}) %copy-start.19) | copy-done | bytes 3670040
  74.1 2.7 %forward.7 = bf16[2,256,512]{2,1,0:T(8,128)(2,1)S(1)} custom-call(s32[4]{0:T(128)S(1)} %pad_add_fusion.3.place_ref, bf16[256,3584]{1,0:T(8,128)(2,1)S(1)} %get-tuple-element.56.refs_0_, bf16[256,128]{1,0:T(8,128)(2,1)S(1)} %get-tuple-element.57.refs_1_, bf16[64,8192]{1,0:T(8,128)(2,1)S(1)} %copy-done.1, bf16[3584,512]{1,0:T(8,128)(2,1)S(1)} %copy-done.16, ...), custom_call_target="tpu_custom_call" | custom-call | flops 1048576 | bytes 1048576 | tf_op jit(solution)/shard_map/forward/pallas_call | solution.py:166
  76.9 1.5 %collective-permute-done.7.refs_5_ = bf16[272,512]{1,0:T(8,128)(2,1)} collective-permute-done((bf16[272,512]{1,0:T(8,128)(2,1)}, bf16[272,512]{1,0:T(8,128)(2,1)}, u32[]{:S(2)}, u32[]{:S(2)}) %collective-permute-start.7) | collective-permute-done | bytes 278560 | tf_op jit(solution)/shard_map/ppermute | solution.py:252
  78.4 3.0 %collective-permute-done.8.refs_6_ = bf16[272,512]{1,0:T(8,128)(2,1)} collective-permute-done((bf16[272,512]{1,0:T(8,128)(2,1)}, bf16[272,512]{1,0:T(8,128)(2,1)}, u32[]{:S(2)}, u32[]{:S(2)}) %collective-permute-start.8) | collective-permute-done | bytes 278560 | tf_op jit(solution)/shard_map/ppermute | solution.py:252
  81.4 3.0 %collective-permute-done.12.refs_7_ = bf16[272,512]{1,0:T(8,128)(2,1)} collective-permute-done((bf16[272,512]{1,0:T(8,128)(2,1)}, bf16[272,512]{1,0:T(8,128)(2,1)}, u32[]{:S(2)}, u32[]{:S(2)}) %collective-permute-start.12) | collective-permute-done | bytes 278560 | tf_op jit(solution)/shard_map/ppermute | solution.py:252
  84.4 1.4 %convert_add_fusion = f32[2,256,512]{2,1,0:T(8,128)S(1)} fusion(bf16[2,256,512]{2,1,0:T(8,128)(2,1)} %collective-permute-done.14, bf16[2,256,512]{2,1,0:T(8,128)(2,1)} %collective-permute-done.13, bf16[2,256,512]{2,1,0:T(8,128)(2,1)S(1)} %forward.7), kind=kLoop, calls=%fused_computation.6 | loop fusion | flops 1310720 | bytes 2621440 | tf_op jit(solution)/shard_map/add | solution.py:304
  85.8 2.1 %collective-permute-start.15 = (bf16[256,512]{1,0:T(8,128)(2,1)S(1)}, bf16[256,512]{1,0:T(8,128)(2,1)S(1)}, u32[]{:S(2)}, u32[]{:S(2)}) collective-permute-start(bf16[256,512]{1,0:T(8,128)(2,1)S(1)} %fusion.10), channel_id=1, source_target_pairs={{0,8},{1,9},{2,10},{3,11},{4,12},{5,13},{6,14},{7,15},{8,0},{9,1},... | collective-permute-start | bytes 786440 | tf_op jit(solution)/shard_map/ppermute | solution.py:252
  88.0 2.0 %copy-done.13 = bf16[3584,512]{1,0:T(8,128)(2,1)S(1)} copy-done((bf16[3584,512]{1,0:T(8,128)(2,1)S(1)}, bf16[3584,512]{1,0:T(8,128)(2,1)}, u32[]{:S(2)}) %copy-start.13) | copy-done | bytes 3670040
  90.0 2.0 %copy-done.17 = bf16[3584,512]{1,0:T(8,128)(2,1)S(1)} copy-done((bf16[3584,512]{1,0:T(8,128)(2,1)S(1)}, bf16[3584,512]{1,0:T(8,128)(2,1)}, u32[]{:S(2)}) %copy-start.17) | copy-done | bytes 3670040
  92.1 2.0 %copy-done.20 = bf16[3584,512]{1,0:T(8,128)(2,1)S(1)} copy-done((bf16[3584,512]{1,0:T(8,128)(2,1)S(1)}, bf16[3584,512]{1,0:T(8,128)(2,1)}, u32[]{:S(2)}) %copy-start.20) | copy-done | bytes 3670040
  94.1 2.0 %copy-done.22 = bf16[3584,512]{1,0:T(8,128)(2,1)S(1)} copy-done((bf16[3584,512]{1,0:T(8,128)(2,1)S(1)}, bf16[3584,512]{1,0:T(8,128)(2,1)}, u32[]{:S(2)}) %copy-start.22) | copy-done | bytes 3670040
  96.2 2.0 %copy-done.24 = bf16[3584,512]{1,0:T(8,128)(2,1)S(1)} copy-done((bf16[3584,512]{1,0:T(8,128)(2,1)S(1)}, bf16[3584,512]{1,0:T(8,128)(2,1)}, u32[]{:S(2)}) %copy-start.24) | copy-done | bytes 3670040
  98.2 8.6 %backward.2 = (f32[128,2048]{1,0:T(8,128)S(1)}, bf16[128,2048]{1,0:T(8,128)(2,1)S(1)}, bf16[256,4096]{1,0:T(8,128)(2,1)S(1)}, f32[256,64]{1,0:T(8,128)S(1)}) custom-call(s32[16]{0:T(128)S(1)} %stack.138.place_ref, bf16[272,512]{1,0:T(8,128)(2,1)S(1)} %copy-done.32, bf16[272,512]{1,0:T(8,128)(2,1)} %collective-permute-done.1.refs_1_, ...), custom_call_target="tpu_custom_call" | custom-call | flops 1048576 | bytes 1048576 | tf_op jit(solution)/shard_map/backward/pallas_call | solution.py:225
  106.9 0.5 collective-permute-start.20
  107.5 1.4 %collective-permute-done.20 = f32[16,512]{1,0:T(8,128)S(1)} collective-permute-done((f32[16,512]{1,0:T(8,128)S(1)}, f32[16,512]{1,0:T(8,128)S(1)}, u32[]{:S(2)}, u32[]{:S(2)}) %collective-permute-start.20) | collective-permute-done | bytes 32800 | tf_op jit(solution)/shard_map/ppermute | solution.py:247
  109.0 0.2 collective-permute-start.16
  109.2 0.4 collective-permute-start.19
  109.6 5.1 %backward.3 = (f32[128,1536]{1,0:T(8,128)S(1)}, bf16[128,1536]{1,0:T(8,128)(2,1)S(1)}) custom-call(s32[16]{0:T(128)S(1)} %stack.138.place_ref, bf16[256,4096]{1,0:T(8,128)(2,1)S(1)} %get-tuple-element.85.refs_0_, f32[256,64]{1,0:T(8,128)S(1)} %get-tuple-element.86.refs_1_, bf16[64,3584]{1,0:T(8,128)(2,1)S(1)} %bitcast.37, bf16[3584,512]{1,0:T(8,128)(2,1)S(1)} %copy-done.17, ...), custom_call_target="tpu_custom_call" | custom-call | flops 1048576 | bytes 1048576 | tf_op jit(solution)/shard_map/backward/pallas_call | solution.py:225
  114.9 0.4 collective-permute-start.22
  115.7 0.8 collective-permute-done.22
  116.7 0.7 fusion.35
  117.3 0.3 fusion.17
  117.7 1.2 %fusion.1 = f32[3584,64]{0,1:T(8,128)} fusion(f32[64,3584]{1,0:T(8,128)S(1)} %fusion.17, bf16[128,3584]{1,0:T(8,128)(2,1)S(1)} %copy-done.28, f32[256,64]{1,0:T(8,128)S(1)} %collective-permute-done.19, f32[256,64]{1,0:T(8,128)S(1)} %get-tuple-element.86.refs_1_), kind=kOutput, calls=%fused_computation.2 | convolution fusion | flops 59195392 | bytes 2883584 | tf_op jit(solution)/shard_map/dot_general | solution.py:21
  118.9 0.8 fusion.7
  119.7 0.8 fusion.9
  120.7 1.0 pad_maximum_fusion
  (105 shorter events, 2.2 us)
Async XLA Ops:
  0.6 40.3 %collective-permute-start.5 = (bf16[128,3584]{1,0:T(8,128)(2,1)}, bf16[128,3584]{1,0:T(8,128)(2,1)S(1)}, u32[]{:S(2)}, u32[]{:S(2)}) collective-permute-start(bf16[128,3584]{1,0:T(8,128)(2,1)} %refs_0_.1), channel_id=1, source_target_pairs={{0,1},{1,0},{2,3},{3,2},{4,5},{5,4},{6,7},{7,6},{8,9},{9,8},{10,11... | collective-permute-start | bytes 2752520 | tf_op jit(solution)/shard_map/ppermute | solution.py:247
  1.1 19.8 %collective-permute-start = (bf16[128,1024]{1,0:T(8,128)(2,1)}, bf16[128,1024]{1,0:T(8,128)(2,1)}, u32[]{:S(2)}, u32[]{:S(2)}) collective-permute-start(bf16[128,1024]{1,0:T(8,128)(2,1)} %own_ref.1), channel_id=1, source_target_pairs={{0,1},{1,0},{2,3},{3,2},{4,5},{5,4},{6,7},{7,6},{8,9},{9,8},{10,11... | collective-permute-start | bytes 786440 | tf_op jit(solution)/shard_map/ppermute | solution.py:247
  2.2 1.2 %copy-start = (bf16[64,8192]{1,0:T(8,128)(2,1)S(1)}, bf16[64,8192]{1,0:T(8,128)(2,1)}, u32[]{:S(2)}) copy-start(bf16[64,8192]{1,0:T(8,128)(2,1)} %refs_9_.1) | copy-start | bytes 3145732
  3.5 1.0 copy-start.25
  4.5 1.2 copy-start.27
  5.7 24.0 %copy-start.1 = (bf16[64,8192]{1,0:T(8,128)(2,1)S(1)}, bf16[64,8192]{1,0:T(8,128)(2,1)}, u32[]{:S(2)}) copy-start(bf16[64,8192]{1,0:T(8,128)(2,1)} %refs_9_.1) | copy-start | bytes 3145732
  5.7 24.0 %copy-start.26 = (bf16[3584,64]{0,1:T(8,128)(2,1)S(1)}, bf16[3584,64]{0,1:T(8,128)(2,1)}, u32[]{:S(2)}) copy-start(bf16[3584,64]{0,1:T(8,128)(2,1)} %param.8) | copy-start | bytes 1376260
  12.8 1.8 %copy-start.2 = (bf16[3584,512]{1,0:T(8,128)(2,1)}, bf16[3584,512]{1,0:T(8,128)(2,1)S(1)}, u32[]{:S(2)}) copy-start(bf16[3584,512]{1,0:T(8,128)(2,1)S(1)} %get-tuple-element.52.refs_4_.refs_17_.refs_9_) | copy-start | bytes 11010052
  14.6 1.8 %copy-start.5 = (bf16[3584,512]{1,0:T(8,128)(2,1)}, bf16[3584,512]{1,0:T(8,128)(2,1)S(1)}, u32[]{:S(2)}) copy-start(bf16[3584,512]{1,0:T(8,128)(2,1)S(1)} %get-tuple-element.53.refs_5_.refs_18_.refs_10_) | copy-start | bytes 11010052
  16.5 1.8 %copy-start.8 = (bf16[3584,512]{1,0:T(8,128)(2,1)}, bf16[3584,512]{1,0:T(8,128)(2,1)S(1)}, u32[]{:S(2)}) copy-start(bf16[3584,512]{1,0:T(8,128)(2,1)S(1)} %get-tuple-element.58.refs_3_.refs_15_.refs_7_) | copy-start | bytes 11010052
  18.3 1.8 %copy-start.11 = (bf16[3584,512]{1,0:T(8,128)(2,1)}, bf16[3584,512]{1,0:T(8,128)(2,1)S(1)}, u32[]{:S(2)}) copy-start(bf16[3584,512]{1,0:T(8,128)(2,1)S(1)} %get-tuple-element.59.refs_4_.refs_16_.refs_8_) | copy-start | bytes 11010052
  20.1 16.5 %copy-start.33 = (bf16[128,3584]{1,0:T(8,128)(2,1)}, bf16[128,3584]{1,0:T(8,128)(2,1)S(1)}, u32[]{:S(2)}) copy-start(bf16[128,3584]{1,0:T(8,128)(2,1)S(1)} %get-tuple-element.51.refs_0_) | copy-start | bytes 2752516
  22.6 19.8 %copy-start.3 = (bf16[3584,512]{1,0:T(8,128)(2,1)S(1)}, bf16[3584,512]{1,0:T(8,128)(2,1)}, u32[]{:S(2)}) copy-start(bf16[3584,512]{1,0:T(8,128)(2,1)} %copy-done.2) | copy-start | bytes 11010052
  22.6 19.8 %copy-start.6 = (bf16[3584,512]{1,0:T(8,128)(2,1)S(1)}, bf16[3584,512]{1,0:T(8,128)(2,1)}, u32[]{:S(2)}) copy-start(bf16[3584,512]{1,0:T(8,128)(2,1)} %copy-done.5) | copy-start | bytes 11010052
  22.6 32.0 %collective-permute-start.1 = (bf16[272,512]{1,0:T(8,128)(2,1)}, bf16[272,512]{1,0:T(8,128)(2,1)}, u32[]{:S(2)}, u32[]{:S(2)}) collective-permute-start(bf16[272,512]{1,0:T(8,128)(2,1)} %own_block.1.refs_0_), channel_id=1, source_target_pairs={{0,8},{1,9},{2,10},{3,11},{4,12},{5,13},{6,14},{7,15},{8,0},{9,1},... | collective-permute-start | bytes 835592 | tf_op jit(solution)/shard_map/ppermute | solution.py:252
  26.6 28.0 %collective-permute-start.2 = (bf16[272,512]{1,0:T(8,128)(2,1)}, bf16[272,512]{1,0:T(8,128)(2,1)}, u32[]{:S(2)}, u32[]{:S(2)}) collective-permute-start(bf16[272,512]{1,0:T(8,128)(2,1)} %own_block.1.refs_0_), channel_id=1, source_target_pairs={{0,4},{1,3},{2,6},{3,1},{4,0},{5,7},{6,2},{7,5},{8,12},{9,11},{10,... | collective-permute-start | bytes 835592 | tf_op jit(solution)/shard_map/ppermute | solution.py:252
  28.2 26.5 %collective-permute-start.3 = (bf16[272,512]{1,0:T(8,128)(2,1)}, bf16[272,512]{1,0:T(8,128)(2,1)S(1)}, u32[]{:S(2)}, u32[]{:S(2)}) collective-permute-start(bf16[272,512]{1,0:T(8,128)(2,1)} %own_block.1.refs_0_), channel_id=1, source_target_pairs={{0,2},{1,5},{2,0},{3,7},{4,6},{5,1},{6,4},{7,3},{8,10},{9,13},{10,... | collective-permute-start | bytes 835592 | tf_op jit(solution)/shard_map/ppermute | solution.py:252
  36.6 1.8 %copy-start.15 = (bf16[3584,512]{1,0:T(8,128)(2,1)}, bf16[3584,512]{1,0:T(8,128)(2,1)S(1)}, u32[]{:S(2)}) copy-start(bf16[3584,512]{1,0:T(8,128)(2,1)S(1)} %get-tuple-element.68.refs_3_.refs_11_) | copy-start | bytes 11010052
  38.5 1.9 %copy-start.18 = (bf16[3584,512]{1,0:T(8,128)(2,1)}, bf16[3584,512]{1,0:T(8,128)(2,1)S(1)}, u32[]{:S(2)}) copy-start(bf16[3584,512]{1,0:T(8,128)(2,1)S(1)} %get-tuple-element.69.refs_4_.refs_12_) | copy-start | bytes 11010052
  40.3 17.1 %copy-start.21 = (bf16[3584,512]{1,0:T(8,128)(2,1)}, bf16[3584,512]{1,0:T(8,128)(2,1)S(1)}, u32[]{:S(2)}) copy-start(bf16[3584,512]{1,0:T(8,128)(2,1)S(1)} %get-tuple-element.64.refs_3_.refs_13_.refs_5_) | copy-start | bytes 11010052
  40.3 17.1 %copy-start.23 = (bf16[3584,512]{1,0:T(8,128)(2,1)}, bf16[3584,512]{1,0:T(8,128)(2,1)S(1)}, u32[]{:S(2)}) copy-start(bf16[3584,512]{1,0:T(8,128)(2,1)S(1)} %get-tuple-element.65.refs_4_.refs_14_.refs_6_) | copy-start | bytes 11010052
  40.3 9.2 %collective-permute-start.4 = (f32[24,512]{1,0:T(8,128)S(1)}, f32[24,512]{1,0:T(8,128)S(1)}, u32[]{:S(2)}, u32[]{:S(2)}) collective-permute-start(f32[24,512]{1,0:T(8,128)S(1)} %get-tuple-element.50), channel_id=1, source_target_pairs={{0,2},{1,5},{2,0},{3,7},{4,6},{5,1},{6,4},{7,3},{8,10},{9,13},{10,... | collective-permute-start | bytes 147464 | tf_op jit(solution)/shard_map/ppermute | solution.py:252
  41.0 1.4 %copy-start.29 = (bf16[128,3584]{1,0:T(8,128)(2,1)}, bf16[128,3584]{1,0:T(8,128)(2,1)S(1)}, u32[]{:S(2)}) copy-start(bf16[128,3584]{1,0:T(8,128)(2,1)S(1)} %collective-permute-done.5.refs_1_) | copy-start | bytes 2752516
  42.4 1.9 %copy-start.30 = (bf16[128,3584]{1,0:T(8,128)(2,1)S(1)}, bf16[128,3584]{1,0:T(8,128)(2,1)}, u32[]{:S(2)}) copy-start(bf16[128,3584]{1,0:T(8,128)(2,1)} %copy-done.29) | copy-start | bytes 2752516
  44.2 1.2 copy-start.34
  45.4 5.7 %copy-start.9 = (bf16[3584,512]{1,0:T(8,128)(2,1)S(1)}, bf16[3584,512]{1,0:T(8,128)(2,1)}, u32[]{:S(2)}) copy-start(bf16[3584,512]{1,0:T(8,128)(2,1)} %copy-done.8) | copy-start | bytes 11010052
  45.4 5.7 %copy-start.12 = (bf16[3584,512]{1,0:T(8,128)(2,1)S(1)}, bf16[3584,512]{1,0:T(8,128)(2,1)}, u32[]{:S(2)}) copy-start(bf16[3584,512]{1,0:T(8,128)(2,1)} %copy-done.11) | copy-start | bytes 11010052
  49.6 14.6 %collective-permute-start.10 = (bf16[2,256,512]{2,1,0:T(8,128)(2,1)S(1)}, bf16[2,256,512]{2,1,0:T(8,128)(2,1)S(1)}, u32[]{:S(2)}, u32[]{:S(2)}) collective-permute-start(bf16[2,256,512]{2,1,0:T(8,128)(2,1)S(1)} %get-tuple-element.62), channel_id=1, source_target_pairs={{0,2},{1,5},{2,0},{3,7},{4,6},{5,1},{6,4},{7,3},{8,10},{9,13},{10,... | collective-permute-start | bytes 1572872 | tf_op jit(solution)/shard_map/ppermute | solution.py:252
  50.5 4.9 %collective-permute-start.6 = (f32[24,512]{1,0:T(8,128)S(1)}, f32[24,512]{1,0:T(8,128)S(1)}, u32[]{:S(2)}, u32[]{:S(2)}) collective-permute-start(f32[24,512]{1,0:T(8,128)S(1)} %add.107), channel_id=1, source_target_pairs={{0,4},{1,3},{2,6},{3,1},{4,0},{5,7},{6,2},{7,5},{8,12},{9,11},{10,... | collective-permute-start | bytes 147464 | tf_op jit(solution)/shard_map/ppermute | solution.py:252
  54.7 0.7 copy-start.35
  55.4 8.8 %collective-permute-start.9 = (bf16[272,512]{1,0:T(8,128)(2,1)}, bf16[272,512]{1,0:T(8,128)(2,1)}, u32[]{:S(2)}, u32[]{:S(2)}) collective-permute-start(bf16[272,512]{1,0:T(8,128)(2,1)} %collective-permute-done.1.refs_1_), channel_id=1, source_target_pairs={{0,4},{1,3},{2,6},{3,1},{4,0},{5,7},{6,2},{7,5},{8,12},{9,11},{10,... | collective-permute-start | bytes 835592 | tf_op jit(solution)/shard_map/ppermute | solution.py:252
  57.0 7.2 %collective-permute-start.11 = (f32[24,512]{1,0:T(8,128)S(1)}, f32[24,512]{1,0:T(8,128)S(1)}, u32[]{:S(2)}, u32[]{:S(2)}) collective-permute-start(f32[24,512]{1,0:T(8,128)S(1)} %add.108), channel_id=1, source_target_pairs={{0,8},{1,9},{2,10},{3,11},{4,12},{5,13},{6,14},{7,15},{8,0},{9,1},... | collective-permute-start | bytes 147464 | tf_op jit(solution)/shard_map/ppermute | solution.py:252
  60.2 21.2 %collective-permute-start.13 = (bf16[2,256,512]{2,1,0:T(8,128)(2,1)}, bf16[2,256,512]{2,1,0:T(8,128)(2,1)}, u32[]{:S(2)}, u32[]{:S(2)}) collective-permute-start(bf16[2,256,512]{2,1,0:T(8,128)(2,1)} %forward.5), channel_id=1, source_target_pairs={{0,2},{1,5},{2,0},{3,7},{4,6},{5,1},{6,4},{7,3},{8,10},{9,13},{10,... | collective-permute-start | bytes 1572872 | tf_op jit(solution)/shard_map/ppermute | solution.py:252
  65.1 19.3 %collective-permute-start.14 = (bf16[2,256,512]{2,1,0:T(8,128)(2,1)}, bf16[2,256,512]{2,1,0:T(8,128)(2,1)}, u32[]{:S(2)}, u32[]{:S(2)}) collective-permute-start(bf16[2,256,512]{2,1,0:T(8,128)(2,1)} %add_convert_fusion.1), channel_id=1, source_target_pairs={{0,4},{1,3},{2,6},{3,1},{4,0},{5,7},{6,2},{7,5},{8,12},{9,11},{10,... | collective-permute-start | bytes 1572872 | tf_op jit(solution)/shard_map/ppermute | solution.py:252
  66.6 11.8 %collective-permute-start.7 = (bf16[272,512]{1,0:T(8,128)(2,1)}, bf16[272,512]{1,0:T(8,128)(2,1)}, u32[]{:S(2)}, u32[]{:S(2)}) collective-permute-start(bf16[272,512]{1,0:T(8,128)(2,1)} %collective-permute-done.1.refs_1_), channel_id=1, source_target_pairs={{0,2},{1,5},{2,0},{3,7},{4,6},{5,1},{6,4},{7,3},{8,10},{9,13},{10,... | collective-permute-start | bytes 835592 | tf_op jit(solution)/shard_map/ppermute | solution.py:252
  67.8 13.5 %collective-permute-start.8 = (bf16[272,512]{1,0:T(8,128)(2,1)}, bf16[272,512]{1,0:T(8,128)(2,1)}, u32[]{:S(2)}, u32[]{:S(2)}) collective-permute-start(bf16[272,512]{1,0:T(8,128)(2,1)} %collective-permute-done.2.refs_2_), channel_id=1, source_target_pairs={{0,2},{1,5},{2,0},{3,7},{4,6},{5,1},{6,4},{7,3},{8,10},{9,13},{10,... | collective-permute-start | bytes 835592 | tf_op jit(solution)/shard_map/ppermute | solution.py:252
  68.6 15.7 %collective-permute-start.12 = (bf16[272,512]{1,0:T(8,128)(2,1)}, bf16[272,512]{1,0:T(8,128)(2,1)}, u32[]{:S(2)}, u32[]{:S(2)}) collective-permute-start(bf16[272,512]{1,0:T(8,128)(2,1)} %collective-permute-done.9.refs_3_), channel_id=1, source_target_pairs={{0,2},{1,5},{2,0},{3,7},{4,6},{5,1},{6,4},{7,3},{8,10},{9,13},{10,... | collective-permute-start | bytes 835592 | tf_op jit(solution)/shard_map/ppermute | solution.py:252
  70.0 2.0 %copy-start.16 = (bf16[3584,512]{1,0:T(8,128)(2,1)S(1)}, bf16[3584,512]{1,0:T(8,128)(2,1)}, u32[]{:S(2)}) copy-start(bf16[3584,512]{1,0:T(8,128)(2,1)} %copy-done.15) | copy-start | bytes 11010052
  72.1 2.0 %copy-start.19 = (bf16[3584,512]{1,0:T(8,128)(2,1)S(1)}, bf16[3584,512]{1,0:T(8,128)(2,1)}, u32[]{:S(2)}) copy-start(bf16[3584,512]{1,0:T(8,128)(2,1)} %copy-done.18) | copy-start | bytes 11010052
  74.1 13.8 %copy-start.4 = (bf16[3584,512]{1,0:T(8,128)(2,1)S(1)}, bf16[3584,512]{1,0:T(8,128)(2,1)}, u32[]{:S(2)}) copy-start(bf16[3584,512]{1,0:T(8,128)(2,1)} %copy-done.2) | copy-start | bytes 11010052
  74.1 13.8 %copy-start.7 = (bf16[3584,512]{1,0:T(8,128)(2,1)S(1)}, bf16[3584,512]{1,0:T(8,128)(2,1)}, u32[]{:S(2)}) copy-start(bf16[3584,512]{1,0:T(8,128)(2,1)} %copy-done.5) | copy-start | bytes 11010052
  74.1 13.8 %copy-start.10 = (bf16[3584,512]{1,0:T(8,128)(2,1)S(1)}, bf16[3584,512]{1,0:T(8,128)(2,1)}, u32[]{:S(2)}) copy-start(bf16[3584,512]{1,0:T(8,128)(2,1)} %copy-done.8) | copy-start | bytes 11010052
  74.1 13.9 %copy-start.32 = (bf16[272,512]{1,0:T(8,128)(2,1)S(1)}, bf16[272,512]{1,0:T(8,128)(2,1)}, u32[]{:S(2)}) copy-start(bf16[272,512]{1,0:T(8,128)(2,1)} %own_block.1.refs_0_) | copy-start | bytes 835588
  74.1 13.9 %copy-start.36 = (bf16[272,512]{1,0:T(8,128)(2,1)S(1)}, bf16[272,512]{1,0:T(8,128)(2,1)}, u32[]{:S(2)}) copy-start(bf16[272,512]{1,0:T(8,128)(2,1)} %copy-done.35) | copy-start | bytes 835588
  85.8 23.0 %collective-permute-start.15 = (bf16[256,512]{1,0:T(8,128)(2,1)S(1)}, bf16[256,512]{1,0:T(8,128)(2,1)S(1)}, u32[]{:S(2)}, u32[]{:S(2)}) collective-permute-start(bf16[256,512]{1,0:T(8,128)(2,1)S(1)} %fusion.10), channel_id=1, source_target_pairs={{0,8},{1,9},{2,10},{3,11},{4,12},{5,13},{6,14},{7,15},{8,0},{9,1},... | collective-permute-start | bytes 786440 | tf_op jit(solution)/shard_map/ppermute | solution.py:252
  88.0 2.0 %copy-start.13 = (bf16[3584,512]{1,0:T(8,128)(2,1)S(1)}, bf16[3584,512]{1,0:T(8,128)(2,1)}, u32[]{:S(2)}) copy-start(bf16[3584,512]{1,0:T(8,128)(2,1)} %copy-done.11) | copy-start | bytes 11010052
  90.0 2.0 %copy-start.17 = (bf16[3584,512]{1,0:T(8,128)(2,1)S(1)}, bf16[3584,512]{1,0:T(8,128)(2,1)}, u32[]{:S(2)}) copy-start(bf16[3584,512]{1,0:T(8,128)(2,1)} %copy-done.15) | copy-start | bytes 11010052
  92.1 2.0 %copy-start.20 = (bf16[3584,512]{1,0:T(8,128)(2,1)S(1)}, bf16[3584,512]{1,0:T(8,128)(2,1)}, u32[]{:S(2)}) copy-start(bf16[3584,512]{1,0:T(8,128)(2,1)} %copy-done.18) | copy-start | bytes 11010052
  94.1 2.0 %copy-start.22 = (bf16[3584,512]{1,0:T(8,128)(2,1)S(1)}, bf16[3584,512]{1,0:T(8,128)(2,1)}, u32[]{:S(2)}) copy-start(bf16[3584,512]{1,0:T(8,128)(2,1)} %copy-done.21) | copy-start | bytes 11010052
  96.2 2.0 %copy-start.24 = (bf16[3584,512]{1,0:T(8,128)(2,1)S(1)}, bf16[3584,512]{1,0:T(8,128)(2,1)}, u32[]{:S(2)}) copy-start(bf16[3584,512]{1,0:T(8,128)(2,1)} %copy-done.23) | copy-start | bytes 11010052
  98.2 9.2 %copy-start.37 = (f32[1024]{0:T(1024)S(1)}, f32[1024]{0:T(1024)}, u32[]{:S(2)}) copy-start(f32[1024]{0:T(1024)} %param.10) | copy-start | bytes 12292
  98.2 11.4 %copy-start.14 = (bf16[3584,512]{1,0:T(8,128)(2,1)S(1)}, bf16[3584,512]{1,0:T(8,128)(2,1)}, u32[]{:S(2)}) copy-start(bf16[3584,512]{1,0:T(8,128)(2,1)} %copy-done.11) | copy-start | bytes 11010052
  106.8 13.7 %collective-permute-start.17 = (bf16[128,2048]{1,0:T(8,128)(2,1)S(1)}, bf16[128,2048]{1,0:T(8,128)(2,1)S(1)}, u32[]{:S(2)}, u32[]{:S(2)}) collective-permute-start(bf16[128,2048]{1,0:T(8,128)(2,1)S(1)} %get-tuple-element.84), channel_id=1, source_target_pairs={{0,1},{1,0},{2,3},{3,2},{4,5},{5,4},{6,7},{7,6},{8,9},{9,8},{10,11... | collective-permute-start | bytes 1572872 | tf_op jit(solution)/shard_map/ppermute | solution.py:247
  106.9 1.9 %collective-permute-start.20 = (f32[16,512]{1,0:T(8,128)S(1)}, f32[16,512]{1,0:T(8,128)S(1)}, u32[]{:S(2)}, u32[]{:S(2)}) collective-permute-start(f32[16,512]{1,0:T(8,128)S(1)} %slice.79), channel_id=1, source_target_pairs={{0,1},{1,0},{2,3},{3,2},{4,5},{5,4},{6,7},{7,6},{8,9},{9,8},{10,11... | collective-permute-start | bytes 98312 | tf_op jit(solution)/shard_map/ppermute | solution.py:247
  109.0 10.6 %collective-permute-start.16 = (bf16[128,512]{1,0:T(8,128)(2,1)S(1)}, bf16[128,512]{1,0:T(8,128)(2,1)S(1)}, u32[]{:S(2)}, u32[]{:S(2)}) collective-permute-start(bf16[128,512]{1,0:T(8,128)(2,1)S(1)} %get-tuple-element.92), channel_id=1, source_target_pairs={{0,1},{1,0},{2,3},{3,2},{4,5},{5,4},{6,7},{7,6},{8,9},{9,8},{10,11... | collective-permute-start | bytes 393224 | tf_op jit(solution)/shard_map/ppermute | solution.py:247
  109.2 8.1 %collective-permute-start.19 = (f32[256,64]{1,0:T(8,128)S(1)}, f32[256,64]{1,0:T(8,128)S(1)}, u32[]{:S(2)}, u32[]{:S(2)}) collective-permute-start(f32[256,64]{1,0:T(8,128)S(1)} %get-tuple-element.86.refs_1_), channel_id=1, source_target_pairs={{0,1},{1,0},{2,3},{3,2},{4,5},{5,4},{6,7},{7,6},{8,9},{9,8},{10,11... | collective-permute-start | bytes 196616 | tf_op jit(solution)/shard_map/ppermute | solution.py:247
  109.6 7.7 %copy-start.31 = (bf16[128,3584]{1,0:T(8,128)(2,1)S(1)}, bf16[128,3584]{1,0:T(8,128)(2,1)}, u32[]{:S(2)}) copy-start(bf16[128,3584]{1,0:T(8,128)(2,1)} %copy-done.29) | copy-start | bytes 2752516
  109.6 8.0 %copy-start.28 = (bf16[128,3584]{1,0:T(8,128)(2,1)S(1)}, bf16[128,3584]{1,0:T(8,128)(2,1)}, u32[]{:S(2)}) copy-start(bf16[128,3584]{1,0:T(8,128)(2,1)} %refs_0_.1) | copy-start | bytes 2752516
  114.7 5.9 %collective-permute-start.18 = (bf16[128,1536]{1,0:T(8,128)(2,1)S(1)}, bf16[128,1536]{1,0:T(8,128)(2,1)S(1)}, u32[]{:S(2)}, u32[]{:S(2)}) collective-permute-start(bf16[128,1536]{1,0:T(8,128)(2,1)S(1)} %get-tuple-element.88), channel_id=1, source_target_pairs={{0,1},{1,0},{2,3},{3,2},{4,5},{5,4},{6,7},{7,6},{8,9},{9,8},{10,11... | collective-permute-start | bytes 1179656 | tf_op jit(solution)/shard_map/ppermute | solution.py:247
  114.9 1.6 %collective-permute-start.22 = (f32[512]{0:T(512)S(1)}, f32[512]{0:T(512)S(1)}, u32[]{:S(2)}, u32[]{:S(2)}) collective-permute-start(f32[512]{0:T(512)S(1)} %div.7), channel_id=1, source_target_pairs={{0,1},{1,0},{2,3},{3,2},{4,5},{5,4},{6,7},{7,6},{8,9},{9,8},{10,11... | collective-permute-start | bytes 6152 | tf_op jit(solution)/shard_map/ppermute | solution.py:247
  116.5 2.4 %collective-permute-start.21 = (f32[64,512]{1,0:T(8,128)S(1)}, f32[64,512]{1,0:T(8,128)S(1)}, u32[]{:S(2)}, u32[]{:S(2)}) collective-permute-start(f32[64,512]{1,0:T(8,128)S(1)} %fusion.2), channel_id=1, source_target_pairs={{0,1},{1,0},{2,3},{3,2},{4,5},{5,4},{6,7},{7,6},{8,9},{9,8},{10,11... | collective-permute-start | bytes 393224 | tf_op jit(solution)/shard_map/ppermute | solution.py:247

commit v4 on v3

--- a/solution.py
+++ b/solution.py
@@ -68,6 +68,7 @@
             out_specs=pl.BlockSpec((padded, half), lambda i, c: (0, 0)),
         ),
         out_shape=jax.ShapeDtypeStruct((padded, half), bf16),
+        compiler_params=params(),
         cost_estimate=small_cost,
         name="own_block",
     )(core, cotangent, other, magnitude_rows)

time: 122 us -> 112 us (0.918)
  local copies, waits for them, and re-layouts: 34.2 us -> 25.1 us
  Pallas kernels: 42.7 us -> 41 us
  starting transfers between devices: 21.6 us -> 23 us
    unnamed x76 -> x68, local copies, waits for them, and re-layouts: 33.8 us -> 24.7 us
    pallas_call x1, Pallas kernels: 1.69 us -> 0.02 us  [own_block(): pl.pallas_call(functools.partial(block_kernel, tokens), grid_spec=pltpu.P...]
    ppermute x14, starting transfers between devices: 19.2 us -> 20.6 us  [send(): return lax.ppermute(x, ('tensor', 'dp'), pairs)]
  transfers between devices with their start and end apart: 23 -> 23, of which waited for: 6 -> 7; matrix products, arithmetic and copies ran while one was open for 6% -> 6% of each run, Pallas kernels for 35% -> 37%
where the time goes in v4:
time: 112 us; the launch traced here: 111 us
  Pallas kernels  41 us (37%)
  local copies, waits for them, and re-layouts  25.1 us (22%)
  starting transfers between devices  23 us (21%)
  waiting for transfers between devices  11.7 us (10%)
  other arithmetic  7.11 us (6%)
  matrix products  1.95 us (2%)
    unnamed x68, local copies, waits for them, and re-layouts  24.7 us
    ppermute x14, starting transfers between devices, send(): return lax.ppermute(x, ('tensor', 'dp'), pairs)  20.6 us
    pallas_call x2, Pallas kernels, load(): pl.pallas_call(functools.partial(load_kernel, tokens, rank, n, first), in...  14.1 us
    pallas_call x2, Pallas kernels, backward(): pl.pallas_call(functools.partial(backward_kernel, tokens, n, start, band,...  13.7 us
    pallas_call x4, Pallas kernels, forward(): pl.pallas_call(functools.partial(forward_kernel, tokens, rank, len(held),...  13.2 us
    ppermute x14, waiting for transfers between devices, send(): return lax.ppermute(x, ('tensor', 'dp'), pairs)  9.5 us
    ppermute x9, starting transfers between devices, split_columns(): swap = lambda x: lax.ppermute(x, 'dp', [(0, 1), (1, 0)])  2.46 us
    concatenate x3, other arithmetic, join(): pair = jnp.concatenate([own, other, own], axis)  2.27 us
  transfers between devices with their start and end apart: 23, of which 7 were waited for; matrix products, arithmetic and copies ran while one was open for 6% of the time, Pallas kernels for 37%

profile of v4, /device:TPU:0, one launch (start us, length us, event | category | flops | bytes accessed | tf_op | source)
XLA Modules:
  0.0 111.0 jit_solution(14167044045231353660)
XLA Ops:
  0.6 0.5 collective-permute-start.5
  1.2 0.7 reduce-precision_convert_fusion.1
  2.2 1.2 %copy-done = bf16[64,8192]{1,0:T(8,128)(2,1)S(1)} copy-done((bf16[64,8192]{1,0:T(8,128)(2,1)S(1)}, bf16[64,8192]{1,0:T(8,128)(2,1)}, u32[]{:S(2)}) %copy-start) | copy-done | bytes 1048600
  3.5 1.0 copy-done.21
  4.5 1.2 %copy-done.23 = bf16[128,3584]{1,0:T(8,128)(2,1)S(1)} copy-done((bf16[128,3584]{1,0:T(8,128)(2,1)S(1)}, bf16[128,3584]{1,0:T(8,128)(2,1)}, u32[]{:S(2)}) %copy-start.23) | copy-done | bytes 917528
  5.7 7.2 %load.2 = (bf16[3584,512]{1,0:T(8,128)(2,1)S(1)}, bf16[3584,512]{1,0:T(8,128)(2,1)S(1)}, bf16[3584,512]{1,0:T(8,128)(2,1)S(1)}, bf16[3584,512]{1,0:T(8,128)(2,1)...) custom-call(s32[8]{0:T(128)S(1)} %stack.121.place_ref, bf16[128,3584]{1,0:T(8,128)(2,1)S(1)} %copy-done.23, ...), custom_call_target="tpu_custom_call" | custom-call | flops 1048576 | bytes 1048576 | tf_op jit(solution)/shard_map/load/pallas_call | solution.py:123
  13.0 4.1 %collective-permute-start.1 = (bf16[272,512]{1,0:T(8,128)(2,1)S(1)}, bf16[272,512]{1,0:T(8,128)(2,1)}, u32[]{:S(2)}, u32[]{:S(2)}) collective-permute-start(bf16[272,512]{1,0:T(8,128)(2,1)S(1)} %own_block.1.refs_0_), channel_id=1, source_target_pairs={{0,8},{1,9},{2,10},{3,11},{4,12},{5,13},{6,14},{7,15},{8,0},{9,1},... | collective-permute-start | bytes 835592 | tf_op jit(solution)/shard_map/ppermute | solution.py:253
  17.1 1.6 %collective-permute-start.2 = (bf16[272,512]{1,0:T(8,128)(2,1)S(1)}, bf16[272,512]{1,0:T(8,128)(2,1)}, u32[]{:S(2)}, u32[]{:S(2)}) collective-permute-start(bf16[272,512]{1,0:T(8,128)(2,1)S(1)} %own_block.1.refs_0_), channel_id=1, source_target_pairs={{0,4},{1,3},{2,6},{3,1},{4,0},{5,7},{6,2},{7,5},{8,12},{9,11},{10,... | collective-permute-start | bytes 835592 | tf_op jit(solution)/shard_map/ppermute | solution.py:253
  18.7 1.5 %collective-permute-start.3 = (bf16[272,512]{1,0:T(8,128)(2,1)S(1)}, bf16[272,512]{1,0:T(8,128)(2,1)S(1)}, u32[]{:S(2)}, u32[]{:S(2)}) collective-permute-start(bf16[272,512]{1,0:T(8,128)(2,1)S(1)} %own_block.1.refs_0_), channel_id=1, source_target_pairs={{0,2},{1,5},{2,0},{3,7},{4,6},{5,1},{6,4},{7,3},{8,10},{9,13},{10,... | collective-permute-start | bytes 835592 | tf_op jit(solution)/shard_map/ppermute | solution.py:253
  20.2 6.9 %load.3 = (bf16[3584,512]{1,0:T(8,128)(2,1)S(1)}, bf16[3584,512]{1,0:T(8,128)(2,1)S(1)}, bf16[3584,512]{1,0:T(8,128)(2,1)S(1)}, bf16[3584,512]{1,0:T(8,128)(2,1)S(1)}, f32[24,512]{1,0:T(8,128)S(1)}) custom-call(s32[8]{0:T(128)S(1)} %stack.133.place_ref, f32[24,512]{1,0:T(8,128)S(1)} %get-tuple-element.49.refs_0_, bf16[64,3584]{1,0:T(8,128)(2,1)S(1)} %bitcast.34, ...), custom_call_target="tpu_custom_call" | custom-call | flops 1048576 | bytes 1048576 | tf_op jit(solution)/shard_map/load/pallas_call | solution.py:123
  27.1 1.8 %copy-done.11 = bf16[3584,512]{1,0:T(8,128)(2,1)} copy-done((bf16[3584,512]{1,0:T(8,128)(2,1)}, bf16[3584,512]{1,0:T(8,128)(2,1)S(1)}, u32[]{:S(2)}) %copy-start.11) | copy-done | bytes 3670040
  29.0 1.9 %copy-done.14 = bf16[3584,512]{1,0:T(8,128)(2,1)} copy-done((bf16[3584,512]{1,0:T(8,128)(2,1)}, bf16[3584,512]{1,0:T(8,128)(2,1)S(1)}, u32[]{:S(2)}) %copy-start.14) | copy-done | bytes 3670040
  30.8 0.5 collective-permute-start.4
  31.5 1.4 %copy-done.25 = bf16[128,3584]{1,0:T(8,128)(2,1)} copy-done((bf16[128,3584]{1,0:T(8,128)(2,1)}, bf16[128,3584]{1,0:T(8,128)(2,1)S(1)}, u32[]{:S(2)}) %copy-start.25) | copy-done | bytes 917528
  32.8 1.9 %copy-done.26 = bf16[128,3584]{1,0:T(8,128)(2,1)S(1)} copy-done((bf16[128,3584]{1,0:T(8,128)(2,1)S(1)}, bf16[128,3584]{1,0:T(8,128)(2,1)}, u32[]{:S(2)}) %copy-start.26) | copy-done | bytes 917528
  34.7 4.2 %forward.4 = (bf16[2,256,512]{2,1,0:T(8,128)(2,1)S(1)}, bf16[256,3584]{1,0:T(8,128)(2,1)S(1)}, bf16[256,128]{1,0:T(8,128)(2,1)S(1)}) custom-call(s32[4]{0:T(128)S(1)} %pad_add_fusion.place_ref, bf16[128,3584]{1,0:T(8,128)(2,1)S(1)} %get-tuple-element.51.refs_0_, bf16[128,3584]{1,0:T(8,128)(2,1)S(1)} %copy-done.26, bf16[64,3584]{1,0:T(8,128)(2,1)S(1)} %bitcast.35, ...), custom_call_target="tpu_custom_call" | custom-call | flops 1048576 | bytes 1048576 | tf_op jit(solution)/shard_map/forward/pallas_call | solution.py:167
  38.9 1.0 collective-permute-start.10
  39.8 0.5 collective-permute-start.6
  40.5 3.6 %forward.5 = bf16[2,256,512]{2,1,0:T(8,128)(2,1)} custom-call(s32[4]{0:T(128)S(1)} %pad_add_fusion.1.place_ref, bf16[256,3584]{1,0:T(8,128)(2,1)S(1)} %get-tuple-element.56.refs_0_, bf16[256,128]{1,0:T(8,128)(2,1)S(1)} %get-tuple-element.57.refs_1_, bf16[64,8192]{1,0:T(8,128)(2,1)S(1)} %copy-done.1, ...), custom_call_target="tpu_custom_call" | custom-call | flops 1048576 | bytes 1048576 | tf_op jit(solution)/shard_map/forward/pallas_call | solution.py:167
  44.0 0.6 collective-permute-done.6
  44.6 1.1 collective-permute-start.9
  45.7 1.9 %collective-permute-start.11 = (f32[24,512]{1,0:T(8,128)S(1)}, f32[24,512]{1,0:T(8,128)S(1)}, u32[]{:S(2)}, u32[]{:S(2)}) collective-permute-start(f32[24,512]{1,0:T(8,128)S(1)} %add.108), channel_id=1, source_target_pairs={{0,8},{1,9},{2,10},{3,11},{4,12},{5,13},{6,14},{7,15},{8,0},{9,1},... | collective-permute-start | bytes 147464 | tf_op jit(solution)/shard_map/ppermute | solution.py:253
  47.7 2.8 %forward.6 = bf16[2,256,512]{2,1,0:T(8,128)(2,1)S(1)} custom-call(s32[4]{0:T(128)S(1)} %pad_add_fusion.2.place_ref, bf16[256,3584]{1,0:T(8,128)(2,1)S(1)} %get-tuple-element.56.refs_0_, bf16[256,128]{1,0:T(8,128)(2,1)S(1)} %get-tuple-element.57.refs_1_, bf16[64,8192]{1,0:T(8,128)(2,1)S(1)} %copy-done.1, ...), custom_call_target="tpu_custom_call" | custom-call | flops 1048576 | bytes 1048576 | tf_op jit(solution)/shard_map/forward/pallas_call | solution.py:167
  50.5 1.2 %collective-permute-start.13 = (bf16[2,256,512]{2,1,0:T(8,128)(2,1)}, bf16[2,256,512]{2,1,0:T(8,128)(2,1)}, u32[]{:S(2)}, u32[]{:S(2)}) collective-permute-start(bf16[2,256,512]{2,1,0:T(8,128)(2,1)} %forward.5), channel_id=1, source_target_pairs={{0,2},{1,5},{2,0},{3,7},{4,6},{5,1},{6,4},{7,3},{8,10},{9,13},{10,... | collective-permute-start | bytes 1572872 | tf_op jit(solution)/shard_map/ppermute | solution.py:253
  51.6 1.0 collective-permute-done.9.refs_3_
  52.6 0.9 add_convert_fusion.1
  53.5 2.8 %collective-permute-start.14 = (bf16[2,256,512]{2,1,0:T(8,128)(2,1)}, bf16[2,256,512]{2,1,0:T(8,128)(2,1)}, u32[]{:S(2)}, u32[]{:S(2)}) collective-permute-start(bf16[2,256,512]{2,1,0:T(8,128)(2,1)} %add_convert_fusion.1), channel_id=1, source_target_pairs={{0,4},{1,3},{2,6},{3,1},{4,0},{5,7},{6,2},{7,5},{8,12},{9,11},{10,... | collective-permute-start | bytes 1572872 | tf_op jit(solution)/shard_map/ppermute | solution.py:253
  56.3 1.3 %collective-permute-start.7 = (bf16[272,512]{1,0:T(8,128)(2,1)}, bf16[272,512]{1,0:T(8,128)(2,1)}, u32[]{:S(2)}, u32[]{:S(2)}) collective-permute-start(bf16[272,512]{1,0:T(8,128)(2,1)} %collective-permute-done.1.refs_1_), channel_id=1, source_target_pairs={{0,2},{1,5},{2,0},{3,7},{4,6},{5,1},{6,4},{7,3},{8,10},{9,13},{10,... | collective-permute-start | bytes 835592 | tf_op jit(solution)/shard_map/ppermute | solution.py:253
  57.6 0.7 collective-permute-start.8
  58.3 1.3 %collective-permute-start.12 = (bf16[272,512]{1,0:T(8,128)(2,1)}, bf16[272,512]{1,0:T(8,128)(2,1)}, u32[]{:S(2)}, u32[]{:S(2)}) collective-permute-start(bf16[272,512]{1,0:T(8,128)(2,1)} %collective-permute-done.9.refs_3_), channel_id=1, source_target_pairs={{0,2},{1,5},{2,0},{3,7},{4,6},{5,1},{6,4},{7,3},{8,10},{9,13},{10,... | collective-permute-start | bytes 835592 | tf_op jit(solution)/shard_map/ppermute | solution.py:253
  59.6 0.1 stack.138.place_ref
  59.8 2.0 %copy-done.12 = bf16[3584,512]{1,0:T(8,128)(2,1)S(1)} copy-done((bf16[3584,512]{1,0:T(8,128)(2,1)S(1)}, bf16[3584,512]{1,0:T(8,128)(2,1)}, u32[]{:S(2)}) %copy-start.12) | copy-done | bytes 3670040
  61.8 2.0 %copy-done.15 = bf16[3584,512]{1,0:T(8,128)(2,1)S(1)} copy-done((bf16[3584,512]{1,0:T(8,128)(2,1)S(1)}, bf16[3584,512]{1,0:T(8,128)(2,1)}, u32[]{:S(2)}) %copy-start.15) | copy-done | bytes 3670040
  63.9 2.7 %forward.7 = bf16[2,256,512]{2,1,0:T(8,128)(2,1)S(1)} custom-call(s32[4]{0:T(128)S(1)} %pad_add_fusion.3.place_ref, bf16[256,3584]{1,0:T(8,128)(2,1)S(1)} %get-tuple-element.56.refs_0_, bf16[256,128]{1,0:T(8,128)(2,1)S(1)} %get-tuple-element.57.refs_1_, bf16[64,8192]{1,0:T(8,128)(2,1)S(1)} %copy-done.1, bf16[3584,512]{1,0:T(8,128)(2,1)S(1)} %copy-done.12, ...), custom_call_target="tpu_custom_call" | custom-call | flops 1048576 | bytes 1048576 | tf_op jit(solution)/shard_map/forward/pallas_call | solution.py:167
  66.6 2.0 %collective-permute-done.7.refs_5_ = bf16[272,512]{1,0:T(8,128)(2,1)} collective-permute-done((bf16[272,512]{1,0:T(8,128)(2,1)}, bf16[272,512]{1,0:T(8,128)(2,1)}, u32[]{:S(2)}, u32[]{:S(2)}) %collective-permute-start.7) | collective-permute-done | bytes 278560 | tf_op jit(solution)/shard_map/ppermute | solution.py:253
  68.6 3.0 %collective-permute-done.8.refs_6_ = bf16[272,512]{1,0:T(8,128)(2,1)} collective-permute-done((bf16[272,512]{1,0:T(8,128)(2,1)}, bf16[272,512]{1,0:T(8,128)(2,1)}, u32[]{:S(2)}, u32[]{:S(2)}) %collective-permute-start.8) | collective-permute-done | bytes 278560 | tf_op jit(solution)/shard_map/ppermute | solution.py:253
  71.6 3.0 %collective-permute-done.12.refs_7_ = bf16[272,512]{1,0:T(8,128)(2,1)} collective-permute-done((bf16[272,512]{1,0:T(8,128)(2,1)}, bf16[272,512]{1,0:T(8,128)(2,1)}, u32[]{:S(2)}, u32[]{:S(2)}) %collective-permute-start.12) | collective-permute-done | bytes 278560 | tf_op jit(solution)/shard_map/ppermute | solution.py:253
  74.6 1.4 %convert_add_fusion = f32[2,256,512]{2,1,0:T(8,128)S(1)} fusion(bf16[2,256,512]{2,1,0:T(8,128)(2,1)} %collective-permute-done.14, bf16[2,256,512]{2,1,0:T(8,128)(2,1)} %collective-permute-done.13, bf16[2,256,512]{2,1,0:T(8,128)(2,1)S(1)} %forward.7), kind=kLoop, calls=%fused_computation.6 | loop fusion | flops 1310720 | bytes 2621440 | tf_op jit(solution)/shard_map/add | solution.py:305
  76.0 1.2 %collective-permute-start.15 = (bf16[256,512]{1,0:T(8,128)(2,1)S(1)}, bf16[256,512]{1,0:T(8,128)(2,1)S(1)}, u32[]{:S(2)}, u32[]{:S(2)}) collective-permute-start(bf16[256,512]{1,0:T(8,128)(2,1)S(1)} %fusion.10), channel_id=1, source_target_pairs={{0,8},{1,9},{2,10},{3,11},{4,12},{5,13},{6,14},{7,15},{8,0},{9,1},... | collective-permute-start | bytes 786440 | tf_op jit(solution)/shard_map/ppermute | solution.py:253
  77.3 2.0 %copy-done.9 = bf16[3584,512]{1,0:T(8,128)(2,1)S(1)} copy-done((bf16[3584,512]{1,0:T(8,128)(2,1)S(1)}, bf16[3584,512]{1,0:T(8,128)(2,1)}, u32[]{:S(2)}) %copy-start.9) | copy-done | bytes 3670040
  79.3 2.0 %copy-done.13 = bf16[3584,512]{1,0:T(8,128)(2,1)S(1)} copy-done((bf16[3584,512]{1,0:T(8,128)(2,1)S(1)}, bf16[3584,512]{1,0:T(8,128)(2,1)}, u32[]{:S(2)}) %copy-start.13) | copy-done | bytes 3670040
  81.3 2.0 %copy-done.16 = bf16[3584,512]{1,0:T(8,128)(2,1)S(1)} copy-done((bf16[3584,512]{1,0:T(8,128)(2,1)S(1)}, bf16[3584,512]{1,0:T(8,128)(2,1)}, u32[]{:S(2)}) %copy-start.16) | copy-done | bytes 3670040
  83.4 2.0 %copy-done.18 = bf16[3584,512]{1,0:T(8,128)(2,1)S(1)} copy-done((bf16[3584,512]{1,0:T(8,128)(2,1)S(1)}, bf16[3584,512]{1,0:T(8,128)(2,1)}, u32[]{:S(2)}) %copy-start.18) | copy-done | bytes 3670040
  85.4 2.0 %copy-done.20 = bf16[3584,512]{1,0:T(8,128)(2,1)S(1)} copy-done((bf16[3584,512]{1,0:T(8,128)(2,1)S(1)}, bf16[3584,512]{1,0:T(8,128)(2,1)}, u32[]{:S(2)}) %copy-start.20) | copy-done | bytes 3670040
  87.5 8.6 %backward.2 = (f32[128,2048]{1,0:T(8,128)S(1)}, bf16[128,2048]{1,0:T(8,128)(2,1)S(1)}, bf16[256,4096]{1,0:T(8,128)(2,1)S(1)}, f32[256,64]{1,0:T(8,128)S(1)}) custom-call(s32[16]{0:T(128)S(1)} %stack.138.place_ref, bf16[272,512]{1,0:T(8,128)(2,1)S(1)} %copy-done.29, bf16[272,512]{1,0:T(8,128)(2,1)} %collective-permute-done.1.refs_1_, ...), custom_call_target="tpu_custom_call" | custom-call | flops 1048576 | bytes 1048576 | tf_op jit(solution)/shard_map/backward/pallas_call | solution.py:226
  96.2 0.5 collective-permute-start.20
  96.7 1.4 %collective-permute-done.20 = f32[16,512]{1,0:T(8,128)S(1)} collective-permute-done((f32[16,512]{1,0:T(8,128)S(1)}, f32[16,512]{1,0:T(8,128)S(1)}, u32[]{:S(2)}, u32[]{:S(2)}) %collective-permute-start.20) | collective-permute-done | bytes 32800 | tf_op jit(solution)/shard_map/ppermute | solution.py:248
  98.1 0.2 fusion.4
  98.3 0.2 collective-permute-start.16
  98.5 0.4 collective-permute-start.19
  98.9 5.1 %backward.3 = (f32[128,1536]{1,0:T(8,128)S(1)}, bf16[128,1536]{1,0:T(8,128)(2,1)S(1)}) custom-call(s32[16]{0:T(128)S(1)} %stack.138.place_ref, bf16[256,4096]{1,0:T(8,128)(2,1)S(1)} %get-tuple-element.85.refs_0_, f32[256,64]{1,0:T(8,128)S(1)} %get-tuple-element.86.refs_1_, bf16[64,3584]{1,0:T(8,128)(2,1)S(1)} %bitcast.37, bf16[3584,512]{1,0:T(8,128)(2,1)S(1)} %copy-done.13, ...), custom_call_target="tpu_custom_call" | custom-call | flops 1048576 | bytes 1048576 | tf_op jit(solution)/shard_map/backward/pallas_call | solution.py:226
  104.0 0.2 collective-permute-start.18
  104.2 0.4 collective-permute-start.22
  104.6 0.2 fusion.12
  104.8 0.2 fusion.2
  105.0 0.8 collective-permute-done.22
  105.8 0.1 collective-permute-start.21
  105.9 0.7 fusion.35
  106.6 0.3 fusion.17
  106.9 1.2 %fusion.1 = f32[3584,64]{0,1:T(8,128)} fusion(f32[64,3584]{1,0:T(8,128)S(1)} %fusion.17, bf16[128,3584]{1,0:T(8,128)(2,1)S(1)} %copy-done.24, f32[256,64]{1,0:T(8,128)S(1)} %collective-permute-done.19, f32[256,64]{1,0:T(8,128)S(1)} %get-tuple-element.86.refs_1_), kind=kOutput, calls=%fused_computation.2 | convolution fusion | flops 59195392 | bytes 2883584 | tf_op jit(solution)/shard_map/dot_general | solution.py:21
  108.2 0.8 fusion.7
  108.9 0.8 fusion.9
  109.8 0.1 add_convert_fusion
  110.0 1.0 pad_maximum_fusion
  (97 shorter events, 1.2 us)
Async XLA Ops:
  0.6 30.8 %collective-permute-start.5 = (bf16[128,3584]{1,0:T(8,128)(2,1)}, bf16[128,3584]{1,0:T(8,128)(2,1)S(1)}, u32[]{:S(2)}, u32[]{:S(2)}) collective-permute-start(bf16[128,3584]{1,0:T(8,128)(2,1)} %refs_0_.1), channel_id=1, source_target_pairs={{0,1},{1,0},{2,3},{3,2},{4,5},{5,4},{6,7},{7,6},{8,9},{9,8},{10,11... | collective-permute-start | bytes 2752520 | tf_op jit(solution)/shard_map/ppermute | solution.py:248
  1.1 11.8 %collective-permute-start = (bf16[128,1024]{1,0:T(8,128)(2,1)}, bf16[128,1024]{1,0:T(8,128)(2,1)S(1)}, u32[]{:S(2)}, u32[]{:S(2)}) collective-permute-start(bf16[128,1024]{1,0:T(8,128)(2,1)} %own_ref.1), channel_id=1, source_target_pairs={{0,1},{1,0},{2,3},{3,2},{4,5},{5,4},{6,7},{7,6},{8,9},{9,8},{10,11... | collective-permute-start | bytes 786440 | tf_op jit(solution)/shard_map/ppermute | solution.py:248
  2.2 1.2 %copy-start = (bf16[64,8192]{1,0:T(8,128)(2,1)S(1)}, bf16[64,8192]{1,0:T(8,128)(2,1)}, u32[]{:S(2)}) copy-start(bf16[64,8192]{1,0:T(8,128)(2,1)} %refs_9_.1) | copy-start | bytes 3145732
  3.5 1.0 copy-start.21
  4.5 1.2 %copy-start.23 = (bf16[128,3584]{1,0:T(8,128)(2,1)S(1)}, bf16[128,3584]{1,0:T(8,128)(2,1)}, u32[]{:S(2)}) copy-start(bf16[128,3584]{1,0:T(8,128)(2,1)} %refs_0_.1) | copy-start | bytes 2752516
  5.7 7.3 %copy-start.32 = (bf16[128,1024]{1,0:T(8,128)(2,1)S(1)}, bf16[128,1024]{1,0:T(8,128)(2,1)}, u32[]{:S(2)}) copy-start(bf16[128,1024]{1,0:T(8,128)(2,1)} %own_ref.1) | copy-start | bytes 786436
  5.7 14.5 %copy-start.1 = (bf16[64,8192]{1,0:T(8,128)(2,1)S(1)}, bf16[64,8192]{1,0:T(8,128)(2,1)}, u32[]{:S(2)}) copy-start(bf16[64,8192]{1,0:T(8,128)(2,1)} %refs_9_.1) | copy-start | bytes 3145732
  5.7 14.5 %copy-start.22 = (bf16[3584,64]{0,1:T(8,128)(2,1)S(1)}, bf16[3584,64]{0,1:T(8,128)(2,1)}, u32[]{:S(2)}) copy-start(bf16[3584,64]{0,1:T(8,128)(2,1)} %param.8) | copy-start | bytes 1376260
  12.8 20.0 %copy-start.2 = (bf16[3584,512]{1,0:T(8,128)(2,1)}, bf16[3584,512]{1,0:T(8,128)(2,1)S(1)}, u32[]{:S(2)}) copy-start(bf16[3584,512]{1,0:T(8,128)(2,1)S(1)} %get-tuple-element.52.refs_4_.refs_17_.refs_9_) | copy-start | bytes 11010052
  12.9 20.0 %copy-start.4 = (bf16[3584,512]{1,0:T(8,128)(2,1)}, bf16[3584,512]{1,0:T(8,128)(2,1)S(1)}, u32[]{:S(2)}) copy-start(bf16[3584,512]{1,0:T(8,128)(2,1)S(1)} %get-tuple-element.53.refs_5_.refs_18_.refs_10_) | copy-start | bytes 11010052
  12.9 27.6 %copy-start.6 = (bf16[3584,512]{1,0:T(8,128)(2,1)}, bf16[3584,512]{1,0:T(8,128)(2,1)S(1)}, u32[]{:S(2)}) copy-start(bf16[3584,512]{1,0:T(8,128)(2,1)S(1)} %get-tuple-element.58.refs_3_.refs_15_.refs_7_) | copy-start | bytes 11010052
  12.9 27.6 %copy-start.8 = (bf16[3584,512]{1,0:T(8,128)(2,1)}, bf16[3584,512]{1,0:T(8,128)(2,1)S(1)}, u32[]{:S(2)}) copy-start(bf16[3584,512]{1,0:T(8,128)(2,1)S(1)} %get-tuple-element.59.refs_4_.refs_16_.refs_8_) | copy-start | bytes 11010052
  13.0 14.1 %copy-start.28 = (bf16[272,512]{1,0:T(8,128)(2,1)}, bf16[272,512]{1,0:T(8,128)(2,1)S(1)}, u32[]{:S(2)}) copy-start(bf16[272,512]{1,0:T(8,128)(2,1)S(1)} %own_block.1.refs_0_) | copy-start | bytes 835588
  13.0 31.0 %collective-permute-start.1 = (bf16[272,512]{1,0:T(8,128)(2,1)S(1)}, bf16[272,512]{1,0:T(8,128)(2,1)}, u32[]{:S(2)}, u32[]{:S(2)}) collective-permute-start(bf16[272,512]{1,0:T(8,128)(2,1)S(1)} %own_block.1.refs_0_), channel_id=1, source_target_pairs={{0,8},{1,9},{2,10},{3,11},{4,12},{5,13},{6,14},{7,15},{8,0},{9,1},... | collective-permute-start | bytes 835592 | tf_op jit(solution)/shard_map/ppermute | solution.py:253
  17.1 26.9 %collective-permute-start.2 = (bf16[272,512]{1,0:T(8,128)(2,1)S(1)}, bf16[272,512]{1,0:T(8,128)(2,1)}, u32[]{:S(2)}, u32[]{:S(2)}) collective-permute-start(bf16[272,512]{1,0:T(8,128)(2,1)S(1)} %own_block.1.refs_0_), channel_id=1, source_target_pairs={{0,4},{1,3},{2,6},{3,1},{4,0},{5,7},{6,2},{7,5},{8,12},{9,11},{10,... | collective-permute-start | bytes 835592 | tf_op jit(solution)/shard_map/ppermute | solution.py:253
  18.7 25.4 %collective-permute-start.3 = (bf16[272,512]{1,0:T(8,128)(2,1)S(1)}, bf16[272,512]{1,0:T(8,128)(2,1)S(1)}, u32[]{:S(2)}, u32[]{:S(2)}) collective-permute-start(bf16[272,512]{1,0:T(8,128)(2,1)S(1)} %own_block.1.refs_0_), channel_id=1, source_target_pairs={{0,2},{1,5},{2,0},{3,7},{4,6},{5,1},{6,4},{7,3},{8,10},{9,13},{10,... | collective-permute-start | bytes 835592 | tf_op jit(solution)/shard_map/ppermute | solution.py:253
  27.1 1.8 %copy-start.11 = (bf16[3584,512]{1,0:T(8,128)(2,1)}, bf16[3584,512]{1,0:T(8,128)(2,1)S(1)}, u32[]{:S(2)}) copy-start(bf16[3584,512]{1,0:T(8,128)(2,1)S(1)} %get-tuple-element.68.refs_3_.refs_11_) | copy-start | bytes 11010052
  29.0 1.9 %copy-start.14 = (bf16[3584,512]{1,0:T(8,128)(2,1)}, bf16[3584,512]{1,0:T(8,128)(2,1)S(1)}, u32[]{:S(2)}) copy-start(bf16[3584,512]{1,0:T(8,128)(2,1)S(1)} %get-tuple-element.69.refs_4_.refs_12_) | copy-start | bytes 11010052
  30.8 16.8 %copy-start.17 = (bf16[3584,512]{1,0:T(8,128)(2,1)}, bf16[3584,512]{1,0:T(8,128)(2,1)S(1)}, u32[]{:S(2)}) copy-start(bf16[3584,512]{1,0:T(8,128)(2,1)S(1)} %get-tuple-element.64.refs_3_.refs_13_.refs_5_) | copy-start | bytes 11010052
  30.8 16.8 %copy-start.19 = (bf16[3584,512]{1,0:T(8,128)(2,1)}, bf16[3584,512]{1,0:T(8,128)(2,1)S(1)}, u32[]{:S(2)}) copy-start(bf16[3584,512]{1,0:T(8,128)(2,1)S(1)} %get-tuple-element.65.refs_4_.refs_14_.refs_6_) | copy-start | bytes 11010052
  30.8 8.0 %collective-permute-start.4 = (f32[24,512]{1,0:T(8,128)S(1)}, f32[24,512]{1,0:T(8,128)S(1)}, u32[]{:S(2)}, u32[]{:S(2)}) collective-permute-start(f32[24,512]{1,0:T(8,128)S(1)} %get-tuple-element.50), channel_id=1, source_target_pairs={{0,2},{1,5},{2,0},{3,7},{4,6},{5,1},{6,4},{7,3},{8,10},{9,13},{10,... | collective-permute-start | bytes 147464 | tf_op jit(solution)/shard_map/ppermute | solution.py:253
  31.4 1.4 %copy-start.25 = (bf16[128,3584]{1,0:T(8,128)(2,1)}, bf16[128,3584]{1,0:T(8,128)(2,1)S(1)}, u32[]{:S(2)}) copy-start(bf16[128,3584]{1,0:T(8,128)(2,1)S(1)} %collective-permute-done.5.refs_1_) | copy-start | bytes 2752516
  32.8 1.9 %copy-start.26 = (bf16[128,3584]{1,0:T(8,128)(2,1)S(1)}, bf16[128,3584]{1,0:T(8,128)(2,1)}, u32[]{:S(2)}) copy-start(bf16[128,3584]{1,0:T(8,128)(2,1)} %copy-done.25) | copy-start | bytes 2752516
  38.9 13.7 %collective-permute-start.10 = (bf16[2,256,512]{2,1,0:T(8,128)(2,1)S(1)}, bf16[2,256,512]{2,1,0:T(8,128)(2,1)S(1)}, u32[]{:S(2)}, u32[]{:S(2)}) collective-permute-start(bf16[2,256,512]{2,1,0:T(8,128)(2,1)S(1)} %get-tuple-element.62), channel_id=1, source_target_pairs={{0,2},{1,5},{2,0},{3,7},{4,6},{5,1},{6,4},{7,3},{8,10},{9,13},{10,... | collective-permute-start | bytes 1572872 | tf_op jit(solution)/shard_map/ppermute | solution.py:253
  39.8 4.7 %collective-permute-start.6 = (f32[24,512]{1,0:T(8,128)S(1)}, f32[24,512]{1,0:T(8,128)S(1)}, u32[]{:S(2)}, u32[]{:S(2)}) collective-permute-start(f32[24,512]{1,0:T(8,128)S(1)} %add.107), channel_id=1, source_target_pairs={{0,4},{1,3},{2,6},{3,1},{4,0},{5,7},{6,2},{7,5},{8,12},{9,11},{10,... | collective-permute-start | bytes 147464 | tf_op jit(solution)/shard_map/ppermute | solution.py:253
  44.0 6.4 %copy-start.30 = (bf16[272,512]{1,0:T(8,128)(2,1)}, bf16[272,512]{1,0:T(8,128)(2,1)S(1)}, u32[]{:S(2)}) copy-start(bf16[272,512]{1,0:T(8,128)(2,1)S(1)} %collective-permute-done.3.refs_4_) | copy-start | bytes 835588
  44.6 8.0 %collective-permute-start.9 = (bf16[272,512]{1,0:T(8,128)(2,1)}, bf16[272,512]{1,0:T(8,128)(2,1)}, u32[]{:S(2)}, u32[]{:S(2)}) collective-permute-start(bf16[272,512]{1,0:T(8,128)(2,1)} %collective-permute-done.1.refs_1_), channel_id=1, source_target_pairs={{0,4},{1,3},{2,6},{3,1},{4,0},{5,7},{6,2},{7,5},{8,12},{9,11},{10,... | collective-permute-start | bytes 835592 | tf_op jit(solution)/shard_map/ppermute | solution.py:253
  45.7 5.9 %collective-permute-start.11 = (f32[24,512]{1,0:T(8,128)S(1)}, f32[24,512]{1,0:T(8,128)S(1)}, u32[]{:S(2)}, u32[]{:S(2)}) collective-permute-start(f32[24,512]{1,0:T(8,128)S(1)} %add.108), channel_id=1, source_target_pairs={{0,8},{1,9},{2,10},{3,11},{4,12},{5,13},{6,14},{7,15},{8,0},{9,1},... | collective-permute-start | bytes 147464 | tf_op jit(solution)/shard_map/ppermute | solution.py:253
  50.5 21.2 %collective-permute-start.13 = (bf16[2,256,512]{2,1,0:T(8,128)(2,1)}, bf16[2,256,512]{2,1,0:T(8,128)(2,1)}, u32[]{:S(2)}, u32[]{:S(2)}) collective-permute-start(bf16[2,256,512]{2,1,0:T(8,128)(2,1)} %forward.5), channel_id=1, source_target_pairs={{0,2},{1,5},{2,0},{3,7},{4,6},{5,1},{6,4},{7,3},{8,10},{9,13},{10,... | collective-permute-start | bytes 1572872 | tf_op jit(solution)/shard_map/ppermute | solution.py:253
  53.5 21.1 %collective-permute-start.14 = (bf16[2,256,512]{2,1,0:T(8,128)(2,1)}, bf16[2,256,512]{2,1,0:T(8,128)(2,1)}, u32[]{:S(2)}, u32[]{:S(2)}) collective-permute-start(bf16[2,256,512]{2,1,0:T(8,128)(2,1)} %add_convert_fusion.1), channel_id=1, source_target_pairs={{0,4},{1,3},{2,6},{3,1},{4,0},{5,7},{6,2},{7,5},{8,12},{9,11},{10,... | collective-permute-start | bytes 1572872 | tf_op jit(solution)/shard_map/ppermute | solution.py:253
  56.3 12.3 %collective-permute-start.7 = (bf16[272,512]{1,0:T(8,128)(2,1)}, bf16[272,512]{1,0:T(8,128)(2,1)}, u32[]{:S(2)}, u32[]{:S(2)}) collective-permute-start(bf16[272,512]{1,0:T(8,128)(2,1)} %collective-permute-done.1.refs_1_), channel_id=1, source_target_pairs={{0,2},{1,5},{2,0},{3,7},{4,6},{5,1},{6,4},{7,3},{8,10},{9,13},{10,... | collective-permute-start | bytes 835592 | tf_op jit(solution)/shard_map/ppermute | solution.py:253
  57.6 14.0 %collective-permute-start.8 = (bf16[272,512]{1,0:T(8,128)(2,1)}, bf16[272,512]{1,0:T(8,128)(2,1)}, u32[]{:S(2)}, u32[]{:S(2)}) collective-permute-start(bf16[272,512]{1,0:T(8,128)(2,1)} %collective-permute-done.2.refs_2_), channel_id=1, source_target_pairs={{0,2},{1,5},{2,0},{3,7},{4,6},{5,1},{6,4},{7,3},{8,10},{9,13},{10,... | collective-permute-start | bytes 835592 | tf_op jit(solution)/shard_map/ppermute | solution.py:253
  58.3 16.2 %collective-permute-start.12 = (bf16[272,512]{1,0:T(8,128)(2,1)}, bf16[272,512]{1,0:T(8,128)(2,1)}, u32[]{:S(2)}, u32[]{:S(2)}) collective-permute-start(bf16[272,512]{1,0:T(8,128)(2,1)} %collective-permute-done.9.refs_3_), channel_id=1, source_target_pairs={{0,2},{1,5},{2,0},{3,7},{4,6},{5,1},{6,4},{7,3},{8,10},{9,13},{10,... | collective-permute-start | bytes 835592 | tf_op jit(solution)/shard_map/ppermute | solution.py:253
  59.8 2.0 %copy-start.12 = (bf16[3584,512]{1,0:T(8,128)(2,1)S(1)}, bf16[3584,512]{1,0:T(8,128)(2,1)}, u32[]{:S(2)}) copy-start(bf16[3584,512]{1,0:T(8,128)(2,1)} %copy-done.11) | copy-start | bytes 11010052
  61.8 2.0 %copy-start.15 = (bf16[3584,512]{1,0:T(8,128)(2,1)S(1)}, bf16[3584,512]{1,0:T(8,128)(2,1)}, u32[]{:S(2)}) copy-start(bf16[3584,512]{1,0:T(8,128)(2,1)} %copy-done.14) | copy-start | bytes 11010052
  63.9 13.3 %copy-start.3 = (bf16[3584,512]{1,0:T(8,128)(2,1)S(1)}, bf16[3584,512]{1,0:T(8,128)(2,1)}, u32[]{:S(2)}) copy-start(bf16[3584,512]{1,0:T(8,128)(2,1)} %copy-done.2) | copy-start | bytes 11010052
  63.9 13.4 %copy-start.5 = (bf16[3584,512]{1,0:T(8,128)(2,1)S(1)}, bf16[3584,512]{1,0:T(8,128)(2,1)}, u32[]{:S(2)}) copy-start(bf16[3584,512]{1,0:T(8,128)(2,1)} %copy-done.4) | copy-start | bytes 11010052
  63.9 13.4 %copy-start.7 = (bf16[3584,512]{1,0:T(8,128)(2,1)S(1)}, bf16[3584,512]{1,0:T(8,128)(2,1)}, u32[]{:S(2)}) copy-start(bf16[3584,512]{1,0:T(8,128)(2,1)} %copy-done.6) | copy-start | bytes 11010052
  63.9 13.4 %copy-start.29 = (bf16[272,512]{1,0:T(8,128)(2,1)S(1)}, bf16[272,512]{1,0:T(8,128)(2,1)}, u32[]{:S(2)}) copy-start(bf16[272,512]{1,0:T(8,128)(2,1)} %copy-done.28) | copy-start | bytes 835588
  63.9 13.4 %copy-start.31 = (bf16[272,512]{1,0:T(8,128)(2,1)S(1)}, bf16[272,512]{1,0:T(8,128)(2,1)}, u32[]{:S(2)}) copy-start(bf16[272,512]{1,0:T(8,128)(2,1)} %copy-done.30) | copy-start | bytes 835588
  76.0 22.1 %collective-permute-start.15 = (bf16[256,512]{1,0:T(8,128)(2,1)S(1)}, bf16[256,512]{1,0:T(8,128)(2,1)S(1)}, u32[]{:S(2)}, u32[]{:S(2)}) collective-permute-start(bf16[256,512]{1,0:T(8,128)(2,1)S(1)} %fusion.10), channel_id=1, source_target_pairs={{0,8},{1,9},{2,10},{3,11},{4,12},{5,13},{6,14},{7,15},{8,0},{9,1},... | collective-permute-start | bytes 786440 | tf_op jit(solution)/shard_map/ppermute | solution.py:253
  77.3 2.0 %copy-start.9 = (bf16[3584,512]{1,0:T(8,128)(2,1)S(1)}, bf16[3584,512]{1,0:T(8,128)(2,1)}, u32[]{:S(2)}) copy-start(bf16[3584,512]{1,0:T(8,128)(2,1)} %copy-done.8) | copy-start | bytes 11010052
  79.3 2.0 %copy-start.13 = (bf16[3584,512]{1,0:T(8,128)(2,1)S(1)}, bf16[3584,512]{1,0:T(8,128)(2,1)}, u32[]{:S(2)}) copy-start(bf16[3584,512]{1,0:T(8,128)(2,1)} %copy-done.11) | copy-start | bytes 11010052
  81.3 2.0 %copy-start.16 = (bf16[3584,512]{1,0:T(8,128)(2,1)S(1)}, bf16[3584,512]{1,0:T(8,128)(2,1)}, u32[]{:S(2)}) copy-start(bf16[3584,512]{1,0:T(8,128)(2,1)} %copy-done.14) | copy-start | bytes 11010052
  83.4 2.0 %copy-start.18 = (bf16[3584,512]{1,0:T(8,128)(2,1)S(1)}, bf16[3584,512]{1,0:T(8,128)(2,1)}, u32[]{:S(2)}) copy-start(bf16[3584,512]{1,0:T(8,128)(2,1)} %copy-done.17) | copy-start | bytes 11010052
  85.4 2.0 %copy-start.20 = (bf16[3584,512]{1,0:T(8,128)(2,1)S(1)}, bf16[3584,512]{1,0:T(8,128)(2,1)}, u32[]{:S(2)}) copy-start(bf16[3584,512]{1,0:T(8,128)(2,1)} %copy-done.19) | copy-start | bytes 11010052
  87.5 9.2 %copy-start.33 = (f32[1024]{0:T(1024)S(1)}, f32[1024]{0:T(1024)}, u32[]{:S(2)}) copy-start(f32[1024]{0:T(1024)} %param.10) | copy-start | bytes 12292
  87.5 11.4 %copy-start.10 = (bf16[3584,512]{1,0:T(8,128)(2,1)S(1)}, bf16[3584,512]{1,0:T(8,128)(2,1)}, u32[]{:S(2)}) copy-start(bf16[3584,512]{1,0:T(8,128)(2,1)} %copy-done.8) | copy-start | bytes 11010052
  96.1 13.7 %collective-permute-start.17 = (bf16[128,2048]{1,0:T(8,128)(2,1)S(1)}, bf16[128,2048]{1,0:T(8,128)(2,1)S(1)}, u32[]{:S(2)}, u32[]{:S(2)}) collective-permute-start(bf16[128,2048]{1,0:T(8,128)(2,1)S(1)} %get-tuple-element.84), channel_id=1, source_target_pairs={{0,1},{1,0},{2,3},{3,2},{4,5},{5,4},{6,7},{7,6},{8,9},{9,8},{10,11... | collective-permute-start | bytes 1572872 | tf_op jit(solution)/shard_map/ppermute | solution.py:248
  96.2 1.9 %collective-permute-start.20 = (f32[16,512]{1,0:T(8,128)S(1)}, f32[16,512]{1,0:T(8,128)S(1)}, u32[]{:S(2)}, u32[]{:S(2)}) collective-permute-start(f32[16,512]{1,0:T(8,128)S(1)} %slice.79), channel_id=1, source_target_pairs={{0,1},{1,0},{2,3},{3,2},{4,5},{5,4},{6,7},{7,6},{8,9},{9,8},{10,11... | collective-permute-start | bytes 98312 | tf_op jit(solution)/shard_map/ppermute | solution.py:248
  98.3 10.6 %collective-permute-start.16 = (bf16[128,512]{1,0:T(8,128)(2,1)S(1)}, bf16[128,512]{1,0:T(8,128)(2,1)S(1)}, u32[]{:S(2)}, u32[]{:S(2)}) collective-permute-start(bf16[128,512]{1,0:T(8,128)(2,1)S(1)} %get-tuple-element.92), channel_id=1, source_target_pairs={{0,1},{1,0},{2,3},{3,2},{4,5},{5,4},{6,7},{7,6},{8,9},{9,8},{10,11... | collective-permute-start | bytes 393224 | tf_op jit(solution)/shard_map/ppermute | solution.py:248
  98.5 8.1 %collective-permute-start.19 = (f32[256,64]{1,0:T(8,128)S(1)}, f32[256,64]{1,0:T(8,128)S(1)}, u32[]{:S(2)}, u32[]{:S(2)}) collective-permute-start(f32[256,64]{1,0:T(8,128)S(1)} %get-tuple-element.86.refs_1_), channel_id=1, source_target_pairs={{0,1},{1,0},{2,3},{3,2},{4,5},{5,4},{6,7},{7,6},{8,9},{9,8},{10,11... | collective-permute-start | bytes 196616 | tf_op jit(solution)/shard_map/ppermute | solution.py:248
  98.9 7.7 %copy-start.27 = (bf16[128,3584]{1,0:T(8,128)(2,1)S(1)}, bf16[128,3584]{1,0:T(8,128)(2,1)}, u32[]{:S(2)}) copy-start(bf16[128,3584]{1,0:T(8,128)(2,1)} %copy-done.25) | copy-start | bytes 2752516
  98.9 8.0 %copy-start.24 = (bf16[128,3584]{1,0:T(8,128)(2,1)S(1)}, bf16[128,3584]{1,0:T(8,128)(2,1)}, u32[]{:S(2)}) copy-start(bf16[128,3584]{1,0:T(8,128)(2,1)} %refs_0_.1) | copy-start | bytes 2752516
  104.0 5.9 %collective-permute-start.18 = (bf16[128,1536]{1,0:T(8,128)(2,1)S(1)}, bf16[128,1536]{1,0:T(8,128)(2,1)S(1)}, u32[]{:S(2)}, u32[]{:S(2)}) collective-permute-start(bf16[128,1536]{1,0:T(8,128)(2,1)S(1)} %get-tuple-element.88), channel_id=1, source_target_pairs={{0,1},{1,0},{2,3},{3,2},{4,5},{5,4},{6,7},{7,6},{8,9},{9,8},{10,11... | collective-permute-start | bytes 1179656 | tf_op jit(solution)/shard_map/ppermute | solution.py:248
  104.2 1.6 %collective-permute-start.22 = (f32[512]{0:T(512)S(1)}, f32[512]{0:T(512)S(1)}, u32[]{:S(2)}, u32[]{:S(2)}) collective-permute-start(f32[512]{0:T(512)S(1)} %div.7), channel_id=1, source_target_pairs={{0,1},{1,0},{2,3},{3,2},{4,5},{5,4},{6,7},{7,6},{8,9},{9,8},{10,11... | collective-permute-start | bytes 6152 | tf_op jit(solution)/shard_map/ppermute | solution.py:248
  105.8 2.4 %collective-permute-start.21 = (f32[64,512]{1,0:T(8,128)S(1)}, f32[64,512]{1,0:T(8,128)S(1)}, u32[]{:S(2)}, u32[]{:S(2)}) collective-permute-start(f32[64,512]{1,0:T(8,128)S(1)} %fusion.2), channel_id=1, source_target_pairs={{0,1},{1,0},{2,3},{3,2},{4,5},{5,4},{6,7},{7,6},{8,9},{9,8},{10,11... | collective-permute-start | bytes 393224 | tf_op jit(solution)/shard_map/ppermute | solution.py:248

commit v5 on v4

--- a/solution.py
+++ b/solution.py
@@ -10,7 +10,7 @@
 adapter_scale = 2.0
 stability_floor = 1e-06
 pad_rows = 16
-vmem_bytes = 5 * 1024 * 1024
+vmem_bytes = 10 * 1024 * 1024
 f32, bf16 = jnp.float32, jnp.bfloat16
 small_cost = pl.CostEstimate(flops=1 << 20, bytes_accessed=1 << 20, transcendentals=0)
 contract_trailing = (((1,), (1,)), ((), ()))
@@ -41,8 +41,12 @@
     return pl.BlockSpec(memory_space=pltpu.VMEM)
 
 
-def params():
-    return pltpu.CompilerParams(vmem_limit_bytes=vmem_bytes)
+def anywhere():
+    return pl.BlockSpec(memory_space=pl.ANY)
+
+
+def params(size=vmem_bytes):
+    return pltpu.CompilerParams(vmem_limit_bytes=size)
 
 
 def block_kernel(tokens, core_ref, own_ref, other_ref, magnitude_ref, out_ref):
@@ -74,25 +78,62 @@
     )(core, cotangent, other, magnitude_rows)
 
 
-def load_kernel(tokens, rank, n, first, place_ref, *refs):
+def block_copies(place_ref, w_hbm, held, sem):
+    half = held[0].shape[1] if held else 0
+    columns = [pl.ds(pl.multiple_of(place_ref[k] * half, half), half) for k in range(len(held))]
+    return [pltpu.make_async_copy(w_hbm.at[:, c], h, sem.at[k]) for k, (c, h) in enumerate(zip(columns, held))]
+
+
+def load_kernel(blocks, place_ref, w_hbm, *refs):
+    count = (len(refs) - 1 - blocks) // 2
+    whole = refs[:count]
+    held, outs, sem = refs[count : count + blocks], refs[count + blocks : -1], refs[-1]
+    copies = [pltpu.make_async_copy(x, o, sem.at[blocks + i]) for i, (x, o) in enumerate(zip(whole, outs))]
+    copies = block_copies(place_ref, w_hbm, held, sem) + copies
+    for copy in copies:
+        copy.start()
+    for copy in copies:
+        copy.wait()
+
+
+def load(place, weight, half, whole=(), size=vmem_bytes):
+    blocks = place.shape[0] // 2
+    return pl.pallas_call(
+        functools.partial(load_kernel, blocks),
+        in_specs=[pl.BlockSpec(memory_space=pltpu.SMEM)] + [anywhere()] * (1 + len(whole)),
+        out_specs=[vmem()] * (blocks + len(whole)),
+        out_shape=[jax.ShapeDtypeStruct((weight.shape[0], half), bf16)] * blocks
+        + [jax.ShapeDtypeStruct(x.shape, x.dtype) for x in whole],
+        scratch_shapes=[pltpu.SemaphoreType.DMA((blocks + len(whole),))],
+        compiler_params=params(size),
+        cost_estimate=small_cost,
+        name="load",
+    )(place, weight, *whole)
+
+
+def forward_kernel(tokens, rank, n, blocks, first, place_ref, next_ref, w_hbm, up_ref, *refs):
+    held, refs = refs[:blocks], refs[blocks:]
     if first:
-        own_ref, at_ref, up_ref, w_hbm, *held, stats_ref, own_out, sem, own_sem = refs
+        own_ref, other_ref, at_ref, out_ref, stats_ref, *ahead, lhs_ref, adapter_ref, sem, other_sem = refs
     else:
-        before_ref, at_ref, up_ref, w_hbm, *held, stats_ref, sem = refs
-    blocks, half = len(held), held[0].shape[1]
-    column = lambda k: pl.ds(pl.multiple_of(place_ref[k] * half, half), half)
-    copy = lambda k: pltpu.make_async_copy(w_hbm.at[:, column(k)], held[k], sem.at[k])
+        lhs_ref, adapter_ref, before_ref, out_ref, stats_ref, *ahead, sem = refs
+    both = 2 * tokens
+    half = out_ref.shape[2]
+    copies = block_copies(next_ref, w_hbm, ahead, sem)
     if first:
-        own_copy = pltpu.make_async_copy(own_ref, own_out, own_sem)
-        own_copy.start()
-    for k in range(blocks):
-        copy(k).start()
-
-    down = at_ref[...]
-    high, low = split_pair(dot(down, down, contract_trailing))
+        other_copy = pltpu.make_async_copy(other_ref, lhs_ref.at[tokens:both], other_sem)
+        other_copy.start()
+    for copy in copies:
+        copy.start()
     if first:
-        own_copy.wait()
-        turned = dot(down, own_out[...], contract_trailing)
+        lhs_ref[:tokens, :] = own_ref[...]
+        lhs_ref[both:, :] = at_ref[...]
+        other_copy.wait()
+        lowrank = dot(lhs_ref[...], at_ref[...], contract_trailing)
+        high, low = split_pair(lowrank)
+        adapter_ref[:, :rank] = high
+        adapter_ref[:, rank:] = low
+        turned = lowrank[:tokens].T
         lanes = half // tokens
         span = rank // lanes
         stats_ref[:n, :] = jnp.zeros((n, half), f32)
@@ -100,91 +141,56 @@
             stats_ref[n:, j * tokens : (j + 1) * tokens] = turned[j * span : (j + 1) * span]
     else:
         stats_ref[...] = before_ref[...]
-
     for k in range(blocks):
-        copy(k).wait()
-        up = up_ref[:, column(k)]
-        cross = 2 * dot(down, held[k][...]) + adapter_scale * (dot(high, up) + dot(low, up))
+        up = up_ref[:, pl.ds(pl.multiple_of(place_ref[k] * half, half), half)]
+        through = adapter_scale * dot(adapter_ref[...], jnp.concatenate([up, up], axis=0))
+        product = dot(lhs_ref[...], held[k][...])
+        out_ref[k] = (product[:both] + through[:both]).astype(bf16)
+        cross = 2 * adapter_scale * product[both:] + adapter_scale * through[both:]
         cross = jnp.sum(up.astype(f32) * cross, axis=0, keepdims=True)
-        stats_ref[pl.ds(place_ref[blocks + k], 1), :] = sum_of_squares(held[k]) + adapter_scale * cross
-
-
-def load(n, place, weight, at, up, half, own=None, before=None):
-    blocks = place.shape[0] // 2
-    rows = weight.shape[0]
-    rank = at.shape[0]
-    any_ = pl.BlockSpec(memory_space=pl.ANY)
-    first = before is None
-    if first:
-        tokens = own.shape[0]
-        stats = (n + rank * tokens // half, half)
-    else:
-        tokens, stats = None, before.shape
-    return pl.pallas_call(
-        functools.partial(load_kernel, tokens, rank, n, first),
-        in_specs=[pl.BlockSpec(memory_space=pltpu.SMEM), any_ if first else vmem(), vmem(), vmem(), any_],
-        out_specs=[vmem()] * (blocks + (2 if first else 1)),
-        out_shape=[jax.ShapeDtypeStruct((rows, half), bf16)] * blocks
-        + [jax.ShapeDtypeStruct(stats, f32)]
-        + ([jax.ShapeDtypeStruct(own.shape, bf16)] if first else []),
-        scratch_shapes=[pltpu.SemaphoreType.DMA((blocks,))] + ([pltpu.SemaphoreType.DMA] if first else []),
-        compiler_params=params(),
-        cost_estimate=small_cost,
-        name="load",
-    )(place, own if first else before, at, up, weight)
-
-
-def forward_kernel(tokens, rank, blocks, first, place_ref, *refs):
-    if first:
-        own_ref, other_ref, at_ref, up_ref, *held, out_ref, lhs_ref, adapter_ref, sem = refs
-        copy = pltpu.make_async_copy(other_ref, lhs_ref.at[tokens:], sem)
-        copy.start()
-        lhs_ref[:tokens, :] = own_ref[...]
+        stats_ref[pl.ds(place_ref[blocks + k], 1), :] = sum_of_squares(held[k]) + cross
+    for copy in copies:
         copy.wait()
-        high, low = split_pair(dot(lhs_ref[...], at_ref[...], contract_trailing))
-        adapter_ref[:, :rank] = high
-        adapter_ref[:, rank:] = low
-    else:
-        lhs_ref, adapter_ref, up_ref, *held, out_ref = refs
-    half = out_ref.shape[2]
-    for i in range(blocks):
-        up = up_ref[:, pl.ds(pl.multiple_of(place_ref[i] * half, half), half)]
-        through = dot(adapter_ref[...], jnp.concatenate([up, up], axis=0))
-        out_ref[i] = (dot(lhs_ref[...], held[i][...]) + adapter_scale * through).astype(bf16)
-
-
-def forward(place, held, up, first=None, later=None):
+
+
+def forward(n, place, following, held, weight, up, first=None, later=None):
+    blocks = len(held)
     rows, half = held[0].shape
     if later is None:
         own, other, at = operands = first
         tokens, rank = own.shape[0], at.shape[0]
-        specs = [vmem(), pl.BlockSpec(memory_space=pl.ANY), vmem()]
+        specs = [vmem(), anywhere(), vmem()]
     else:
-        lhs, adapter = operands = later
-        rank, tokens = adapter.shape[1] // 2, lhs.shape[0] // 2
-        specs = [vmem()] * 2
-    extra = [((2 * tokens, rows), bf16), ((2 * tokens, 2 * rank), bf16)] if first else []
+        lhs, adapter, before = operands = later
+        rank = adapter.shape[1] // 2
+        tokens = (lhs.shape[0] - rank) // 2
+        specs = [vmem()] * 3
+    stats = (n + rank * tokens // half, half)
+    extra = [((2 * tokens + rank, rows), bf16), ((2 * tokens + rank, 2 * rank), bf16)] if first else []
+    ahead = 0 if following is None else blocks
+    smem = pl.BlockSpec(memory_space=pltpu.SMEM)
     return pl.pallas_call(
-        functools.partial(forward_kernel, tokens, rank, len(held), later is None),
-        in_specs=[pl.BlockSpec(memory_space=pltpu.SMEM), *specs] + [vmem()] * (1 + len(held)),
-        out_specs=[vmem()] * (1 + len(extra)),
-        out_shape=[jax.ShapeDtypeStruct((len(held), 2 * tokens, half), bf16)]
+        functools.partial(forward_kernel, tokens, rank, n, blocks, later is None),
+        in_specs=[smem, smem, anywhere(), vmem()] + [vmem()] * blocks + specs,
+        out_specs=[vmem()] * (2 + ahead + len(extra)),
+        out_shape=[jax.ShapeDtypeStruct((blocks, 2 * tokens, half), bf16), jax.ShapeDtypeStruct(stats, f32)]
+        + [jax.ShapeDtypeStruct((rows, half), bf16)] * ahead
         + [jax.ShapeDtypeStruct(*e) for e in extra],
-        scratch_shapes=[pltpu.SemaphoreType.DMA] if first else [],
+        scratch_shapes=[pltpu.SemaphoreType.DMA((blocks,))] + ([pltpu.SemaphoreType.DMA] if first else []),
         compiler_params=params(),
         cost_estimate=small_cost,
         name="forward",
-    )(place, *operands, up, *held)
+    )(place, place if following is None else following, weight, up, *held, *operands)
 
 
 def backward_kernel(tokens, n, start, band, first, place_ref, *refs):
     if first:
-        cots, (stats_ref, up_ref, at_ref, *held) = refs[:n], refs[n : 2 * n + 3]
+        cots, (stats_ref, up_ref, at_ref, *w_refs) = refs[:n], refs[n : 2 * n + 3]
         own_out, other_out, scaled_ref, proj_ref = refs[2 * n + 3 :]
     else:
-        scaled_ref, proj_ref, at_ref, *held, own_out, other_out = refs
+        scaled_ref, proj_ref, at_ref, *w_refs, own_out, other_out = refs
     both = 2 * tokens
-    half = held[0].shape[1]
+    half = w_refs[0].shape[1]
     spans = [slice(k * half, (k + 1) * half) for k in range(n)]
 
     if first:
@@ -205,12 +211,13 @@
     row = pl.ds(pl.multiple_of((start + pl.program_id(0)) * band, band), band)
     total = adapter_scale * dot(proj_ref[...].astype(bf16), at_ref[:, row])
     for k in range(n):
-        total = total + dot(scaled_ref[:, spans[k]], held[k][row, :], contract_trailing)
+        band_ref = w_refs[k] if w_refs[k].shape[0] == band else w_refs[k].at[row]
+        total = total + dot(scaled_ref[:, spans[k]], band_ref[...], contract_trailing)
     own_out[...] = total[:tokens]
     other_out[...] = total[tokens:].astype(bf16)
 
 
-def backward(place, start, bands, band, at, held, first=None, later=None):
+def backward(place, start, bands, band, at, held, weight, first=None, later=None):
     n = place.shape[0] // 2
     half = held[0].shape[1]
     rank = at.shape[0]
@@ -223,11 +230,16 @@
         operands, extra = later, []
         both = later[0].shape[0]
     tokens = both // 2
+    part = lambda k: pl.BlockSpec((band, half), lambda i, p: (start + i, p[k]))
+    streamed = range(len(held), n)
     return pl.pallas_call(
         functools.partial(backward_kernel, tokens, n, start, band, later is None),
-        grid=(bands,),
-        in_specs=[pl.BlockSpec(memory_space=pltpu.SMEM)] + [vmem()] * (len(operands) + 1 + n),
-        out_specs=[pl.BlockSpec((tokens, band), lambda i: (0, i))] * 2 + [vmem()] * len(extra),
+        grid_spec=pltpu.PrefetchScalarGridSpec(
+            num_scalar_prefetch=1,
+            grid=(bands,),
+            in_specs=[vmem()] * (len(operands) + 1 + len(held)) + [part(k) for k in streamed],
+            out_specs=[pl.BlockSpec((tokens, band), lambda i, p: (0, i))] * 2 + [vmem()] * len(extra),
+        ),
         out_shape=[
             jax.ShapeDtypeStruct((tokens, bands * band), f32),
             jax.ShapeDtypeStruct((tokens, bands * band), bf16),
@@ -236,7 +248,7 @@
         compiler_params=params(),
         cost_estimate=small_cost,
         name="backward",
-    )(place, *operands, at, *held)
+    )(place, *operands, at, *held, *[weight] * len(streamed))
 
 
 def split_columns(hidden, weight, down, up, magnitude, cotangent):
@@ -260,14 +272,14 @@
         return jnp.stack([2 * s + core for s in shard] + shard).astype(jnp.int32)
 
     mine = lambda x, axis: lax.dynamic_slice_in_dim(x, core * half, half, axis)
-    at = down.T
     tie = lax.optimization_barrier
 
     cot_other = swap(cotangent)
     hidden_other = swap(hidden)
-    run_load = functools.partial(load, n, weight=weight, at=at, up=up, half=half)
-    *far, stats, own = run_load(place(0b100, 0b101, 0b110, 0b111), own=hidden)
-    cot_other, stats = tie((cot_other, stats))
+    pieces = [(0b110, 0b111), (0b100, 0b101), (0b010, 0b011), (0b000, 0b001)]
+    places = [place(*vs) for vs in pieces]
+    ahead, at = list(load(places[0], weight, half)), down.T
+    cot_other, ahead[0] = tie((cot_other, ahead[0]))
     first = lax.reduce_precision(magnitude, 8, 7)
     second = lax.reduce_precision(magnitude - first, 8, 7)
     third = magnitude - first - second
@@ -277,33 +289,32 @@
     block = own_block(core.astype(jnp.int32).reshape(1), cotangent, cot_other, magnitude_rows)
 
     cots = {0b000: block, 0b001: send(block, 2), 0b010: send(block, 1), 0b100: send(block, 0)}
-    *near, stats = run_load(place(0b000, 0b001, 0b010, 0b011), before=stats)
+
+    run = lambda i, *rest, **more: forward(n, places[i], *rest, weight=weight, up=up, **more)
+    far1, stats, *ahead, lhs, adapter = run(0, places[1], ahead, first=(hidden, hidden_other, at))
+    from1 = send(far1, 0)
+    far0, stats, *ahead = run(1, places[2], ahead, later=(lhs, adapter, stats))
+    from0 = send(far0, 0)
+    *got, stats = tie((*(cots[v] for v in (0b001, 0b010, 0b100)), stats))
+    cots[0b001], cots[0b010], cots[0b100] = got
+    cots[0b011], cots[0b101], cots[0b110] = send(cots[0b001], 1), send(cots[0b001], 0), send(cots[0b010], 0)
+    held = ahead
+    near1, stats, *ahead = run(2, places[3], ahead, later=(lhs, adapter, stats))
+    cots[0b011], from1, stats = tie((cots[0b011], from1, stats))
+    cots[0b111] = send(cots[0b011], 0)
+    sent = (near1.astype(f32) + from1.astype(f32)).astype(bf16)
+    arrived = send(sent, 1)
+    held = ahead + held
+    near0, stats = run(3, None, ahead, later=(lhs, adapter, stats))
+    cots[0b101], cots[0b110], from0, stats = tie((cots[0b101], cots[0b110], from0, stats))
 
     got = send(stats, 0)
-    far1, lhs, adapter = forward(place(0b110, 0b111), far[2:], up, first=(own, hidden_other, at))
-    run = functools.partial(forward, up=up, later=(lhs, adapter))
-    got, far1 = tie((got, far1))
     stats = stats + got
-    got = send(stats, 1)
-    from1 = send(far1, 0)
-    far0 = run(place(0b100, 0b101), far[:2])[0]
-    *arrived, got, far0 = tie((*(cots[v] for v in (0b001, 0b010, 0b100)), got, far0))
-    cots[0b001], cots[0b010], cots[0b100] = arrived
-    stats = stats + got
-    got = send(stats, 2)
-    from0 = send(far0, 0)
-    cots[0b011], cots[0b101], cots[0b110] = send(cots[0b001], 1), send(cots[0b001], 0), send(cots[0b010], 0)
-    near1 = run(place(0b010, 0b011), near[2:])[0]
-    cots[0b011], from1, got, near1 = tie((cots[0b011], from1, got, near1))
-    stats = stats + got
-    cots[0b111] = send(cots[0b011], 0)
-    arrived = send((near1.astype(f32) + from1.astype(f32)).astype(bf16), 1)
-    near0 = run(place(0b000, 0b001), near[:2])[0]
-    cots[0b101], cots[0b110], cots[0b111], from0, near0, arrived, stats = tie(
-        (cots[0b101], cots[0b110], cots[0b111], from0, near0, arrived, stats)
-    )
+    stats = stats + send(stats, 1)
+    arrived, cots[0b111], stats = tie((arrived, cots[0b111], stats))
     kept = near0.astype(f32) + from0.astype(f32) + arrived.astype(f32)
     last = send(kept[1].astype(bf16), 2)
+    stats = stats + send(stats, 2)
     lowrank_rows = stats[n:]
     lowrank_other = swap(lowrank_rows)
 
@@ -311,7 +322,7 @@
     bands = rows // band
     many = (bands + 2) // 2
     order = place(*range(n))
-    run = functools.partial(backward, order, band=band, at=at, held=near + far)
+    run = functools.partial(backward, order, band=band, at=at, held=held, weight=weight)
     grad_a, other_a, scaled, proj = run(0, many, first=([cots[v] for v in range(n)], stats, up))
     got_a = swap(other_a)
     last, proj = tie((last, proj))

time: 112 us -> 121 us (1.080)
  waiting for transfers between devices: 11.7 us -> 19.5 us
  Pallas kernels: 41 us -> 46.4 us
  local copies, waits for them, and re-layouts: 25.1 us -> 20.5 us
  other arithmetic: 7.11 us -> 9.51 us
  starting transfers between devices: 23 us -> 21.1 us
    ppermute x14, waiting for transfers between devices: 9.5 us -> 17.3 us  [send(): return lax.ppermute(x, ('tensor', 'dp'), pairs)]
    pallas_call x2, Pallas kernels: 13.7 us -> 19.7 us  [backward(): pl.pallas_call(functools.partial(backward_kernel, tokens, n, start, band,...]
    unnamed x68 -> x64, local copies, waits for them, and re-layouts: 24.7 us -> 20.2 us
    ppermute x14, starting transfers between devices: 20.6 us -> 18.6 us  [send(): return lax.ppermute(x, ('tensor', 'dp'), pairs)]
    convert_element_type x1, other arithmetic: 0.93 us -> 2.37 us  [split_columns(): sent = (near1.astype(f32) + from1.astype(f32)).astype(bf16)]
    pallas_call x6 -> x5, Pallas kernels: 27.3 us -> 26 us  [the longest x4 22 us: forward(): pl.pallas_call(functools.partial(forward_kernel, tokens, rank, n, blocks,...]
  transfers between devices with their start and end apart: 23 -> 23, of which waited for: 7 -> 8; matrix products, arithmetic and copies ran while one was open for 6% -> 9% of each run, Pallas kernels for 37% -> 39%
where the time goes in v5:
time: 121 us; the launch traced here: 120 us
  Pallas kernels  46.4 us (38%)
  starting transfers between devices  21.1 us (17%)
  local copies, waits for them, and re-layouts  20.5 us (17%)
  waiting for transfers between devices  19.5 us (16%)
  other arithmetic  9.51 us (8%)
  matrix products  1.95 us (2%)
    pallas_call x4, Pallas kernels, forward(): pl.pallas_call(functools.partial(forward_kernel, tokens, rank, n, blocks,...  22 us
    unnamed x64, local copies, waits for them, and re-layouts  20.2 us
    pallas_call x2, Pallas kernels, backward(): pl.pallas_call(functools.partial(backward_kernel, tokens, n, start, band,...  19.7 us
    ppermute x14, starting transfers between devices, send(): return lax.ppermute(x, ('tensor', 'dp'), pairs)  18.6 us
    ppermute x14, waiting for transfers between devices, send(): return lax.ppermute(x, ('tensor', 'dp'), pairs)  17.3 us
    pallas_call x1, Pallas kernels, load(): pl.pallas_call(functools.partial(load_kernel, blocks), in_specs=[pl.Block...  3.97 us
    ppermute x9, starting transfers between devices, split_columns(): swap = lambda x: lax.ppermute(x, 'dp', [(0, 1), (1, 0)])  2.46 us
  transfers between devices with their start and end apart: 23, of which 8 were waited for; matrix products, arithmetic and copies ran while one was open for 9% of the time, Pallas kernels for 39%

profile of v5, /device:TPU:0, one launch (start us, length us, event | category | flops | bytes accessed | tf_op | source)
XLA Modules:
  0.0 120.0 jit_solution(6916272933601512089)
XLA Ops:
  0.6 0.5 collective-permute-start.1
  1.2 0.7 reduce-precision_convert_fusion.1
  2.1 4.0 %load.1 = (bf16[3584,512]{1,0:T(8,128)(2,1)S(1)}, bf16[3584,512]{1,0:T(8,128)(2,1)S(1)}) custom-call(s32[4]{0:T(128)S(1)} %get-tuple-element.108.place_ref, bf16[3584,8192]{1,0:T(8,128)(2,1)} %refs_10_.1), custom_call_target="tpu_custom_call" | custom-call | flops 1048576 | bytes 1048576 | tf_op jit(solution)/shard_map/load/pallas_call | solution.py:101
  6.2 0.7 own_block.1.refs_0_
  6.9 4.0 %collective-permute-start.2 = (bf16[272,512]{1,0:T(8,128)(2,1)}, bf16[272,512]{1,0:T(8,128)(2,1)}, u32[]{:S(2)}, u32[]{:S(2)}) collective-permute-start(bf16[272,512]{1,0:T(8,128)(2,1)} %own_block.1.refs_0_), channel_id=1, source_target_pairs={{0,8},{1,9},{2,10},{3,11},{4,12},{5,13},{6,14},{7,15},{8,0},{9,1},... | collective-permute-start | bytes 835592 | tf_op jit(solution)/shard_map/ppermute | solution.py:265
  10.9 1.6 %collective-permute-start.3 = (bf16[272,512]{1,0:T(8,128)(2,1)}, bf16[272,512]{1,0:T(8,128)(2,1)}, u32[]{:S(2)}, u32[]{:S(2)}) collective-permute-start(bf16[272,512]{1,0:T(8,128)(2,1)} %own_block.1.refs_0_), channel_id=1, source_target_pairs={{0,4},{1,3},{2,6},{3,1},{4,0},{5,7},{6,2},{7,5},{8,12},{9,11},{10,... | collective-permute-start | bytes 835592 | tf_op jit(solution)/shard_map/ppermute | solution.py:265
  12.5 1.5 %collective-permute-start.4 = (bf16[272,512]{1,0:T(8,128)(2,1)}, bf16[272,512]{1,0:T(8,128)(2,1)}, u32[]{:S(2)}, u32[]{:S(2)}) collective-permute-start(bf16[272,512]{1,0:T(8,128)(2,1)} %own_block.1.refs_0_), channel_id=1, source_target_pairs={{0,2},{1,5},{2,0},{3,7},{4,6},{5,1},{6,4},{7,3},{8,10},{9,13},{10,... | collective-permute-start | bytes 835592 | tf_op jit(solution)/shard_map/ppermute | solution.py:265
  14.0 0.9 copy-done.17
  15.0 1.2 copy-done.18
  16.1 5.5 %forward.4 = (bf16[2,256,512]{2,1,0:T(8,128)(2,1)}, f32[24,512]{1,0:T(8,128)S(1)}, bf16[3584,512]{1,0:T(8,128)(2,1)S(1)}, bf16[3584,512]{1,0:T(8,128)(2,1)S(1)},...) custom-call(s32[4]{0:T(128)S(1)} %get-tuple-element.108.place_ref, ...), custom_call_target="tpu_custom_call" | custom-call | flops 1048576 | bytes 1048576 | tf_op jit(solution)/shard_map/forward/pallas_call | solution.py:172
  21.6 1.8 %copy-done.20 = bf16[3584,512]{1,0:T(8,128)(2,1)} copy-done((bf16[3584,512]{1,0:T(8,128)(2,1)}, bf16[3584,512]{1,0:T(8,128)(2,1)S(1)}, u32[]{:S(2)}) %copy-start.20) | copy-done | bytes 3670040
  23.4 1.8 %copy-done.22 = bf16[3584,512]{1,0:T(8,128)(2,1)} copy-done((bf16[3584,512]{1,0:T(8,128)(2,1)}, bf16[3584,512]{1,0:T(8,128)(2,1)S(1)}, u32[]{:S(2)}) %copy-start.22) | copy-done | bytes 3670040
  25.2 0.5 collective-permute-start.6
  25.9 2.0 %copy-done.21 = bf16[3584,512]{1,0:T(8,128)(2,1)S(1)} copy-done((bf16[3584,512]{1,0:T(8,128)(2,1)S(1)}, bf16[3584,512]{1,0:T(8,128)(2,1)}, u32[]{:S(2)}) %copy-start.21) | copy-done | bytes 3670040
  27.9 2.0 %copy-done.23 = bf16[3584,512]{1,0:T(8,128)(2,1)S(1)} copy-done((bf16[3584,512]{1,0:T(8,128)(2,1)S(1)}, bf16[3584,512]{1,0:T(8,128)(2,1)}, u32[]{:S(2)}) %copy-start.23) | copy-done | bytes 3670040
  29.9 6.5 %forward.5 = (bf16[2,256,512]{2,1,0:T(8,128)(2,1)S(1)}, f32[24,512]{1,0:T(8,128)S(1)}, bf16[3584,512]{1,0:T(8,128)(2,1)S(1)}, bf16[3584,512]{1,0:T(8,128)(2,1)S(1)}) custom-call(s32[4]{0:T(128)S(1)} %get-tuple-element.107.next_ref.place_ref, s32[4]{0:T(128)S(1)} %get-tuple-element.106.next_ref.place_ref, bf16[3584,8192]{1,0:T(8,128)(2,1)} %refs_10_.1, ...), custom_call_target="tpu_custom_call" | custom-call | flops 1048576 | bytes 1048576 | tf_op jit(solution)/shard_map/forward/pallas_call | solution.py:172
  36.5 0.5 collective-permute-start.5
  37.0 1.5 %collective-permute-start.9 = (bf16[2,256,512]{2,1,0:T(8,128)(2,1)S(1)}, bf16[2,256,512]{2,1,0:T(8,128)(2,1)S(1)}, u32[]{:S(2)}, u32[]{:S(2)}) collective-permute-start(bf16[2,256,512]{2,1,0:T(8,128)(2,1)S(1)} %get-tuple-element.68), channel_id=1, source_target_pairs={{0,2},{1,5},{2,0},{3,7},{4,6},{5,1},{6,4},{7,3},{8,10},{9,13},{10,... | collective-permute-start | bytes 1572872 | tf_op jit(solution)/shard_map/ppermute | solution.py:265
  38.5 6.5 %forward.6 = (bf16[2,256,512]{2,1,0:T(8,128)(2,1)S(1)}, f32[24,512]{1,0:T(8,128)S(1)}, bf16[3584,512]{1,0:T(8,128)(2,1)S(1)}, bf16[3584,512]{1,0:T(8,128)(2,1)S(1)}) custom-call(s32[4]{0:T(128)S(1)} %get-tuple-element.106.next_ref.place_ref, s32[4]{0:T(128)S(1)} %get-tuple-element.105.next_ref.place_ref, bf16[3584,8192]{1,0:T(8,128)(2,1)} %refs_10_.1, ...), custom_call_target="tpu_custom_call" | custom-call | flops 1048576 | bytes 1048576 | tf_op jit(solution)/shard_map/forward/pallas_call | solution.py:172
  45.1 1.4 %collective-permute-done.5.refs_3_ = bf16[272,512]{1,0:T(8,128)(2,1)} collective-permute-done((bf16[272,512]{1,0:T(8,128)(2,1)}, bf16[272,512]{1,0:T(8,128)(2,1)}, u32[]{:S(2)}, u32[]{:S(2)}) %collective-permute-start.5) | collective-permute-done | bytes 278560 | tf_op jit(solution)/shard_map/ppermute | solution.py:265
  46.5 2.4 %add_convert_fusion.1 = bf16[2,256,512]{2,1,0:T(8,128)(2,1)} fusion(bf16[2,256,512]{2,1,0:T(8,128)(2,1)} %collective-permute-done.6, bf16[2,256,512]{2,1,0:T(8,128)(2,1)S(1)} %get-tuple-element.71), kind=kLoop, calls=%fused_computation.7 | loop fusion | flops 1048576 | bytes 1572864 | tf_op jit(solution)/shard_map/convert_element_type | solution.py:305
  48.9 1.0 collective-permute-start.10
  49.9 0.9 collective-permute-start.7
  50.7 1.2 collective-permute-start.8
  51.9 0.9 collective-permute-start.11
  52.8 3.5 %forward.7 = (bf16[2,256,512]{2,1,0:T(8,128)(2,1)S(1)}, f32[24,512]{1,0:T(8,128)S(1)}) custom-call(s32[4]{0:T(128)S(1)} %get-tuple-element.105.next_ref.place_ref, s32[4]{0:T(128)S(1)} %get-tuple-element.105.next_ref.place_ref, bf16[3584,8192]{1,0:T(8,128)(2,1)} %refs_10_.1, bf16[64,8192]{1,0:T(8,128)(2,1)S(1)} %copy-done.12, ...), custom_call_target="tpu_custom_call" | custom-call | flops 1048576 | bytes 1048576 | tf_op jit(solution)/shard_map/forward/pallas_call | solution.py:172
  56.3 0.8 copy-done.24
  57.1 0.9 collective-permute-done.7.refs_5_
  58.0 0.7 copy-done.25
  58.7 2.3 %collective-permute-done.8.refs_6_ = bf16[272,512]{1,0:T(8,128)(2,1)S(1)} collective-permute-done((bf16[272,512]{1,0:T(8,128)(2,1)}, bf16[272,512]{1,0:T(8,128)(2,1)S(1)}, u32[]{:S(2)}, u32[]{:S(2)}) %collective-permute-start.8) | collective-permute-done | bytes 278560 | tf_op jit(solution)/shard_map/ppermute | solution.py:265
  61.0 0.7 copy-done.27
  61.7 1.5 %collective-permute-start.12 = (f32[24,512]{1,0:T(8,128)S(1)}, f32[24,512]{1,0:T(8,128)S(1)}, u32[]{:S(2)}, u32[]{:S(2)}) collective-permute-start(f32[24,512]{1,0:T(8,128)S(1)} %get-tuple-element.74), channel_id=1, source_target_pairs={{0,2},{1,5},{2,0},{3,7},{4,6},{5,1},{6,4},{7,3},{8,10},{9,13},{10,... | collective-permute-start | bytes 147464 | tf_op jit(solution)/shard_map/ppermute | solution.py:265
  63.2 2.6 %collective-permute-done.12 = f32[24,512]{1,0:T(8,128)S(1)} collective-permute-done((f32[24,512]{1,0:T(8,128)S(1)}, f32[24,512]{1,0:T(8,128)S(1)}, u32[]{:S(2)}, u32[]{:S(2)}) %collective-permute-start.12) | collective-permute-done | bytes 49184 | tf_op jit(solution)/shard_map/ppermute | solution.py:265
  65.9 0.5 collective-permute-start.13
  66.4 0.1 stack.114.place_ref
  66.5 3.5 %collective-permute-done.13 = f32[24,512]{1,0:T(8,128)S(1)} collective-permute-done((f32[24,512]{1,0:T(8,128)S(1)}, f32[24,512]{1,0:T(8,128)S(1)}, u32[]{:S(2)}, u32[]{:S(2)}) %collective-permute-start.13) | collective-permute-done | bytes 49184 | tf_op jit(solution)/shard_map/ppermute | solution.py:265
  70.0 0.4 collective-permute-start.15
  70.4 1.6 %convert_add_fusion = f32[2,256,512]{2,1,0:T(8,128)S(1)} fusion(bf16[2,256,512]{2,1,0:T(8,128)(2,1)} %collective-permute-done.10, bf16[2,256,512]{2,1,0:T(8,128)(2,1)} %copy-done.30, bf16[2,256,512]{2,1,0:T(8,128)(2,1)} %copy-done.24), kind=kLoop, calls=%fused_computation.6 | loop fusion | flops 1310720 | bytes 2621440 | tf_op jit(solution)/shard_map/add | solution.py:315
  72.1 2.7 %collective-permute-start.14 = (bf16[256,512]{1,0:T(8,128)(2,1)S(1)}, bf16[256,512]{1,0:T(8,128)(2,1)S(1)}, u32[]{:S(2)}, u32[]{:S(2)}) collective-permute-start(bf16[256,512]{1,0:T(8,128)(2,1)S(1)} %fusion.10), channel_id=1, source_target_pairs={{0,8},{1,9},{2,10},{3,11},{4,12},{5,13},{6,14},{7,15},{8,0},{9,1},... | collective-permute-start | bytes 786440 | tf_op jit(solution)/shard_map/ppermute | solution.py:265
  74.7 6.5 %collective-permute-done.15 = f32[24,512]{1,0:T(8,128)S(1)} collective-permute-done((f32[24,512]{1,0:T(8,128)S(1)}, f32[24,512]{1,0:T(8,128)S(1)}, u32[]{:S(2)}, u32[]{:S(2)}) %collective-permute-start.15) | collective-permute-done | bytes 49184 | tf_op jit(solution)/shard_map/ppermute | solution.py:265
  81.4 2.0 %copy-done.1 = bf16[3584,512]{1,0:T(8,128)(2,1)S(1)} copy-done((bf16[3584,512]{1,0:T(8,128)(2,1)S(1)}, bf16[3584,512]{1,0:T(8,128)(2,1)}, u32[]{:S(2)}) %copy-start.1) | copy-done | bytes 3670040
  83.4 2.0 %copy-done.4 = bf16[3584,512]{1,0:T(8,128)(2,1)S(1)} copy-done((bf16[3584,512]{1,0:T(8,128)(2,1)S(1)}, bf16[3584,512]{1,0:T(8,128)(2,1)}, u32[]{:S(2)}) %copy-start.4) | copy-done | bytes 3670040
  85.4 2.0 %copy-done.7 = bf16[3584,512]{1,0:T(8,128)(2,1)S(1)} copy-done((bf16[3584,512]{1,0:T(8,128)(2,1)S(1)}, bf16[3584,512]{1,0:T(8,128)(2,1)}, u32[]{:S(2)}) %copy-start.7) | copy-done | bytes 3670040
  87.5 2.0 %copy-done.10 = bf16[3584,512]{1,0:T(8,128)(2,1)S(1)} copy-done((bf16[3584,512]{1,0:T(8,128)(2,1)S(1)}, bf16[3584,512]{1,0:T(8,128)(2,1)}, u32[]{:S(2)}) %copy-start.10) | copy-done | bytes 3670040
  89.5 12.3 %backward.2 = (f32[128,2048]{1,0:T(8,128)S(1)}, bf16[128,2048]{1,0:T(8,128)(2,1)S(1)}, bf16[256,4096]{1,0:T(8,128)(2,1)S(1)}, f32[256,64]{1,0:T(8,128)S(1)}) custom-call(s32[16]{0:T(128)S(1)} %stack.114.place_ref, bf16[272,512]{1,0:T(8,128)(2,1)} %own_block.1.refs_0_, bf16[272,512]{1,0:T(8,128)(2,1)} %collective-permute-done.2.refs_1_, ...), custom_call_target="tpu_custom_call" | custom-call | flops 1048576 | bytes 1048576 | tf_op jit(solution)/shard_map/backward/pallas_call | solution.py:235
  101.9 0.5 collective-permute-start.20
  102.5 1.4 %collective-permute-done.20 = f32[16,512]{1,0:T(8,128)S(1)} collective-permute-done((f32[16,512]{1,0:T(8,128)S(1)}, f32[16,512]{1,0:T(8,128)S(1)}, u32[]{:S(2)}, u32[]{:S(2)}) %collective-permute-start.20) | collective-permute-done | bytes 32800 | tf_op jit(solution)/shard_map/ppermute | solution.py:260
  103.8 1.1 fusion.4
  105.0 0.2 collective-permute-start.16
  105.2 0.4 collective-permute-start.19
  105.6 7.4 %backward.3 = (f32[128,1536]{1,0:T(8,128)S(1)}, bf16[128,1536]{1,0:T(8,128)(2,1)S(1)}) custom-call(s32[16]{0:T(128)S(1)} %stack.114.place_ref, bf16[256,4096]{1,0:T(8,128)(2,1)S(1)} %get-tuple-element.85.refs_0_, f32[256,64]{1,0:T(8,128)S(1)} %get-tuple-element.86.refs_1_, bf16[64,3584]{1,0:T(8,128)(2,1)S(1)} %bitcast.35, bf16[3584,512]{1,0:T(8,128)(2,1)S(1)} %copy-done.8, ...), custom_call_target="tpu_custom_call" | custom-call | flops 1048576 | bytes 1048576 | tf_op jit(solution)/shard_map/backward/pallas_call | solution.py:235
  113.0 0.2 collective-permute-start.18
  113.2 0.4 collective-permute-start.22
  113.6 0.2 fusion.11
  113.8 0.2 fusion.2
  114.0 0.8 collective-permute-done.22
  114.8 0.1 collective-permute-start.21
  114.9 0.7 fusion.35
  115.6 0.3 fusion.17
  116.0 1.2 %fusion.1 = f32[3584,64]{0,1:T(8,128)} fusion(f32[64,3584]{1,0:T(8,128)S(1)} %fusion.17, bf16[128,3584]{1,0:T(8,128)(2,1)S(1)} %copy-done.16, f32[256,64]{1,0:T(8,128)S(1)} %collective-permute-done.19, f32[256,64]{1,0:T(8,128)S(1)} %get-tuple-element.86.refs_1_), kind=kOutput, calls=%fused_computation.2 | convolution fusion | flops 59195392 | bytes 2883584 | tf_op jit(solution)/shard_map/dot_general | solution.py:21
  117.2 0.8 fusion.7
  118.0 0.8 fusion.9
  118.8 0.1 add_convert_fusion
  119.0 1.0 pad_maximum_fusion
  (88 shorter events, 0.9 us)
Async XLA Ops:
  0.6 13.4 %collective-permute-start.1 = (bf16[128,3584]{1,0:T(8,128)(2,1)}, bf16[128,3584]{1,0:T(8,128)(2,1)S(1)}, u32[]{:S(2)}, u32[]{:S(2)}) collective-permute-start(bf16[128,3584]{1,0:T(8,128)(2,1)} %refs_2_.1), channel_id=1, source_target_pairs={{0,1},{1,0},{2,3},{3,2},{4,5},{5,4},{6,7},{7,6},{8,9},{9,8},{10,11... | collective-permute-start | bytes 2752520 | tf_op jit(solution)/shard_map/ppermute | solution.py:260
  1.1 5.0 %collective-permute-start = (bf16[128,1024]{1,0:T(8,128)(2,1)}, bf16[128,1024]{1,0:T(8,128)(2,1)S(1)}, u32[]{:S(2)}, u32[]{:S(2)}) collective-permute-start(bf16[128,1024]{1,0:T(8,128)(2,1)} %own_ref.1), channel_id=1, source_target_pairs={{0,1},{1,0},{2,3},{3,2},{4,5},{5,4},{6,7},{7,6},{8,9},{9,8},{10,11... | collective-permute-start | bytes 786440 | tf_op jit(solution)/shard_map/ppermute | solution.py:260
  2.1 4.1 %copy-start.29 = (bf16[128,1024]{1,0:T(8,128)(2,1)S(1)}, bf16[128,1024]{1,0:T(8,128)(2,1)}, u32[]{:S(2)}) copy-start(bf16[128,1024]{1,0:T(8,128)(2,1)} %own_ref.1) | copy-start | bytes 786436
  2.1 12.8 %copy-start.12 = (bf16[64,8192]{1,0:T(8,128)(2,1)S(1)}, bf16[64,8192]{1,0:T(8,128)(2,1)}, u32[]{:S(2)}) copy-start(bf16[64,8192]{1,0:T(8,128)(2,1)} %refs_9_.2) | copy-start | bytes 3145732
  2.1 12.8 %copy-start.13 = (bf16[3584,64]{0,1:T(8,128)(2,1)S(1)}, bf16[3584,64]{0,1:T(8,128)(2,1)}, u32[]{:S(2)}) copy-start(bf16[3584,64]{0,1:T(8,128)(2,1)} %param.8) | copy-start | bytes 1376260
  2.1 12.8 %copy-start.15 = (bf16[128,3584]{1,0:T(8,128)(2,1)S(1)}, bf16[128,3584]{1,0:T(8,128)(2,1)}, u32[]{:S(2)}) copy-start(bf16[128,3584]{1,0:T(8,128)(2,1)} %refs_2_.1) | copy-start | bytes 2752516
  6.9 29.6 %collective-permute-start.2 = (bf16[272,512]{1,0:T(8,128)(2,1)}, bf16[272,512]{1,0:T(8,128)(2,1)}, u32[]{:S(2)}, u32[]{:S(2)}) collective-permute-start(bf16[272,512]{1,0:T(8,128)(2,1)} %own_block.1.refs_0_), channel_id=1, source_target_pairs={{0,8},{1,9},{2,10},{3,11},{4,12},{5,13},{6,14},{7,15},{8,0},{9,1},... | collective-permute-start | bytes 835592 | tf_op jit(solution)/shard_map/ppermute | solution.py:265
  10.9 25.6 %collective-permute-start.3 = (bf16[272,512]{1,0:T(8,128)(2,1)}, bf16[272,512]{1,0:T(8,128)(2,1)}, u32[]{:S(2)}, u32[]{:S(2)}) collective-permute-start(bf16[272,512]{1,0:T(8,128)(2,1)} %own_block.1.refs_0_), channel_id=1, source_target_pairs={{0,4},{1,3},{2,6},{3,1},{4,0},{5,7},{6,2},{7,5},{8,12},{9,11},{10,... | collective-permute-start | bytes 835592 | tf_op jit(solution)/shard_map/ppermute | solution.py:265
  12.5 24.0 %collective-permute-start.4 = (bf16[272,512]{1,0:T(8,128)(2,1)}, bf16[272,512]{1,0:T(8,128)(2,1)}, u32[]{:S(2)}, u32[]{:S(2)}) collective-permute-start(bf16[272,512]{1,0:T(8,128)(2,1)} %own_block.1.refs_0_), channel_id=1, source_target_pairs={{0,2},{1,5},{2,0},{3,7},{4,6},{5,1},{6,4},{7,3},{8,10},{9,13},{10,... | collective-permute-start | bytes 835592 | tf_op jit(solution)/shard_map/ppermute | solution.py:265
  14.0 0.9 copy-start.17
  14.9 1.2 copy-start.18
  21.6 1.8 %copy-start.20 = (bf16[3584,512]{1,0:T(8,128)(2,1)}, bf16[3584,512]{1,0:T(8,128)(2,1)S(1)}, u32[]{:S(2)}) copy-start(bf16[3584,512]{1,0:T(8,128)(2,1)S(1)} %get-tuple-element.50.refs_0_) | copy-start | bytes 11010052
  23.4 1.8 %copy-start.22 = (bf16[3584,512]{1,0:T(8,128)(2,1)}, bf16[3584,512]{1,0:T(8,128)(2,1)S(1)}, u32[]{:S(2)}) copy-start(bf16[3584,512]{1,0:T(8,128)(2,1)S(1)} %get-tuple-element.51.refs_1_) | copy-start | bytes 11010052
  25.2 21.3 %collective-permute-start.6 = (bf16[2,256,512]{2,1,0:T(8,128)(2,1)}, bf16[2,256,512]{2,1,0:T(8,128)(2,1)}, u32[]{:S(2)}, u32[]{:S(2)}) collective-permute-start(bf16[2,256,512]{2,1,0:T(8,128)(2,1)} %get-tuple-element.63), channel_id=1, source_target_pairs={{0,2},{1,5},{2,0},{3,7},{4,6},{5,1},{6,4},{7,3},{8,10},{9,13},{10,... | collective-permute-start | bytes 1572872 | tf_op jit(solution)/shard_map/ppermute | solution.py:265
  25.9 2.0 %copy-start.21 = (bf16[3584,512]{1,0:T(8,128)(2,1)S(1)}, bf16[3584,512]{1,0:T(8,128)(2,1)}, u32[]{:S(2)}) copy-start(bf16[3584,512]{1,0:T(8,128)(2,1)} %copy-done.20) | copy-start | bytes 11010052
  27.9 2.0 %copy-start.23 = (bf16[3584,512]{1,0:T(8,128)(2,1)S(1)}, bf16[3584,512]{1,0:T(8,128)(2,1)}, u32[]{:S(2)}) copy-start(bf16[3584,512]{1,0:T(8,128)(2,1)} %copy-done.22) | copy-start | bytes 11010052
  36.5 8.6 %copy-start = (bf16[3584,512]{1,0:T(8,128)(2,1)}, bf16[3584,512]{1,0:T(8,128)(2,1)S(1)}, u32[]{:S(2)}) copy-start(bf16[3584,512]{1,0:T(8,128)(2,1)S(1)} %get-tuple-element.55.refs_0_.refs_13_.refs_5_) | copy-start | bytes 11010052
  36.5 8.6 %copy-start.3 = (bf16[3584,512]{1,0:T(8,128)(2,1)}, bf16[3584,512]{1,0:T(8,128)(2,1)S(1)}, u32[]{:S(2)}) copy-start(bf16[3584,512]{1,0:T(8,128)(2,1)S(1)} %get-tuple-element.56.refs_1_.refs_14_.refs_6_) | copy-start | bytes 11010052
  36.5 10.0 %collective-permute-start.5 = (bf16[272,512]{1,0:T(8,128)(2,1)}, bf16[272,512]{1,0:T(8,128)(2,1)}, u32[]{:S(2)}, u32[]{:S(2)}) collective-permute-start(bf16[272,512]{1,0:T(8,128)(2,1)} %collective-permute-done.2.refs_1_), channel_id=1, source_target_pairs={{0,4},{1,3},{2,6},{3,1},{4,0},{5,7},{6,2},{7,5},{8,12},{9,11},{10,... | collective-permute-start | bytes 835592 | tf_op jit(solution)/shard_map/ppermute | solution.py:265
  37.0 24.6 %collective-permute-start.9 = (bf16[2,256,512]{2,1,0:T(8,128)(2,1)S(1)}, bf16[2,256,512]{2,1,0:T(8,128)(2,1)S(1)}, u32[]{:S(2)}, u32[]{:S(2)}) collective-permute-start(bf16[2,256,512]{2,1,0:T(8,128)(2,1)S(1)} %get-tuple-element.68), channel_id=1, source_target_pairs={{0,2},{1,5},{2,0},{3,7},{4,6},{5,1},{6,4},{7,3},{8,10},{9,13},{10,... | collective-permute-start | bytes 1572872 | tf_op jit(solution)/shard_map/ppermute | solution.py:265
  45.1 11.2 %copy-start.6 = (bf16[3584,512]{1,0:T(8,128)(2,1)}, bf16[3584,512]{1,0:T(8,128)(2,1)S(1)}, u32[]{:S(2)}) copy-start(bf16[3584,512]{1,0:T(8,128)(2,1)S(1)} %get-tuple-element.60.refs_0_.refs_11_.refs_3_) | copy-start | bytes 11010052
  45.1 11.2 %copy-start.9 = (bf16[3584,512]{1,0:T(8,128)(2,1)}, bf16[3584,512]{1,0:T(8,128)(2,1)S(1)}, u32[]{:S(2)}) copy-start(bf16[3584,512]{1,0:T(8,128)(2,1)S(1)} %get-tuple-element.61.refs_1_.refs_12_.refs_4_) | copy-start | bytes 11010052
  48.9 21.2 %collective-permute-start.10 = (bf16[2,256,512]{2,1,0:T(8,128)(2,1)}, bf16[2,256,512]{2,1,0:T(8,128)(2,1)}, u32[]{:S(2)}, u32[]{:S(2)}) collective-permute-start(bf16[2,256,512]{2,1,0:T(8,128)(2,1)} %add_convert_fusion.1), channel_id=1, source_target_pairs={{0,4},{1,3},{2,6},{3,1},{4,0},{5,7},{6,2},{7,5},{8,12},{9,11},{10,... | collective-permute-start | bytes 1572872 | tf_op jit(solution)/shard_map/ppermute | solution.py:265
  49.9 8.1 %collective-permute-start.7 = (bf16[272,512]{1,0:T(8,128)(2,1)}, bf16[272,512]{1,0:T(8,128)(2,1)S(1)}, u32[]{:S(2)}, u32[]{:S(2)}) collective-permute-start(bf16[272,512]{1,0:T(8,128)(2,1)} %collective-permute-done.2.refs_1_), channel_id=1, source_target_pairs={{0,2},{1,5},{2,0},{3,7},{4,6},{5,1},{6,4},{7,3},{8,10},{9,13},{10,... | collective-permute-start | bytes 835592 | tf_op jit(solution)/shard_map/ppermute | solution.py:265
  50.7 10.2 %collective-permute-start.8 = (bf16[272,512]{1,0:T(8,128)(2,1)}, bf16[272,512]{1,0:T(8,128)(2,1)S(1)}, u32[]{:S(2)}, u32[]{:S(2)}) collective-permute-start(bf16[272,512]{1,0:T(8,128)(2,1)} %collective-permute-done.3.refs_2_), channel_id=1, source_target_pairs={{0,2},{1,5},{2,0},{3,7},{4,6},{5,1},{6,4},{7,3},{8,10},{9,13},{10,... | collective-permute-start | bytes 835592 | tf_op jit(solution)/shard_map/ppermute | solution.py:265
  51.9 18.1 %collective-permute-start.11 = (bf16[272,512]{1,0:T(8,128)(2,1)}, bf16[272,512]{1,0:T(8,128)(2,1)}, u32[]{:S(2)}, u32[]{:S(2)}) collective-permute-start(bf16[272,512]{1,0:T(8,128)(2,1)} %collective-permute-done.5.refs_3_), channel_id=1, source_target_pairs={{0,2},{1,5},{2,0},{3,7},{4,6},{5,1},{6,4},{7,3},{8,10},{9,13},{10,... | collective-permute-start | bytes 835592 | tf_op jit(solution)/shard_map/ppermute | solution.py:265
  56.3 0.8 copy-start.24
  57.1 24.2 %copy-start.14 = (bf16[3584,64]{0,1:T(8,128)(2,1)S(1)}, bf16[3584,64]{0,1:T(8,128)(2,1)}, u32[]{:S(2)}) copy-start(bf16[3584,64]{0,1:T(8,128)(2,1)} %param.8) | copy-start | bytes 1376260
  58.0 0.7 copy-start.25
  61.0 0.7 copy-start.27
  61.7 19.7 %copy-start.26 = (bf16[272,512]{1,0:T(8,128)(2,1)S(1)}, bf16[272,512]{1,0:T(8,128)(2,1)}, u32[]{:S(2)}) copy-start(bf16[272,512]{1,0:T(8,128)(2,1)} %copy-done.25) | copy-start | bytes 835588
  61.7 4.2 %copy-start.30 = (bf16[2,256,512]{2,1,0:T(8,128)(2,1)}, bf16[2,256,512]{2,1,0:T(8,128)(2,1)S(1)}, u32[]{:S(2)}) copy-start(bf16[2,256,512]{2,1,0:T(8,128)(2,1)S(1)} %collective-permute-done.9) | copy-start | bytes 1572868
  61.7 19.7 %copy-start.28 = (bf16[272,512]{1,0:T(8,128)(2,1)S(1)}, bf16[272,512]{1,0:T(8,128)(2,1)}, u32[]{:S(2)}) copy-start(bf16[272,512]{1,0:T(8,128)(2,1)} %copy-done.27) | copy-start | bytes 835588
  61.7 4.2 %collective-permute-start.12 = (f32[24,512]{1,0:T(8,128)S(1)}, f32[24,512]{1,0:T(8,128)S(1)}, u32[]{:S(2)}, u32[]{:S(2)}) collective-permute-start(f32[24,512]{1,0:T(8,128)S(1)} %get-tuple-element.74), channel_id=1, source_target_pairs={{0,2},{1,5},{2,0},{3,7},{4,6},{5,1},{6,4},{7,3},{8,10},{9,13},{10,... | collective-permute-start | bytes 147464 | tf_op jit(solution)/shard_map/ppermute | solution.py:265
  65.9 4.2 %collective-permute-start.13 = (f32[24,512]{1,0:T(8,128)S(1)}, f32[24,512]{1,0:T(8,128)S(1)}, u32[]{:S(2)}, u32[]{:S(2)}) collective-permute-start(f32[24,512]{1,0:T(8,128)S(1)} %add.101), channel_id=1, source_target_pairs={{0,4},{1,3},{2,6},{3,1},{4,0},{5,7},{6,2},{7,5},{8,12},{9,11},{10,... | collective-permute-start | bytes 147464 | tf_op jit(solution)/shard_map/ppermute | solution.py:265
  70.0 11.2 %collective-permute-start.15 = (f32[24,512]{1,0:T(8,128)S(1)}, f32[24,512]{1,0:T(8,128)S(1)}, u32[]{:S(2)}, u32[]{:S(2)}) collective-permute-start(f32[24,512]{1,0:T(8,128)S(1)} %add.102), channel_id=1, source_target_pairs={{0,8},{1,9},{2,10},{3,11},{4,12},{5,13},{6,14},{7,15},{8,0},{9,1},... | collective-permute-start | bytes 147464 | tf_op jit(solution)/shard_map/ppermute | solution.py:265
  72.1 31.8 %collective-permute-start.14 = (bf16[256,512]{1,0:T(8,128)(2,1)S(1)}, bf16[256,512]{1,0:T(8,128)(2,1)S(1)}, u32[]{:S(2)}, u32[]{:S(2)}) collective-permute-start(bf16[256,512]{1,0:T(8,128)(2,1)S(1)} %fusion.10), channel_id=1, source_target_pairs={{0,8},{1,9},{2,10},{3,11},{4,12},{5,13},{6,14},{7,15},{8,0},{9,1},... | collective-permute-start | bytes 786440 | tf_op jit(solution)/shard_map/ppermute | solution.py:265
  81.3 2.0 %copy-start.1 = (bf16[3584,512]{1,0:T(8,128)(2,1)S(1)}, bf16[3584,512]{1,0:T(8,128)(2,1)}, u32[]{:S(2)}) copy-start(bf16[3584,512]{1,0:T(8,128)(2,1)} %copy-done) | copy-start | bytes 11010052
  83.4 2.0 %copy-start.4 = (bf16[3584,512]{1,0:T(8,128)(2,1)S(1)}, bf16[3584,512]{1,0:T(8,128)(2,1)}, u32[]{:S(2)}) copy-start(bf16[3584,512]{1,0:T(8,128)(2,1)} %copy-done.3) | copy-start | bytes 11010052
  85.4 2.0 %copy-start.7 = (bf16[3584,512]{1,0:T(8,128)(2,1)S(1)}, bf16[3584,512]{1,0:T(8,128)(2,1)}, u32[]{:S(2)}) copy-start(bf16[3584,512]{1,0:T(8,128)(2,1)} %copy-done.6) | copy-start | bytes 11010052
  87.5 2.0 %copy-start.10 = (bf16[3584,512]{1,0:T(8,128)(2,1)S(1)}, bf16[3584,512]{1,0:T(8,128)(2,1)}, u32[]{:S(2)}) copy-start(bf16[3584,512]{1,0:T(8,128)(2,1)} %copy-done.9) | copy-start | bytes 11010052
  89.5 12.9 %copy-start.31 = (f32[1024]{0:T(1024)S(1)}, f32[1024]{0:T(1024)}, u32[]{:S(2)}) copy-start(f32[1024]{0:T(1024)} %param.10) | copy-start | bytes 12292
  89.5 16.0 %copy-start.2 = (bf16[3584,512]{1,0:T(8,128)(2,1)S(1)}, bf16[3584,512]{1,0:T(8,128)(2,1)}, u32[]{:S(2)}) copy-start(bf16[3584,512]{1,0:T(8,128)(2,1)} %copy-done) | copy-start | bytes 11010052
  89.5 16.0 %copy-start.5 = (bf16[3584,512]{1,0:T(8,128)(2,1)S(1)}, bf16[3584,512]{1,0:T(8,128)(2,1)}, u32[]{:S(2)}) copy-start(bf16[3584,512]{1,0:T(8,128)(2,1)} %copy-done.3) | copy-start | bytes 11010052
  89.5 16.0 %copy-start.8 = (bf16[3584,512]{1,0:T(8,128)(2,1)S(1)}, bf16[3584,512]{1,0:T(8,128)(2,1)}, u32[]{:S(2)}) copy-start(bf16[3584,512]{1,0:T(8,128)(2,1)} %copy-done.6) | copy-start | bytes 11010052
  89.5 16.0 %copy-start.11 = (bf16[3584,512]{1,0:T(8,128)(2,1)S(1)}, bf16[3584,512]{1,0:T(8,128)(2,1)}, u32[]{:S(2)}) copy-start(bf16[3584,512]{1,0:T(8,128)(2,1)} %copy-done.9) | copy-start | bytes 11010052
  101.8 17.0 %collective-permute-start.17 = (bf16[128,2048]{1,0:T(8,128)(2,1)S(1)}, bf16[128,2048]{1,0:T(8,128)(2,1)S(1)}, u32[]{:S(2)}, u32[]{:S(2)}) collective-permute-start(bf16[128,2048]{1,0:T(8,128)(2,1)S(1)} %get-tuple-element.84), channel_id=1, source_target_pairs={{0,1},{1,0},{2,3},{3,2},{4,5},{5,4},{6,7},{7,6},{8,9},{9,8},{10,11... | collective-permute-start | bytes 1572872 | tf_op jit(solution)/shard_map/ppermute | solution.py:260
  101.9 1.9 %collective-permute-start.20 = (f32[16,512]{1,0:T(8,128)S(1)}, f32[16,512]{1,0:T(8,128)S(1)}, u32[]{:S(2)}, u32[]{:S(2)}) collective-permute-start(f32[16,512]{1,0:T(8,128)S(1)} %slice.97), channel_id=1, source_target_pairs={{0,1},{1,0},{2,3},{3,2},{4,5},{5,4},{6,7},{7,6},{8,9},{9,8},{10,11... | collective-permute-start | bytes 98312 | tf_op jit(solution)/shard_map/ppermute | solution.py:260
  105.0 13.0 %collective-permute-start.16 = (bf16[128,512]{1,0:T(8,128)(2,1)S(1)}, bf16[128,512]{1,0:T(8,128)(2,1)S(1)}, u32[]{:S(2)}, u32[]{:S(2)}) collective-permute-start(bf16[128,512]{1,0:T(8,128)(2,1)S(1)} %get-tuple-element.92), channel_id=1, source_target_pairs={{0,1},{1,0},{2,3},{3,2},{4,5},{5,4},{6,7},{7,6},{8,9},{9,8},{10,11... | collective-permute-start | bytes 393224 | tf_op jit(solution)/shard_map/ppermute | solution.py:260
  105.2 10.5 %collective-permute-start.19 = (f32[256,64]{1,0:T(8,128)S(1)}, f32[256,64]{1,0:T(8,128)S(1)}, u32[]{:S(2)}, u32[]{:S(2)}) collective-permute-start(f32[256,64]{1,0:T(8,128)S(1)} %get-tuple-element.86.refs_1_), channel_id=1, source_target_pairs={{0,1},{1,0},{2,3},{3,2},{4,5},{5,4},{6,7},{7,6},{8,9},{9,8},{10,11... | collective-permute-start | bytes 196616 | tf_op jit(solution)/shard_map/ppermute | solution.py:260
  105.6 10.1 %copy-start.19 = (bf16[128,3584]{1,0:T(8,128)(2,1)S(1)}, bf16[128,3584]{1,0:T(8,128)(2,1)}, u32[]{:S(2)}) copy-start(bf16[128,3584]{1,0:T(8,128)(2,1)} %copy-done.17) | copy-start | bytes 2752516
  105.6 10.4 %copy-start.16 = (bf16[128,3584]{1,0:T(8,128)(2,1)S(1)}, bf16[128,3584]{1,0:T(8,128)(2,1)}, u32[]{:S(2)}) copy-start(bf16[128,3584]{1,0:T(8,128)(2,1)} %refs_2_.1) | copy-start | bytes 2752516
  113.0 5.9 %collective-permute-start.18 = (bf16[128,1536]{1,0:T(8,128)(2,1)S(1)}, bf16[128,1536]{1,0:T(8,128)(2,1)S(1)}, u32[]{:S(2)}, u32[]{:S(2)}) collective-permute-start(bf16[128,1536]{1,0:T(8,128)(2,1)S(1)} %get-tuple-element.88), channel_id=1, source_target_pairs={{0,1},{1,0},{2,3},{3,2},{4,5},{5,4},{6,7},{7,6},{8,9},{9,8},{10,11... | collective-permute-start | bytes 1179656 | tf_op jit(solution)/shard_map/ppermute | solution.py:260
  113.2 1.6 %collective-permute-start.22 = (f32[512]{0:T(512)S(1)}, f32[512]{0:T(512)S(1)}, u32[]{:S(2)}, u32[]{:S(2)}) collective-permute-start(f32[512]{0:T(512)S(1)} %div.7), channel_id=1, source_target_pairs={{0,1},{1,0},{2,3},{3,2},{4,5},{5,4},{6,7},{7,6},{8,9},{9,8},{10,11... | collective-permute-start | bytes 6152 | tf_op jit(solution)/shard_map/ppermute | solution.py:260
  114.8 2.4 %collective-permute-start.21 = (f32[64,512]{1,0:T(8,128)S(1)}, f32[64,512]{1,0:T(8,128)S(1)}, u32[]{:S(2)}, u32[]{:S(2)}) collective-permute-start(f32[64,512]{1,0:T(8,128)S(1)} %fusion.2), channel_id=1, source_target_pairs={{0,1},{1,0},{2,3},{3,2},{4,5},{5,4},{6,7},{7,6},{8,9},{9,8},{10,11... | collective-permute-start | bytes 393224 | tf_op jit(solution)/shard_map/ppermute | solution.py:260

commit v6 on v4

--- a/solution.py
+++ b/solution.py
@@ -10,7 +10,7 @@
 adapter_scale = 2.0
 stability_floor = 1e-06
 pad_rows = 16
-vmem_bytes = 5 * 1024 * 1024
+vmem_bytes = 8 * 1024 * 1024
 f32, bf16 = jnp.float32, jnp.bfloat16
 small_cost = pl.CostEstimate(flops=1 << 20, bytes_accessed=1 << 20, transcendentals=0)
 contract_trailing = (((1,), (1,)), ((), ()))
@@ -45,13 +45,13 @@
     return pltpu.CompilerParams(vmem_limit_bytes=vmem_bytes)
 
 
-def block_kernel(tokens, core_ref, own_ref, other_ref, magnitude_ref, out_ref):
+def block_kernel(tokens, order_ref, own_ref, other_ref, magnitude_ref, out_ref):
     out_ref[:tokens, :] = own_ref[...]
     out_ref[tokens : 2 * tokens, :] = other_ref[...]
     out_ref[2 * tokens :, :] = magnitude_ref[...]
 
 
-def own_block(core, cotangent, other, magnitude_rows):
+def own_block(order, cotangent, other, magnitude_rows):
     tokens, columns = cotangent.shape
     half = columns // 2
     padded = 2 * tokens + pad_rows
@@ -61,80 +61,64 @@
             num_scalar_prefetch=1,
             grid=(1,),
             in_specs=[
-                pl.BlockSpec((tokens, half), lambda i, c: (0, c[0])),
-                pl.BlockSpec((tokens, half), lambda i, c: (0, c[0])),
-                pl.BlockSpec((pad_rows, half), lambda i, c: (0, c[0])),
+                pl.BlockSpec((tokens, half), lambda i, p: (0, lax.rem(p[0], 2))),
+                pl.BlockSpec((tokens, half), lambda i, p: (0, lax.rem(p[0], 2))),
+                pl.BlockSpec((pad_rows, half), lambda i, p: (0, lax.rem(p[0], 2))),
             ],
-            out_specs=pl.BlockSpec((padded, half), lambda i, c: (0, 0)),
+            out_specs=pl.BlockSpec((padded, half), lambda i, p: (0, 0)),
         ),
         out_shape=jax.ShapeDtypeStruct((padded, half), bf16),
         compiler_params=params(),
         cost_estimate=small_cost,
         name="own_block",
-    )(core, cotangent, other, magnitude_rows)
-
-
-def load_kernel(tokens, rank, n, first, place_ref, *refs):
-    if first:
-        own_ref, at_ref, up_ref, w_hbm, *held, stats_ref, own_out, sem, own_sem = refs
-    else:
-        before_ref, at_ref, up_ref, w_hbm, *held, stats_ref, sem = refs
-    blocks, half = len(held), held[0].shape[1]
-    column = lambda k: pl.ds(pl.multiple_of(place_ref[k] * half, half), half)
-    copy = lambda k: pltpu.make_async_copy(w_hbm.at[:, column(k)], held[k], sem.at[k])
-    if first:
-        own_copy = pltpu.make_async_copy(own_ref, own_out, own_sem)
-        own_copy.start()
-    for k in range(blocks):
-        copy(k).start()
+    )(order, cotangent, other, magnitude_rows)
+
+
+def load_kernel(tokens, rank, n, order_ref, own_ref, at_ref, up_ref, w_hbm, *refs):
+    held, (stats_ref, lhs_ref, sem, own_sem) = refs[:n], refs[n:]
+    half = held[0].shape[1]
+    columns = [pl.ds(pl.multiple_of(order_ref[k] * half, half), half) for k in range(n)]
+    copies = [pltpu.make_async_copy(w_hbm.at[:, c], h, sem.at[k]) for k, (c, h) in enumerate(zip(columns, held))]
+    own_copy = pltpu.make_async_copy(own_ref, lhs_ref, own_sem)
+    own_copy.start()
+    for copy in copies:
+        copy.start()
 
     down = at_ref[...]
     high, low = split_pair(dot(down, down, contract_trailing))
-    if first:
-        own_copy.wait()
-        turned = dot(down, own_out[...], contract_trailing)
-        lanes = half // tokens
-        span = rank // lanes
-        stats_ref[:n, :] = jnp.zeros((n, half), f32)
-        for j in range(lanes):
-            stats_ref[n:, j * tokens : (j + 1) * tokens] = turned[j * span : (j + 1) * span]
-    else:
-        stats_ref[...] = before_ref[...]
-
-    for k in range(blocks):
-        copy(k).wait()
-        up = up_ref[:, column(k)]
+    own_copy.wait()
+    turned = dot(down, lhs_ref[...], contract_trailing)
+    lanes = half // tokens
+    span = rank // lanes
+    for j in range(lanes):
+        stats_ref[n:, j * tokens : (j + 1) * tokens] = turned[j * span : (j + 1) * span]
+    for k in range(n):
+        copies[k].wait()
+        up = up_ref[:, columns[k]]
         cross = 2 * dot(down, held[k][...]) + adapter_scale * (dot(high, up) + dot(low, up))
         cross = jnp.sum(up.astype(f32) * cross, axis=0, keepdims=True)
-        stats_ref[pl.ds(place_ref[blocks + k], 1), :] = sum_of_squares(held[k]) + adapter_scale * cross
-
-
-def load(n, place, weight, at, up, half, own=None, before=None):
-    blocks = place.shape[0] // 2
-    rows = weight.shape[0]
+        stats_ref[pl.ds(order_ref[n + k], 1), :] = sum_of_squares(held[k]) + adapter_scale * cross
+
+
+def load(order, own, at, up, weight, half):
+    n = order.shape[0] // 2
+    tokens, rows = own.shape
     rank = at.shape[0]
     any_ = pl.BlockSpec(memory_space=pl.ANY)
-    first = before is None
-    if first:
-        tokens = own.shape[0]
-        stats = (n + rank * tokens // half, half)
-    else:
-        tokens, stats = None, before.shape
     return pl.pallas_call(
-        functools.partial(load_kernel, tokens, rank, n, first),
-        in_specs=[pl.BlockSpec(memory_space=pltpu.SMEM), any_ if first else vmem(), vmem(), vmem(), any_],
-        out_specs=[vmem()] * (blocks + (2 if first else 1)),
-        out_shape=[jax.ShapeDtypeStruct((rows, half), bf16)] * blocks
-        + [jax.ShapeDtypeStruct(stats, f32)]
-        + ([jax.ShapeDtypeStruct(own.shape, bf16)] if first else []),
-        scratch_shapes=[pltpu.SemaphoreType.DMA((blocks,))] + ([pltpu.SemaphoreType.DMA] if first else []),
+        functools.partial(load_kernel, tokens, rank, n),
+        in_specs=[pl.BlockSpec(memory_space=pltpu.SMEM), any_, vmem(), vmem(), any_],
+        out_specs=[vmem()] * (n + 2),
+        out_shape=[jax.ShapeDtypeStruct((rows, half), bf16)] * n
+        + [jax.ShapeDtypeStruct((n + rank * tokens // half, half), f32), jax.ShapeDtypeStruct(own.shape, bf16)],
+        scratch_shapes=[pltpu.SemaphoreType.DMA((n,)), pltpu.SemaphoreType.DMA],
         compiler_params=params(),
         cost_estimate=small_cost,
         name="load",
-    )(place, own if first else before, at, up, weight)
-
-
-def forward_kernel(tokens, rank, blocks, first, place_ref, *refs):
+    )(order, own, at, up, weight)
+
+
+def forward_kernel(tokens, rank, vs, first, order_ref, *refs):
     if first:
         own_ref, other_ref, at_ref, up_ref, *held, out_ref, lhs_ref, adapter_ref, sem = refs
         copy = pltpu.make_async_copy(other_ref, lhs_ref.at[tokens:], sem)
@@ -147,13 +131,14 @@
     else:
         lhs_ref, adapter_ref, up_ref, *held, out_ref = refs
     half = out_ref.shape[2]
-    for i in range(blocks):
-        up = up_ref[:, pl.ds(pl.multiple_of(place_ref[i] * half, half), half)]
+    for i, v in enumerate(vs):
+        up = up_ref[:, pl.ds(pl.multiple_of(order_ref[v] * half, half), half)]
         through = dot(adapter_ref[...], jnp.concatenate([up, up], axis=0))
         out_ref[i] = (dot(lhs_ref[...], held[i][...]) + adapter_scale * through).astype(bf16)
 
 
-def forward(place, held, up, first=None, later=None):
+def forward(vs, order, held, up, first=None, later=None):
+    held = [held[v] for v in vs]
     rows, half = held[0].shape
     if later is None:
         own, other, at = operands = first
@@ -165,7 +150,7 @@
         specs = [vmem()] * 2
     extra = [((2 * tokens, rows), bf16), ((2 * tokens, 2 * rank), bf16)] if first else []
     return pl.pallas_call(
-        functools.partial(forward_kernel, tokens, rank, len(held), later is None),
+        functools.partial(forward_kernel, tokens, rank, vs, later is None),
         in_specs=[pl.BlockSpec(memory_space=pltpu.SMEM), *specs] + [vmem()] * (1 + len(held)),
         out_specs=[vmem()] * (1 + len(extra)),
         out_shape=[jax.ShapeDtypeStruct((len(held), 2 * tokens, half), bf16)]
@@ -174,13 +159,13 @@
         compiler_params=params(),
         cost_estimate=small_cost,
         name="forward",
-    )(place, *operands, up, *held)
-
-
-def backward_kernel(tokens, n, start, band, first, place_ref, *refs):
+    )(order, *operands, up, *held)
+
+
+def backward_kernel(tokens, n, start, band, first, order_ref, *refs):
     if first:
         cots, (stats_ref, up_ref, at_ref, *held) = refs[:n], refs[n : 2 * n + 3]
-        own_out, other_out, scaled_ref, proj_ref = refs[2 * n + 3 :]
+        own_out, other_out, scaled_ref, proj_ref, scales_ref, block_ref = refs[2 * n + 3 :]
     else:
         scaled_ref, proj_ref, at_ref, *held, own_out, other_out = refs
     both = 2 * tokens
@@ -194,11 +179,17 @@
             projected = jnp.zeros(proj_ref.shape, f32)
             for k in range(n):
                 magnitude = jnp.sum(cots[k][both:, :].astype(f32), axis=0, keepdims=True)
-                squares = stats_ref[pl.ds(place_ref[n + k], 1), :]
-                rescale = magnitude / jnp.sqrt(squares + stability_floor)
+                squares = stats_ref[pl.ds(order_ref[n + k], 1), :]
+                norm = jnp.sqrt(squares + stability_floor)
+                rescale = magnitude / norm
+                if k == 0:
+                    scales_ref[0:1, :] = norm
+                    scales_ref[1:2, :] = rescale
                 scaled = (cots[k][:both, :].astype(f32) * rescale).astype(bf16)
+                if k == 0:
+                    block_ref[...] = scaled
                 scaled_ref[:, spans[k]] = scaled
-                up = up_ref[:, pl.ds(pl.multiple_of(place_ref[k] * half, half), half)]
+                up = up_ref[:, pl.ds(pl.multiple_of(order_ref[k] * half, half), half)]
                 projected = projected + dot(scaled, up, contract_trailing)
             proj_ref[...] = projected
 
@@ -210,15 +201,15 @@
     other_out[...] = total[tokens:].astype(bf16)
 
 
-def backward(place, start, bands, band, at, held, first=None, later=None):
-    n = place.shape[0] // 2
+def backward(order, start, bands, band, at, held, first=None, later=None):
+    n = order.shape[0] // 2
     half = held[0].shape[1]
     rank = at.shape[0]
     if later is None:
         cots, stats, up = first
         both = cots[0].shape[0] - pad_rows
         operands = [*cots, stats, up]
-        extra = [((both, n * half), bf16), ((both, rank), f32)]
+        extra = [((both, n * half), bf16), ((both, rank), f32), ((2, half), f32), ((both, half), bf16)]
     else:
         operands, extra = later, []
         both = later[0].shape[0]
@@ -236,7 +227,7 @@
         compiler_params=params(),
         cost_estimate=small_cost,
         name="backward",
-    )(place, *operands, at, *held)
+    )(order, *operands, at, *held)
 
 
 def split_columns(hidden, weight, down, up, magnitude, cotangent):
@@ -259,49 +250,49 @@
         shard = [me ^ jnp.where(core == 0, reach(v, 0), reach(v, 1)) for v in vs]
         return jnp.stack([2 * s + core for s in shard] + shard).astype(jnp.int32)
 
-    mine = lambda x, axis: lax.dynamic_slice_in_dim(x, core * half, half, axis)
+    tie = lax.optimization_barrier
     at = down.T
-    tie = lax.optimization_barrier
+    order = place(*range(n))
+    low_core = core == 0
 
     cot_other = swap(cotangent)
     hidden_other = swap(hidden)
-    run_load = functools.partial(load, n, weight=weight, at=at, up=up, half=half)
-    *far, stats, own = run_load(place(0b100, 0b101, 0b110, 0b111), own=hidden)
-    cot_other, stats = tie((cot_other, stats))
     first = lax.reduce_precision(magnitude, 8, 7)
     second = lax.reduce_precision(magnitude - first, 8, 7)
     third = magnitude - first - second
     magnitude_rows = jnp.concatenate(
         [jnp.stack([first, second, third]), jnp.zeros((pad_rows - 3, 2 * half), f32)]
     ).astype(bf16)
-    block = own_block(core.astype(jnp.int32).reshape(1), cotangent, cot_other, magnitude_rows)
+    low_core, order, cot_other = tie((low_core, order, cot_other))
+    block = own_block(order, cotangent, cot_other, magnitude_rows)
 
     cots = {0b000: block, 0b001: send(block, 2), 0b010: send(block, 1), 0b100: send(block, 0)}
-    *near, stats = run_load(place(0b000, 0b001, 0b010, 0b011), before=stats)
+    block, order = tie((block, order))
+    *held, stats, own = load(order, hidden, at, up, weight, half)
 
     got = send(stats, 0)
-    far1, lhs, adapter = forward(place(0b110, 0b111), far[2:], up, first=(own, hidden_other, at))
-    run = functools.partial(forward, up=up, later=(lhs, adapter))
-    got, far1 = tie((got, far1))
+    far1, lhs, adapter = forward((0b110, 0b111), order, held, up, first=(own, hidden_other, at))
+    run = lambda *vs: forward(vs, order, held, up, later=(lhs, adapter))[0]
+    *arrived, got, far1 = tie((*(cots[v] for v in (0b001, 0b010, 0b100)), got, far1))
+    cots[0b001], cots[0b010], cots[0b100] = arrived
     stats = stats + got
     got = send(stats, 1)
     from1 = send(far1, 0)
-    far0 = run(place(0b100, 0b101), far[:2])[0]
-    *arrived, got, far0 = tie((*(cots[v] for v in (0b001, 0b010, 0b100)), got, far0))
-    cots[0b001], cots[0b010], cots[0b100] = arrived
+    cots[0b011], cots[0b101], cots[0b110] = send(cots[0b001], 1), send(cots[0b001], 0), send(cots[0b010], 0)
+    far0 = run(0b100, 0b101)
+    got, far0 = tie((got, far0))
     stats = stats + got
     got = send(stats, 2)
     from0 = send(far0, 0)
-    cots[0b011], cots[0b101], cots[0b110] = send(cots[0b001], 1), send(cots[0b001], 0), send(cots[0b010], 0)
-    near1 = run(place(0b010, 0b011), near[2:])[0]
-    cots[0b011], from1, got, near1 = tie((cots[0b011], from1, got, near1))
+    near1 = run(0b010, 0b011)
+    cots[0b011], cots[0b101], cots[0b110], from1, got, near1 = tie(
+        (cots[0b011], cots[0b101], cots[0b110], from1, got, near1)
+    )
     stats = stats + got
     cots[0b111] = send(cots[0b011], 0)
     arrived = send((near1.astype(f32) + from1.astype(f32)).astype(bf16), 1)
-    near0 = run(place(0b000, 0b001), near[:2])[0]
-    cots[0b101], cots[0b110], cots[0b111], from0, near0, arrived, stats = tie(
-        (cots[0b101], cots[0b110], cots[0b111], from0, near0, arrived, stats)
-    )
+    near0 = run(0b000, 0b001)
+    cots[0b111], from0, near0, arrived, stats = tie((cots[0b111], from0, near0, arrived, stats))
     kept = near0.astype(f32) + from0.astype(f32) + arrived.astype(f32)
     last = send(kept[1].astype(bf16), 2)
     lowrank_rows = stats[n:]
@@ -310,9 +301,8 @@
     band = 256
     bands = rows // band
     many = (bands + 2) // 2
-    order = place(*range(n))
-    run = functools.partial(backward, order, band=band, at=at, held=near + far)
-    grad_a, other_a, scaled, proj = run(0, many, first=([cots[v] for v in range(n)], stats, up))
+    run = functools.partial(backward, order, band=band, at=at, held=held)
+    grad_a, other_a, scaled, proj, scales, scaled_own = run(0, many, first=([cots[v] for v in range(n)], stats, up))
     got_a = swap(other_a)
     last, proj = tie((last, proj))
     unscaled = kept[0] + last.astype(f32)
@@ -328,10 +318,9 @@
         dot(proj_own, hidden, contract_first) + dot(proj_other, hidden_other, contract_first)
     ).T
 
-    norm = jnp.sqrt(lax.dynamic_slice_in_dim(stats, me, 1, 0)[0] + stability_floor)
-    rescale = mine(magnitude, 0) / norm
+    norm, rescale = scales[0], scales[1]
     upstream = block[: 2 * tokens].astype(f32)
-    scaled_own = (upstream * rescale).astype(bf16).astype(f32)
+    scaled_own = scaled_own.astype(f32)
 
     def turned(part):
         lanes = half // tokens
@@ -345,8 +334,7 @@
     magnitude_half = jnp.sum(upstream * unscaled, axis=0) / norm
 
     def join(own, other, axis):
-        pair = jnp.concatenate([own, other, own], axis)
-        return lax.dynamic_slice_in_dim(pair, core * half, 2 * half, axis)
+        return jnp.where(low_core, jnp.concatenate([own, other], axis), jnp.concatenate([other, own], axis))
 
     mixed = join(mixed[:tokens], swap(mixed[tokens:]), 1)
     up_weight_gradient = join(up_half, swap(up_half), 1)

time: 112 us -> 92.4 us (0.83)
  local copies, waits for them, and re-layouts: 25.1 us -> 4.65 us
  waiting for transfers between devices: 11.7 us -> 22.4 us
  Pallas kernels: 41 us -> 37.4 us
  starting transfers between devices: 23 us -> 20.2 us
  other arithmetic: 7.11 us -> 4.58 us
    unnamed x68 -> x18, local copies, waits for them, and re-layouts: 24.7 us -> 4.39 us
    ppermute x14, waiting for transfers between devices: 9.5 us -> 18.5 us  [send(): return lax.ppermute(x, ('tensor', 'dp'), pairs)]
    pallas_call x6 -> x5, Pallas kernels: 27.3 us -> 24.1 us  [the longest x4 12.3 us: forward(): pl.pallas_call(functools.partial(forward_kernel, tokens, rank, vs, later...]
    ppermute x14, starting transfers between devices: 20.6 us -> 17.5 us  [send(): return lax.ppermute(x, ('tensor', 'dp'), pairs)]
    concatenate x3 -> x0, other arithmetic: 2.27 us -> none  [join(): pair = jnp.concatenate([own, other, own], axis)]
    select_n x0 -> x3, other arithmetic: none -> 2.11 us  [join(): jnp.where(low_core, jnp.concatenate([own, other], axis), jnp.concatenate(...]
    ppermute x9, waiting for transfers between devices: 2.18 us -> 3.92 us  [split_columns(): swap = lambda x: lax.ppermute(x, 'dp', [(0, 1), (1, 0)])]
    add x1, other arithmetic: 1.39 us -> 0.19 us  [split_columns(): kept = near0.astype(f32) + from0.astype(f32) + arrived.astype(f32)]
  transfers between devices with their start and end apart: 23 -> 23, of which waited for: 7 -> 8; matrix products, arithmetic and copies ran while one was open for 6% -> 6% of each run, Pallas kernels for 37% -> 41%
where the time goes in v6:
time: 92.4 us; the launch traced here: 92.1 us
  Pallas kernels  37.4 us (40%)
  waiting for transfers between devices  22.4 us (24%)
  starting transfers between devices  20.2 us (22%)
  local copies, waits for them, and re-layouts  4.65 us (5%)
  other arithmetic  4.58 us (5%)
  matrix products  1.94 us (2%)
    ppermute x14, waiting for transfers between devices, send(): return lax.ppermute(x, ('tensor', 'dp'), pairs)  18.5 us
    ppermute x14, starting transfers between devices, send(): return lax.ppermute(x, ('tensor', 'dp'), pairs)  17.5 us
    pallas_call x2, Pallas kernels, backward(): pl.pallas_call(functools.partial(backward_kernel, tokens, n, start, band,...  12.7 us
    pallas_call x4, Pallas kernels, forward(): pl.pallas_call(functools.partial(forward_kernel, tokens, rank, vs, later...  12.3 us
    pallas_call x1, Pallas kernels, load(): pl.pallas_call(functools.partial(load_kernel, tokens, rank, n), in_specs=...  11.8 us
    unnamed x18, local copies, waits for them, and re-layouts  4.39 us
    ppermute x9, waiting for transfers between devices, split_columns(): swap = lambda x: lax.ppermute(x, 'dp', [(0, 1), (1, 0)])  3.92 us
    ppermute x9, starting transfers between devices, split_columns(): swap = lambda x: lax.ppermute(x, 'dp', [(0, 1), (1, 0)])  2.74 us
  transfers between devices with their start and end apart: 23, of which 8 were waited for; matrix products, arithmetic and copies ran while one was open for 6% of the time, Pallas kernels for 41%

profile of v6, /device:TPU:0, one launch (start us, length us, event | category | flops | bytes accessed | tf_op | source)
XLA Modules:
  0.0 92.1 jit_solution(11364945552981442406)
XLA Ops:
  0.6 0.5 collective-permute-start.5
  1.1 0.1 collective-permute-start
  1.2 0.7 reduce-precision_convert_fusion.1
  2.0 0.1 pad.25.clone
  2.0 0.1 stack.79.order_ref
  2.1 0.1 maximum_maximum_fusion.magnitude_ref
  2.2 1.6 %collective-permute-done.other_ref = bf16[128,1024]{1,0:T(8,128)(2,1)S(1)} collective-permute-done((bf16[128,1024]{1,0:T(8,128)(2,1)}, bf16[128,1024]{1,0:T(8,128)(2,1)S(1)}, u32[]{:S(2)}, u32[]{:S(2)}) %collective-permute-start) | collective-permute-done | bytes 262176 | tf_op jit(solution)/shard_map/ppermute | solution.py:239
  3.8 0.9 %copy-done.8 = bf16[128,1024]{1,0:T(8,128)(2,1)S(1)} copy-done((bf16[128,1024]{1,0:T(8,128)(2,1)S(1)}, bf16[128,1024]{1,0:T(8,128)(2,1)}, u32[]{:S(2)}) %copy-start.8) | copy-done | bytes 262168
  4.8 0.6 own_block.1.refs_0_
  5.4 4.0 %collective-permute-start.1 = (bf16[272,512]{1,0:T(8,128)(2,1)S(1)}, bf16[272,512]{1,0:T(8,128)(2,1)S(1)}, u32[]{:S(2)}, u32[]{:S(2)}) collective-permute-start(bf16[272,512]{1,0:T(8,128)(2,1)S(1)} %own_block.1.refs_0_), channel_id=1, source_target_pairs={{0,8},{1,9},{2,10},{3,11},{4,12},{5,13},{6,14},{7,15},{8,0},{9,1},... | collective-permute-start | bytes 835592 | tf_op jit(solution)/shard_map/ppermute | solution.py:244
  9.4 1.6 %collective-permute-start.2 = (bf16[272,512]{1,0:T(8,128)(2,1)S(1)}, bf16[272,512]{1,0:T(8,128)(2,1)S(1)}, u32[]{:S(2)}, u32[]{:S(2)}) collective-permute-start(bf16[272,512]{1,0:T(8,128)(2,1)S(1)} %own_block.1.refs_0_), channel_id=1, source_target_pairs={{0,4},{1,3},{2,6},{3,1},{4,0},{5,7},{6,2},{7,5},{8,12},{9,11},{10,... | collective-permute-start | bytes 835592 | tf_op jit(solution)/shard_map/ppermute | solution.py:244
  11.0 1.5 %collective-permute-start.3 = (bf16[272,512]{1,0:T(8,128)(2,1)S(1)}, bf16[272,512]{1,0:T(8,128)(2,1)S(1)}, u32[]{:S(2)}, u32[]{:S(2)}) collective-permute-start(bf16[272,512]{1,0:T(8,128)(2,1)S(1)} %own_block.1.refs_0_), channel_id=1, source_target_pairs={{0,2},{1,5},{2,0},{3,7},{4,6},{5,1},{6,4},{7,3},{8,10},{9,13},{10,... | collective-permute-start | bytes 835592 | tf_op jit(solution)/shard_map/ppermute | solution.py:244
  12.4 1.2 %copy-done = bf16[64,8192]{1,0:T(8,128)(2,1)S(1)} copy-done((bf16[64,8192]{1,0:T(8,128)(2,1)S(1)}, bf16[64,8192]{1,0:T(8,128)(2,1)}, u32[]{:S(2)}) %copy-start) | copy-done | bytes 1048600
  13.7 1.0 %copy-done.4 = bf16[3584,64]{0,1:T(8,128)(2,1)S(1)} copy-done((bf16[3584,64]{0,1:T(8,128)(2,1)S(1)}, bf16[3584,64]{0,1:T(8,128)(2,1)}, u32[]{:S(2)}) %copy-start.4) | copy-done | bytes 458776
  14.7 1.2 %copy-done.6 = bf16[128,3584]{1,0:T(8,128)(2,1)S(1)} copy-done((bf16[128,3584]{1,0:T(8,128)(2,1)S(1)}, bf16[128,3584]{1,0:T(8,128)(2,1)}, u32[]{:S(2)}) %copy-start.6) | copy-done | bytes 917528
  15.9 11.8 %load.1 = (bf16[3584,512]{1,0:T(8,128)(2,1)S(1)}, bf16[3584,512]{1,0:T(8,128)(2,1)S(1)}, bf16[3584,512]{1,0:T(8,128)(2,1)S(1)}, bf16[3584,512]{1,0:T(8,128)(2,1)...) custom-call(s32[16]{0:T(128)S(1)} %stack.79.order_ref, ...), custom_call_target="tpu_custom_call" | custom-call | flops 1048576 | bytes 1048576 | tf_op jit(solution)/shard_map/load/pallas_call | solution.py:108
  27.6 0.6 collective-permute-start.4
  28.3 4.1 %forward.4 = (bf16[2,256,512]{2,1,0:T(8,128)(2,1)S(1)}, bf16[256,3584]{1,0:T(8,128)(2,1)S(1)}, bf16[256,128]{1,0:T(8,128)(2,1)S(1)}) custom-call(s32[16]{0:T(128)S(1)} %stack.79.order_ref, bf16[128,3584]{1,0:T(8,128)(2,1)S(1)} %get-tuple-element.56.refs_0_, bf16[128,3584]{1,0:T(8,128)(2,1)S(1)} %collective-permute-done.5.refs_1_, ...), custom_call_target="tpu_custom_call" | custom-call | flops 1048576 | bytes 1048576 | tf_op jit(solution)/shard_map/forward/pallas_call | solution.py:152
  32.3 0.0 collective-permute-done.4
  32.4 0.0 collective-permute-done.1.refs_1_
  32.4 0.0 collective-permute-done.3.refs_4_
  32.4 1.6 %collective-permute-start.9 = (bf16[2,256,512]{2,1,0:T(8,128)(2,1)S(1)}, bf16[2,256,512]{2,1,0:T(8,128)(2,1)S(1)}, u32[]{:S(2)}, u32[]{:S(2)}) collective-permute-start(bf16[2,256,512]{2,1,0:T(8,128)(2,1)S(1)} %get-tuple-element.62), channel_id=1, source_target_pairs={{0,2},{1,5},{2,0},{3,7},{4,6},{5,1},{6,4},{7,3},{8,10},{9,13},{10,... | collective-permute-start | bytes 1572872 | tf_op jit(solution)/shard_map/ppermute | solution.py:244
  34.0 0.4 collective-permute-start.6
  34.4 0.5 collective-permute-start.7
  34.9 1.5 %collective-permute-start.8 = (bf16[272,512]{1,0:T(8,128)(2,1)S(1)}, bf16[272,512]{1,0:T(8,128)(2,1)S(1)}, u32[]{:S(2)}, u32[]{:S(2)}) collective-permute-start(bf16[272,512]{1,0:T(8,128)(2,1)S(1)} %collective-permute-done.2.refs_2_), channel_id=1, source_target_pairs={{0,2},{1,5},{2,0},{3,7},{4,6},{5,1},{6,4},{7,3},{8,10},{9,13},{10,... | collective-permute-start | bytes 835592 | tf_op jit(solution)/shard_map/ppermute | solution.py:244
  36.4 1.6 %collective-permute-start.10 = (f32[24,512]{1,0:T(8,128)S(1)}, f32[24,512]{1,0:T(8,128)S(1)}, u32[]{:S(2)}, u32[]{:S(2)}) collective-permute-start(f32[24,512]{1,0:T(8,128)S(1)} %add.73), channel_id=1, source_target_pairs={{0,4},{1,3},{2,6},{3,1},{4,0},{5,7},{6,2},{7,5},{8,12},{9,11},{10,... | collective-permute-start | bytes 147464 | tf_op jit(solution)/shard_map/ppermute | solution.py:244
  38.1 2.8 %forward.5 = bf16[2,256,512]{2,1,0:T(8,128)(2,1)S(1)} custom-call(s32[16]{0:T(128)S(1)} %stack.79.order_ref, bf16[256,3584]{1,0:T(8,128)(2,1)S(1)} %get-tuple-element.64.refs_0_, bf16[256,128]{1,0:T(8,128)(2,1)S(1)} %get-tuple-element.65.refs_1_, bf16[64,8192]{1,0:T(8,128)(2,1)S(1)} %copy-done.1, ...), custom_call_target="tpu_custom_call" | custom-call | flops 1048576 | bytes 1048576 | tf_op jit(solution)/shard_map/forward/pallas_call | solution.py:152
  40.9 3.7 %collective-permute-done.10 = f32[24,512]{1,0:T(8,128)S(1)} collective-permute-done((f32[24,512]{1,0:T(8,128)S(1)}, f32[24,512]{1,0:T(8,128)S(1)}, u32[]{:S(2)}, u32[]{:S(2)}) %collective-permute-start.10) | collective-permute-done | bytes 49184 | tf_op jit(solution)/shard_map/ppermute | solution.py:244
  44.6 0.4 collective-permute-start.11
  45.0 2.7 %forward.6 = bf16[2,256,512]{2,1,0:T(8,128)(2,1)S(1)} custom-call(s32[16]{0:T(128)S(1)} %stack.79.order_ref, bf16[256,3584]{1,0:T(8,128)(2,1)S(1)} %get-tuple-element.64.refs_0_, bf16[256,128]{1,0:T(8,128)(2,1)S(1)} %get-tuple-element.65.refs_1_, bf16[64,8192]{1,0:T(8,128)(2,1)S(1)} %copy-done.1, ...), custom_call_target="tpu_custom_call" | custom-call | flops 1048576 | bytes 1048576 | tf_op jit(solution)/shard_map/forward/pallas_call | solution.py:152
  47.7 2.6 %collective-permute-done.11 = f32[24,512]{1,0:T(8,128)S(1)} collective-permute-done((f32[24,512]{1,0:T(8,128)S(1)}, f32[24,512]{1,0:T(8,128)S(1)}, u32[]{:S(2)}, u32[]{:S(2)}) %collective-permute-start.11) | collective-permute-done | bytes 49184 | tf_op jit(solution)/shard_map/ppermute | solution.py:244
  50.4 0.5 collective-permute-start.13
  50.9 0.1 add_convert_fusion.1
  51.1 0.1 collective-permute-start.14
  51.2 1.5 %collective-permute-start.12 = (bf16[272,512]{1,0:T(8,128)(2,1)S(1)}, bf16[272,512]{1,0:T(8,128)(2,1)S(1)}, u32[]{:S(2)}, u32[]{:S(2)}) collective-permute-start(bf16[272,512]{1,0:T(8,128)(2,1)S(1)} %collective-permute-done.6.refs_3_), channel_id=1, source_target_pairs={{0,2},{1,5},{2,0},{3,7},{4,6},{5,1},{6,4},{7,3},{8,10},{9,13},{10,... | collective-permute-start | bytes 835592 | tf_op jit(solution)/shard_map/ppermute | solution.py:244
  52.7 2.7 %forward.7 = bf16[2,256,512]{2,1,0:T(8,128)(2,1)S(1)} custom-call(s32[16]{0:T(128)S(1)} %stack.79.order_ref, bf16[256,3584]{1,0:T(8,128)(2,1)S(1)} %get-tuple-element.64.refs_0_, bf16[256,128]{1,0:T(8,128)(2,1)S(1)} %get-tuple-element.65.refs_1_, bf16[64,8192]{1,0:T(8,128)(2,1)S(1)} %copy-done.1, bf16[3584,512]{1,0:T(8,128)(2,1)S(1)} %get-tuple-element.73.refs_3_.refs_11_, ...), custom_call_target="tpu_custom_call" | custom-call | flops 1048576 | bytes 1048576 | tf_op jit(solution)/shard_map/forward/pallas_call | solution.py:152
  55.5 0.0 copy-start.5
  55.5 8.5 %collective-permute-done.13 = bf16[2,256,512]{2,1,0:T(8,128)(2,1)S(1)} collective-permute-done((bf16[2,256,512]{2,1,0:T(8,128)(2,1)S(1)}, bf16[2,256,512]{2,1,0:T(8,128)(2,1)S(1)}, u32[]{:S(2)}, u32[]{:S(2)}) %collective-permute-start.13) | collective-permute-done | bytes 524320 | tf_op jit(solution)/shard_map/ppermute | solution.py:244
  64.0 3.0 %collective-permute-done.12.refs_7_ = bf16[272,512]{1,0:T(8,128)(2,1)S(1)} collective-permute-done((bf16[272,512]{1,0:T(8,128)(2,1)S(1)}, bf16[272,512]{1,0:T(8,128)(2,1)S(1)}, u32[]{:S(2)}, u32[]{:S(2)}) %collective-permute-start.12) | collective-permute-done | bytes 278560 | tf_op jit(solution)/shard_map/ppermute | solution.py:244
  67.0 0.2 convert_add_fusion
  67.2 1.5 %collective-permute-start.15 = (bf16[256,512]{1,0:T(8,128)(2,1)S(1)}, bf16[256,512]{1,0:T(8,128)(2,1)S(1)}, u32[]{:S(2)}, u32[]{:S(2)}) collective-permute-start(bf16[256,512]{1,0:T(8,128)(2,1)S(1)} %fusion.4), channel_id=1, source_target_pairs={{0,8},{1,9},{2,10},{3,11},{4,12},{5,13},{6,14},{7,15},{8,0},{9,1},... | collective-permute-start | bytes 786440 | tf_op jit(solution)/shard_map/ppermute | solution.py:244
  68.7 7.6 %backward.2 = (f32[128,2048]{1,0:T(8,128)S(1)}, bf16[128,2048]{1,0:T(8,128)(2,1)S(1)}, bf16[256,4096]{1,0:T(8,128)(2,1)S(1)}, f32[256,64]{1,0:T(8,128)S(1)}, f32...) custom-call(s32[16]{0:T(128)S(1)} %stack.79.order_ref, bf16[272,512]{1,0:T(8,128)(2,1)S(1)} %own_block.1.refs_0_, ...), custom_call_target="tpu_custom_call" | custom-call | flops 1048576 | bytes 1048576 | tf_op jit(solution)/shard_map/backward/pallas_call | solution.py:217
  76.3 0.4 collective-permute-start.17
  76.7 0.2 collective-permute-start.20
  76.9 0.2 fusion.6
  77.1 1.2 %collective-permute-done.20 = f32[16,512]{1,0:T(8,128)S(1)} collective-permute-done((f32[16,512]{1,0:T(8,128)S(1)}, f32[16,512]{1,0:T(8,128)S(1)}, u32[]{:S(2)}, u32[]{:S(2)}) %collective-permute-start.20) | collective-permute-done | bytes 32800 | tf_op jit(solution)/shard_map/ppermute | solution.py:239
  78.3 0.2 fusion.2
  78.5 0.4 collective-permute-start.21
  78.9 1.0 %collective-permute-done.21 = f32[64,512]{1,0:T(8,128)S(1)} collective-permute-done((f32[64,512]{1,0:T(8,128)S(1)}, f32[64,512]{1,0:T(8,128)S(1)}, u32[]{:S(2)}, u32[]{:S(2)}) %collective-permute-start.21) | collective-permute-done | bytes 131104 | tf_op jit(solution)/shard_map/ppermute | solution.py:239
  80.0 0.7 maximum_select_fusion.1
  80.7 0.7 collective-permute-done.15
  81.4 0.2 multiply_reduce_fusion
  81.5 0.1 collective-permute-start.22
  81.6 0.6 collective-permute-start.16
  82.2 0.1 collective-permute-start.19
  82.3 5.1 %backward.3 = (f32[128,1536]{1,0:T(8,128)S(1)}, bf16[128,1536]{1,0:T(8,128)(2,1)S(1)}) custom-call(s32[16]{0:T(128)S(1)} %stack.79.order_ref, bf16[256,4096]{1,0:T(8,128)(2,1)S(1)} %get-tuple-element.91.refs_0_, f32[256,64]{1,0:T(8,128)S(1)} %get-tuple-element.92.refs_1_, bf16[64,3584]{1,0:T(8,128)(2,1)S(1)} %bitcast.36, ...), custom_call_target="tpu_custom_call" | custom-call | flops 1048576 | bytes 1048576 | tf_op jit(solution)/shard_map/backward/pallas_call | solution.py:217
  87.4 0.5 collective-permute-start.18
  87.9 0.6 maximum_select_fusion.2
  88.5 0.3 fusion.11
  88.9 1.2 %fusion.1 = f32[3584,64]{0,1:T(8,128)} fusion(f32[64,3584]{1,0:T(8,128)S(1)} %fusion.11, bf16[128,3584]{1,0:T(8,128)(2,1)S(1)} %copy-done.7, f32[256,64]{1,0:T(8,128)S(1)} %collective-permute-done.19, f32[256,64]{1,0:T(8,128)S(1)} %get-tuple-element.92.refs_1_), kind=kOutput, calls=%fused_computation.2 | convolution fusion | flops 59195392 | bytes 2883584 | tf_op jit(solution)/shard_map/dot_general | solution.py:21
  90.1 0.8 maximum_select_fusion
  90.9 0.1 add_convert_fusion
  91.0 0.1 add_convert_fusion.2
  91.1 1.0 %pad_maximum_fusion = bf16[128,3584]{1,0:T(8,128)(2,1)} fusion(bf16[128,1536]{1,0:T(8,128)(2,1)S(1)} %add_convert_fusion.2, bf16[128,2048]{1,0:T(8,128)(2,1)S(1)} %add_convert_fusion), kind=kLoop, calls=%fused_computation.8 | loop fusion | flops 1835008 | bytes 1835008 | tf_op jit(solution)/shard_map/concatenate | solution.py:311
  (39 shorter events, 0.2 us)
Async XLA Ops:
  0.6 27.6 %collective-permute-start.5 = (bf16[128,3584]{1,0:T(8,128)(2,1)}, bf16[128,3584]{1,0:T(8,128)(2,1)S(1)}, u32[]{:S(2)}, u32[]{:S(2)}) collective-permute-start(bf16[128,3584]{1,0:T(8,128)(2,1)} %own_ref.3), channel_id=1, source_target_pairs={{0,1},{1,0},{2,3},{3,2},{4,5},{5,4},{6,7},{7,6},{8,9},{9,8},{10,11... | collective-permute-start | bytes 2752520 | tf_op jit(solution)/shard_map/ppermute | solution.py:239
  1.1 2.7 %collective-permute-start = (bf16[128,1024]{1,0:T(8,128)(2,1)}, bf16[128,1024]{1,0:T(8,128)(2,1)S(1)}, u32[]{:S(2)}, u32[]{:S(2)}) collective-permute-start(bf16[128,1024]{1,0:T(8,128)(2,1)} %own_ref.2), channel_id=1, source_target_pairs={{0,1},{1,0},{2,3},{3,2},{4,5},{5,4},{6,7},{7,6},{8,9},{9,8},{10,11... | collective-permute-start | bytes 786440 | tf_op jit(solution)/shard_map/ppermute | solution.py:239
  3.8 0.9 %copy-start.8 = (bf16[128,1024]{1,0:T(8,128)(2,1)S(1)}, bf16[128,1024]{1,0:T(8,128)(2,1)}, u32[]{:S(2)}) copy-start(bf16[128,1024]{1,0:T(8,128)(2,1)} %own_ref.2) | copy-start | bytes 786436
  5.4 27.0 %collective-permute-start.1 = (bf16[272,512]{1,0:T(8,128)(2,1)S(1)}, bf16[272,512]{1,0:T(8,128)(2,1)S(1)}, u32[]{:S(2)}, u32[]{:S(2)}) collective-permute-start(bf16[272,512]{1,0:T(8,128)(2,1)S(1)} %own_block.1.refs_0_), channel_id=1, source_target_pairs={{0,8},{1,9},{2,10},{3,11},{4,12},{5,13},{6,14},{7,15},{8,0},{9,1},... | collective-permute-start | bytes 835592 | tf_op jit(solution)/shard_map/ppermute | solution.py:244
  9.4 23.0 %collective-permute-start.2 = (bf16[272,512]{1,0:T(8,128)(2,1)S(1)}, bf16[272,512]{1,0:T(8,128)(2,1)S(1)}, u32[]{:S(2)}, u32[]{:S(2)}) collective-permute-start(bf16[272,512]{1,0:T(8,128)(2,1)S(1)} %own_block.1.refs_0_), channel_id=1, source_target_pairs={{0,4},{1,3},{2,6},{3,1},{4,0},{5,7},{6,2},{7,5},{8,12},{9,11},{10,... | collective-permute-start | bytes 835592 | tf_op jit(solution)/shard_map/ppermute | solution.py:244
  11.0 21.4 %collective-permute-start.3 = (bf16[272,512]{1,0:T(8,128)(2,1)S(1)}, bf16[272,512]{1,0:T(8,128)(2,1)S(1)}, u32[]{:S(2)}, u32[]{:S(2)}) collective-permute-start(bf16[272,512]{1,0:T(8,128)(2,1)S(1)} %own_block.1.refs_0_), channel_id=1, source_target_pairs={{0,2},{1,5},{2,0},{3,7},{4,6},{5,1},{6,4},{7,3},{8,10},{9,13},{10,... | collective-permute-start | bytes 835592 | tf_op jit(solution)/shard_map/ppermute | solution.py:244
  12.4 1.2 %copy-start = (bf16[64,8192]{1,0:T(8,128)(2,1)S(1)}, bf16[64,8192]{1,0:T(8,128)(2,1)}, u32[]{:S(2)}) copy-start(bf16[64,8192]{1,0:T(8,128)(2,1)} %refs_9_.1) | copy-start | bytes 3145732
  13.7 1.0 %copy-start.4 = (bf16[3584,64]{0,1:T(8,128)(2,1)S(1)}, bf16[3584,64]{0,1:T(8,128)(2,1)}, u32[]{:S(2)}) copy-start(bf16[3584,64]{0,1:T(8,128)(2,1)} %param.8) | copy-start | bytes 1376260
  14.7 1.2 %copy-start.6 = (bf16[128,3584]{1,0:T(8,128)(2,1)S(1)}, bf16[128,3584]{1,0:T(8,128)(2,1)}, u32[]{:S(2)}) copy-start(bf16[128,3584]{1,0:T(8,128)(2,1)} %own_ref.3) | copy-start | bytes 2752516
  15.9 12.4 %copy-start.1 = (bf16[64,8192]{1,0:T(8,128)(2,1)S(1)}, bf16[64,8192]{1,0:T(8,128)(2,1)}, u32[]{:S(2)}) copy-start(bf16[64,8192]{1,0:T(8,128)(2,1)} %refs_9_.1) | copy-start | bytes 3145732
  27.6 10.5 %copy-start.2 = (bf16[3584,512]{1,0:T(8,128)(2,1)}, bf16[3584,512]{1,0:T(8,128)(2,1)S(1)}, u32[]{:S(2)}) copy-start(bf16[3584,512]{1,0:T(8,128)(2,1)S(1)} %get-tuple-element.66.refs_3_.refs_15_.refs_7_) | copy-start | bytes 11010052
  27.6 4.7 %collective-permute-start.4 = (f32[24,512]{1,0:T(8,128)S(1)}, f32[24,512]{1,0:T(8,128)S(1)}, u32[]{:S(2)}, u32[]{:S(2)}) collective-permute-start(f32[24,512]{1,0:T(8,128)S(1)} %get-tuple-element.55), channel_id=1, source_target_pairs={{0,2},{1,5},{2,0},{3,7},{4,6},{5,1},{6,4},{7,3},{8,10},{9,13},{10,... | collective-permute-start | bytes 147464 | tf_op jit(solution)/shard_map/ppermute | solution.py:244
  32.4 18.5 %collective-permute-start.9 = (bf16[2,256,512]{2,1,0:T(8,128)(2,1)S(1)}, bf16[2,256,512]{2,1,0:T(8,128)(2,1)S(1)}, u32[]{:S(2)}, u32[]{:S(2)}) collective-permute-start(bf16[2,256,512]{2,1,0:T(8,128)(2,1)S(1)} %get-tuple-element.62), channel_id=1, source_target_pairs={{0,2},{1,5},{2,0},{3,7},{4,6},{5,1},{6,4},{7,3},{8,10},{9,13},{10,... | collective-permute-start | bytes 1572872 | tf_op jit(solution)/shard_map/ppermute | solution.py:244
  34.0 16.9 %collective-permute-start.6 = (bf16[272,512]{1,0:T(8,128)(2,1)S(1)}, bf16[272,512]{1,0:T(8,128)(2,1)S(1)}, u32[]{:S(2)}, u32[]{:S(2)}) collective-permute-start(bf16[272,512]{1,0:T(8,128)(2,1)S(1)} %collective-permute-done.1.refs_1_), channel_id=1, source_target_pairs={{0,4},{1,3},{2,6},{3,1},{4,0},{5,7},{6,2},{7,5},{8,12},{9,11},{10,... | collective-permute-start | bytes 835592 | tf_op jit(solution)/shard_map/ppermute | solution.py:244
  34.4 16.5 %collective-permute-start.7 = (bf16[272,512]{1,0:T(8,128)(2,1)S(1)}, bf16[272,512]{1,0:T(8,128)(2,1)S(1)}, u32[]{:S(2)}, u32[]{:S(2)}) collective-permute-start(bf16[272,512]{1,0:T(8,128)(2,1)S(1)} %collective-permute-done.1.refs_1_), channel_id=1, source_target_pairs={{0,2},{1,5},{2,0},{3,7},{4,6},{5,1},{6,4},{7,3},{8,10},{9,13},{10,... | collective-permute-start | bytes 835592 | tf_op jit(solution)/shard_map/ppermute | solution.py:244
  34.9 16.0 %collective-permute-start.8 = (bf16[272,512]{1,0:T(8,128)(2,1)S(1)}, bf16[272,512]{1,0:T(8,128)(2,1)S(1)}, u32[]{:S(2)}, u32[]{:S(2)}) collective-permute-start(bf16[272,512]{1,0:T(8,128)(2,1)S(1)} %collective-permute-done.2.refs_2_), channel_id=1, source_target_pairs={{0,2},{1,5},{2,0},{3,7},{4,6},{5,1},{6,4},{7,3},{8,10},{9,13},{10,... | collective-permute-start | bytes 835592 | tf_op jit(solution)/shard_map/ppermute | solution.py:244
  36.4 8.2 %collective-permute-start.10 = (f32[24,512]{1,0:T(8,128)S(1)}, f32[24,512]{1,0:T(8,128)S(1)}, u32[]{:S(2)}, u32[]{:S(2)}) collective-permute-start(f32[24,512]{1,0:T(8,128)S(1)} %add.73), channel_id=1, source_target_pairs={{0,4},{1,3},{2,6},{3,1},{4,0},{5,7},{6,2},{7,5},{8,12},{9,11},{10,... | collective-permute-start | bytes 147464 | tf_op jit(solution)/shard_map/ppermute | solution.py:244
  44.6 5.7 %collective-permute-start.11 = (f32[24,512]{1,0:T(8,128)S(1)}, f32[24,512]{1,0:T(8,128)S(1)}, u32[]{:S(2)}, u32[]{:S(2)}) collective-permute-start(f32[24,512]{1,0:T(8,128)S(1)} %add.74), channel_id=1, source_target_pairs={{0,8},{1,9},{2,10},{3,11},{4,12},{5,13},{6,14},{7,15},{8,0},{9,1},... | collective-permute-start | bytes 147464 | tf_op jit(solution)/shard_map/ppermute | solution.py:244
  50.4 13.6 %collective-permute-start.13 = (bf16[2,256,512]{2,1,0:T(8,128)(2,1)S(1)}, bf16[2,256,512]{2,1,0:T(8,128)(2,1)S(1)}, u32[]{:S(2)}, u32[]{:S(2)}) collective-permute-start(bf16[2,256,512]{2,1,0:T(8,128)(2,1)S(1)} %forward.5), channel_id=1, source_target_pairs={{0,2},{1,5},{2,0},{3,7},{4,6},{5,1},{6,4},{7,3},{8,10},{9,13},{10,... | collective-permute-start | bytes 1572872 | tf_op jit(solution)/shard_map/ppermute | solution.py:244
  51.1 15.9 %collective-permute-start.14 = (bf16[2,256,512]{2,1,0:T(8,128)(2,1)S(1)}, bf16[2,256,512]{2,1,0:T(8,128)(2,1)S(1)}, u32[]{:S(2)}, u32[]{:S(2)}) collective-permute-start(bf16[2,256,512]{2,1,0:T(8,128)(2,1)S(1)} %add_convert_fusion.1), channel_id=1, source_target_pairs={{0,4},{1,3},{2,6},{3,1},{4,0},{5,7},{6,2},{7,5},{8,12},{9,11},{10,... | collective-permute-start | bytes 1572872 | tf_op jit(solution)/shard_map/ppermute | solution.py:244
  51.2 15.8 %collective-permute-start.12 = (bf16[272,512]{1,0:T(8,128)(2,1)S(1)}, bf16[272,512]{1,0:T(8,128)(2,1)S(1)}, u32[]{:S(2)}, u32[]{:S(2)}) collective-permute-start(bf16[272,512]{1,0:T(8,128)(2,1)S(1)} %collective-permute-done.6.refs_3_), channel_id=1, source_target_pairs={{0,2},{1,5},{2,0},{3,7},{4,6},{5,1},{6,4},{7,3},{8,10},{9,13},{10,... | collective-permute-start | bytes 835592 | tf_op jit(solution)/shard_map/ppermute | solution.py:244
  52.7 16.0 %copy-start.3 = (bf16[3584,512]{1,0:T(8,128)(2,1)S(1)}, bf16[3584,512]{1,0:T(8,128)(2,1)}, u32[]{:S(2)}) copy-start(bf16[3584,512]{1,0:T(8,128)(2,1)} %copy-done.2) | copy-start | bytes 11010052
  55.5 13.2 %copy-start.5 = (bf16[3584,64]{0,1:T(8,128)(2,1)S(1)}, bf16[3584,64]{0,1:T(8,128)(2,1)}, u32[]{:S(2)}) copy-start(bf16[3584,64]{0,1:T(8,128)(2,1)} %param.8) | copy-start | bytes 1376260
  67.2 14.2 %collective-permute-start.15 = (bf16[256,512]{1,0:T(8,128)(2,1)S(1)}, bf16[256,512]{1,0:T(8,128)(2,1)S(1)}, u32[]{:S(2)}, u32[]{:S(2)}) collective-permute-start(bf16[256,512]{1,0:T(8,128)(2,1)S(1)} %fusion.4), channel_id=1, source_target_pairs={{0,8},{1,9},{2,10},{3,11},{4,12},{5,13},{6,14},{7,15},{8,0},{9,1},... | collective-permute-start | bytes 786440 | tf_op jit(solution)/shard_map/ppermute | solution.py:244
  76.3 14.6 %collective-permute-start.17 = (bf16[128,2048]{1,0:T(8,128)(2,1)S(1)}, bf16[128,2048]{1,0:T(8,128)(2,1)S(1)}, u32[]{:S(2)}, u32[]{:S(2)}) collective-permute-start(bf16[128,2048]{1,0:T(8,128)(2,1)S(1)} %get-tuple-element.90), channel_id=1, source_target_pairs={{0,1},{1,0},{2,3},{3,2},{4,5},{5,4},{6,7},{7,6},{8,9},{9,8},{10,11... | collective-permute-start | bytes 1572872 | tf_op jit(solution)/shard_map/ppermute | solution.py:239
  76.7 1.7 %collective-permute-start.20 = (f32[16,512]{1,0:T(8,128)S(1)}, f32[16,512]{1,0:T(8,128)S(1)}, u32[]{:S(2)}, u32[]{:S(2)}) collective-permute-start(f32[16,512]{1,0:T(8,128)S(1)} %slice.85), channel_id=1, source_target_pairs={{0,1},{1,0},{2,3},{3,2},{4,5},{5,4},{6,7},{7,6},{8,9},{9,8},{10,11... | collective-permute-start | bytes 98312 | tf_op jit(solution)/shard_map/ppermute | solution.py:239
  78.5 1.4 %collective-permute-start.21 = (f32[64,512]{1,0:T(8,128)S(1)}, f32[64,512]{1,0:T(8,128)S(1)}, u32[]{:S(2)}, u32[]{:S(2)}) collective-permute-start(f32[64,512]{1,0:T(8,128)S(1)} %fusion.2), channel_id=1, source_target_pairs={{0,1},{1,0},{2,3},{3,2},{4,5},{5,4},{6,7},{7,6},{8,9},{9,8},{10,11... | collective-permute-start | bytes 393224 | tf_op jit(solution)/shard_map/ppermute | solution.py:239
  81.5 6.4 %collective-permute-start.22 = (f32[512]{0:T(512)S(1)}, f32[512]{0:T(512)S(1)}, u32[]{:S(2)}, u32[]{:S(2)}) collective-permute-start(f32[512]{0:T(512)S(1)} %div.3), channel_id=1, source_target_pairs={{0,1},{1,0},{2,3},{3,2},{4,5},{5,4},{6,7},{7,6},{8,9},{9,8},{10,11... | collective-permute-start | bytes 6152 | tf_op jit(solution)/shard_map/ppermute | solution.py:239
  81.6 8.5 %collective-permute-start.16 = (bf16[128,512]{1,0:T(8,128)(2,1)S(1)}, bf16[128,512]{1,0:T(8,128)(2,1)S(1)}, u32[]{:S(2)}, u32[]{:S(2)}) collective-permute-start(bf16[128,512]{1,0:T(8,128)(2,1)S(1)} %get-tuple-element.100), channel_id=1, source_target_pairs={{0,1},{1,0},{2,3},{3,2},{4,5},{5,4},{6,7},{7,6},{8,9},{9,8},{10,11... | collective-permute-start | bytes 393224 | tf_op jit(solution)/shard_map/ppermute | solution.py:239
  82.2 6.3 %collective-permute-start.19 = (f32[256,64]{1,0:T(8,128)S(1)}, f32[256,64]{1,0:T(8,128)S(1)}, u32[]{:S(2)}, u32[]{:S(2)}) collective-permute-start(f32[256,64]{1,0:T(8,128)S(1)} %get-tuple-element.92.refs_1_), channel_id=1, source_target_pairs={{0,1},{1,0},{2,3},{3,2},{4,5},{5,4},{6,7},{7,6},{8,9},{9,8},{10,11... | collective-permute-start | bytes 196616 | tf_op jit(solution)/shard_map/ppermute | solution.py:239
  82.3 6.6 %copy-start.7 = (bf16[128,3584]{1,0:T(8,128)(2,1)S(1)}, bf16[128,3584]{1,0:T(8,128)(2,1)}, u32[]{:S(2)}) copy-start(bf16[128,3584]{1,0:T(8,128)(2,1)} %own_ref.3) | copy-start | bytes 2752516
  87.4 3.6 %collective-permute-start.18 = (bf16[128,1536]{1,0:T(8,128)(2,1)S(1)}, bf16[128,1536]{1,0:T(8,128)(2,1)S(1)}, u32[]{:S(2)}, u32[]{:S(2)}) collective-permute-start(bf16[128,1536]{1,0:T(8,128)(2,1)S(1)} %get-tuple-element.94), channel_id=1, source_target_pairs={{0,1},{1,0},{2,3},{3,2},{4,5},{5,4},{6,7},{7,6},{8,9},{9,8},{10,11... | collective-permute-start | bytes 1179656 | tf_op jit(solution)/shard_map/ppermute | solution.py:239

commit v7 on v6

--- a/solution.py
+++ b/solution.py
@@ -41,17 +41,22 @@
     return pl.BlockSpec(memory_space=pltpu.VMEM)
 
 
+def anywhere():
+    return pl.BlockSpec(memory_space=pl.ANY)
+
+
 def params():
     return pltpu.CompilerParams(vmem_limit_bytes=vmem_bytes)
 
 
-def block_kernel(tokens, order_ref, own_ref, other_ref, magnitude_ref, out_ref):
+def block_kernel(tokens, order_ref, own_ref, other_ref, magnitude_ref, *refs):
+    out_ref = refs[-1]
     out_ref[:tokens, :] = own_ref[...]
     out_ref[tokens : 2 * tokens, :] = other_ref[...]
     out_ref[2 * tokens :, :] = magnitude_ref[...]
 
 
-def own_block(order, cotangent, other, magnitude_rows):
+def own_block(order, cotangent, other, magnitude_rows, *early):
     tokens, columns = cotangent.shape
     half = columns // 2
     padded = 2 * tokens + pad_rows
@@ -64,6 +69,7 @@
                 pl.BlockSpec((tokens, half), lambda i, p: (0, lax.rem(p[0], 2))),
                 pl.BlockSpec((tokens, half), lambda i, p: (0, lax.rem(p[0], 2))),
                 pl.BlockSpec((pad_rows, half), lambda i, p: (0, lax.rem(p[0], 2))),
+                *[vmem()] * len(early),
             ],
             out_specs=pl.BlockSpec((padded, half), lambda i, p: (0, 0)),
         ),
@@ -71,51 +77,52 @@
         compiler_params=params(),
         cost_estimate=small_cost,
         name="own_block",
-    )(order, cotangent, other, magnitude_rows)
-
-
-def load_kernel(tokens, rank, n, order_ref, own_ref, at_ref, up_ref, w_hbm, *refs):
-    held, (stats_ref, lhs_ref, sem, own_sem) = refs[:n], refs[n:]
+    )(order, cotangent, other, magnitude_rows, *early)
+
+
+def load_kernel(tokens, rank, n, vs, first, order_ref, before_ref, at_ref, up_ref, w_hbm, *refs):
+    held, (stats_ref, sem) = refs[: len(vs)], refs[len(vs) :]
     half = held[0].shape[1]
-    columns = [pl.ds(pl.multiple_of(order_ref[k] * half, half), half) for k in range(n)]
+    columns = [pl.ds(pl.multiple_of(order_ref[v] * half, half), half) for v in vs]
     copies = [pltpu.make_async_copy(w_hbm.at[:, c], h, sem.at[k]) for k, (c, h) in enumerate(zip(columns, held))]
-    own_copy = pltpu.make_async_copy(own_ref, lhs_ref, own_sem)
-    own_copy.start()
     for copy in copies:
         copy.start()
 
     down = at_ref[...]
     high, low = split_pair(dot(down, down, contract_trailing))
-    own_copy.wait()
-    turned = dot(down, lhs_ref[...], contract_trailing)
-    lanes = half // tokens
-    span = rank // lanes
-    for j in range(lanes):
-        stats_ref[n:, j * tokens : (j + 1) * tokens] = turned[j * span : (j + 1) * span]
-    for k in range(n):
+    if first:
+        turned = dot(down, before_ref[...], contract_trailing)
+        lanes = half // tokens
+        span = rank // lanes
+        stats_ref[:n, :] = jnp.zeros((n, half), f32)
+        for j in range(lanes):
+            stats_ref[n:, j * tokens : (j + 1) * tokens] = turned[j * span : (j + 1) * span]
+    else:
+        stats_ref[...] = before_ref[...]
+    for k, v in enumerate(vs):
         copies[k].wait()
         up = up_ref[:, columns[k]]
         cross = 2 * dot(down, held[k][...]) + adapter_scale * (dot(high, up) + dot(low, up))
         cross = jnp.sum(up.astype(f32) * cross, axis=0, keepdims=True)
-        stats_ref[pl.ds(order_ref[n + k], 1), :] = sum_of_squares(held[k]) + adapter_scale * cross
-
-
-def load(order, own, at, up, weight, half):
+        stats_ref[pl.ds(order_ref[n + v], 1), :] = sum_of_squares(held[k]) + adapter_scale * cross
+
+
+def load(vs, order, at, up, weight, half, own=None, before=None):
     n = order.shape[0] // 2
-    tokens, rows = own.shape
-    rank = at.shape[0]
-    any_ = pl.BlockSpec(memory_space=pl.ANY)
+    rank, rows = at.shape
+    first = before is None
+    tokens = own.shape[0] if first else None
+    stats = (n + rank * tokens // half, half) if first else before.shape
     return pl.pallas_call(
-        functools.partial(load_kernel, tokens, rank, n),
-        in_specs=[pl.BlockSpec(memory_space=pltpu.SMEM), any_, vmem(), vmem(), any_],
-        out_specs=[vmem()] * (n + 2),
-        out_shape=[jax.ShapeDtypeStruct((rows, half), bf16)] * n
-        + [jax.ShapeDtypeStruct((n + rank * tokens // half, half), f32), jax.ShapeDtypeStruct(own.shape, bf16)],
-        scratch_shapes=[pltpu.SemaphoreType.DMA((n,)), pltpu.SemaphoreType.DMA],
+        functools.partial(load_kernel, tokens, rank, n, vs, first),
+        in_specs=[pl.BlockSpec(memory_space=pltpu.SMEM), vmem(), vmem(), vmem(), anywhere()],
+        out_specs=[vmem()] * (len(vs) + 1),
+        out_shape=[jax.ShapeDtypeStruct((rows, half), bf16)] * len(vs) + [jax.ShapeDtypeStruct(stats, f32)],
+        scratch_shapes=[pltpu.SemaphoreType.DMA((len(vs),))],
         compiler_params=params(),
         cost_estimate=small_cost,
         name="load",
-    )(order, own, at, up, weight)
+    )(order, own if first else before, at, up, weight)
 
 
 def forward_kernel(tokens, rank, vs, first, order_ref, *refs):
@@ -138,12 +145,11 @@
 
 
 def forward(vs, order, held, up, first=None, later=None):
-    held = [held[v] for v in vs]
     rows, half = held[0].shape
     if later is None:
         own, other, at = operands = first
         tokens, rank = own.shape[0], at.shape[0]
-        specs = [vmem(), pl.BlockSpec(memory_space=pl.ANY), vmem()]
+        specs = [vmem(), anywhere(), vmem()]
     else:
         lhs, adapter = operands = later
         rank, tokens = adapter.shape[1] // 2, lhs.shape[0] // 2
@@ -264,39 +270,41 @@
         [jnp.stack([first, second, third]), jnp.zeros((pad_rows - 3, 2 * half), f32)]
     ).astype(bf16)
     low_core, order, cot_other = tie((low_core, order, cot_other))
-    block = own_block(order, cotangent, cot_other, magnitude_rows)
+    block = own_block(order, cotangent, cot_other, magnitude_rows, at, up, hidden)
 
     cots = {0b000: block, 0b001: send(block, 2), 0b010: send(block, 1), 0b100: send(block, 0)}
-    block, order = tie((block, order))
-    *held, stats, own = load(order, hidden, at, up, weight, half)
-
+
+    run_load = functools.partial(load, at=at, up=up, weight=weight, half=half)
+    *far, stats = run_load((0b100, 0b101, 0b110, 0b111), order, own=hidden)
+    *arrived, stats = tie((*(cots[v] for v in (0b001, 0b010, 0b100)), stats))
+    cots[0b001], cots[0b010], cots[0b100] = arrived
+    cots[0b011] = send(cots[0b001], 1)
+    pair = send(jnp.stack([cots[0b001], cots[0b010]]), 0)
+    sent, lhs, adapter = forward((0b100, 0b101, 0b110, 0b111), order, far, up, first=(hidden, hidden_other, at))
+    run = lambda vs, held: forward(vs, order, held, up, later=(lhs, adapter))[0]
+    cots[0b011], pair, order_after, sent = tie((cots[0b011], pair, order, sent))
+    cots[0b101], cots[0b110] = pair[0], pair[1]
+    from_far = send(sent, 0)
+    cots[0b111] = send(cots[0b011], 0)
+    *near, stats = run_load((0b000, 0b001, 0b010, 0b011), order_after, before=stats)
+    cots[0b111], stats = tie((cots[0b111], stats))
     got = send(stats, 0)
-    far1, lhs, adapter = forward((0b110, 0b111), order, held, up, first=(own, hidden_other, at))
-    run = lambda *vs: forward(vs, order, held, up, later=(lhs, adapter))[0]
-    *arrived, got, far1 = tie((*(cots[v] for v in (0b001, 0b010, 0b100)), got, far1))
-    cots[0b001], cots[0b010], cots[0b100] = arrived
+    near1 = run((0b010, 0b011), near[2:])
+    from_far, got, near1 = tie((from_far, got, near1))
     stats = stats + got
     got = send(stats, 1)
-    from1 = send(far1, 0)
-    cots[0b011], cots[0b101], cots[0b110] = send(cots[0b001], 1), send(cots[0b001], 0), send(cots[0b010], 0)
-    far0 = run(0b100, 0b101)
-    got, far0 = tie((got, far0))
+    arrived = send((near1.astype(f32) + from_far[2:].astype(f32)).astype(bf16), 1)
+    near0 = run((0b000, 0b001), near[:2])
+    got, near0 = tie((got, near0))
     stats = stats + got
     got = send(stats, 2)
-    from0 = send(far0, 0)
-    near1 = run(0b010, 0b011)
-    cots[0b011], cots[0b101], cots[0b110], from1, got, near1 = tie(
-        (cots[0b011], cots[0b101], cots[0b110], from1, got, near1)
-    )
+    arrived, got = tie((arrived, got))
     stats = stats + got
-    cots[0b111] = send(cots[0b011], 0)
-    arrived = send((near1.astype(f32) + from1.astype(f32)).astype(bf16), 1)
-    near0 = run(0b000, 0b001)
-    cots[0b111], from0, near0, arrived, stats = tie((cots[0b111], from0, near0, arrived, stats))
-    kept = near0.astype(f32) + from0.astype(f32) + arrived.astype(f32)
+    kept = near0.astype(f32) + from_far[:2].astype(f32) + arrived.astype(f32)
     last = send(kept[1].astype(bf16), 2)
     lowrank_rows = stats[n:]
     lowrank_other = swap(lowrank_rows)
+    held = near + far
 
     band = 256
     bands = rows // band
@@ -304,14 +312,25 @@
     run = functools.partial(backward, order, band=band, at=at, held=held)
     grad_a, other_a, scaled, proj, scales, scaled_own = run(0, many, first=([cots[v] for v in range(n)], stats, up))
     got_a = swap(other_a)
-    last, proj = tie((last, proj))
-    unscaled = kept[0] + last.astype(f32)
+    from_sibling = swap(proj)
+    lowrank_other, scaled_own = tie((lowrank_other, scaled_own))
+    scaled_own = scaled_own.astype(f32)
+
+    def turned(part):
+        lanes = half // tokens
+        return jnp.concatenate([part[:, j * tokens : (j + 1) * tokens] for j in range(lanes)])
+
+    up_half = adapter_scale * (
+        jnp.dot(turned(lowrank_rows), scaled_own[:tokens], precision=lax.Precision.HIGHEST)
+        + jnp.dot(turned(lowrank_other), scaled_own[tokens:], precision=lax.Precision.HIGHEST)
+    )
+    up_other = swap(up_half)
     grad_b, other_b = run(many, bands - many, later=(scaled, proj))
+    got_a, from_sibling, up_other, last, other_b = tie((got_a, from_sibling, up_other, last, other_b))
     got_b = swap(other_b)
     hidden_gradient = jnp.concatenate(
         [(own + got.astype(f32)).astype(bf16) for own, got in ((grad_a, got_a), (grad_b, got_b))], axis=1
     )
-    from_sibling = swap(proj)
     proj_own = (proj[:tokens] + from_sibling[tokens:]).astype(bf16)
     proj_other = (proj[tokens:] + from_sibling[:tokens]).astype(bf16)
     down_weight_gradient = adapter_scale * (
@@ -319,25 +338,15 @@
     ).T
 
     norm, rescale = scales[0], scales[1]
-    upstream = block[: 2 * tokens].astype(f32)
-    scaled_own = scaled_own.astype(f32)
-
-    def turned(part):
-        lanes = half // tokens
-        return jnp.concatenate([part[:, j * tokens : (j + 1) * tokens] for j in range(lanes)])
-
-    up_half = adapter_scale * (
-        jnp.dot(turned(lowrank_rows), scaled_own[:tokens], precision=lax.Precision.HIGHEST)
-        + jnp.dot(turned(lowrank_other), scaled_own[tokens:], precision=lax.Precision.HIGHEST)
-    )
+    unscaled = kept[0] + last.astype(f32)
     mixed = (unscaled * rescale).astype(bf16)
-    magnitude_half = jnp.sum(upstream * unscaled, axis=0) / norm
+    magnitude_half = jnp.sum(block[: 2 * tokens].astype(f32) * unscaled, axis=0) / norm
 
     def join(own, other, axis):
         return jnp.where(low_core, jnp.concatenate([own, other], axis), jnp.concatenate([other, own], axis))
 
     mixed = join(mixed[:tokens], swap(mixed[tokens:]), 1)
-    up_weight_gradient = join(up_half, swap(up_half), 1)
+    up_weight_gradient = join(up_half, up_other, 1)
     grad_magnitude = join(magnitude_half, swap(magnitude_half), 0)
     return (mixed, hidden_gradient, down_weight_gradient, up_weight_gradient, grad_magnitude)
 

time: 92.4 us -> 98.6 us (1.067)
  Pallas kernels: 37.4 us -> 41.7 us
  waiting for transfers between devices: 22.4 us -> 24.2 us
  matrix products: 1.94 us -> 3.13 us
  local copies, waits for them, and re-layouts: 4.65 us -> 3.5 us
    ppermute x14 -> x12, waiting for transfers between devices: 18.5 us -> 23.8 us  [send(): return lax.ppermute(x, ('tensor', 'dp'), pairs)]
    ppermute x9, waiting for transfers between devices: 3.92 us -> 0.41 us  [split_columns(): swap = lambda x: lax.ppermute(x, 'dp', [(0, 1), (1, 0)])]
    pallas_call x1 -> x2, Pallas kernels: 11.8 us -> 14.6 us  [load(): pl.pallas_call(functools.partial(load_kernel, tokens, rank, n, vs, first)...]
    unnamed x18 -> x14, local copies, waits for them, and re-layouts: 4.39 us -> 3.21 us
    dot_general x2, matrix products: 1.55 us -> 2.73 us  [dot(): return lax.dot_general(a, b, dims, preferred_element_type=f32)]
    pallas_call x1, Pallas kernels: 0.56 us -> 1.74 us  [own_block(): pl.pallas_call(functools.partial(block_kernel, tokens), grid_spec=pltpu.P...]
    ppermute x14 -> x12, starting transfers between devices: 17.5 us -> 17.8 us  [send(): return lax.ppermute(x, ('tensor', 'dp'), pairs)]
    pallas_call x4 -> x3, Pallas kernels: 12.3 us -> 12.6 us  [forward(): pl.pallas_call(functools.partial(forward_kernel, tokens, rank, vs, later...]
  transfers between devices with their start and end apart: 23 -> 21, of which waited for: 8 -> 8; matrix products, arithmetic and copies ran while one was open for 6% -> 7% of each run, Pallas kernels for 41% -> 41%
where the time goes in v7:
time: 98.6 us; the launch traced here: 98.2 us
  Pallas kernels  41.7 us (42%)
  waiting for transfers between devices  24.2 us (25%)
  starting transfers between devices  20.2 us (20%)
  other arithmetic  4.61 us (5%)
  local copies, waits for them, and re-layouts  3.5 us (4%)
  matrix products  3.13 us (3%)
    ppermute x12, waiting for transfers between devices, send(): return lax.ppermute(x, ('tensor', 'dp'), pairs)  23.8 us
    ppermute x12, starting transfers between devices, send(): return lax.ppermute(x, ('tensor', 'dp'), pairs)  17.8 us
    pallas_call x2, Pallas kernels, load(): pl.pallas_call(functools.partial(load_kernel, tokens, rank, n, vs, first)...  14.6 us
    pallas_call x2, Pallas kernels, backward(): pl.pallas_call(functools.partial(backward_kernel, tokens, n, start, band,...  12.7 us
    pallas_call x3, Pallas kernels, forward(): pl.pallas_call(functools.partial(forward_kernel, tokens, rank, vs, later...  12.6 us
    unnamed x14, local copies, waits for them, and re-layouts  3.21 us
    dot_general x2, matrix products, dot(): return lax.dot_general(a, b, dims, preferred_element_type=f32)  2.73 us
    ppermute x9, starting transfers between devices, split_columns(): swap = lambda x: lax.ppermute(x, 'dp', [(0, 1), (1, 0)])  2.38 us
  transfers between devices with their start and end apart: 21, of which 8 were waited for; matrix products, arithmetic and copies ran while one was open for 7% of the time, Pallas kernels for 41%

profile of v7, /device:TPU:0, one launch (start us, length us, event | category | flops | bytes accessed | tf_op | source)
XLA Modules:
  0.0 98.2 jit_solution(18382800119145924021)
XLA Ops:
  0.6 0.5 collective-permute-start
  1.1 0.7 reduce-precision_convert_fusion.1
  1.9 0.1 pad.27.clone
  2.0 0.1 stack.88.order_ref
  2.1 0.1 maximum_maximum_fusion.magnitude_ref
  2.1 0.4 collective-permute-done.other_ref
  2.5 1.2 %copy-done = bf16[64,8192]{1,0:T(8,128)(2,1)S(1)} copy-done((bf16[64,8192]{1,0:T(8,128)(2,1)S(1)}, bf16[64,8192]{1,0:T(8,128)(2,1)}, u32[]{:S(2)}) %copy-start) | copy-done | bytes 1048600
  3.7 1.0 %copy-done.4 = bf16[3584,64]{0,1:T(8,128)(2,1)S(1)} copy-done((bf16[3584,64]{0,1:T(8,128)(2,1)S(1)}, bf16[3584,64]{0,1:T(8,128)(2,1)}, u32[]{:S(2)}) %copy-start.4) | copy-done | bytes 458776
  4.8 0.9 copy-done.6
  5.7 1.7 %own_block.1.refs_0_ = bf16[272,512]{1,0:T(8,128)(2,1)S(1)} custom-call(s32[16]{0:T(128)S(1)} %stack.88.order_ref, bf16[128,1024]{1,0:T(8,128)(2,1)S(1)} %copy-done.6, bf16[128,1024]{1,0:T(8,128)(2,1)S(1)} %collective-permute-done.other_ref, bf16[16,1024]{1,0:T(8,128)(2,1)S(1)} %maximum_maximum_fusion.magnitude_ref, bf16[64,3584]{1,0:T(8,128)(2,1)S(1)} %bitcast.39, ...), custom_call_target="tpu_custom_call" | custom-call | flops 1048576 | bytes 1048576 | tf_op jit(solution)/shard_map/own_block/pallas_call | solution.py:63
  7.5 0.0 copy-start.1
  7.5 0.0 copy-start.5
  7.5 2.9 %collective-permute-start.3 = (bf16[272,512]{1,0:T(8,128)(2,1)S(1)}, bf16[272,512]{1,0:T(8,128)(2,1)S(1)}, u32[]{:S(2)}, u32[]{:S(2)}) collective-permute-start(bf16[272,512]{1,0:T(8,128)(2,1)S(1)} %own_block.1.refs_0_), channel_id=1, source_target_pairs={{0,2},{1,5},{2,0},{3,7},{4,6},{5,1},{6,4},{7,3},{8,10},{9,13},{10,... | collective-permute-start | bytes 835592 | tf_op jit(solution)/shard_map/ppermute | solution.py:250
  10.4 1.6 %collective-permute-start.2 = (bf16[272,512]{1,0:T(8,128)(2,1)S(1)}, bf16[272,512]{1,0:T(8,128)(2,1)S(1)}, u32[]{:S(2)}, u32[]{:S(2)}) collective-permute-start(bf16[272,512]{1,0:T(8,128)(2,1)S(1)} %own_block.1.refs_0_), channel_id=1, source_target_pairs={{0,4},{1,3},{2,6},{3,1},{4,0},{5,7},{6,2},{7,5},{8,12},{9,11},{10,... | collective-permute-start | bytes 835592 | tf_op jit(solution)/shard_map/ppermute | solution.py:250
  12.0 2.6 %collective-permute-start.1 = (bf16[272,512]{1,0:T(8,128)(2,1)S(1)}, bf16[272,512]{1,0:T(8,128)(2,1)S(1)}, u32[]{:S(2)}, u32[]{:S(2)}) collective-permute-start(bf16[272,512]{1,0:T(8,128)(2,1)S(1)} %own_block.1.refs_0_), channel_id=1, source_target_pairs={{0,8},{1,9},{2,10},{3,11},{4,12},{5,13},{6,14},{7,15},{8,0},{9,1},... | collective-permute-start | bytes 835592 | tf_op jit(solution)/shard_map/ppermute | solution.py:250
  14.6 7.6 %load.2 = (bf16[3584,512]{1,0:T(8,128)(2,1)S(1)}, bf16[3584,512]{1,0:T(8,128)(2,1)S(1)}, bf16[3584,512]{1,0:T(8,128)(2,1)S(1)}, bf16[3584,512]{1,0:T(8,128)(2,1)S(1)}, f32[24,512]{1,0:T(8,128)S(1)}) custom-call(s32[16]{0:T(128)S(1)} %stack.88.order_ref, bf16[128,3584]{1,0:T(8,128)(2,1)} %refs_0_.1, bf16[64,3584]{1,0:T(8,128)(2,1)S(1)} %bitcast.40, ...), custom_call_target="tpu_custom_call" | custom-call | flops 1048576 | bytes 1048576 | tf_op jit(solution)/shard_map/load/pallas_call | solution.py:116
  22.2 0.0 collective-permute-done.3.refs_4_
  22.2 0.0 collective-permute-done.2.refs_2_
  22.2 4.9 %collective-permute-done.1.refs_1_ = bf16[272,512]{1,0:T(8,128)(2,1)S(1)} collective-permute-done((bf16[272,512]{1,0:T(8,128)(2,1)S(1)}, bf16[272,512]{1,0:T(8,128)(2,1)S(1)}, u32[]{:S(2)}, u32[]{:S(2)}) %collective-permute-start.1) | collective-permute-done | bytes 278560 | tf_op jit(solution)/shard_map/ppermute | solution.py:250
  27.1 0.1 pad_maximum_fusion.1
  27.1 0.6 collective-permute-start.5
  27.7 0.2 collective-permute-start.4
  27.9 0.0 collective-permute-done.6.refs_1_
  27.9 7.1 %forward.3 = (bf16[4,256,512]{2,1,0:T(8,128)(2,1)S(1)}, bf16[256,3584]{1,0:T(8,128)(2,1)S(1)}, bf16[256,128]{1,0:T(8,128)(2,1)S(1)}) custom-call(s32[16]{0:T(128)S(1)} %stack.88.order_ref, bf16[128,3584]{1,0:T(8,128)(2,1)} %refs_0_.1, bf16[128,3584]{1,0:T(8,128)(2,1)S(1)} %collective-permute-done.6.refs_1_, bf16[64,3584]{1,0:T(8,128)(2,1)S(1)} %bitcast.41, ...), custom_call_target="tpu_custom_call" | custom-call | flops 1048576 | bytes 1048576 | tf_op jit(solution)/shard_map/forward/pallas_call | solution.py:158
  35.1 0.9 collective-permute-done.4.refs_3_
  36.0 1.0 collective-permute-done.5
  37.0 0.8 collective-permute-start.8
  37.8 1.2 %collective-permute-start.7 = (bf16[272,512]{1,0:T(8,128)(2,1)S(1)}, bf16[272,512]{1,0:T(8,128)(2,1)S(1)}, u32[]{:S(2)}, u32[]{:S(2)}) collective-permute-start(bf16[272,512]{1,0:T(8,128)(2,1)S(1)} %collective-permute-done.4.refs_3_), channel_id=1, source_target_pairs={{0,2},{1,5},{2,0},{3,7},{4,6},{5,1},{6,4},{7,3},{8,10},{9,13},{10,... | collective-permute-start | bytes 835592 | tf_op jit(solution)/shard_map/ppermute | solution.py:250
  39.0 6.9 %load.3 = (bf16[3584,512]{1,0:T(8,128)(2,1)S(1)}, bf16[3584,512]{1,0:T(8,128)(2,1)S(1)}, bf16[3584,512]{1,0:T(8,128)(2,1)S(1)}, bf16[3584,512]{1,0:T(8,128)(2,1)S(1)}, f32[24,512]{1,0:T(8,128)S(1)}) custom-call(s32[16]{0:T(128)S(1)} %stack.88.order_ref, f32[24,512]{1,0:T(8,128)S(1)} %get-tuple-element.66.before_ref, bf16[64,3584]{1,0:T(8,128)(2,1)S(1)} %bitcast.42, ...), custom_call_target="tpu_custom_call" | custom-call | flops 1048576 | bytes 1048576 | tf_op jit(solution)/shard_map/load/pallas_call | solution.py:116
  45.9 8.8 %collective-permute-done.7.refs_7_ = bf16[272,512]{1,0:T(8,128)(2,1)S(1)} collective-permute-done((bf16[272,512]{1,0:T(8,128)(2,1)S(1)}, bf16[272,512]{1,0:T(8,128)(2,1)S(1)}, u32[]{:S(2)}, u32[]{:S(2)}) %collective-permute-start.7) | collective-permute-done | bytes 278560 | tf_op jit(solution)/shard_map/ppermute | solution.py:250
  54.7 0.8 collective-permute-start.9
  55.6 2.7 %forward.4 = bf16[2,256,512]{2,1,0:T(8,128)(2,1)S(1)} custom-call(s32[16]{0:T(128)S(1)} %stack.88.order_ref, bf16[256,3584]{1,0:T(8,128)(2,1)S(1)} %get-tuple-element.70.refs_0_, bf16[256,128]{1,0:T(8,128)(2,1)S(1)} %get-tuple-element.71.refs_1_, bf16[64,8192]{1,0:T(8,128)(2,1)S(1)} %copy-done.1, ...), custom_call_target="tpu_custom_call" | custom-call | flops 1048576 | bytes 1048576 | tf_op jit(solution)/shard_map/forward/pallas_call | solution.py:158
  58.3 0.5 collective-permute-done.9
  58.8 0.1 add_convert_fusion.1
  59.0 0.4 collective-permute-start.11
  59.4 1.7 %collective-permute-start.10 = (f32[24,512]{1,0:T(8,128)S(1)}, f32[24,512]{1,0:T(8,128)S(1)}, u32[]{:S(2)}, u32[]{:S(2)}) collective-permute-start(f32[24,512]{1,0:T(8,128)S(1)} %add.73), channel_id=1, source_target_pairs={{0,4},{1,3},{2,6},{3,1},{4,0},{5,7},{6,2},{7,5},{8,12},{9,11},{10,... | collective-permute-start | bytes 147464 | tf_op jit(solution)/shard_map/ppermute | solution.py:250
  61.1 2.7 %forward.5 = bf16[2,256,512]{2,1,0:T(8,128)(2,1)S(1)} custom-call(s32[16]{0:T(128)S(1)} %stack.88.order_ref, bf16[256,3584]{1,0:T(8,128)(2,1)S(1)} %get-tuple-element.70.refs_0_, bf16[256,128]{1,0:T(8,128)(2,1)S(1)} %get-tuple-element.71.refs_1_, bf16[64,8192]{1,0:T(8,128)(2,1)S(1)} %copy-done.1, bf16[3584,512]{1,0:T(8,128)(2,1)S(1)} %get-tuple-element.75.refs_3_.refs_11_, ...), custom_call_target="tpu_custom_call" | custom-call | flops 1048576 | bytes 1048576 | tf_op jit(solution)/shard_map/forward/pallas_call | solution.py:158
  63.9 4.8 %collective-permute-done.10 = f32[24,512]{1,0:T(8,128)S(1)} collective-permute-done((f32[24,512]{1,0:T(8,128)S(1)}, f32[24,512]{1,0:T(8,128)S(1)}, u32[]{:S(2)}, u32[]{:S(2)}) %collective-permute-start.10) | collective-permute-done | bytes 49184 | tf_op jit(solution)/shard_map/ppermute | solution.py:250
  68.8 2.7 %collective-permute-start.12 = (f32[24,512]{1,0:T(8,128)S(1)}, f32[24,512]{1,0:T(8,128)S(1)}, u32[]{:S(2)}, u32[]{:S(2)}) collective-permute-start(f32[24,512]{1,0:T(8,128)S(1)} %add.76), channel_id=1, source_target_pairs={{0,8},{1,9},{2,10},{3,11},{4,12},{5,13},{6,14},{7,15},{8,0},{9,1},... | collective-permute-start | bytes 147464 | tf_op jit(solution)/shard_map/ppermute | solution.py:250
  71.5 2.9 %collective-permute-done.12 = f32[24,512]{1,0:T(8,128)S(1)} collective-permute-done((f32[24,512]{1,0:T(8,128)S(1)}, f32[24,512]{1,0:T(8,128)S(1)}, u32[]{:S(2)}, u32[]{:S(2)}) %collective-permute-start.12) | collective-permute-done | bytes 49184 | tf_op jit(solution)/shard_map/ppermute | solution.py:250
  74.3 0.0 collective-permute-done.11
  74.4 0.1 collective-permute-start.15
  74.4 0.2 convert_add_fusion
  74.7 2.3 %collective-permute-start.17 = (bf16[256,512]{1,0:T(8,128)(2,1)S(1)}, bf16[256,512]{1,0:T(8,128)(2,1)S(1)}, u32[]{:S(2)}, u32[]{:S(2)}) collective-permute-start(bf16[256,512]{1,0:T(8,128)(2,1)S(1)} %fusion.4), channel_id=1, source_target_pairs={{0,8},{1,9},{2,10},{3,11},{4,12},{5,13},{6,14},{7,15},{8,0},{9,1},... | collective-permute-start | bytes 786440 | tf_op jit(solution)/shard_map/ppermute | solution.py:250
  77.0 7.6 %backward.2 = (f32[128,2048]{1,0:T(8,128)S(1)}, bf16[128,2048]{1,0:T(8,128)(2,1)S(1)}, bf16[256,4096]{1,0:T(8,128)(2,1)S(1)}, f32[256,64]{1,0:T(8,128)S(1)}, f32...) custom-call(s32[16]{0:T(128)S(1)} %stack.88.order_ref, bf16[272,512]{1,0:T(8,128)(2,1)S(1)} %own_block.1.refs_0_, ...), custom_call_target="tpu_custom_call" | custom-call | flops 1048576 | bytes 1048576 | tf_op jit(solution)/shard_map/backward/pallas_call | solution.py:223
  84.5 0.3 collective-permute-start.14
  84.8 0.3 collective-permute-start.13
  85.1 0.0 collective-permute-done.15
  85.1 0.2 fusion.5
  85.3 0.2 fusion.2
  85.5 0.3 collective-permute-start.16
  85.8 5.1 %backward.3 = (f32[128,1536]{1,0:T(8,128)S(1)}, bf16[128,1536]{1,0:T(8,128)(2,1)S(1)}) custom-call(s32[16]{0:T(128)S(1)} %stack.88.order_ref, bf16[256,4096]{1,0:T(8,128)(2,1)S(1)} %get-tuple-element.91.refs_0_, f32[256,64]{1,0:T(8,128)S(1)} %get-tuple-element.87.refs_1_, bf16[64,3584]{1,0:T(8,128)(2,1)S(1)} %bitcast.44, ...), custom_call_target="tpu_custom_call" | custom-call | flops 1048576 | bytes 1048576 | tf_op jit(solution)/shard_map/backward/pallas_call | solution.py:223
  91.0 0.2 multiply_reduce_fusion
  91.2 0.4 collective-permute-start.20
  91.6 0.3 collective-permute-start.18
  91.8 0.3 collective-permute-start.19
  92.1 1.5 %fusion.8 = f32[64,3584]{1,0:T(8,128)S(1)} fusion(bf16[128,3584]{1,0:T(8,128)(2,1)} %refs_0_.1, f32[256,64]{1,0:T(8,128)S(1)} %collective-permute-done.14, f32[256,64]{1,0:T(8,128)S(1)} %get-tuple-element.87.refs_1_), kind=kOutput, calls=%fused_computation.26 | convolution fusion | flops 58736640 | bytes 1966080 | tf_op jit(solution)/shard_map/dot_general | solution.py:21
  93.6 0.1 add_convert_fusion
  93.7 1.2 %fusion.1 = f32[3584,64]{0,1:T(8,128)} fusion(f32[64,3584]{1,0:T(8,128)S(1)} %fusion.8, bf16[128,3584]{1,0:T(8,128)(2,1)S(1)} %collective-permute-done.6.refs_1_, f32[256,64]{1,0:T(8,128)S(1)} %collective-permute-done.14, f32[256,64]{1,0:T(8,128)S(1)} %get-tuple-element.87.refs_1_), kind=kOutput, calls=%fused_computation.2 | convolution fusion | flops 59195392 | bytes 2883584 | tf_op jit(solution)/shard_map/dot_general | solution.py:21
  95.0 0.7 maximum_select_fusion.1
  95.7 0.6 maximum_select_fusion.2
  96.3 0.8 maximum_select_fusion
  97.1 0.1 add_convert_fusion.2
  97.2 1.0 %pad_maximum_fusion = bf16[128,3584]{1,0:T(8,128)(2,1)} fusion(bf16[128,1536]{1,0:T(8,128)(2,1)S(1)} %add_convert_fusion.2, bf16[128,2048]{1,0:T(8,128)(2,1)S(1)} %add_convert_fusion), kind=kLoop, calls=%fused_computation.8 | loop fusion | flops 1835008 | bytes 1835008 | tf_op jit(solution)/shard_map/concatenate | solution.py:331
  (33 shorter events, 0.2 us)
Async XLA Ops:
  0.6 1.9 %collective-permute-start = (bf16[128,1024]{1,0:T(8,128)(2,1)}, bf16[128,1024]{1,0:T(8,128)(2,1)S(1)}, u32[]{:S(2)}, u32[]{:S(2)}) collective-permute-start(bf16[128,1024]{1,0:T(8,128)(2,1)} %own_ref.1), channel_id=1, source_target_pairs={{0,1},{1,0},{2,3},{3,2},{4,5},{5,4},{6,7},{7,6},{8,9},{9,8},{10,11... | collective-permute-start | bytes 786440 | tf_op jit(solution)/shard_map/ppermute | solution.py:245
  2.5 1.2 %copy-start = (bf16[64,8192]{1,0:T(8,128)(2,1)S(1)}, bf16[64,8192]{1,0:T(8,128)(2,1)}, u32[]{:S(2)}) copy-start(bf16[64,8192]{1,0:T(8,128)(2,1)} %refs_9_.1) | copy-start | bytes 3145732
  3.7 1.0 %copy-start.4 = (bf16[3584,64]{0,1:T(8,128)(2,1)S(1)}, bf16[3584,64]{0,1:T(8,128)(2,1)}, u32[]{:S(2)}) copy-start(bf16[3584,64]{0,1:T(8,128)(2,1)} %param.8) | copy-start | bytes 1376260
  4.8 0.9 copy-start.6
  7.5 20.4 %copy-start.1 = (bf16[64,8192]{1,0:T(8,128)(2,1)S(1)}, bf16[64,8192]{1,0:T(8,128)(2,1)}, u32[]{:S(2)}) copy-start(bf16[64,8192]{1,0:T(8,128)(2,1)} %refs_9_.1) | copy-start | bytes 3145732
  7.5 20.4 %copy-start.5 = (bf16[3584,64]{0,1:T(8,128)(2,1)S(1)}, bf16[3584,64]{0,1:T(8,128)(2,1)}, u32[]{:S(2)}) copy-start(bf16[3584,64]{0,1:T(8,128)(2,1)} %param.8) | copy-start | bytes 1376260
  7.5 14.7 %collective-permute-start.3 = (bf16[272,512]{1,0:T(8,128)(2,1)S(1)}, bf16[272,512]{1,0:T(8,128)(2,1)S(1)}, u32[]{:S(2)}, u32[]{:S(2)}) collective-permute-start(bf16[272,512]{1,0:T(8,128)(2,1)S(1)} %own_block.1.refs_0_), channel_id=1, source_target_pairs={{0,2},{1,5},{2,0},{3,7},{4,6},{5,1},{6,4},{7,3},{8,10},{9,13},{10,... | collective-permute-start | bytes 835592 | tf_op jit(solution)/shard_map/ppermute | solution.py:250
  10.4 11.8 %collective-permute-start.2 = (bf16[272,512]{1,0:T(8,128)(2,1)S(1)}, bf16[272,512]{1,0:T(8,128)(2,1)S(1)}, u32[]{:S(2)}, u32[]{:S(2)}) collective-permute-start(bf16[272,512]{1,0:T(8,128)(2,1)S(1)} %own_block.1.refs_0_), channel_id=1, source_target_pairs={{0,4},{1,3},{2,6},{3,1},{4,0},{5,7},{6,2},{7,5},{8,12},{9,11},{10,... | collective-permute-start | bytes 835592 | tf_op jit(solution)/shard_map/ppermute | solution.py:250
  12.0 15.1 %collective-permute-start.1 = (bf16[272,512]{1,0:T(8,128)(2,1)S(1)}, bf16[272,512]{1,0:T(8,128)(2,1)S(1)}, u32[]{:S(2)}, u32[]{:S(2)}) collective-permute-start(bf16[272,512]{1,0:T(8,128)(2,1)S(1)} %own_block.1.refs_0_), channel_id=1, source_target_pairs={{0,8},{1,9},{2,10},{3,11},{4,12},{5,13},{6,14},{7,15},{8,0},{9,1},... | collective-permute-start | bytes 835592 | tf_op jit(solution)/shard_map/ppermute | solution.py:250
  14.6 13.3 %collective-permute-start.6 = (bf16[128,3584]{1,0:T(8,128)(2,1)}, bf16[128,3584]{1,0:T(8,128)(2,1)S(1)}, u32[]{:S(2)}, u32[]{:S(2)}) collective-permute-start(bf16[128,3584]{1,0:T(8,128)(2,1)} %refs_0_.1), channel_id=1, source_target_pairs={{0,1},{1,0},{2,3},{3,2},{4,5},{5,4},{6,7},{7,6},{8,9},{9,8},{10,11... | collective-permute-start | bytes 2752520 | tf_op jit(solution)/shard_map/ppermute | solution.py:245
  27.1 9.8 %collective-permute-start.5 = (bf16[2,272,512]{2,1,0:T(8,128)(2,1)S(1)}, bf16[2,272,512]{2,1,0:T(8,128)(2,1)S(1)}, u32[]{:S(2)}, u32[]{:S(2)}) collective-permute-start(bf16[2,272,512]{2,1,0:T(8,128)(2,1)S(1)} %pad_maximum_fusion.1), channel_id=1, source_target_pairs={{0,2},{1,5},{2,0},{3,7},{4,6},{5,1},{6,4},{7,3},{8,10},{9,13},{10,... | collective-permute-start | bytes 1671176 | tf_op jit(solution)/shard_map/ppermute | solution.py:250
  27.7 8.3 %collective-permute-start.4 = (bf16[272,512]{1,0:T(8,128)(2,1)S(1)}, bf16[272,512]{1,0:T(8,128)(2,1)S(1)}, u32[]{:S(2)}, u32[]{:S(2)}) collective-permute-start(bf16[272,512]{1,0:T(8,128)(2,1)S(1)} %collective-permute-done.1.refs_1_), channel_id=1, source_target_pairs={{0,4},{1,3},{2,6},{3,1},{4,0},{5,7},{6,2},{7,5},{8,12},{9,11},{10,... | collective-permute-start | bytes 835592 | tf_op jit(solution)/shard_map/ppermute | solution.py:250
  37.0 21.9 %collective-permute-start.8 = (bf16[4,256,512]{2,1,0:T(8,128)(2,1)S(1)}, bf16[4,256,512]{2,1,0:T(8,128)(2,1)S(1)}, u32[]{:S(2)}, u32[]{:S(2)}) collective-permute-start(bf16[4,256,512]{2,1,0:T(8,128)(2,1)S(1)} %get-tuple-element.69), channel_id=1, source_target_pairs={{0,2},{1,5},{2,0},{3,7},{4,6},{5,1},{6,4},{7,3},{8,10},{9,13},{10,... | collective-permute-start | bytes 3145736 | tf_op jit(solution)/shard_map/ppermute | solution.py:250
  37.8 16.9 %collective-permute-start.7 = (bf16[272,512]{1,0:T(8,128)(2,1)S(1)}, bf16[272,512]{1,0:T(8,128)(2,1)S(1)}, u32[]{:S(2)}, u32[]{:S(2)}) collective-permute-start(bf16[272,512]{1,0:T(8,128)(2,1)S(1)} %collective-permute-done.4.refs_3_), channel_id=1, source_target_pairs={{0,2},{1,5},{2,0},{3,7},{4,6},{5,1},{6,4},{7,3},{8,10},{9,13},{10,... | collective-permute-start | bytes 835592 | tf_op jit(solution)/shard_map/ppermute | solution.py:250
  45.9 12.4 %copy-start.2 = (bf16[3584,512]{1,0:T(8,128)(2,1)}, bf16[3584,512]{1,0:T(8,128)(2,1)S(1)}, u32[]{:S(2)}) copy-start(bf16[3584,512]{1,0:T(8,128)(2,1)S(1)} %get-tuple-element.72.refs_3_.refs_13_.refs_5_) | copy-start | bytes 11010052
  54.7 4.1 %collective-permute-start.9 = (f32[24,512]{1,0:T(8,128)S(1)}, f32[24,512]{1,0:T(8,128)S(1)}, u32[]{:S(2)}, u32[]{:S(2)}) collective-permute-start(f32[24,512]{1,0:T(8,128)S(1)} %get-tuple-element.68), channel_id=1, source_target_pairs={{0,2},{1,5},{2,0},{3,7},{4,6},{5,1},{6,4},{7,3},{8,10},{9,13},{10,... | collective-permute-start | bytes 147464 | tf_op jit(solution)/shard_map/ppermute | solution.py:250
  59.0 15.4 %collective-permute-start.11 = (bf16[2,256,512]{2,1,0:T(8,128)(2,1)S(1)}, bf16[2,256,512]{2,1,0:T(8,128)(2,1)S(1)}, u32[]{:S(2)}, u32[]{:S(2)}) collective-permute-start(bf16[2,256,512]{2,1,0:T(8,128)(2,1)S(1)} %add_convert_fusion.1), channel_id=1, source_target_pairs={{0,4},{1,3},{2,6},{3,1},{4,0},{5,7},{6,2},{7,5},{8,12},{9,11},{10,... | collective-permute-start | bytes 1572872 | tf_op jit(solution)/shard_map/ppermute | solution.py:250
  59.4 9.3 %collective-permute-start.10 = (f32[24,512]{1,0:T(8,128)S(1)}, f32[24,512]{1,0:T(8,128)S(1)}, u32[]{:S(2)}, u32[]{:S(2)}) collective-permute-start(f32[24,512]{1,0:T(8,128)S(1)} %add.73), channel_id=1, source_target_pairs={{0,4},{1,3},{2,6},{3,1},{4,0},{5,7},{6,2},{7,5},{8,12},{9,11},{10,... | collective-permute-start | bytes 147464 | tf_op jit(solution)/shard_map/ppermute | solution.py:250
  63.9 13.1 %copy-start.3 = (bf16[3584,512]{1,0:T(8,128)(2,1)S(1)}, bf16[3584,512]{1,0:T(8,128)(2,1)}, u32[]{:S(2)}) copy-start(bf16[3584,512]{1,0:T(8,128)(2,1)} %copy-done.2) | copy-start | bytes 11010052
  68.8 5.6 %collective-permute-start.12 = (f32[24,512]{1,0:T(8,128)S(1)}, f32[24,512]{1,0:T(8,128)S(1)}, u32[]{:S(2)}, u32[]{:S(2)}) collective-permute-start(f32[24,512]{1,0:T(8,128)S(1)} %add.76), channel_id=1, source_target_pairs={{0,8},{1,9},{2,10},{3,11},{4,12},{5,13},{6,14},{7,15},{8,0},{9,1},... | collective-permute-start | bytes 147464 | tf_op jit(solution)/shard_map/ppermute | solution.py:250
  74.4 10.8 %collective-permute-start.15 = (f32[16,512]{1,0:T(8,128)S(1)}, f32[16,512]{1,0:T(8,128)S(1)}, u32[]{:S(2)}, u32[]{:S(2)}) collective-permute-start(f32[16,512]{1,0:T(8,128)S(1)} %slice.114), channel_id=1, source_target_pairs={{0,1},{1,0},{2,3},{3,2},{4,5},{5,4},{6,7},{7,6},{8,9},{9,8},{10,11... | collective-permute-start | bytes 98312 | tf_op jit(solution)/shard_map/ppermute | solution.py:245
  74.7 16.3 %collective-permute-start.17 = (bf16[256,512]{1,0:T(8,128)(2,1)S(1)}, bf16[256,512]{1,0:T(8,128)(2,1)S(1)}, u32[]{:S(2)}, u32[]{:S(2)}) collective-permute-start(bf16[256,512]{1,0:T(8,128)(2,1)S(1)} %fusion.4), channel_id=1, source_target_pairs={{0,8},{1,9},{2,10},{3,11},{4,12},{5,13},{6,14},{7,15},{8,0},{9,1},... | collective-permute-start | bytes 786440 | tf_op jit(solution)/shard_map/ppermute | solution.py:250
  84.5 6.4 %collective-permute-start.14 = (f32[256,64]{1,0:T(8,128)S(1)}, f32[256,64]{1,0:T(8,128)S(1)}, u32[]{:S(2)}, u32[]{:S(2)}) collective-permute-start(f32[256,64]{1,0:T(8,128)S(1)} %get-tuple-element.87.refs_1_), channel_id=1, source_target_pairs={{0,1},{1,0},{2,3},{3,2},{4,5},{5,4},{6,7},{7,6},{8,9},{9,8},{10,11... | collective-permute-start | bytes 196616 | tf_op jit(solution)/shard_map/ppermute | solution.py:245
  84.8 6.2 %collective-permute-start.13 = (bf16[128,2048]{1,0:T(8,128)(2,1)S(1)}, bf16[128,2048]{1,0:T(8,128)(2,1)S(1)}, u32[]{:S(2)}, u32[]{:S(2)}) collective-permute-start(bf16[128,2048]{1,0:T(8,128)(2,1)S(1)} %get-tuple-element.86), channel_id=1, source_target_pairs={{0,1},{1,0},{2,3},{3,2},{4,5},{5,4},{6,7},{7,6},{8,9},{9,8},{10,11... | collective-permute-start | bytes 1572872 | tf_op jit(solution)/shard_map/ppermute | solution.py:245
  85.5 5.4 %collective-permute-start.16 = (f32[64,512]{1,0:T(8,128)S(1)}, f32[64,512]{1,0:T(8,128)S(1)}, u32[]{:S(2)}, u32[]{:S(2)}) collective-permute-start(f32[64,512]{1,0:T(8,128)S(1)} %fusion.2), channel_id=1, source_target_pairs={{0,1},{1,0},{2,3},{3,2},{4,5},{5,4},{6,7},{7,6},{8,9},{9,8},{10,11... | collective-permute-start | bytes 393224 | tf_op jit(solution)/shard_map/ppermute | solution.py:245
  91.2 4.5 %collective-permute-start.20 = (f32[512]{0:T(512)S(1)}, f32[512]{0:T(512)S(1)}, u32[]{:S(2)}, u32[]{:S(2)}) collective-permute-start(f32[512]{0:T(512)S(1)} %div.3), channel_id=1, source_target_pairs={{0,1},{1,0},{2,3},{3,2},{4,5},{5,4},{6,7},{7,6},{8,9},{9,8},{10,11... | collective-permute-start | bytes 6152 | tf_op jit(solution)/shard_map/ppermute | solution.py:245
  91.6 4.8 %collective-permute-start.18 = (bf16[128,512]{1,0:T(8,128)(2,1)S(1)}, bf16[128,512]{1,0:T(8,128)(2,1)S(1)}, u32[]{:S(2)}, u32[]{:S(2)}) collective-permute-start(bf16[128,512]{1,0:T(8,128)(2,1)S(1)} %get-tuple-element.106), channel_id=1, source_target_pairs={{0,1},{1,0},{2,3},{3,2},{4,5},{5,4},{6,7},{7,6},{8,9},{9,8},{10,11... | collective-permute-start | bytes 393224 | tf_op jit(solution)/shard_map/ppermute | solution.py:245
  91.8 5.3 %collective-permute-start.19 = (bf16[128,1536]{1,0:T(8,128)(2,1)S(1)}, bf16[128,1536]{1,0:T(8,128)(2,1)S(1)}, u32[]{:S(2)}, u32[]{:S(2)}) collective-permute-start(bf16[128,1536]{1,0:T(8,128)(2,1)S(1)} %get-tuple-element.98), channel_id=1, source_target_pairs={{0,1},{1,0},{2,3},{3,2},{4,5},{5,4},{6,7},{7,6},{8,9},{9,8},{10,11... | collective-permute-start | bytes 1179656 | tf_op jit(solution)/shard_map/ppermute | solution.py:245

commit v8 on v7

--- a/solution.py
+++ b/solution.py
@@ -243,7 +243,7 @@
     rows = weight.shape[0]
     me, core = lax.axis_index("tensor"), lax.axis_index("dp")
     swap = lambda x: lax.ppermute(x, "dp", [(0, 1), (1, 0)])
-    orders = [[1, 2, 4], [2, 1, 4]]
+    orders = [[1, 2, 4], [2, 4, 1]]
 
     def send(x, k):
         pairs = [(2 * t + c, 2 * (t ^ orders[c][k]) + c) for t in range(n) for c in range(2)]
@@ -276,44 +276,46 @@
 
     run_load = functools.partial(load, at=at, up=up, weight=weight, half=half)
     *far, stats = run_load((0b100, 0b101, 0b110, 0b111), order, own=hidden)
-    *arrived, stats = tie((*(cots[v] for v in (0b001, 0b010, 0b100)), stats))
-    cots[0b001], cots[0b010], cots[0b100] = arrived
+    cots[0b100], cots[0b010], cots[0b001], stats = tie((cots[0b100], cots[0b010], cots[0b001], stats))
     cots[0b011] = send(cots[0b001], 1)
     pair = send(jnp.stack([cots[0b001], cots[0b010]]), 0)
-    sent, lhs, adapter = forward((0b100, 0b101, 0b110, 0b111), order, far, up, first=(hidden, hidden_other, at))
-    run = lambda vs, held: forward(vs, order, held, up, later=(lhs, adapter))[0]
-    cots[0b011], pair, order_after, sent = tie((cots[0b011], pair, order, sent))
+    *near, stats = run_load((0b000, 0b001, 0b010, 0b011), order, before=stats)
+    cots[0b011], stats = tie((cots[0b011], stats))
+    got = send(stats, 0)
+    cots[0b111] = send(cots[0b011], 0)
+    far1, lhs, adapter = forward((0b110, 0b111), order, far[2:], up, first=(hidden, hidden_other, at))
+    run = lambda order, vs, held: forward(vs, order, held, up, later=(lhs, adapter))[0]
+    got, pair, cots[0b111], far1, order = tie((got, pair, cots[0b111], far1, order))
     cots[0b101], cots[0b110] = pair[0], pair[1]
-    from_far = send(sent, 0)
-    cots[0b111] = send(cots[0b011], 0)
-    *near, stats = run_load((0b000, 0b001, 0b010, 0b011), order_after, before=stats)
-    cots[0b111], stats = tie((cots[0b111], stats))
-    got = send(stats, 0)
-    near1 = run((0b010, 0b011), near[2:])
-    from_far, got, near1 = tie((from_far, got, near1))
     stats = stats + got
     got = send(stats, 1)
-    arrived = send((near1.astype(f32) + from_far[2:].astype(f32)).astype(bf16), 1)
-    near0 = run((0b000, 0b001), near[:2])
-    got, near0 = tie((got, near0))
+    from1 = send(far1, 0)
+    far0 = run(order, (0b100, 0b101), far[:2])
+    got, far0, order = tie((got, far0, order))
     stats = stats + got
     got = send(stats, 2)
-    arrived, got = tie((arrived, got))
+    from0 = send(far0, 0)
+    near1 = run(order, (0b010, 0b011), near[2:])
+    got, from1, near1, order = tie((got, from1, near1, order))
     stats = stats + got
-    kept = near0.astype(f32) + from_far[:2].astype(f32) + arrived.astype(f32)
-    last = send(kept[1].astype(bf16), 2)
+    arrived = send((near1.astype(f32) + from1.astype(f32)).astype(bf16), 1)
     lowrank_rows = stats[n:]
     lowrank_other = swap(lowrank_rows)
+    near0 = run(order, (0b000, 0b001), near[:2])
+    from0, lowrank_other, near0, order = tie((from0, lowrank_other, near0, order))
+    kept = near0.astype(f32) + from0.astype(f32)
     held = near + far
 
     band = 256
     bands = rows // band
-    many = (bands + 2) // 2
+    many = bands // 2
     run = functools.partial(backward, order, band=band, at=at, held=held)
     grad_a, other_a, scaled, proj, scales, scaled_own = run(0, many, first=([cots[v] for v in range(n)], stats, up))
     got_a = swap(other_a)
     from_sibling = swap(proj)
-    lowrank_other, scaled_own = tie((lowrank_other, scaled_own))
+    arrived, scaled_own = tie((arrived, scaled_own))
+    kept = kept + arrived.astype(f32)
+    last = send(kept[1].astype(bf16), 2)
     scaled_own = scaled_own.astype(f32)
 
     def turned(part):

time: 98.6 us -> 92.4 us (0.937)
  waiting for transfers between devices: 24.2 us -> 9.17 us
  starting transfers between devices: 20.2 us -> 28.5 us
    ppermute x12 -> x13, waiting for transfers between devices: 23.8 us -> 8.76 us  [send(): return lax.ppermute(x, ('tensor', 'dp'), pairs)]
    ppermute x9, starting transfers between devices: 2.38 us -> 10.7 us  [split_columns(): swap = lambda x: lax.ppermute(x, 'dp', [(0, 1), (1, 0)])]
    pallas_call x3 -> x4, Pallas kernels: 12.6 us -> 13 us  [forward(): pl.pallas_call(functools.partial(forward_kernel, tokens, rank, vs, later...]
    ppermute x12 -> x13, starting transfers between devices: 17.8 us -> 17.7 us  [send(): return lax.ppermute(x, ('tensor', 'dp'), pairs)]
  transfers between devices with their start and end apart: 21 -> 22, of which waited for: 8 -> 7; matrix products, arithmetic and copies ran while one was open for 7% -> 7% of each run, Pallas kernels for 41% -> 44%
where the time goes in v8:
time: 92.4 us; the launch traced here: 91.9 us
  Pallas kernels  42.1 us (46%)
  starting transfers between devices  28.5 us (31%)
  waiting for transfers between devices  9.17 us (10%)
  other arithmetic  4.62 us (5%)
  local copies, waits for them, and re-layouts  3.5 us (4%)
  matrix products  3.14 us (3%)
  between operations  0.94 us (1%)
    ppermute x13, starting transfers between devices, send(): return lax.ppermute(x, ('tensor', 'dp'), pairs)  17.7 us
    pallas_call x2, Pallas kernels, load(): pl.pallas_call(functools.partial(load_kernel, tokens, rank, n, vs, first)...  14.6 us
    pallas_call x4, Pallas kernels, forward(): pl.pallas_call(functools.partial(forward_kernel, tokens, rank, vs, later...  13 us
    pallas_call x2, Pallas kernels, backward(): pl.pallas_call(functools.partial(backward_kernel, tokens, n, start, band,...  12.8 us
    ppermute x9, starting transfers between devices, split_columns(): swap = lambda x: lax.ppermute(x, 'dp', [(0, 1), (1, 0)])  10.7 us
    ppermute x13, waiting for transfers between devices, send(): return lax.ppermute(x, ('tensor', 'dp'), pairs)  8.76 us
    unnamed x14, local copies, waits for them, and re-layouts  3.21 us
    dot_general x2, matrix products, dot(): return lax.dot_general(a, b, dims, preferred_element_type=f32)  2.74 us
  transfers between devices with their start and end apart: 22, of which 7 were waited for; matrix products, arithmetic and copies ran while one was open for 7% of the time, Pallas kernels for 44%

profile of v8, /device:TPU:0, one launch (start us, length us, event | category | flops | bytes accessed | tf_op | source)
XLA Modules:
  0.0 91.9 jit_solution(816194250831525892)
XLA Ops:
  0.6 0.5 collective-permute-start
  1.1 0.7 reduce-precision_convert_fusion.1
  1.9 0.1 pad.27.clone
  2.0 0.1 stack.88.order_ref
  2.1 0.1 maximum_maximum_fusion.magnitude_ref
  2.1 0.4 collective-permute-done.other_ref
  2.5 1.2 %copy-done = bf16[64,8192]{1,0:T(8,128)(2,1)S(1)} copy-done((bf16[64,8192]{1,0:T(8,128)(2,1)S(1)}, bf16[64,8192]{1,0:T(8,128)(2,1)}, u32[]{:S(2)}) %copy-start) | copy-done | bytes 1048600
  3.7 1.0 %copy-done.4 = bf16[3584,64]{0,1:T(8,128)(2,1)S(1)} copy-done((bf16[3584,64]{0,1:T(8,128)(2,1)S(1)}, bf16[3584,64]{0,1:T(8,128)(2,1)}, u32[]{:S(2)}) %copy-start.4) | copy-done | bytes 458776
  4.8 0.9 %copy-done.6 = bf16[128,1024]{1,0:T(8,128)(2,1)S(1)} copy-done((bf16[128,1024]{1,0:T(8,128)(2,1)S(1)}, bf16[128,1024]{1,0:T(8,128)(2,1)}, u32[]{:S(2)}) %copy-start.6) | copy-done | bytes 262168
  5.7 1.7 %own_block.1.refs_0_ = bf16[272,512]{1,0:T(8,128)(2,1)S(1)} custom-call(s32[16]{0:T(128)S(1)} %stack.88.order_ref, bf16[128,1024]{1,0:T(8,128)(2,1)S(1)} %copy-done.6, bf16[128,1024]{1,0:T(8,128)(2,1)S(1)} %collective-permute-done.other_ref, bf16[16,1024]{1,0:T(8,128)(2,1)S(1)} %maximum_maximum_fusion.magnitude_ref, bf16[64,3584]{1,0:T(8,128)(2,1)S(1)} %bitcast.39, ...), custom_call_target="tpu_custom_call" | custom-call | flops 1048576 | bytes 1048576 | tf_op jit(solution)/shard_map/own_block/pallas_call | solution.py:63
  7.5 0.0 copy-start.1
  7.5 0.0 copy-start.5
  7.5 4.0 %collective-permute-start.3 = (bf16[272,512]{1,0:T(8,128)(2,1)S(1)}, bf16[272,512]{1,0:T(8,128)(2,1)S(1)}, u32[]{:S(2)}, u32[]{:S(2)}) collective-permute-start(bf16[272,512]{1,0:T(8,128)(2,1)S(1)} %own_block.1.refs_0_), channel_id=1, source_target_pairs={{0,8},{1,3},{2,10},{3,1},{4,12},{5,7},{6,14},{7,5},{8,0},{9,11},{1... | collective-permute-start | bytes 835592 | tf_op jit(solution)/shard_map/ppermute | solution.py:250
  11.5 1.6 %collective-permute-start.2 = (bf16[272,512]{1,0:T(8,128)(2,1)S(1)}, bf16[272,512]{1,0:T(8,128)(2,1)S(1)}, u32[]{:S(2)}, u32[]{:S(2)}) collective-permute-start(bf16[272,512]{1,0:T(8,128)(2,1)S(1)} %own_block.1.refs_0_), channel_id=1, source_target_pairs={{0,4},{1,9},{2,6},{3,11},{4,0},{5,13},{6,2},{7,15},{8,12},{9,1},{1... | collective-permute-start | bytes 835592 | tf_op jit(solution)/shard_map/ppermute | solution.py:250
  13.1 1.5 %collective-permute-start.1 = (bf16[272,512]{1,0:T(8,128)(2,1)S(1)}, bf16[272,512]{1,0:T(8,128)(2,1)S(1)}, u32[]{:S(2)}, u32[]{:S(2)}) collective-permute-start(bf16[272,512]{1,0:T(8,128)(2,1)S(1)} %own_block.1.refs_0_), channel_id=1, source_target_pairs={{0,2},{1,5},{2,0},{3,7},{4,6},{5,1},{6,4},{7,3},{8,10},{9,13},{10,... | collective-permute-start | bytes 835592 | tf_op jit(solution)/shard_map/ppermute | solution.py:250
  14.6 0.0 collective-permute-start.8
  14.6 7.6 %load.2 = (bf16[3584,512]{1,0:T(8,128)(2,1)S(1)}, bf16[3584,512]{1,0:T(8,128)(2,1)S(1)}, bf16[3584,512]{1,0:T(8,128)(2,1)S(1)}, bf16[3584,512]{1,0:T(8,128)(2,1)S(1)}, f32[24,512]{1,0:T(8,128)S(1)}) custom-call(s32[16]{0:T(128)S(1)} %stack.88.order_ref, bf16[128,3584]{1,0:T(8,128)(2,1)} %refs_0_.1, bf16[64,3584]{1,0:T(8,128)(2,1)S(1)} %bitcast.40, ...), custom_call_target="tpu_custom_call" | custom-call | flops 1048576 | bytes 1048576 | tf_op jit(solution)/shard_map/load/pallas_call | solution.py:116
  22.2 2.2 %collective-permute-done.3.refs_1_ = bf16[272,512]{1,0:T(8,128)(2,1)S(1)} collective-permute-done((bf16[272,512]{1,0:T(8,128)(2,1)S(1)}, bf16[272,512]{1,0:T(8,128)(2,1)S(1)}, u32[]{:S(2)}, u32[]{:S(2)}) %collective-permute-start.3) | collective-permute-done | bytes 278560 | tf_op jit(solution)/shard_map/ppermute | solution.py:250
  24.4 1.0 %collective-permute-done.2.refs_2_ = bf16[272,512]{1,0:T(8,128)(2,1)S(1)} collective-permute-done((bf16[272,512]{1,0:T(8,128)(2,1)S(1)}, bf16[272,512]{1,0:T(8,128)(2,1)S(1)}, u32[]{:S(2)}, u32[]{:S(2)}) %collective-permute-start.2) | collective-permute-done | bytes 278560 | tf_op jit(solution)/shard_map/ppermute | solution.py:250
  25.5 1.3 %collective-permute-start.4 = (bf16[272,512]{1,0:T(8,128)(2,1)S(1)}, bf16[272,512]{1,0:T(8,128)(2,1)S(1)}, u32[]{:S(2)}, u32[]{:S(2)}) collective-permute-start(bf16[272,512]{1,0:T(8,128)(2,1)S(1)} %collective-permute-done.3.refs_1_), channel_id=1, source_target_pairs={{0,4},{1,9},{2,6},{3,11},{4,0},{5,13},{6,2},{7,15},{8,12},{9,1},{1... | collective-permute-start | bytes 835592 | tf_op jit(solution)/shard_map/ppermute | solution.py:250
  26.8 0.1 pad_maximum_fusion.1
  26.8 1.3 %collective-permute-start.6 = (bf16[2,272,512]{2,1,0:T(8,128)(2,1)S(1)}, bf16[2,272,512]{2,1,0:T(8,128)(2,1)S(1)}, u32[]{:S(2)}, u32[]{:S(2)}) collective-permute-start(bf16[2,272,512]{2,1,0:T(8,128)(2,1)S(1)} %pad_maximum_fusion.1), channel_id=1, source_target_pairs={{0,2},{1,5},{2,0},{3,7},{4,6},{5,1},{6,4},{7,3},{8,10},{9,13},{10,... | collective-permute-start | bytes 1671176 | tf_op jit(solution)/shard_map/ppermute | solution.py:250
  28.1 6.9 %load.3 = (bf16[3584,512]{1,0:T(8,128)(2,1)S(1)}, bf16[3584,512]{1,0:T(8,128)(2,1)S(1)}, bf16[3584,512]{1,0:T(8,128)(2,1)S(1)}, bf16[3584,512]{1,0:T(8,128)(2,1)S(1)}, f32[24,512]{1,0:T(8,128)S(1)}) custom-call(s32[16]{0:T(128)S(1)} %stack.88.order_ref, f32[24,512]{1,0:T(8,128)S(1)} %get-tuple-element.63.before_ref, bf16[64,3584]{1,0:T(8,128)(2,1)S(1)} %bitcast.41, ...), custom_call_target="tpu_custom_call" | custom-call | flops 1048576 | bytes 1048576 | tf_op jit(solution)/shard_map/load/pallas_call | solution.py:116
  35.1 2.6 %collective-permute-done.4.refs_3_ = bf16[272,512]{1,0:T(8,128)(2,1)S(1)} collective-permute-done((bf16[272,512]{1,0:T(8,128)(2,1)S(1)}, bf16[272,512]{1,0:T(8,128)(2,1)S(1)}, u32[]{:S(2)}, u32[]{:S(2)}) %collective-permute-start.4) | collective-permute-done | bytes 278560 | tf_op jit(solution)/shard_map/ppermute | solution.py:250
  37.7 0.2 collective-permute-start.7
  37.9 1.8 %collective-permute-start.5 = (f32[24,512]{1,0:T(8,128)S(1)}, f32[24,512]{1,0:T(8,128)S(1)}, u32[]{:S(2)}, u32[]{:S(2)}) collective-permute-start(f32[24,512]{1,0:T(8,128)S(1)} %get-tuple-element.65), channel_id=1, source_target_pairs={{0,2},{1,5},{2,0},{3,7},{4,6},{5,1},{6,4},{7,3},{8,10},{9,13},{10,... | collective-permute-start | bytes 147464 | tf_op jit(solution)/shard_map/ppermute | solution.py:250
  39.7 0.0 collective-permute-done.8.refs_1_
  39.7 4.8 %forward.4 = (bf16[2,256,512]{2,1,0:T(8,128)(2,1)S(1)}, bf16[256,3584]{1,0:T(8,128)(2,1)S(1)}, bf16[256,128]{1,0:T(8,128)(2,1)S(1)}) custom-call(s32[16]{0:T(128)S(1)} %stack.88.order_ref, bf16[128,3584]{1,0:T(8,128)(2,1)} %refs_0_.1, bf16[128,3584]{1,0:T(8,128)(2,1)S(1)} %collective-permute-done.8.refs_1_, bf16[64,3584]{1,0:T(8,128)(2,1)S(1)} %bitcast.42, ...), custom_call_target="tpu_custom_call" | custom-call | flops 1048576 | bytes 1048576 | tf_op jit(solution)/shard_map/forward/pallas_call | solution.py:158
  44.5 0.2 collective-permute-done.5
  44.8 0.0 collective-permute-done.6
  44.8 0.0 collective-permute-done.7.refs_7_
  44.8 0.2 collective-permute-start.12
  45.0 0.1 collective-permute-start.9
  45.1 2.8 %forward.5 = bf16[2,256,512]{2,1,0:T(8,128)(2,1)S(1)} custom-call(s32[16]{0:T(128)S(1)} %stack.88.order_ref, bf16[256,3584]{1,0:T(8,128)(2,1)S(1)} %get-tuple-element.73.refs_0_, bf16[256,128]{1,0:T(8,128)(2,1)S(1)} %get-tuple-element.74.refs_1_, bf16[64,8192]{1,0:T(8,128)(2,1)S(1)} %copy-done.1, ...), custom_call_target="tpu_custom_call" | custom-call | flops 1048576 | bytes 1048576 | tf_op jit(solution)/shard_map/forward/pallas_call | solution.py:158
  47.8 2.4 %collective-permute-done.9 = f32[24,512]{1,0:T(8,128)S(1)} collective-permute-done((f32[24,512]{1,0:T(8,128)S(1)}, f32[24,512]{1,0:T(8,128)S(1)}, u32[]{:S(2)}, u32[]{:S(2)}) %collective-permute-start.9) | collective-permute-done | bytes 49184 | tf_op jit(solution)/shard_map/ppermute | solution.py:250
  50.2 2.6 %collective-permute-start.11 = (f32[24,512]{1,0:T(8,128)S(1)}, f32[24,512]{1,0:T(8,128)S(1)}, u32[]{:S(2)}, u32[]{:S(2)}) collective-permute-start(f32[24,512]{1,0:T(8,128)S(1)} %add.74), channel_id=1, source_target_pairs={{0,8},{1,3},{2,10},{3,1},{4,12},{5,7},{6,14},{7,5},{8,0},{9,11},{1... | collective-permute-start | bytes 147464 | tf_op jit(solution)/shard_map/ppermute | solution.py:250
  52.8 1.1 %collective-permute-start.10 = (bf16[2,256,512]{2,1,0:T(8,128)(2,1)S(1)}, bf16[2,256,512]{2,1,0:T(8,128)(2,1)S(1)}, u32[]{:S(2)}, u32[]{:S(2)}) collective-permute-start(bf16[2,256,512]{2,1,0:T(8,128)(2,1)S(1)} %forward.5), channel_id=1, source_target_pairs={{0,2},{1,5},{2,0},{3,7},{4,6},{5,1},{6,4},{7,3},{8,10},{9,13},{10,... | collective-permute-start | bytes 1572872 | tf_op jit(solution)/shard_map/ppermute | solution.py:250
  53.8 2.7 %forward.6 = bf16[2,256,512]{2,1,0:T(8,128)(2,1)S(1)} custom-call(s32[16]{0:T(128)S(1)} %stack.88.order_ref, bf16[256,3584]{1,0:T(8,128)(2,1)S(1)} %get-tuple-element.73.refs_0_, bf16[256,128]{1,0:T(8,128)(2,1)S(1)} %get-tuple-element.74.refs_1_, bf16[64,8192]{1,0:T(8,128)(2,1)S(1)} %copy-done.1, ...), custom_call_target="tpu_custom_call" | custom-call | flops 1048576 | bytes 1048576 | tf_op jit(solution)/shard_map/forward/pallas_call | solution.py:158
  56.6 0.1 add_convert_fusion
  56.8 2.0 %collective-permute-start.14 = (bf16[2,256,512]{2,1,0:T(8,128)(2,1)S(1)}, bf16[2,256,512]{2,1,0:T(8,128)(2,1)S(1)}, u32[]{:S(2)}, u32[]{:S(2)}) collective-permute-start(bf16[2,256,512]{2,1,0:T(8,128)(2,1)S(1)} %add_convert_fusion), channel_id=1, source_target_pairs={{0,4},{1,9},{2,6},{3,11},{4,0},{5,13},{6,2},{7,15},{8,12},{9,1},{1... | collective-permute-start | bytes 1572872 | tf_op jit(solution)/shard_map/ppermute | solution.py:250
  58.8 0.1 collective-permute-start.13
  58.9 2.8 %forward.7 = bf16[2,256,512]{2,1,0:T(8,128)(2,1)S(1)} custom-call(s32[16]{0:T(128)S(1)} %stack.88.order_ref, bf16[256,3584]{1,0:T(8,128)(2,1)S(1)} %get-tuple-element.73.refs_0_, bf16[256,128]{1,0:T(8,128)(2,1)S(1)} %get-tuple-element.74.refs_1_, bf16[64,8192]{1,0:T(8,128)(2,1)S(1)} %copy-done.1, bf16[3584,512]{1,0:T(8,128)(2,1)S(1)} %get-tuple-element.85.refs_3_.refs_11_, ...), custom_call_target="tpu_custom_call" | custom-call | flops 1048576 | bytes 1048576 | tf_op jit(solution)/shard_map/forward/pallas_call | solution.py:158
  61.7 0.3 collective-permute-done.10
  62.0 6.8 %backward.2 = (f32[128,1792]{1,0:T(8,128)S(1)}, bf16[128,1792]{1,0:T(8,128)(2,1)S(1)}, bf16[256,4096]{1,0:T(8,128)(2,1)S(1)}, f32[256,64]{1,0:T(8,128)S(1)}, f32...) custom-call(s32[16]{0:T(128)S(1)} %stack.88.order_ref, bf16[272,512]{1,0:T(8,128)(2,1)S(1)} %own_block.1.refs_0_, ...), custom_call_target="tpu_custom_call" | custom-call | flops 1048576 | bytes 1048576 | tf_op jit(solution)/shard_map/backward/pallas_call | solution.py:223
  68.8 6.5 %collective-permute-start.16 = (f32[256,64]{1,0:T(8,128)S(1)}, f32[256,64]{1,0:T(8,128)S(1)}, u32[]{:S(2)}, u32[]{:S(2)}) collective-permute-start(f32[256,64]{1,0:T(8,128)S(1)} %get-tuple-element.98.refs_1_), channel_id=1, source_target_pairs={{0,1},{1,0},{2,3},{3,2},{4,5},{5,4},{6,7},{7,6},{8,9},{9,8},{10,11... | collective-permute-start | bytes 196616 | tf_op jit(solution)/shard_map/ppermute | solution.py:245
  75.3 0.1 collective-permute-start.15
  75.4 0.2 convert_add_fusion
  75.6 0.1 collective-permute-start.18
  75.8 0.2 fusion.5
  76.0 0.2 fusion.2
  76.2 2.8 %collective-permute-start.17 = (f32[64,512]{1,0:T(8,128)S(1)}, f32[64,512]{1,0:T(8,128)S(1)}, u32[]{:S(2)}, u32[]{:S(2)}) collective-permute-start(f32[64,512]{1,0:T(8,128)S(1)} %fusion.2), channel_id=1, source_target_pairs={{0,1},{1,0},{2,3},{3,2},{4,5},{5,4},{6,7},{7,6},{8,9},{9,8},{10,11... | collective-permute-start | bytes 393224 | tf_op jit(solution)/shard_map/ppermute | solution.py:245
  79.0 5.9 %backward.3 = (f32[128,1792]{1,0:T(8,128)S(1)}, bf16[128,1792]{1,0:T(8,128)(2,1)S(1)}) custom-call(s32[16]{0:T(128)S(1)} %stack.88.order_ref, bf16[256,4096]{1,0:T(8,128)(2,1)S(1)} %get-tuple-element.101.refs_0_, f32[256,64]{1,0:T(8,128)S(1)} %get-tuple-element.98.refs_1_, bf16[64,3584]{1,0:T(8,128)(2,1)S(1)} %bitcast.44, ...), custom_call_target="tpu_custom_call" | custom-call | flops 1048576 | bytes 1048576 | tf_op jit(solution)/shard_map/backward/pallas_call | solution.py:223
  85.0 0.1 multiply_reduce_fusion
  85.1 0.1 collective-permute-start.21
  85.3 0.5 collective-permute-start.19
  85.8 0.1 collective-permute-start.20
  85.9 1.5 %fusion.8 = f32[64,3584]{1,0:T(8,128)S(1)} fusion(bf16[128,3584]{1,0:T(8,128)(2,1)} %refs_0_.1, f32[256,64]{1,0:T(8,128)S(1)} %collective-permute-done.16, f32[256,64]{1,0:T(8,128)S(1)} %get-tuple-element.98.refs_1_), kind=kOutput, calls=%fused_computation.26 | convolution fusion | flops 58736640 | bytes 1966080 | tf_op jit(solution)/shard_map/dot_general | solution.py:21
  87.4 0.1 add_convert_fusion.2
  87.5 1.2 %fusion.1 = f32[3584,64]{0,1:T(8,128)} fusion(f32[64,3584]{1,0:T(8,128)S(1)} %fusion.8, bf16[128,3584]{1,0:T(8,128)(2,1)S(1)} %collective-permute-done.8.refs_1_, f32[256,64]{1,0:T(8,128)S(1)} %collective-permute-done.16, f32[256,64]{1,0:T(8,128)S(1)} %get-tuple-element.98.refs_1_), kind=kOutput, calls=%fused_computation.2 | convolution fusion | flops 59195392 | bytes 2883584 | tf_op jit(solution)/shard_map/dot_general | solution.py:21
  88.7 0.7 maximum_select_fusion.1
  89.4 0.6 maximum_select_fusion.2
  90.0 0.8 maximum_select_fusion
  90.8 0.1 add_convert_fusion.1
  90.9 1.0 %pad_maximum_fusion = bf16[128,3584]{1,0:T(8,128)(2,1)} fusion(bf16[128,1792]{1,0:T(8,128)(2,1)S(1)} %add_convert_fusion.1, bf16[128,1792]{1,0:T(8,128)(2,1)S(1)} %add_convert_fusion.2), kind=kLoop, calls=%fused_computation.7 | loop fusion | flops 1835008 | bytes 1835008 | tf_op jit(solution)/shard_map/concatenate | solution.py:333
  (36 shorter events, 0.2 us)
Async XLA Ops:
  0.6 1.9 %collective-permute-start = (bf16[128,1024]{1,0:T(8,128)(2,1)}, bf16[128,1024]{1,0:T(8,128)(2,1)S(1)}, u32[]{:S(2)}, u32[]{:S(2)}) collective-permute-start(bf16[128,1024]{1,0:T(8,128)(2,1)} %own_ref.1), channel_id=1, source_target_pairs={{0,1},{1,0},{2,3},{3,2},{4,5},{5,4},{6,7},{7,6},{8,9},{9,8},{10,11... | collective-permute-start | bytes 786440 | tf_op jit(solution)/shard_map/ppermute | solution.py:245
  2.5 1.2 %copy-start = (bf16[64,8192]{1,0:T(8,128)(2,1)S(1)}, bf16[64,8192]{1,0:T(8,128)(2,1)}, u32[]{:S(2)}) copy-start(bf16[64,8192]{1,0:T(8,128)(2,1)} %refs_9_.1) | copy-start | bytes 3145732
  3.7 1.0 %copy-start.4 = (bf16[3584,64]{0,1:T(8,128)(2,1)S(1)}, bf16[3584,64]{0,1:T(8,128)(2,1)}, u32[]{:S(2)}) copy-start(bf16[3584,64]{0,1:T(8,128)(2,1)} %param.8) | copy-start | bytes 1376260
  4.8 0.9 %copy-start.6 = (bf16[128,1024]{1,0:T(8,128)(2,1)S(1)}, bf16[128,1024]{1,0:T(8,128)(2,1)}, u32[]{:S(2)}) copy-start(bf16[128,1024]{1,0:T(8,128)(2,1)} %own_ref.1) | copy-start | bytes 786436
  7.5 20.6 %copy-start.1 = (bf16[64,8192]{1,0:T(8,128)(2,1)S(1)}, bf16[64,8192]{1,0:T(8,128)(2,1)}, u32[]{:S(2)}) copy-start(bf16[64,8192]{1,0:T(8,128)(2,1)} %refs_9_.1) | copy-start | bytes 3145732
  7.5 20.6 %copy-start.5 = (bf16[3584,64]{0,1:T(8,128)(2,1)S(1)}, bf16[3584,64]{0,1:T(8,128)(2,1)}, u32[]{:S(2)}) copy-start(bf16[3584,64]{0,1:T(8,128)(2,1)} %param.8) | copy-start | bytes 1376260
  7.5 16.9 %collective-permute-start.3 = (bf16[272,512]{1,0:T(8,128)(2,1)S(1)}, bf16[272,512]{1,0:T(8,128)(2,1)S(1)}, u32[]{:S(2)}, u32[]{:S(2)}) collective-permute-start(bf16[272,512]{1,0:T(8,128)(2,1)S(1)} %own_block.1.refs_0_), channel_id=1, source_target_pairs={{0,8},{1,3},{2,10},{3,1},{4,12},{5,7},{6,14},{7,5},{8,0},{9,11},{1... | collective-permute-start | bytes 835592 | tf_op jit(solution)/shard_map/ppermute | solution.py:250
  11.5 14.0 %collective-permute-start.2 = (bf16[272,512]{1,0:T(8,128)(2,1)S(1)}, bf16[272,512]{1,0:T(8,128)(2,1)S(1)}, u32[]{:S(2)}, u32[]{:S(2)}) collective-permute-start(bf16[272,512]{1,0:T(8,128)(2,1)S(1)} %own_block.1.refs_0_), channel_id=1, source_target_pairs={{0,4},{1,9},{2,6},{3,11},{4,0},{5,13},{6,2},{7,15},{8,12},{9,1},{1... | collective-permute-start | bytes 835592 | tf_op jit(solution)/shard_map/ppermute | solution.py:250
  13.1 12.4 %collective-permute-start.1 = (bf16[272,512]{1,0:T(8,128)(2,1)S(1)}, bf16[272,512]{1,0:T(8,128)(2,1)S(1)}, u32[]{:S(2)}, u32[]{:S(2)}) collective-permute-start(bf16[272,512]{1,0:T(8,128)(2,1)S(1)} %own_block.1.refs_0_), channel_id=1, source_target_pairs={{0,2},{1,5},{2,0},{3,7},{4,6},{5,1},{6,4},{7,3},{8,10},{9,13},{10,... | collective-permute-start | bytes 835592 | tf_op jit(solution)/shard_map/ppermute | solution.py:250
  14.6 25.1 %collective-permute-start.8 = (bf16[128,3584]{1,0:T(8,128)(2,1)}, bf16[128,3584]{1,0:T(8,128)(2,1)S(1)}, u32[]{:S(2)}, u32[]{:S(2)}) collective-permute-start(bf16[128,3584]{1,0:T(8,128)(2,1)} %refs_0_.1), channel_id=1, source_target_pairs={{0,1},{1,0},{2,3},{3,2},{4,5},{5,4},{6,7},{7,6},{8,9},{9,8},{10,11... | collective-permute-start | bytes 2752520 | tf_op jit(solution)/shard_map/ppermute | solution.py:245
  25.5 12.2 %collective-permute-start.4 = (bf16[272,512]{1,0:T(8,128)(2,1)S(1)}, bf16[272,512]{1,0:T(8,128)(2,1)S(1)}, u32[]{:S(2)}, u32[]{:S(2)}) collective-permute-start(bf16[272,512]{1,0:T(8,128)(2,1)S(1)} %collective-permute-done.3.refs_1_), channel_id=1, source_target_pairs={{0,4},{1,9},{2,6},{3,11},{4,0},{5,13},{6,2},{7,15},{8,12},{9,1},{1... | collective-permute-start | bytes 835592 | tf_op jit(solution)/shard_map/ppermute | solution.py:250
  26.8 18.0 %collective-permute-start.6 = (bf16[2,272,512]{2,1,0:T(8,128)(2,1)S(1)}, bf16[2,272,512]{2,1,0:T(8,128)(2,1)S(1)}, u32[]{:S(2)}, u32[]{:S(2)}) collective-permute-start(bf16[2,272,512]{2,1,0:T(8,128)(2,1)S(1)} %pad_maximum_fusion.1), channel_id=1, source_target_pairs={{0,2},{1,5},{2,0},{3,7},{4,6},{5,1},{6,4},{7,3},{8,10},{9,13},{10,... | collective-permute-start | bytes 1671176 | tf_op jit(solution)/shard_map/ppermute | solution.py:250
  35.0 18.8 %copy-start.2 = (bf16[3584,512]{1,0:T(8,128)(2,1)}, bf16[3584,512]{1,0:T(8,128)(2,1)S(1)}, u32[]{:S(2)}) copy-start(bf16[3584,512]{1,0:T(8,128)(2,1)S(1)} %get-tuple-element.81.refs_3_.refs_13_.refs_5_) | copy-start | bytes 11010052
  37.7 7.1 %collective-permute-start.7 = (bf16[272,512]{1,0:T(8,128)(2,1)S(1)}, bf16[272,512]{1,0:T(8,128)(2,1)S(1)}, u32[]{:S(2)}, u32[]{:S(2)}) collective-permute-start(bf16[272,512]{1,0:T(8,128)(2,1)S(1)} %collective-permute-done.4.refs_3_), channel_id=1, source_target_pairs={{0,2},{1,5},{2,0},{3,7},{4,6},{5,1},{6,4},{7,3},{8,10},{9,13},{10,... | collective-permute-start | bytes 835592 | tf_op jit(solution)/shard_map/ppermute | solution.py:250
  37.9 6.9 %collective-permute-start.5 = (f32[24,512]{1,0:T(8,128)S(1)}, f32[24,512]{1,0:T(8,128)S(1)}, u32[]{:S(2)}, u32[]{:S(2)}) collective-permute-start(f32[24,512]{1,0:T(8,128)S(1)} %get-tuple-element.65), channel_id=1, source_target_pairs={{0,2},{1,5},{2,0},{3,7},{4,6},{5,1},{6,4},{7,3},{8,10},{9,13},{10,... | collective-permute-start | bytes 147464 | tf_op jit(solution)/shard_map/ppermute | solution.py:250
  44.8 11.8 %collective-permute-start.12 = (bf16[2,256,512]{2,1,0:T(8,128)(2,1)S(1)}, bf16[2,256,512]{2,1,0:T(8,128)(2,1)S(1)}, u32[]{:S(2)}, u32[]{:S(2)}) collective-permute-start(bf16[2,256,512]{2,1,0:T(8,128)(2,1)S(1)} %get-tuple-element.79), channel_id=1, source_target_pairs={{0,2},{1,5},{2,0},{3,7},{4,6},{5,1},{6,4},{7,3},{8,10},{9,13},{10,... | collective-permute-start | bytes 1572872 | tf_op jit(solution)/shard_map/ppermute | solution.py:250
  45.0 5.2 %collective-permute-start.9 = (f32[24,512]{1,0:T(8,128)S(1)}, f32[24,512]{1,0:T(8,128)S(1)}, u32[]{:S(2)}, u32[]{:S(2)}) collective-permute-start(f32[24,512]{1,0:T(8,128)S(1)} %add.73), channel_id=1, source_target_pairs={{0,4},{1,9},{2,6},{3,11},{4,0},{5,13},{6,2},{7,15},{8,12},{9,1},{1... | collective-permute-start | bytes 147464 | tf_op jit(solution)/shard_map/ppermute | solution.py:250
  50.2 6.4 %collective-permute-start.11 = (f32[24,512]{1,0:T(8,128)S(1)}, f32[24,512]{1,0:T(8,128)S(1)}, u32[]{:S(2)}, u32[]{:S(2)}) collective-permute-start(f32[24,512]{1,0:T(8,128)S(1)} %add.74), channel_id=1, source_target_pairs={{0,8},{1,3},{2,10},{3,1},{4,12},{5,7},{6,14},{7,5},{8,0},{9,11},{1... | collective-permute-start | bytes 147464 | tf_op jit(solution)/shard_map/ppermute | solution.py:250
  52.8 9.2 %collective-permute-start.10 = (bf16[2,256,512]{2,1,0:T(8,128)(2,1)S(1)}, bf16[2,256,512]{2,1,0:T(8,128)(2,1)S(1)}, u32[]{:S(2)}, u32[]{:S(2)}) collective-permute-start(bf16[2,256,512]{2,1,0:T(8,128)(2,1)S(1)} %forward.5), channel_id=1, source_target_pairs={{0,2},{1,5},{2,0},{3,7},{4,6},{5,1},{6,4},{7,3},{8,10},{9,13},{10,... | collective-permute-start | bytes 1572872 | tf_op jit(solution)/shard_map/ppermute | solution.py:250
  56.8 18.6 %collective-permute-start.14 = (bf16[2,256,512]{2,1,0:T(8,128)(2,1)S(1)}, bf16[2,256,512]{2,1,0:T(8,128)(2,1)S(1)}, u32[]{:S(2)}, u32[]{:S(2)}) collective-permute-start(bf16[2,256,512]{2,1,0:T(8,128)(2,1)S(1)} %add_convert_fusion), channel_id=1, source_target_pairs={{0,4},{1,9},{2,6},{3,11},{4,0},{5,13},{6,2},{7,15},{8,12},{9,1},{1... | collective-permute-start | bytes 1572872 | tf_op jit(solution)/shard_map/ppermute | solution.py:250
  58.8 2.9 %collective-permute-start.13 = (f32[16,512]{1,0:T(8,128)S(1)}, f32[16,512]{1,0:T(8,128)S(1)}, u32[]{:S(2)}, u32[]{:S(2)}) collective-permute-start(f32[16,512]{1,0:T(8,128)S(1)} %slice.101), channel_id=1, source_target_pairs={{0,1},{1,0},{2,3},{3,2},{4,5},{5,4},{6,7},{7,6},{8,9},{9,8},{10,11... | collective-permute-start | bytes 98312 | tf_op jit(solution)/shard_map/ppermute | solution.py:245
  58.9 3.1 %copy-start.3 = (bf16[3584,512]{1,0:T(8,128)(2,1)S(1)}, bf16[3584,512]{1,0:T(8,128)(2,1)}, u32[]{:S(2)}) copy-start(bf16[3584,512]{1,0:T(8,128)(2,1)} %copy-done.2) | copy-start | bytes 11010052
  68.8 16.1 %collective-permute-start.16 = (f32[256,64]{1,0:T(8,128)S(1)}, f32[256,64]{1,0:T(8,128)S(1)}, u32[]{:S(2)}, u32[]{:S(2)}) collective-permute-start(f32[256,64]{1,0:T(8,128)S(1)} %get-tuple-element.98.refs_1_), channel_id=1, source_target_pairs={{0,1},{1,0},{2,3},{3,2},{4,5},{5,4},{6,7},{7,6},{8,9},{9,8},{10,11... | collective-permute-start | bytes 196616 | tf_op jit(solution)/shard_map/ppermute | solution.py:245
  75.3 9.6 %collective-permute-start.15 = (bf16[128,1792]{1,0:T(8,128)(2,1)S(1)}, bf16[128,1792]{1,0:T(8,128)(2,1)S(1)}, u32[]{:S(2)}, u32[]{:S(2)}) collective-permute-start(bf16[128,1792]{1,0:T(8,128)(2,1)S(1)} %get-tuple-element.97), channel_id=1, source_target_pairs={{0,1},{1,0},{2,3},{3,2},{4,5},{5,4},{6,7},{7,6},{8,9},{9,8},{10,11... | collective-permute-start | bytes 1376264 | tf_op jit(solution)/shard_map/ppermute | solution.py:245
  75.6 9.3 %collective-permute-start.18 = (bf16[256,512]{1,0:T(8,128)(2,1)S(1)}, bf16[256,512]{1,0:T(8,128)(2,1)S(1)}, u32[]{:S(2)}, u32[]{:S(2)}) collective-permute-start(bf16[256,512]{1,0:T(8,128)(2,1)S(1)} %fusion.4), channel_id=1, source_target_pairs={{0,8},{1,3},{2,10},{3,1},{4,12},{5,7},{6,14},{7,5},{8,0},{9,11},{1... | collective-permute-start | bytes 786440 | tf_op jit(solution)/shard_map/ppermute | solution.py:250
  76.2 8.8 %collective-permute-start.17 = (f32[64,512]{1,0:T(8,128)S(1)}, f32[64,512]{1,0:T(8,128)S(1)}, u32[]{:S(2)}, u32[]{:S(2)}) collective-permute-start(f32[64,512]{1,0:T(8,128)S(1)} %fusion.2), channel_id=1, source_target_pairs={{0,1},{1,0},{2,3},{3,2},{4,5},{5,4},{6,7},{7,6},{8,9},{9,8},{10,11... | collective-permute-start | bytes 393224 | tf_op jit(solution)/shard_map/ppermute | solution.py:245
  85.1 4.3 %collective-permute-start.21 = (f32[512]{0:T(512)S(1)}, f32[512]{0:T(512)S(1)}, u32[]{:S(2)}, u32[]{:S(2)}) collective-permute-start(f32[512]{0:T(512)S(1)} %div.3), channel_id=1, source_target_pairs={{0,1},{1,0},{2,3},{3,2},{4,5},{5,4},{6,7},{7,6},{8,9},{9,8},{10,11... | collective-permute-start | bytes 6152 | tf_op jit(solution)/shard_map/ppermute | solution.py:245
  85.3 4.8 %collective-permute-start.19 = (bf16[128,512]{1,0:T(8,128)(2,1)S(1)}, bf16[128,512]{1,0:T(8,128)(2,1)S(1)}, u32[]{:S(2)}, u32[]{:S(2)}) collective-permute-start(bf16[128,512]{1,0:T(8,128)(2,1)S(1)} %get-tuple-element.116), channel_id=1, source_target_pairs={{0,1},{1,0},{2,3},{3,2},{4,5},{5,4},{6,7},{7,6},{8,9},{9,8},{10,11... | collective-permute-start | bytes 393224 | tf_op jit(solution)/shard_map/ppermute | solution.py:245
  85.8 5.0 %collective-permute-start.20 = (bf16[128,1792]{1,0:T(8,128)(2,1)S(1)}, bf16[128,1792]{1,0:T(8,128)(2,1)S(1)}, u32[]{:S(2)}, u32[]{:S(2)}) collective-permute-start(bf16[128,1792]{1,0:T(8,128)(2,1)S(1)} %get-tuple-element.108), channel_id=1, source_target_pairs={{0,1},{1,0},{2,3},{3,2},{4,5},{5,4},{6,7},{7,6},{8,9},{9,8},{10,11... | collective-permute-start | bytes 1376264 | tf_op jit(solution)/shard_map/ppermute | solution.py:245

commit v9 on v8

--- a/solution.py
+++ b/solution.py
@@ -236,6 +236,79 @@
     )(order, *operands, at, *held)
 
 
+def core_halves(order_ref, ref, own, other, axis):
+    half = own.shape[axis]
+    low, high = (slice(None),) * axis + (slice(0, half),), (slice(None),) * axis + (slice(half, 2 * half),)
+    core = lax.rem(order_ref[0], 2)
+
+    @pl.when(core == 0)
+    def _():
+        ref[low] = own
+        ref[high] = other
+
+    @pl.when(core == 1)
+    def _():
+        ref[low] = other
+        ref[high] = own
+
+
+def weights_kernel(tokens, order_ref, proj_ref, from_ref, own_ref, other_ref, up_ref, up_other_ref, down_out, up_out):
+    proj_own = (proj_ref[:tokens, :] + from_ref[tokens:, :]).astype(bf16)
+    proj_other = (proj_ref[tokens:, :] + from_ref[:tokens, :]).astype(bf16)
+    down_out[...] = adapter_scale * (
+        dot(proj_own, own_ref[...], contract_first) + dot(proj_other, other_ref[...], contract_first)
+    )
+    core_halves(order_ref, up_out, up_ref[...], up_other_ref[...], 1)
+
+
+def tokens_kernel(order_ref, ga_ref, ra_ref, gb_ref, rb_ref, m_ref, m_other_ref, g_ref, g_other_ref, *outs):
+    hidden_out, mixed_out, magnitude_out = outs
+    tokens, split = ga_ref.shape
+    hidden_out[:, :split] = (ga_ref[...] + ra_ref[...].astype(f32)).astype(bf16)
+    hidden_out[:, split:] = (gb_ref[...] + rb_ref[...].astype(f32)).astype(bf16)
+    core_halves(order_ref, mixed_out, m_ref[:tokens, :], m_other_ref[...], 1)
+    rows = g_ref.shape[1] // 128
+    stacked = [jnp.concatenate([r[:, i * 128 : (i + 1) * 128] for i in range(rows)]) for r in (g_ref, g_other_ref)]
+    core_halves(order_ref, magnitude_out, *stacked, 0)
+
+
+def finish(kernel, name, out_shape, order, *operands):
+    whole = lambda x: pl.BlockSpec(x.shape, lambda i, p: (0,) * len(x.shape))
+    return pl.pallas_call(
+        kernel,
+        grid_spec=pltpu.PrefetchScalarGridSpec(
+            num_scalar_prefetch=1,
+            grid=(1,),
+            in_specs=[vmem()] * len(operands),
+            out_specs=[whole(x) for x in out_shape],
+        ),
+        out_shape=out_shape,
+        compiler_params=params(),
+        cost_estimate=small_cost,
+        name=name,
+    )(order, *operands)
+
+
+def finish_weights(order, proj, from_sibling, own, other, up_half, up_other):
+    tokens, rows = own.shape
+    rank, half = up_half.shape
+    shapes = [jax.ShapeDtypeStruct((rank, rows), f32), jax.ShapeDtypeStruct((rank, 2 * half), f32)]
+    kernel = functools.partial(weights_kernel, tokens)
+    return finish(kernel, "weights", shapes, order, proj, from_sibling, own, other, up_half, up_other)
+
+
+def finish_tokens(order, grad_a, got_a, grad_b, got_b, mixed, mixed_other, magnitude, magnitude_other):
+    tokens, half = mixed_other.shape
+    rows = grad_a.shape[1] + grad_b.shape[1]
+    shapes = [
+        jax.ShapeDtypeStruct((tokens, rows), bf16),
+        jax.ShapeDtypeStruct((tokens, 2 * half), bf16),
+        jax.ShapeDtypeStruct((2 * half // 128, 128), f32),
+    ]
+    operands = (grad_a, got_a, grad_b, got_b, mixed, mixed_other, magnitude, magnitude_other)
+    return finish(tokens_kernel, "tokens", shapes, order, *operands)
+
+
 def split_columns(hidden, weight, down, up, magnitude, cotangent):
     n, bits = 8, 3
     tokens = hidden.shape[0]
@@ -243,7 +316,7 @@
     rows = weight.shape[0]
     me, core = lax.axis_index("tensor"), lax.axis_index("dp")
     swap = lambda x: lax.ppermute(x, "dp", [(0, 1), (1, 0)])
-    orders = [[1, 2, 4], [2, 4, 1]]
+    orders = [[1, 2, 4], [2, 1, 4]]
 
     def send(x, k):
         pairs = [(2 * t + c, 2 * (t ^ orders[c][k]) + c) for t in range(n) for c in range(2)]
@@ -270,51 +343,49 @@
         [jnp.stack([first, second, third]), jnp.zeros((pad_rows - 3, 2 * half), f32)]
     ).astype(bf16)
     low_core, order, cot_other = tie((low_core, order, cot_other))
-    block = own_block(order, cotangent, cot_other, magnitude_rows, at, up, hidden)
+    block = own_block(order, cotangent, cot_other, magnitude_rows)
 
     cots = {0b000: block, 0b001: send(block, 2), 0b010: send(block, 1), 0b100: send(block, 0)}
 
     run_load = functools.partial(load, at=at, up=up, weight=weight, half=half)
-    *far, stats = run_load((0b100, 0b101, 0b110, 0b111), order, own=hidden)
+    block, order = tie((block, order))
+    *held, stats = run_load(tuple(range(n)), order, own=hidden)
+    near, far = held[: n // 2], held[n // 2 :]
     cots[0b100], cots[0b010], cots[0b001], stats = tie((cots[0b100], cots[0b010], cots[0b001], stats))
     cots[0b011] = send(cots[0b001], 1)
     pair = send(jnp.stack([cots[0b001], cots[0b010]]), 0)
-    *near, stats = run_load((0b000, 0b001, 0b010, 0b011), order, before=stats)
-    cots[0b011], stats = tie((cots[0b011], stats))
     got = send(stats, 0)
-    cots[0b111] = send(cots[0b011], 0)
     far1, lhs, adapter = forward((0b110, 0b111), order, far[2:], up, first=(hidden, hidden_other, at))
     run = lambda order, vs, held: forward(vs, order, held, up, later=(lhs, adapter))[0]
-    got, pair, cots[0b111], far1, order = tie((got, pair, cots[0b111], far1, order))
-    cots[0b101], cots[0b110] = pair[0], pair[1]
+    got, cots[0b011], far1, order = tie((got, cots[0b011], far1, order))
+    cots[0b111] = send(cots[0b011], 0)
     stats = stats + got
     got = send(stats, 1)
     from1 = send(far1, 0)
     far0 = run(order, (0b100, 0b101), far[:2])
-    got, far0, order = tie((got, far0, order))
+    got, pair, far0, order = tie((got, pair, far0, order))
+    cots[0b101], cots[0b110] = pair[0], pair[1]
     stats = stats + got
     got = send(stats, 2)
     from0 = send(far0, 0)
     near1 = run(order, (0b010, 0b011), near[2:])
-    got, from1, near1, order = tie((got, from1, near1, order))
+    got, from1, cots[0b111], near1, order = tie((got, from1, cots[0b111], near1, order))
     stats = stats + got
     arrived = send((near1.astype(f32) + from1.astype(f32)).astype(bf16), 1)
     lowrank_rows = stats[n:]
     lowrank_other = swap(lowrank_rows)
     near0 = run(order, (0b000, 0b001), near[:2])
-    from0, lowrank_other, near0, order = tie((from0, lowrank_other, near0, order))
-    kept = near0.astype(f32) + from0.astype(f32)
-    held = near + far
+    near0, order = tie((near0, order))
 
     band = 256
     bands = rows // band
-    many = bands // 2
+    many = max(bands * 5 // 14, 1)
     run = functools.partial(backward, order, band=band, at=at, held=held)
     grad_a, other_a, scaled, proj, scales, scaled_own = run(0, many, first=([cots[v] for v in range(n)], stats, up))
     got_a = swap(other_a)
     from_sibling = swap(proj)
-    arrived, scaled_own = tie((arrived, scaled_own))
-    kept = kept + arrived.astype(f32)
+    arrived, from0, lowrank_other, scaled_own = tie((arrived, from0, lowrank_other, scaled_own))
+    kept = near0.astype(f32) + from0.astype(f32) + arrived.astype(f32)
     last = send(kept[1].astype(bf16), 2)
     scaled_own = scaled_own.astype(f32)
 
@@ -327,29 +398,21 @@
         + jnp.dot(turned(lowrank_other), scaled_own[tokens:], precision=lax.Precision.HIGHEST)
     )
     up_other = swap(up_half)
-    grad_b, other_b = run(many, bands - many, later=(scaled, proj))
+    grad_b, other_b = backward(order, many, bands - many, band, at, held, later=(scaled, proj))
     got_a, from_sibling, up_other, last, other_b = tie((got_a, from_sibling, up_other, last, other_b))
     got_b = swap(other_b)
-    hidden_gradient = jnp.concatenate(
-        [(own + got.astype(f32)).astype(bf16) for own, got in ((grad_a, got_a), (grad_b, got_b))], axis=1
-    )
-    proj_own = (proj[:tokens] + from_sibling[tokens:]).astype(bf16)
-    proj_other = (proj[tokens:] + from_sibling[:tokens]).astype(bf16)
-    down_weight_gradient = adapter_scale * (
-        dot(proj_own, hidden, contract_first) + dot(proj_other, hidden_other, contract_first)
-    ).T
-
-    norm, rescale = scales[0], scales[1]
+
     unscaled = kept[0] + last.astype(f32)
-    mixed = (unscaled * rescale).astype(bf16)
-    magnitude_half = jnp.sum(block[: 2 * tokens].astype(f32) * unscaled, axis=0) / norm
-
-    def join(own, other, axis):
-        return jnp.where(low_core, jnp.concatenate([own, other], axis), jnp.concatenate([other, own], axis))
-
-    mixed = join(mixed[:tokens], swap(mixed[tokens:]), 1)
-    up_weight_gradient = join(up_half, up_other, 1)
-    grad_magnitude = join(magnitude_half, swap(magnitude_half), 0)
+    mixed = (unscaled * scales[1]).astype(bf16)
+    magnitude_half = jnp.sum(block[: 2 * tokens].astype(f32) * unscaled, axis=0, keepdims=True) / scales[0:1]
+    mixed_other, magnitude_other = swap(mixed[tokens:]), swap(magnitude_half)
+    down_weight_gradient, up_weight_gradient = finish_weights(
+        order, proj, from_sibling, hidden, hidden_other, up_half, up_other
+    )
+    hidden_gradient, mixed, grad_magnitude = finish_tokens(
+        order, grad_a, got_a, grad_b, got_b, mixed, mixed_other, magnitude_half, magnitude_other
+    )
+    down_weight_gradient, grad_magnitude = down_weight_gradient.T, grad_magnitude.reshape(2 * half)
     return (mixed, hidden_gradient, down_weight_gradient, up_weight_gradient, grad_magnitude)
 
 

time: 92.4 us -> 81.4 us (0.88)
  starting transfers between devices: 28.5 us -> 17.4 us
  waiting for transfers between devices: 9.17 us -> 15.6 us
  other arithmetic: 4.62 us -> 1.34 us
  matrix products: 3.14 us -> 0.4 us
  Pallas kernels: 42.1 us -> 40.7 us
  local copies, waits for them, and re-layouts: 3.5 us -> 4.67 us
    ppermute x9, starting transfers between devices: 10.7 us -> 2.69 us  [split_columns(): swap = lambda x: lax.ppermute(x, 'dp', [(0, 1), (1, 0)])]
    ppermute x13, waiting for transfers between devices: 8.76 us -> 15.3 us  [send(): return lax.ppermute(x, ('tensor', 'dp'), pairs)]
    pallas_call x0 -> x2, Pallas kernels: none -> 3.8 us  [finish(): pl.pallas_call(kernel, grid_spec=pltpu.PrefetchScalarGridSpec(num_scalar_...]
    pallas_call x2 -> x1, Pallas kernels: 14.6 us -> 11.3 us  [load(): pl.pallas_call(functools.partial(load_kernel, tokens, rank, n, vs, first)...]
    ppermute x13, starting transfers between devices: 17.7 us -> 14.7 us  [send(): return lax.ppermute(x, ('tensor', 'dp'), pairs)]
    dot_general x2 -> x0, matrix products: 2.74 us -> none  [dot(): return lax.dot_general(a, b, dims, preferred_element_type=f32)]
    select_n x3 -> x0, other arithmetic: 2.11 us -> none  [join(): jnp.where(low_core, jnp.concatenate([own, other], axis), jnp.concatenate(...]
    unnamed x14 -> x18, local copies, waits for them, and re-layouts: 3.21 us -> 4.39 us
  transfers between devices with their start and end apart: 22 -> 22, of which waited for: 7 -> 6; matrix products, arithmetic and copies ran while one was open for 7% -> 2% of each run, Pallas kernels for 44% -> 48%
where the time goes in v9:
time: 81.4 us; the launch traced here: 81.1 us
  Pallas kernels  40.7 us (50%)
  starting transfers between devices  17.4 us (21%)
  waiting for transfers between devices  15.6 us (19%)
  local copies, waits for them, and re-layouts  4.67 us (6%)
  other arithmetic  1.34 us (2%)
  between operations  0.92 us (1%)
    ppermute x13, waiting for transfers between devices, send(): return lax.ppermute(x, ('tensor', 'dp'), pairs)  15.3 us
    ppermute x13, starting transfers between devices, send(): return lax.ppermute(x, ('tensor', 'dp'), pairs)  14.7 us
    pallas_call x2, Pallas kernels, backward(): pl.pallas_call(functools.partial(backward_kernel, tokens, n, start, band,...  12.7 us
    pallas_call x4, Pallas kernels, forward(): pl.pallas_call(functools.partial(forward_kernel, tokens, rank, vs, later...  12.3 us
    pallas_call x1, Pallas kernels, load(): pl.pallas_call(functools.partial(load_kernel, tokens, rank, n, vs, first)...  11.3 us
    unnamed x18, local copies, waits for them, and re-layouts  4.39 us
    pallas_call x2, Pallas kernels, finish(): pl.pallas_call(kernel, grid_spec=pltpu.PrefetchScalarGridSpec(num_scalar_...  3.8 us
    ppermute x9, starting transfers between devices, split_columns(): swap = lambda x: lax.ppermute(x, 'dp', [(0, 1), (1, 0)])  2.69 us
  transfers between devices with their start and end apart: 22, of which 6 were waited for; matrix products, arithmetic and copies ran while one was open for 2% of the time, Pallas kernels for 48%

profile of v9, /device:TPU:0, one launch (start us, length us, event | category | flops | bytes accessed | tf_op | source)
XLA Modules:
  0.0 81.1 jit_solution(16217749757933330275)
XLA Ops:
  0.6 0.5 collective-permute-start
  1.1 0.1 collective-permute-start.6
  1.2 0.7 reduce-precision_convert_fusion.1
  2.0 0.1 pad.13.clone
  2.0 0.1 stack.88.order_ref
  2.1 0.1 maximum_maximum_fusion.magnitude_ref
  2.2 0.3 collective-permute-done.other_ref
  2.5 0.9 %copy-done.8 = bf16[128,1024]{1,0:T(8,128)(2,1)S(1)} copy-done((bf16[128,1024]{1,0:T(8,128)(2,1)S(1)}, bf16[128,1024]{1,0:T(8,128)(2,1)}, u32[]{:S(2)}) %copy-start.8) | copy-done | bytes 262168
  3.5 0.6 own_block.1.refs_0_
  4.0 4.0 %collective-permute-start.3 = (bf16[272,512]{1,0:T(8,128)(2,1)S(1)}, bf16[272,512]{1,0:T(8,128)(2,1)S(1)}, u32[]{:S(2)}, u32[]{:S(2)}) collective-permute-start(bf16[272,512]{1,0:T(8,128)(2,1)S(1)} %own_block.1.refs_0_), channel_id=1, source_target_pairs={{0,8},{1,9},{2,10},{3,11},{4,12},{5,13},{6,14},{7,15},{8,0},{9,1},... | collective-permute-start | bytes 835592 | tf_op jit(solution)/shard_map/ppermute | solution.py:323
  8.1 1.6 %collective-permute-start.2 = (bf16[272,512]{1,0:T(8,128)(2,1)S(1)}, bf16[272,512]{1,0:T(8,128)(2,1)S(1)}, u32[]{:S(2)}, u32[]{:S(2)}) collective-permute-start(bf16[272,512]{1,0:T(8,128)(2,1)S(1)} %own_block.1.refs_0_), channel_id=1, source_target_pairs={{0,4},{1,3},{2,6},{3,1},{4,0},{5,7},{6,2},{7,5},{8,12},{9,11},{10,... | collective-permute-start | bytes 835592 | tf_op jit(solution)/shard_map/ppermute | solution.py:323
  9.6 1.5 %collective-permute-start.1 = (bf16[272,512]{1,0:T(8,128)(2,1)S(1)}, bf16[272,512]{1,0:T(8,128)(2,1)S(1)}, u32[]{:S(2)}, u32[]{:S(2)}) collective-permute-start(bf16[272,512]{1,0:T(8,128)(2,1)S(1)} %own_block.1.refs_0_), channel_id=1, source_target_pairs={{0,2},{1,5},{2,0},{3,7},{4,6},{5,1},{6,4},{7,3},{8,10},{9,13},{10,... | collective-permute-start | bytes 835592 | tf_op jit(solution)/shard_map/ppermute | solution.py:323
  11.1 1.2 %copy-done = bf16[64,8192]{1,0:T(8,128)(2,1)S(1)} copy-done((bf16[64,8192]{1,0:T(8,128)(2,1)S(1)}, bf16[64,8192]{1,0:T(8,128)(2,1)}, u32[]{:S(2)}) %copy-start) | copy-done | bytes 1048600
  12.4 1.2 %copy-done.4 = bf16[128,3584]{1,0:T(8,128)(2,1)S(1)} copy-done((bf16[128,3584]{1,0:T(8,128)(2,1)S(1)}, bf16[128,3584]{1,0:T(8,128)(2,1)}, u32[]{:S(2)}) %copy-start.4) | copy-done | bytes 917528
  13.5 1.0 %copy-done.6 = bf16[3584,64]{0,1:T(8,128)(2,1)S(1)} copy-done((bf16[3584,64]{0,1:T(8,128)(2,1)S(1)}, bf16[3584,64]{0,1:T(8,128)(2,1)}, u32[]{:S(2)}) %copy-start.6) | copy-done | bytes 458776
  14.6 11.3 %load.1 = (bf16[3584,512]{1,0:T(8,128)(2,1)S(1)}, bf16[3584,512]{1,0:T(8,128)(2,1)S(1)}, bf16[3584,512]{1,0:T(8,128)(2,1)S(1)}, bf16[3584,512]{1,0:T(8,128)(2,1)...) custom-call(s32[16]{0:T(128)S(1)} %stack.88.order_ref, ...), custom_call_target="tpu_custom_call" | custom-call | flops 1048576 | bytes 1048576 | tf_op jit(solution)/shard_map/load/pallas_call | solution.py:116
  25.9 0.0 collective-permute-done.3.refs_1_
  25.9 0.0 collective-permute-done.2.refs_2_
  25.9 0.0 collective-permute-done.1.refs_4_
  25.9 0.5 collective-permute-start.5
  26.5 0.1 pad_maximum_fusion
  26.5 0.6 collective-permute-start.8
  27.1 1.5 %collective-permute-start.4 = (f32[24,512]{1,0:T(8,128)S(1)}, f32[24,512]{1,0:T(8,128)S(1)}, u32[]{:S(2)}, u32[]{:S(2)}) collective-permute-start(f32[24,512]{1,0:T(8,128)S(1)} %get-tuple-element.66), channel_id=1, source_target_pairs={{0,2},{1,5},{2,0},{3,7},{4,6},{5,1},{6,4},{7,3},{8,10},{9,13},{10,... | collective-permute-start | bytes 147464 | tf_op jit(solution)/shard_map/ppermute | solution.py:323
  28.6 0.0 collective-permute-done.6.refs_1_.other_ref
  28.6 4.1 %forward.4 = (bf16[2,256,512]{2,1,0:T(8,128)(2,1)S(1)}, bf16[256,3584]{1,0:T(8,128)(2,1)S(1)}, bf16[256,128]{1,0:T(8,128)(2,1)S(1)}) custom-call(s32[16]{0:T(128)S(1)} %stack.88.order_ref, bf16[128,3584]{1,0:T(8,128)(2,1)S(1)} %copy-done.5, bf16[128,3584]{1,0:T(8,128)(2,1)S(1)} %collective-permute-done.6.refs_1_.other_ref, bf16[64,3584]{1,0:T(8,128)(2,1)S(1)} %bitcast.38, ...), custom_call_target="tpu_custom_call" | custom-call | flops 1048576 | bytes 1048576 | tf_op jit(solution)/shard_map/forward/pallas_call | solution.py:158
  32.7 4.6 %collective-permute-done.4 = f32[24,512]{1,0:T(8,128)S(1)} collective-permute-done((f32[24,512]{1,0:T(8,128)S(1)}, f32[24,512]{1,0:T(8,128)S(1)}, u32[]{:S(2)}, u32[]{:S(2)}) %collective-permute-start.4) | collective-permute-done | bytes 49184 | tf_op jit(solution)/shard_map/ppermute | solution.py:323
  37.3 0.0 collective-permute-done.5.refs_3_
  37.3 0.5 collective-permute-start.10
  37.9 1.5 %collective-permute-start.11 = (bf16[272,512]{1,0:T(8,128)(2,1)S(1)}, bf16[272,512]{1,0:T(8,128)(2,1)S(1)}, u32[]{:S(2)}, u32[]{:S(2)}) collective-permute-start(bf16[272,512]{1,0:T(8,128)(2,1)S(1)} %collective-permute-done.5.refs_3_), channel_id=1, source_target_pairs={{0,2},{1,5},{2,0},{3,7},{4,6},{5,1},{6,4},{7,3},{8,10},{9,13},{10,... | collective-permute-start | bytes 835592 | tf_op jit(solution)/shard_map/ppermute | solution.py:323
  39.4 1.0 %collective-permute-start.7 = (f32[24,512]{1,0:T(8,128)S(1)}, f32[24,512]{1,0:T(8,128)S(1)}, u32[]{:S(2)}, u32[]{:S(2)}) collective-permute-start(f32[24,512]{1,0:T(8,128)S(1)} %add.56), channel_id=1, source_target_pairs={{0,4},{1,3},{2,6},{3,1},{4,0},{5,7},{6,2},{7,5},{8,12},{9,11},{10,... | collective-permute-start | bytes 147464 | tf_op jit(solution)/shard_map/ppermute | solution.py:323
  40.3 2.8 %forward.5 = bf16[2,256,512]{2,1,0:T(8,128)(2,1)S(1)} custom-call(s32[16]{0:T(128)S(1)} %stack.88.order_ref, bf16[256,3584]{1,0:T(8,128)(2,1)S(1)} %get-tuple-element.74.refs_0_, bf16[256,128]{1,0:T(8,128)(2,1)S(1)} %get-tuple-element.75.refs_1_, bf16[64,8192]{1,0:T(8,128)(2,1)S(1)} %copy-done.1, ...), custom_call_target="tpu_custom_call" | custom-call | flops 1048576 | bytes 1048576 | tf_op jit(solution)/shard_map/forward/pallas_call | solution.py:158
  43.1 1.0 %collective-permute-done.7 = f32[24,512]{1,0:T(8,128)S(1)} collective-permute-done((f32[24,512]{1,0:T(8,128)S(1)}, f32[24,512]{1,0:T(8,128)S(1)}, u32[]{:S(2)}, u32[]{:S(2)}) %collective-permute-start.7) | collective-permute-done | bytes 49184 | tf_op jit(solution)/shard_map/ppermute | solution.py:323
  44.1 0.0 collective-permute-done.8
  44.1 0.4 collective-permute-start.9
  44.5 0.5 collective-permute-start.15
  45.1 2.7 %forward.6 = bf16[2,256,512]{2,1,0:T(8,128)(2,1)S(1)} custom-call(s32[16]{0:T(128)S(1)} %stack.88.order_ref, bf16[256,3584]{1,0:T(8,128)(2,1)S(1)} %get-tuple-element.74.refs_0_, bf16[256,128]{1,0:T(8,128)(2,1)S(1)} %get-tuple-element.75.refs_1_, bf16[64,8192]{1,0:T(8,128)(2,1)S(1)} %copy-done.1, ...), custom_call_target="tpu_custom_call" | custom-call | flops 1048576 | bytes 1048576 | tf_op jit(solution)/shard_map/forward/pallas_call | solution.py:158
  47.8 2.5 %collective-permute-done.9 = f32[24,512]{1,0:T(8,128)S(1)} collective-permute-done((f32[24,512]{1,0:T(8,128)S(1)}, f32[24,512]{1,0:T(8,128)S(1)}, u32[]{:S(2)}, u32[]{:S(2)}) %collective-permute-start.9) | collective-permute-done | bytes 49184 | tf_op jit(solution)/shard_map/ppermute | solution.py:323
  50.3 0.0 collective-permute-done.11.refs_7_
  50.3 0.0 collective-permute-done.10
  50.3 0.1 add_convert_fusion
  50.5 0.6 collective-permute-start.14
  51.2 0.8 collective-permute-start.16
  52.0 2.7 %forward.7 = bf16[2,256,512]{2,1,0:T(8,128)(2,1)S(1)} custom-call(s32[16]{0:T(128)S(1)} %stack.88.order_ref, bf16[256,3584]{1,0:T(8,128)(2,1)S(1)} %get-tuple-element.74.refs_0_, bf16[256,128]{1,0:T(8,128)(2,1)S(1)} %get-tuple-element.75.refs_1_, bf16[64,8192]{1,0:T(8,128)(2,1)S(1)} %copy-done.1, bf16[3584,512]{1,0:T(8,128)(2,1)S(1)} %get-tuple-element.85.refs_3_.refs_11_, ...), custom_call_target="tpu_custom_call" | custom-call | flops 1048576 | bytes 1048576 | tf_op jit(solution)/shard_map/forward/pallas_call | solution.py:158
  54.7 5.3 %backward.2 = (f32[128,1280]{1,0:T(8,128)S(1)}, bf16[128,1280]{1,0:T(8,128)(2,1)S(1)}, bf16[256,4096]{1,0:T(8,128)(2,1)S(1)}, f32[256,64]{1,0:T(8,128)S(1)}, f32...) custom-call(s32[16]{0:T(128)S(1)} %stack.88.order_ref, bf16[272,512]{1,0:T(8,128)(2,1)S(1)} %own_block.1.refs_0_, ...), custom_call_target="tpu_custom_call" | custom-call | flops 1048576 | bytes 1048576 | tf_op jit(solution)/shard_map/backward/pallas_call | solution.py:223
  60.0 0.1 collective-permute-start.12
  60.1 0.0 collective-permute-done.16
  60.1 0.0 collective-permute-done.15
  60.1 1.4 %collective-permute-done.14 = bf16[2,256,512]{2,1,0:T(8,128)(2,1)S(1)} collective-permute-done((bf16[2,256,512]{2,1,0:T(8,128)(2,1)S(1)}, bf16[2,256,512]{2,1,0:T(8,128)(2,1)S(1)}, u32[]{:S(2)}, u32[]{:S(2)}) %collective-permute-start.14) | collective-permute-done | bytes 524320 | tf_op jit(solution)/shard_map/ppermute | solution.py:323
  61.5 0.2 convert_add_fusion
  61.8 0.5 collective-permute-start.18
  62.3 0.2 fusion.3
  62.5 0.2 fusion.up_ref
  62.7 0.1 collective-permute-start.17
  62.7 0.5 collective-permute-start.13
  63.2 7.4 %backward.3 = (f32[128,2304]{1,0:T(8,128)S(1)}, bf16[128,2304]{1,0:T(8,128)(2,1)S(1)}) custom-call(s32[16]{0:T(128)S(1)} %stack.88.order_ref, bf16[256,4096]{1,0:T(8,128)(2,1)S(1)} %get-tuple-element.104.refs_0_, f32[256,64]{1,0:T(8,128)S(1)} %get-tuple-element.94.refs_1_.proj_ref, bf16[64,3584]{1,0:T(8,128)(2,1)S(1)} %bitcast.40, ...), custom_call_target="tpu_custom_call" | custom-call | flops 1048576 | bytes 1048576 | tf_op jit(solution)/shard_map/backward/pallas_call | solution.py:223
  70.7 0.0 collective-permute-done.13.from_ref
  70.7 5.7 %collective-permute-done.18 = bf16[256,512]{1,0:T(8,128)(2,1)S(1)} collective-permute-done((bf16[256,512]{1,0:T(8,128)(2,1)S(1)}, bf16[256,512]{1,0:T(8,128)(2,1)S(1)}, u32[]{:S(2)}, u32[]{:S(2)}) %collective-permute-start.18) | collective-permute-done | bytes 262176 | tf_op jit(solution)/shard_map/ppermute | solution.py:323
  76.4 0.1 multiply_reduce_fusion
  76.6 0.6 collective-permute-start.20
  77.2 0.1 collective-permute-start.21
  77.2 2.0 %weights.1 = (f32[64,3584]{1,0:T(8,128)}, f32[64,1024]{1,0:T(8,128)}) custom-call(s32[16]{0:T(128)S(1)} %stack.88.order_ref, f32[256,64]{1,0:T(8,128)S(1)} %get-tuple-element.94.refs_1_.proj_ref, f32[256,64]{1,0:T(8,128)S(1)} %collective-permute-done.13.from_ref, bf16[128,3584]{1,0:T(8,128)(2,1)S(1)} %copy-done.5, ...), custom_call_target="tpu_custom_call" | custom-call | flops 1048576 | bytes 1048576 | tf_op jit(solution)/shard_map/weights/pallas_call | solution.py:277
  79.2 0.0 collective-permute-done.20.m_other_ref
  79.2 0.0 collective-permute-done.19.rb_ref
  79.2 1.8 %tokens.1 = (bf16[128,3584]{1,0:T(8,128)(2,1)}, bf16[128,1024]{1,0:T(8,128)(2,1)}, f32[8,128]{1,0:T(8,128)}) custom-call(s32[16]{0:T(128)S(1)} %stack.88.order_ref, f32[128,1280]{1,0:T(8,128)S(1)} %get-tuple-element.92.ga_ref, bf16[128,1280]{1,0:T(8,128)(2,1)S(1)} %collective-permute-done.12.ra_ref, f32[128,2304]{1,0:T(8,128)S(1)} %get-tuple-element.107.gb_ref, ...), custom_call_target="tpu_custom_call" | custom-call | flops 1048576 | bytes 1048576 | tf_op jit(solution)/shard_map/tokens/pallas_call | solution.py:277
  (33 shorter events, 0.2 us)
Async XLA Ops:
  0.6 1.9 %collective-permute-start = (bf16[128,1024]{1,0:T(8,128)(2,1)}, bf16[128,1024]{1,0:T(8,128)(2,1)S(1)}, u32[]{:S(2)}, u32[]{:S(2)}) collective-permute-start(bf16[128,1024]{1,0:T(8,128)(2,1)} %own_ref.2), channel_id=1, source_target_pairs={{0,1},{1,0},{2,3},{3,2},{4,5},{5,4},{6,7},{7,6},{8,9},{9,8},{10,11... | collective-permute-start | bytes 786440 | tf_op jit(solution)/shard_map/ppermute | solution.py:318
  1.1 27.5 %collective-permute-start.6 = (bf16[128,3584]{1,0:T(8,128)(2,1)}, bf16[128,3584]{1,0:T(8,128)(2,1)S(1)}, u32[]{:S(2)}, u32[]{:S(2)}) collective-permute-start(bf16[128,3584]{1,0:T(8,128)(2,1)} %own_ref.3), channel_id=1, source_target_pairs={{0,1},{1,0},{2,3},{3,2},{4,5},{5,4},{6,7},{7,6},{8,9},{9,8},{10,11... | collective-permute-start | bytes 2752520 | tf_op jit(solution)/shard_map/ppermute | solution.py:318
  2.5 0.9 %copy-start.8 = (bf16[128,1024]{1,0:T(8,128)(2,1)S(1)}, bf16[128,1024]{1,0:T(8,128)(2,1)}, u32[]{:S(2)}) copy-start(bf16[128,1024]{1,0:T(8,128)(2,1)} %own_ref.2) | copy-start | bytes 786436
  4.0 21.9 %collective-permute-start.3 = (bf16[272,512]{1,0:T(8,128)(2,1)S(1)}, bf16[272,512]{1,0:T(8,128)(2,1)S(1)}, u32[]{:S(2)}, u32[]{:S(2)}) collective-permute-start(bf16[272,512]{1,0:T(8,128)(2,1)S(1)} %own_block.1.refs_0_), channel_id=1, source_target_pairs={{0,8},{1,9},{2,10},{3,11},{4,12},{5,13},{6,14},{7,15},{8,0},{9,1},... | collective-permute-start | bytes 835592 | tf_op jit(solution)/shard_map/ppermute | solution.py:323
  8.1 17.9 %collective-permute-start.2 = (bf16[272,512]{1,0:T(8,128)(2,1)S(1)}, bf16[272,512]{1,0:T(8,128)(2,1)S(1)}, u32[]{:S(2)}, u32[]{:S(2)}) collective-permute-start(bf16[272,512]{1,0:T(8,128)(2,1)S(1)} %own_block.1.refs_0_), channel_id=1, source_target_pairs={{0,4},{1,3},{2,6},{3,1},{4,0},{5,7},{6,2},{7,5},{8,12},{9,11},{10,... | collective-permute-start | bytes 835592 | tf_op jit(solution)/shard_map/ppermute | solution.py:323
  9.6 16.3 %collective-permute-start.1 = (bf16[272,512]{1,0:T(8,128)(2,1)S(1)}, bf16[272,512]{1,0:T(8,128)(2,1)S(1)}, u32[]{:S(2)}, u32[]{:S(2)}) collective-permute-start(bf16[272,512]{1,0:T(8,128)(2,1)S(1)} %own_block.1.refs_0_), channel_id=1, source_target_pairs={{0,2},{1,5},{2,0},{3,7},{4,6},{5,1},{6,4},{7,3},{8,10},{9,13},{10,... | collective-permute-start | bytes 835592 | tf_op jit(solution)/shard_map/ppermute | solution.py:323
  11.1 1.2 %copy-start = (bf16[64,8192]{1,0:T(8,128)(2,1)S(1)}, bf16[64,8192]{1,0:T(8,128)(2,1)}, u32[]{:S(2)}) copy-start(bf16[64,8192]{1,0:T(8,128)(2,1)} %refs_9_.1) | copy-start | bytes 3145732
  12.4 1.2 %copy-start.4 = (bf16[128,3584]{1,0:T(8,128)(2,1)S(1)}, bf16[128,3584]{1,0:T(8,128)(2,1)}, u32[]{:S(2)}) copy-start(bf16[128,3584]{1,0:T(8,128)(2,1)} %own_ref.3) | copy-start | bytes 2752516
  13.5 1.0 %copy-start.6 = (bf16[3584,64]{0,1:T(8,128)(2,1)S(1)}, bf16[3584,64]{0,1:T(8,128)(2,1)}, u32[]{:S(2)}) copy-start(bf16[3584,64]{0,1:T(8,128)(2,1)} %param.8) | copy-start | bytes 1376260
  14.6 14.0 %copy-start.1 = (bf16[64,8192]{1,0:T(8,128)(2,1)S(1)}, bf16[64,8192]{1,0:T(8,128)(2,1)}, u32[]{:S(2)}) copy-start(bf16[64,8192]{1,0:T(8,128)(2,1)} %refs_9_.1) | copy-start | bytes 3145732
  14.6 14.0 %copy-start.5 = (bf16[128,3584]{1,0:T(8,128)(2,1)S(1)}, bf16[128,3584]{1,0:T(8,128)(2,1)}, u32[]{:S(2)}) copy-start(bf16[128,3584]{1,0:T(8,128)(2,1)} %own_ref.3) | copy-start | bytes 2752516
  14.6 14.0 %copy-start.7 = (bf16[3584,64]{0,1:T(8,128)(2,1)S(1)}, bf16[3584,64]{0,1:T(8,128)(2,1)}, u32[]{:S(2)}) copy-start(bf16[3584,64]{0,1:T(8,128)(2,1)} %param.8) | copy-start | bytes 1376260
  25.9 14.4 %copy-start.2 = (bf16[3584,512]{1,0:T(8,128)(2,1)}, bf16[3584,512]{1,0:T(8,128)(2,1)S(1)}, u32[]{:S(2)}) copy-start(bf16[3584,512]{1,0:T(8,128)(2,1)S(1)} %get-tuple-element.76.refs_3_.refs_15_.refs_7_) | copy-start | bytes 11010052
  25.9 11.4 %collective-permute-start.5 = (bf16[272,512]{1,0:T(8,128)(2,1)S(1)}, bf16[272,512]{1,0:T(8,128)(2,1)S(1)}, u32[]{:S(2)}, u32[]{:S(2)}) collective-permute-start(bf16[272,512]{1,0:T(8,128)(2,1)S(1)} %collective-permute-done.3.refs_1_), channel_id=1, source_target_pairs={{0,4},{1,3},{2,6},{3,1},{4,0},{5,7},{6,2},{7,5},{8,12},{9,11},{10,... | collective-permute-start | bytes 835592 | tf_op jit(solution)/shard_map/ppermute | solution.py:323
  26.5 17.6 %collective-permute-start.8 = (bf16[2,272,512]{2,1,0:T(8,128)(2,1)S(1)}, bf16[2,272,512]{2,1,0:T(8,128)(2,1)S(1)}, u32[]{:S(2)}, u32[]{:S(2)}) collective-permute-start(bf16[2,272,512]{2,1,0:T(8,128)(2,1)S(1)} %pad_maximum_fusion), channel_id=1, source_target_pairs={{0,2},{1,5},{2,0},{3,7},{4,6},{5,1},{6,4},{7,3},{8,10},{9,13},{10,... | collective-permute-start | bytes 1671176 | tf_op jit(solution)/shard_map/ppermute | solution.py:323
  27.1 10.2 %collective-permute-start.4 = (f32[24,512]{1,0:T(8,128)S(1)}, f32[24,512]{1,0:T(8,128)S(1)}, u32[]{:S(2)}, u32[]{:S(2)}) collective-permute-start(f32[24,512]{1,0:T(8,128)S(1)} %get-tuple-element.66), channel_id=1, source_target_pairs={{0,2},{1,5},{2,0},{3,7},{4,6},{5,1},{6,4},{7,3},{8,10},{9,13},{10,... | collective-permute-start | bytes 147464 | tf_op jit(solution)/shard_map/ppermute | solution.py:323
  37.3 13.0 %collective-permute-start.10 = (bf16[2,256,512]{2,1,0:T(8,128)(2,1)S(1)}, bf16[2,256,512]{2,1,0:T(8,128)(2,1)S(1)}, u32[]{:S(2)}, u32[]{:S(2)}) collective-permute-start(bf16[2,256,512]{2,1,0:T(8,128)(2,1)S(1)} %get-tuple-element.79), channel_id=1, source_target_pairs={{0,2},{1,5},{2,0},{3,7},{4,6},{5,1},{6,4},{7,3},{8,10},{9,13},{10,... | collective-permute-start | bytes 1572872 | tf_op jit(solution)/shard_map/ppermute | solution.py:323
  37.9 12.5 %collective-permute-start.11 = (bf16[272,512]{1,0:T(8,128)(2,1)S(1)}, bf16[272,512]{1,0:T(8,128)(2,1)S(1)}, u32[]{:S(2)}, u32[]{:S(2)}) collective-permute-start(bf16[272,512]{1,0:T(8,128)(2,1)S(1)} %collective-permute-done.5.refs_3_), channel_id=1, source_target_pairs={{0,2},{1,5},{2,0},{3,7},{4,6},{5,1},{6,4},{7,3},{8,10},{9,13},{10,... | collective-permute-start | bytes 835592 | tf_op jit(solution)/shard_map/ppermute | solution.py:323
  39.4 4.7 %collective-permute-start.7 = (f32[24,512]{1,0:T(8,128)S(1)}, f32[24,512]{1,0:T(8,128)S(1)}, u32[]{:S(2)}, u32[]{:S(2)}) collective-permute-start(f32[24,512]{1,0:T(8,128)S(1)} %add.56), channel_id=1, source_target_pairs={{0,4},{1,3},{2,6},{3,1},{4,0},{5,7},{6,2},{7,5},{8,12},{9,11},{10,... | collective-permute-start | bytes 147464 | tf_op jit(solution)/shard_map/ppermute | solution.py:323
  44.1 6.2 %collective-permute-start.9 = (f32[24,512]{1,0:T(8,128)S(1)}, f32[24,512]{1,0:T(8,128)S(1)}, u32[]{:S(2)}, u32[]{:S(2)}) collective-permute-start(f32[24,512]{1,0:T(8,128)S(1)} %add.57), channel_id=1, source_target_pairs={{0,8},{1,9},{2,10},{3,11},{4,12},{5,13},{6,14},{7,15},{8,0},{9,1},... | collective-permute-start | bytes 147464 | tf_op jit(solution)/shard_map/ppermute | solution.py:323
  44.5 15.6 %collective-permute-start.15 = (bf16[2,256,512]{2,1,0:T(8,128)(2,1)S(1)}, bf16[2,256,512]{2,1,0:T(8,128)(2,1)S(1)}, u32[]{:S(2)}, u32[]{:S(2)}) collective-permute-start(bf16[2,256,512]{2,1,0:T(8,128)(2,1)S(1)} %forward.5), channel_id=1, source_target_pairs={{0,2},{1,5},{2,0},{3,7},{4,6},{5,1},{6,4},{7,3},{8,10},{9,13},{10,... | collective-permute-start | bytes 1572872 | tf_op jit(solution)/shard_map/ppermute | solution.py:323
  50.5 11.0 %collective-permute-start.14 = (bf16[2,256,512]{2,1,0:T(8,128)(2,1)S(1)}, bf16[2,256,512]{2,1,0:T(8,128)(2,1)S(1)}, u32[]{:S(2)}, u32[]{:S(2)}) collective-permute-start(bf16[2,256,512]{2,1,0:T(8,128)(2,1)S(1)} %add_convert_fusion), channel_id=1, source_target_pairs={{0,4},{1,3},{2,6},{3,1},{4,0},{5,7},{6,2},{7,5},{8,12},{9,11},{10,... | collective-permute-start | bytes 1572872 | tf_op jit(solution)/shard_map/ppermute | solution.py:323
  51.2 8.9 %collective-permute-start.16 = (f32[16,512]{1,0:T(8,128)S(1)}, f32[16,512]{1,0:T(8,128)S(1)}, u32[]{:S(2)}, u32[]{:S(2)}) collective-permute-start(f32[16,512]{1,0:T(8,128)S(1)} %slice.85), channel_id=1, source_target_pairs={{0,1},{1,0},{2,3},{3,2},{4,5},{5,4},{6,7},{7,6},{8,9},{9,8},{10,11... | collective-permute-start | bytes 98312 | tf_op jit(solution)/shard_map/ppermute | solution.py:318
  52.0 2.7 %copy-start.3 = (bf16[3584,512]{1,0:T(8,128)(2,1)S(1)}, bf16[3584,512]{1,0:T(8,128)(2,1)}, u32[]{:S(2)}) copy-start(bf16[3584,512]{1,0:T(8,128)(2,1)} %copy-done.2) | copy-start | bytes 11010052
  60.0 10.6 %collective-permute-start.12 = (bf16[128,1280]{1,0:T(8,128)(2,1)S(1)}, bf16[128,1280]{1,0:T(8,128)(2,1)S(1)}, u32[]{:S(2)}, u32[]{:S(2)}) collective-permute-start(bf16[128,1280]{1,0:T(8,128)(2,1)S(1)} %get-tuple-element.93), channel_id=1, source_target_pairs={{0,1},{1,0},{2,3},{3,2},{4,5},{5,4},{6,7},{7,6},{8,9},{9,8},{10,11... | collective-permute-start | bytes 983048 | tf_op jit(solution)/shard_map/ppermute | solution.py:318
  61.8 14.6 %collective-permute-start.18 = (bf16[256,512]{1,0:T(8,128)(2,1)S(1)}, bf16[256,512]{1,0:T(8,128)(2,1)S(1)}, u32[]{:S(2)}, u32[]{:S(2)}) collective-permute-start(bf16[256,512]{1,0:T(8,128)(2,1)S(1)} %fusion.2), channel_id=1, source_target_pairs={{0,8},{1,9},{2,10},{3,11},{4,12},{5,13},{6,14},{7,15},{8,0},{9,1},... | collective-permute-start | bytes 786440 | tf_op jit(solution)/shard_map/ppermute | solution.py:323
  62.7 8.0 %collective-permute-start.17 = (f32[64,512]{1,0:T(8,128)S(1)}, f32[64,512]{1,0:T(8,128)S(1)}, u32[]{:S(2)}, u32[]{:S(2)}) collective-permute-start(f32[64,512]{1,0:T(8,128)S(1)} %fusion.up_ref), channel_id=1, source_target_pairs={{0,1},{1,0},{2,3},{3,2},{4,5},{5,4},{6,7},{7,6},{8,9},{9,8},{10,11... | collective-permute-start | bytes 393224 | tf_op jit(solution)/shard_map/ppermute | solution.py:318
  62.7 7.9 %collective-permute-start.13 = (f32[256,64]{1,0:T(8,128)S(1)}, f32[256,64]{1,0:T(8,128)S(1)}, u32[]{:S(2)}, u32[]{:S(2)}) collective-permute-start(f32[256,64]{1,0:T(8,128)S(1)} %get-tuple-element.94.refs_1_.proj_ref), channel_id=1, source_target_pairs={{0,1},{1,0},{2,3},{3,2},{4,5},{5,4},{6,7},{7,6},{8,9},{9,8},{10,11... | collective-permute-start | bytes 196616 | tf_op jit(solution)/shard_map/ppermute | solution.py:318
  76.4 2.8 %collective-permute-start.19 = (bf16[128,2304]{1,0:T(8,128)(2,1)S(1)}, bf16[128,2304]{1,0:T(8,128)(2,1)S(1)}, u32[]{:S(2)}, u32[]{:S(2)}) collective-permute-start(bf16[128,2304]{1,0:T(8,128)(2,1)S(1)} %get-tuple-element.108), channel_id=1, source_target_pairs={{0,1},{1,0},{2,3},{3,2},{4,5},{5,4},{6,7},{7,6},{8,9},{9,8},{10,11... | collective-permute-start | bytes 1769480 | tf_op jit(solution)/shard_map/ppermute | solution.py:318
  76.6 2.7 %collective-permute-start.20 = (bf16[128,512]{1,0:T(8,128)(2,1)S(1)}, bf16[128,512]{1,0:T(8,128)(2,1)S(1)}, u32[]{:S(2)}, u32[]{:S(2)}) collective-permute-start(bf16[128,512]{1,0:T(8,128)(2,1)S(1)} %slice.88), channel_id=1, source_target_pairs={{0,1},{1,0},{2,3},{3,2},{4,5},{5,4},{6,7},{7,6},{8,9},{9,8},{10,11... | collective-permute-start | bytes 393224 | tf_op jit(solution)/shard_map/ppermute | solution.py:318
  77.2 2.1 %collective-permute-start.21 = (f32[1,512]{1,0:T(1,128)S(1)}, f32[1,512]{1,0:T(1,128)S(1)}, u32[]{:S(2)}, u32[]{:S(2)}) collective-permute-start(f32[1,512]{1,0:T(1,128)S(1)} %slice_divide_fusion.g_ref), channel_id=1, source_target_pairs={{0,1},{1,0},{2,3},{3,2},{4,5},{5,4},{6,7},{7,6},{8,9},{9,8},{10,11... | collective-permute-start | bytes 6152 | tf_op jit(solution)/shard_map/ppermute | solution.py:318

commit v10 on v9

--- a/solution.py
+++ b/solution.py
@@ -12,7 +12,7 @@
 pad_rows = 16
 vmem_bytes = 8 * 1024 * 1024
 f32, bf16 = jnp.float32, jnp.bfloat16
-small_cost = pl.CostEstimate(flops=1 << 20, bytes_accessed=1 << 20, transcendentals=0)
+small_cost = pl.CostEstimate(flops=0, bytes_accessed=0, transcendentals=0)
 contract_trailing = (((1,), (1,)), ((), ()))
 contract_first = (((0,), (0,)), ((), ()))
 
@@ -261,11 +261,14 @@
     core_halves(order_ref, up_out, up_ref[...], up_other_ref[...], 1)
 
 
-def tokens_kernel(order_ref, ga_ref, ra_ref, gb_ref, rb_ref, m_ref, m_other_ref, g_ref, g_other_ref, *outs):
-    hidden_out, mixed_out, magnitude_out = outs
-    tokens, split = ga_ref.shape
-    hidden_out[:, :split] = (ga_ref[...] + ra_ref[...].astype(f32)).astype(bf16)
-    hidden_out[:, split:] = (gb_ref[...] + rb_ref[...].astype(f32)).astype(bf16)
+def hidden_kernel(order_ref, ga_ref, ra_ref, gb_ref, rb_ref, out_ref):
+    split = ga_ref.shape[1]
+    out_ref[:, :split] = (ga_ref[...] + ra_ref[...].astype(f32)).astype(bf16)
+    out_ref[:, split:] = (gb_ref[...] + rb_ref[...].astype(f32)).astype(bf16)
+
+
+def mixed_kernel(order_ref, m_ref, m_other_ref, g_ref, g_other_ref, mixed_out, magnitude_out):
+    tokens = m_other_ref.shape[0]
     core_halves(order_ref, mixed_out, m_ref[:tokens, :], m_other_ref[...], 1)
     rows = g_ref.shape[1] // 128
     stacked = [jnp.concatenate([r[:, i * 128 : (i + 1) * 128] for i in range(rows)]) for r in (g_ref, g_other_ref)]
@@ -297,16 +300,19 @@
     return finish(kernel, "weights", shapes, order, proj, from_sibling, own, other, up_half, up_other)
 
 
-def finish_tokens(order, grad_a, got_a, grad_b, got_b, mixed, mixed_other, magnitude, magnitude_other):
+def finish_hidden(order, grad_a, got_a, grad_b, got_b):
+    tokens = grad_a.shape[0]
+    shape = jax.ShapeDtypeStruct((tokens, grad_a.shape[1] + grad_b.shape[1]), bf16)
+    return finish(hidden_kernel, "hidden", [shape], order, grad_a, got_a, grad_b, got_b)[0]
+
+
+def finish_mixed(order, mixed, mixed_other, magnitude, magnitude_other):
     tokens, half = mixed_other.shape
-    rows = grad_a.shape[1] + grad_b.shape[1]
     shapes = [
-        jax.ShapeDtypeStruct((tokens, rows), bf16),
         jax.ShapeDtypeStruct((tokens, 2 * half), bf16),
         jax.ShapeDtypeStruct((2 * half // 128, 128), f32),
     ]
-    operands = (grad_a, got_a, grad_b, got_b, mixed, mixed_other, magnitude, magnitude_other)
-    return finish(tokens_kernel, "tokens", shapes, order, *operands)
+    return finish(mixed_kernel, "mixed", shapes, order, mixed, mixed_other, magnitude, magnitude_other)
 
 
 def split_columns(hidden, weight, down, up, magnitude, cotangent):
@@ -316,7 +322,7 @@
     rows = weight.shape[0]
     me, core = lax.axis_index("tensor"), lax.axis_index("dp")
     swap = lambda x: lax.ppermute(x, "dp", [(0, 1), (1, 0)])
-    orders = [[1, 2, 4], [2, 1, 4]]
+    orders = [[1, 2, 4], [2, 4, 1]]
 
     def send(x, k):
         pairs = [(2 * t + c, 2 * (t ^ orders[c][k]) + c) for t in range(n) for c in range(2)]
@@ -349,27 +355,30 @@
 
     run_load = functools.partial(load, at=at, up=up, weight=weight, half=half)
     block, order = tie((block, order))
-    *held, stats = run_load(tuple(range(n)), order, own=hidden)
-    near, far = held[: n // 2], held[n // 2 :]
-    cots[0b100], cots[0b010], cots[0b001], stats = tie((cots[0b100], cots[0b010], cots[0b001], stats))
+    *far_pair, stats = run_load((0b110, 0b111), order, own=hidden)
+    cots[0b001], cots[0b010], stats = tie((cots[0b001], cots[0b010], stats))
     cots[0b011] = send(cots[0b001], 1)
     pair = send(jnp.stack([cots[0b001], cots[0b010]]), 0)
+    *held, stats = run_load(tuple(range(n - 2)), order, before=stats)
+    held = held + far_pair
+    near, far = held[: n // 2], held[n // 2 :]
+    cots[0b100], cots[0b011], pair, stats = tie((cots[0b100], cots[0b011], pair, stats))
+    cots[0b101], cots[0b110] = pair[0], pair[1]
     got = send(stats, 0)
+    cots[0b111] = send(cots[0b011], 0)
     far1, lhs, adapter = forward((0b110, 0b111), order, far[2:], up, first=(hidden, hidden_other, at))
     run = lambda order, vs, held: forward(vs, order, held, up, later=(lhs, adapter))[0]
-    got, cots[0b011], far1, order = tie((got, cots[0b011], far1, order))
-    cots[0b111] = send(cots[0b011], 0)
+    got, cots[0b111], far1, order = tie((got, cots[0b111], far1, order))
     stats = stats + got
     got = send(stats, 1)
     from1 = send(far1, 0)
     far0 = run(order, (0b100, 0b101), far[:2])
-    got, pair, far0, order = tie((got, pair, far0, order))
-    cots[0b101], cots[0b110] = pair[0], pair[1]
+    got, far0, order = tie((got, far0, order))
     stats = stats + got
     got = send(stats, 2)
     from0 = send(far0, 0)
     near1 = run(order, (0b010, 0b011), near[2:])
-    got, from1, cots[0b111], near1, order = tie((got, from1, cots[0b111], near1, order))
+    got, from1, near1, order = tie((got, from1, near1, order))
     stats = stats + got
     arrived = send((near1.astype(f32) + from1.astype(f32)).astype(bf16), 1)
     lowrank_rows = stats[n:]
@@ -399,19 +408,21 @@
     )
     up_other = swap(up_half)
     grad_b, other_b = backward(order, many, bands - many, band, at, held, later=(scaled, proj))
-    got_a, from_sibling, up_other, last, other_b = tie((got_a, from_sibling, up_other, last, other_b))
+    got_a, from_sibling, up_other, other_b = tie((got_a, from_sibling, up_other, other_b))
     got_b = swap(other_b)
 
+    down_weight_gradient, up_weight_gradient = finish_weights(
+        order, proj, from_sibling, hidden, hidden_other, up_half, up_other
+    )
+
+    last, down_weight_gradient = tie((last, down_weight_gradient))
     unscaled = kept[0] + last.astype(f32)
     mixed = (unscaled * scales[1]).astype(bf16)
     magnitude_half = jnp.sum(block[: 2 * tokens].astype(f32) * unscaled, axis=0, keepdims=True) / scales[0:1]
     mixed_other, magnitude_other = swap(mixed[tokens:]), swap(magnitude_half)
-    down_weight_gradient, up_weight_gradient = finish_weights(
-        order, proj, from_sibling, hidden, hidden_other, up_half, up_other
-    )
-    hidden_gradient, mixed, grad_magnitude = finish_tokens(
-        order, grad_a, got_a, grad_b, got_b, mixed, mixed_other, magnitude_half, magnitude_other
-    )
+    hidden_gradient = finish_hidden(order, grad_a, got_a, grad_b, got_b)
+    mixed_other, magnitude_other, hidden_gradient = tie((mixed_other, magnitude_other, hidden_gradient))
+    mixed, grad_magnitude = finish_mixed(order, mixed, mixed_other, magnitude_half, magnitude_other)
     down_weight_gradient, grad_magnitude = down_weight_gradient.T, grad_magnitude.reshape(2 * half)
     return (mixed, hidden_gradient, down_weight_gradient, up_weight_gradient, grad_magnitude)
 

time: 81.4 us -> 91.1 us (1.12)
  starting transfers between devices: 17.4 us -> 26 us
  Pallas kernels: 40.7 us -> 44.8 us
  waiting for transfers between devices: 15.6 us -> 12.7 us
    ppermute x13, starting transfers between devices: 14.7 us -> 20 us  [send(): return lax.ppermute(x, ('tensor', 'dp'), pairs)]
    ppermute x9, starting transfers between devices: 2.69 us -> 6.04 us  [split_columns(): swap = lambda x: lax.ppermute(x, 'dp', [(0, 1), (1, 0)])]
    ppermute x13, waiting for transfers between devices: 15.3 us -> 12.3 us  [send(): return lax.ppermute(x, ('tensor', 'dp'), pairs)]
    pallas_call x1 -> x2, Pallas kernels: 11.3 us -> 14.2 us  [load(): pl.pallas_call(functools.partial(load_kernel, tokens, rank, n, vs, first)...]
    pallas_call x2 -> x3, Pallas kernels: 3.8 us -> 4.92 us  [finish(): pl.pallas_call(kernel, grid_spec=pltpu.PrefetchScalarGridSpec(num_scalar_...]
  transfers between devices with their start and end apart: 22 -> 22, of which waited for: 6 -> 6; matrix products, arithmetic and copies ran while one was open for 2% -> 2% of each run, Pallas kernels for 48% -> 47%
where the time goes in v10:
time: 91.1 us; the launch traced here: 90.8 us
  Pallas kernels  44.8 us (49%)
  starting transfers between devices  26 us (29%)
  waiting for transfers between devices  12.7 us (14%)
  local copies, waits for them, and re-layouts  4.67 us (5%)
  other arithmetic  1.34 us (1%)
    ppermute x13, starting transfers between devices, send(): return lax.ppermute(x, ('tensor', 'dp'), pairs)  20 us
    pallas_call x2, Pallas kernels, load(): pl.pallas_call(functools.partial(load_kernel, tokens, rank, n, vs, first)...  14.2 us
    pallas_call x2, Pallas kernels, backward(): pl.pallas_call(functools.partial(backward_kernel, tokens, n, start, band,...  12.7 us
    pallas_call x4, Pallas kernels, forward(): pl.pallas_call(functools.partial(forward_kernel, tokens, rank, vs, later...  12.3 us
    ppermute x13, waiting for transfers between devices, send(): return lax.ppermute(x, ('tensor', 'dp'), pairs)  12.3 us
    ppermute x9, starting transfers between devices, split_columns(): swap = lambda x: lax.ppermute(x, 'dp', [(0, 1), (1, 0)])  6.04 us
    pallas_call x3, Pallas kernels, finish(): pl.pallas_call(kernel, grid_spec=pltpu.PrefetchScalarGridSpec(num_scalar_...  4.92 us
    unnamed x18, local copies, waits for them, and re-layouts  4.39 us
  transfers between devices with their start and end apart: 22, of which 6 were waited for; matrix products, arithmetic and copies ran while one was open for 2% of the time, Pallas kernels for 47%

profile of v10, /device:TPU:0, one launch (start us, length us, event | category | flops | bytes accessed | tf_op | source)
XLA Modules:
  0.0 90.8 jit_solution(4597707084446118312)
XLA Ops:
  0.6 0.5 collective-permute-start
  1.1 0.7 reduce-precision_convert_fusion.1
  1.9 0.1 pad.13.clone
  2.0 0.1 stack.88.order_ref
  2.1 0.1 maximum_maximum_fusion.magnitude_ref
  2.1 0.4 collective-permute-done.other_ref
  2.5 0.9 %copy-done.8 = bf16[128,1024]{1,0:T(8,128)(2,1)S(1)} copy-done((bf16[128,1024]{1,0:T(8,128)(2,1)S(1)}, bf16[128,1024]{1,0:T(8,128)(2,1)}, u32[]{:S(2)}) %copy-start.8) | copy-done | bytes 262168
  3.5 0.6 own_block.1.refs_0_
  4.0 4.0 %collective-permute-start.2 = (bf16[272,512]{1,0:T(8,128)(2,1)S(1)}, bf16[272,512]{1,0:T(8,128)(2,1)S(1)}, u32[]{:S(2)}, u32[]{:S(2)}) collective-permute-start(bf16[272,512]{1,0:T(8,128)(2,1)S(1)} %own_block.1.refs_0_), channel_id=1, source_target_pairs={{0,8},{1,3},{2,10},{3,1},{4,12},{5,7},{6,14},{7,5},{8,0},{9,11},{1... | collective-permute-start | bytes 835592 | tf_op jit(solution)/shard_map/ppermute | solution.py:329
  8.1 1.6 %collective-permute-start.3 = (bf16[272,512]{1,0:T(8,128)(2,1)S(1)}, bf16[272,512]{1,0:T(8,128)(2,1)S(1)}, u32[]{:S(2)}, u32[]{:S(2)}) collective-permute-start(bf16[272,512]{1,0:T(8,128)(2,1)S(1)} %own_block.1.refs_0_), channel_id=1, source_target_pairs={{0,4},{1,9},{2,6},{3,11},{4,0},{5,13},{6,2},{7,15},{8,12},{9,1},{1... | collective-permute-start | bytes 835592 | tf_op jit(solution)/shard_map/ppermute | solution.py:329
  9.6 0.0 collective-permute-start.8
  9.6 1.2 %copy-done = bf16[64,8192]{1,0:T(8,128)(2,1)S(1)} copy-done((bf16[64,8192]{1,0:T(8,128)(2,1)S(1)}, bf16[64,8192]{1,0:T(8,128)(2,1)}, u32[]{:S(2)}) %copy-start) | copy-done | bytes 1048600
  10.9 1.0 %copy-done.4 = bf16[3584,64]{0,1:T(8,128)(2,1)S(1)} copy-done((bf16[3584,64]{0,1:T(8,128)(2,1)S(1)}, bf16[3584,64]{0,1:T(8,128)(2,1)}, u32[]{:S(2)}) %copy-start.4) | copy-done | bytes 458776
  11.9 1.2 %copy-done.6 = bf16[128,3584]{1,0:T(8,128)(2,1)S(1)} copy-done((bf16[128,3584]{1,0:T(8,128)(2,1)S(1)}, bf16[128,3584]{1,0:T(8,128)(2,1)}, u32[]{:S(2)}) %copy-start.6) | copy-done | bytes 917528
  13.1 5.0 %load.2 = (bf16[3584,512]{1,0:T(8,128)(2,1)S(1)}, bf16[3584,512]{1,0:T(8,128)(2,1)S(1)}, f32[24,512]{1,0:T(8,128)S(1)}) custom-call(s32[16]{0:T(128)S(1)} %stack.88.order_ref, bf16[128,3584]{1,0:T(8,128)(2,1)S(1)} %copy-done.6, bf16[64,3584]{1,0:T(8,128)(2,1)S(1)} %bitcast.37, bf16[64,8192]{1,0:T(8,128)(2,1)S(1)} %copy-done, bf16[3584,8192]{1,0:T(8,128)(2,1)} %w_hbm.3), custom_call_target="tpu_custom_call" | custom-call | tf_op jit(solution)/shard_map/load/pallas_call | solution.py:116
  18.1 2.8 %collective-permute-done.2.refs_1_ = bf16[272,512]{1,0:T(8,128)(2,1)S(1)} collective-permute-done((bf16[272,512]{1,0:T(8,128)(2,1)S(1)}, bf16[272,512]{1,0:T(8,128)(2,1)S(1)}, u32[]{:S(2)}, u32[]{:S(2)}) %collective-permute-start.2) | collective-permute-done | bytes 278560 | tf_op jit(solution)/shard_map/ppermute | solution.py:329
  20.9 0.0 collective-permute-done.3.refs_2_
  20.9 0.1 pad_maximum_fusion
  20.9 0.0 copy-start.7
  21.0 1.9 %collective-permute-start.5 = (bf16[2,272,512]{2,1,0:T(8,128)(2,1)S(1)}, bf16[2,272,512]{2,1,0:T(8,128)(2,1)S(1)}, u32[]{:S(2)}, u32[]{:S(2)}) collective-permute-start(bf16[2,272,512]{2,1,0:T(8,128)(2,1)S(1)} %pad_maximum_fusion), channel_id=1, source_target_pairs={{0,2},{1,5},{2,0},{3,7},{4,6},{5,1},{6,4},{7,3},{8,10},{9,13},{10,... | collective-permute-start | bytes 1671176 | tf_op jit(solution)/shard_map/ppermute | solution.py:329
  22.9 0.2 collective-permute-start.1
  23.0 1.6 %collective-permute-start.4 = (bf16[272,512]{1,0:T(8,128)(2,1)S(1)}, bf16[272,512]{1,0:T(8,128)(2,1)S(1)}, u32[]{:S(2)}, u32[]{:S(2)}) collective-permute-start(bf16[272,512]{1,0:T(8,128)(2,1)S(1)} %collective-permute-done.2.refs_1_), channel_id=1, source_target_pairs={{0,4},{1,9},{2,6},{3,11},{4,0},{5,13},{6,2},{7,15},{8,12},{9,1},{1... | collective-permute-start | bytes 835592 | tf_op jit(solution)/shard_map/ppermute | solution.py:329
  24.7 9.2 %load.3 = (bf16[3584,512]{1,0:T(8,128)(2,1)S(1)}, bf16[3584,512]{1,0:T(8,128)(2,1)S(1)}, bf16[3584,512]{1,0:T(8,128)(2,1)S(1)}, bf16[3584,512]{1,0:T(8,128)(2,1)...) custom-call(s32[16]{0:T(128)S(1)} %stack.88.order_ref, ...), custom_call_target="tpu_custom_call" | custom-call | tf_op jit(solution)/shard_map/load/pallas_call | solution.py:116
  33.9 0.0 collective-permute-done.1.refs_4_
  33.9 1.8 %collective-permute-done.4.refs_3_ = bf16[272,512]{1,0:T(8,128)(2,1)S(1)} collective-permute-done((bf16[272,512]{1,0:T(8,128)(2,1)S(1)}, bf16[272,512]{1,0:T(8,128)(2,1)S(1)}, u32[]{:S(2)}, u32[]{:S(2)}) %collective-permute-start.4) | collective-permute-done | bytes 278560 | tf_op jit(solution)/shard_map/ppermute | solution.py:329
  35.6 1.2 %collective-permute-start.7 = (bf16[272,512]{1,0:T(8,128)(2,1)S(1)}, bf16[272,512]{1,0:T(8,128)(2,1)S(1)}, u32[]{:S(2)}, u32[]{:S(2)}) collective-permute-start(bf16[272,512]{1,0:T(8,128)(2,1)S(1)} %collective-permute-done.4.refs_3_), channel_id=1, source_target_pairs={{0,2},{1,5},{2,0},{3,7},{4,6},{5,1},{6,4},{7,3},{8,10},{9,13},{10,... | collective-permute-start | bytes 835592 | tf_op jit(solution)/shard_map/ppermute | solution.py:329
  36.8 0.9 collective-permute-start.6
  37.7 0.0 collective-permute-done.8.refs_1_.other_ref
  37.7 4.1 %forward.4 = (bf16[2,256,512]{2,1,0:T(8,128)(2,1)S(1)}, bf16[256,3584]{1,0:T(8,128)(2,1)S(1)}, bf16[256,128]{1,0:T(8,128)(2,1)S(1)}) custom-call(s32[16]{0:T(128)S(1)} %stack.88.order_ref, bf16[128,3584]{1,0:T(8,128)(2,1)S(1)} %copy-done.7, bf16[128,3584]{1,0:T(8,128)(2,1)S(1)} %collective-permute-done.8.refs_1_.other_ref, bf16[64,3584]{1,0:T(8,128)(2,1)S(1)} %bitcast.39, ...), custom_call_target="tpu_custom_call" | custom-call | tf_op jit(solution)/shard_map/forward/pallas_call | solution.py:158
  41.8 0.9 %collective-permute-done.6 = f32[24,512]{1,0:T(8,128)S(1)} collective-permute-done((f32[24,512]{1,0:T(8,128)S(1)}, f32[24,512]{1,0:T(8,128)S(1)}, u32[]{:S(2)}, u32[]{:S(2)}) %collective-permute-start.6) | collective-permute-done | bytes 49184 | tf_op jit(solution)/shard_map/ppermute | solution.py:329
  42.7 1.2 %collective-permute-start.11 = (bf16[2,256,512]{2,1,0:T(8,128)(2,1)S(1)}, bf16[2,256,512]{2,1,0:T(8,128)(2,1)S(1)}, u32[]{:S(2)}, u32[]{:S(2)}) collective-permute-start(bf16[2,256,512]{2,1,0:T(8,128)(2,1)S(1)} %get-tuple-element.87), channel_id=1, source_target_pairs={{0,2},{1,5},{2,0},{3,7},{4,6},{5,1},{6,4},{7,3},{8,10},{9,13},{10,... | collective-permute-start | bytes 1572872 | tf_op jit(solution)/shard_map/ppermute | solution.py:329
  43.9 0.1 collective-permute-start.9
  44.0 2.8 %forward.5 = bf16[2,256,512]{2,1,0:T(8,128)(2,1)S(1)} custom-call(s32[16]{0:T(128)S(1)} %stack.88.order_ref, bf16[256,3584]{1,0:T(8,128)(2,1)S(1)} %get-tuple-element.82.refs_0_, bf16[256,128]{1,0:T(8,128)(2,1)S(1)} %get-tuple-element.83.refs_1_, bf16[64,8192]{1,0:T(8,128)(2,1)S(1)} %copy-done.1, ...), custom_call_target="tpu_custom_call" | custom-call | tf_op jit(solution)/shard_map/forward/pallas_call | solution.py:158
  46.7 1.3 %collective-permute-done.9 = f32[24,512]{1,0:T(8,128)S(1)} collective-permute-done((f32[24,512]{1,0:T(8,128)S(1)}, f32[24,512]{1,0:T(8,128)S(1)}, u32[]{:S(2)}, u32[]{:S(2)}) %collective-permute-start.9) | collective-permute-done | bytes 49184 | tf_op jit(solution)/shard_map/ppermute | solution.py:329
  48.1 3.1 %collective-permute-start.10 = (f32[24,512]{1,0:T(8,128)S(1)}, f32[24,512]{1,0:T(8,128)S(1)}, u32[]{:S(2)}, u32[]{:S(2)}) collective-permute-start(f32[24,512]{1,0:T(8,128)S(1)} %add.57), channel_id=1, source_target_pairs={{0,8},{1,3},{2,10},{3,1},{4,12},{5,7},{6,14},{7,5},{8,0},{9,11},{1... | collective-permute-start | bytes 147464 | tf_op jit(solution)/shard_map/ppermute | solution.py:329
  51.1 1.1 %collective-permute-start.13 = (bf16[2,256,512]{2,1,0:T(8,128)(2,1)S(1)}, bf16[2,256,512]{2,1,0:T(8,128)(2,1)S(1)}, u32[]{:S(2)}, u32[]{:S(2)}) collective-permute-start(bf16[2,256,512]{2,1,0:T(8,128)(2,1)S(1)} %forward.5), channel_id=1, source_target_pairs={{0,2},{1,5},{2,0},{3,7},{4,6},{5,1},{6,4},{7,3},{8,10},{9,13},{10,... | collective-permute-start | bytes 1572872 | tf_op jit(solution)/shard_map/ppermute | solution.py:329
  52.3 2.8 %forward.6 = bf16[2,256,512]{2,1,0:T(8,128)(2,1)S(1)} custom-call(s32[16]{0:T(128)S(1)} %stack.88.order_ref, bf16[256,3584]{1,0:T(8,128)(2,1)S(1)} %get-tuple-element.82.refs_0_, bf16[256,128]{1,0:T(8,128)(2,1)S(1)} %get-tuple-element.83.refs_1_, bf16[64,8192]{1,0:T(8,128)(2,1)S(1)} %copy-done.1, ...), custom_call_target="tpu_custom_call" | custom-call | tf_op jit(solution)/shard_map/forward/pallas_call | solution.py:158
  55.0 0.0 collective-permute-done.10
  55.1 0.1 add_convert_fusion
  55.2 2.4 %collective-permute-start.12 = (bf16[2,256,512]{2,1,0:T(8,128)(2,1)S(1)}, bf16[2,256,512]{2,1,0:T(8,128)(2,1)S(1)}, u32[]{:S(2)}, u32[]{:S(2)}) collective-permute-start(bf16[2,256,512]{2,1,0:T(8,128)(2,1)S(1)} %add_convert_fusion), channel_id=1, source_target_pairs={{0,4},{1,9},{2,6},{3,11},{4,0},{5,13},{6,2},{7,15},{8,12},{9,1},{1... | collective-permute-start | bytes 1572872 | tf_op jit(solution)/shard_map/ppermute | solution.py:329
  57.7 4.1 %collective-permute-start.14 = (f32[16,512]{1,0:T(8,128)S(1)}, f32[16,512]{1,0:T(8,128)S(1)}, u32[]{:S(2)}, u32[]{:S(2)}) collective-permute-start(f32[16,512]{1,0:T(8,128)S(1)} %slice.81), channel_id=1, source_target_pairs={{0,1},{1,0},{2,3},{3,2},{4,5},{5,4},{6,7},{7,6},{8,9},{9,8},{10,11... | collective-permute-start | bytes 98312 | tf_op jit(solution)/shard_map/ppermute | solution.py:324
  61.8 2.7 %forward.7 = bf16[2,256,512]{2,1,0:T(8,128)(2,1)S(1)} custom-call(s32[16]{0:T(128)S(1)} %stack.88.order_ref, bf16[256,3584]{1,0:T(8,128)(2,1)S(1)} %get-tuple-element.82.refs_0_, bf16[256,128]{1,0:T(8,128)(2,1)S(1)} %get-tuple-element.83.refs_1_, bf16[64,8192]{1,0:T(8,128)(2,1)S(1)} %copy-done.1, bf16[3584,512]{1,0:T(8,128)(2,1)S(1)} %get-tuple-element.92.refs_3_.refs_11_, ...), custom_call_target="tpu_custom_call" | custom-call | tf_op jit(solution)/shard_map/forward/pallas_call | solution.py:158
  64.5 5.3 %backward.2 = (f32[128,1280]{1,0:T(8,128)S(1)}, bf16[128,1280]{1,0:T(8,128)(2,1)S(1)}, bf16[256,4096]{1,0:T(8,128)(2,1)S(1)}, f32[256,64]{1,0:T(8,128)S(1)}, f32...) custom-call(s32[16]{0:T(128)S(1)} %stack.88.order_ref, bf16[272,512]{1,0:T(8,128)(2,1)S(1)} %own_block.1.refs_0_, ...), custom_call_target="tpu_custom_call" | custom-call | tf_op jit(solution)/shard_map/backward/pallas_call | solution.py:223
  69.9 0.1 collective-permute-start.16
  69.9 0.0 collective-permute-done.14
  70.0 0.0 collective-permute-done.13
  70.0 5.5 %collective-permute-done.12 = bf16[2,256,512]{2,1,0:T(8,128)(2,1)S(1)} collective-permute-done((bf16[2,256,512]{2,1,0:T(8,128)(2,1)S(1)}, bf16[2,256,512]{2,1,0:T(8,128)(2,1)S(1)}, u32[]{:S(2)}, u32[]{:S(2)}) %collective-permute-start.12) | collective-permute-done | bytes 524320 | tf_op jit(solution)/shard_map/ppermute | solution.py:329
  75.5 0.2 convert_add_fusion
  75.7 0.8 collective-permute-start.15
  76.5 0.2 fusion.3
  76.7 0.2 fusion.up_ref
  76.9 0.1 collective-permute-start.18
  77.0 0.5 collective-permute-start.17
  77.5 7.4 %backward.3 = (f32[128,2304]{1,0:T(8,128)S(1)}, bf16[128,2304]{1,0:T(8,128)(2,1)S(1)}) custom-call(s32[16]{0:T(128)S(1)} %stack.88.order_ref, bf16[256,4096]{1,0:T(8,128)(2,1)S(1)} %get-tuple-element.110.refs_0_, f32[256,64]{1,0:T(8,128)S(1)} %get-tuple-element.106.refs_1_.proj_ref, bf16[64,3584]{1,0:T(8,128)(2,1)S(1)} %bitcast.41, ...), custom_call_target="tpu_custom_call" | custom-call | tf_op jit(solution)/shard_map/backward/pallas_call | solution.py:223
  84.9 0.0 collective-permute-done.17.from_ref
  84.9 0.0 collective-permute-done.16.ra_ref
  84.9 0.1 collective-permute-start.21
  85.1 2.0 %weights.1 = (f32[64,3584]{1,0:T(8,128)}, f32[64,1024]{1,0:T(8,128)}) custom-call(s32[16]{0:T(128)S(1)} %stack.88.order_ref, f32[256,64]{1,0:T(8,128)S(1)} %get-tuple-element.106.refs_1_.proj_ref, f32[256,64]{1,0:T(8,128)S(1)} %collective-permute-done.17.from_ref, bf16[128,3584]{1,0:T(8,128)(2,1)S(1)} %copy-done.7, ...), custom_call_target="tpu_custom_call" | custom-call | tf_op jit(solution)/shard_map/weights/pallas_call | solution.py:280
  87.1 0.1 multiply_reduce_fusion
  87.2 0.5 collective-permute-start.19
  87.8 0.1 collective-permute-start.20
  87.9 0.0 collective-permute-done.21.rb_ref
  87.9 1.6 %hidden.1 = bf16[128,3584]{1,0:T(8,128)(2,1)} custom-call(s32[16]{0:T(128)S(1)} %stack.88.order_ref, f32[128,1280]{1,0:T(8,128)S(1)} %get-tuple-element.118.ga_ref, bf16[128,1280]{1,0:T(8,128)(2,1)S(1)} %collective-permute-done.16.ra_ref, f32[128,2304]{1,0:T(8,128)S(1)} %get-tuple-element.120.gb_ref, bf16[128,2304]{1,0:T(8,128)(2,1)S(1)} %collective-permute-done.21.rb_ref), custom_call_target="tpu_custom_call" | custom-call | tf_op jit(solution)/shard_map/hidden/pallas_call | solution.py:280
  89.5 1.3 %mixed.1 = (bf16[128,1024]{1,0:T(8,128)(2,1)}, f32[8,128]{1,0:T(8,128)}) custom-call(s32[16]{0:T(128)S(1)} %stack.88.order_ref, bf16[256,512]{1,0:T(8,128)(2,1)S(1)} %get-tuple-element.130.m_ref, bf16[128,512]{1,0:T(8,128)(2,1)S(1)} %collective-permute-done.19.m_other_ref, f32[1,512]{1,0:T(1,128)S(1)} %slice_divide_fusion.g_ref, ...), custom_call_target="tpu_custom_call" | custom-call | tf_op jit(solution)/shard_map/mixed/pallas_call | solution.py:280
  (35 shorter events, 0.2 us)
Async XLA Ops:
  0.6 1.9 %collective-permute-start = (bf16[128,1024]{1,0:T(8,128)(2,1)}, bf16[128,1024]{1,0:T(8,128)(2,1)S(1)}, u32[]{:S(2)}, u32[]{:S(2)}) collective-permute-start(bf16[128,1024]{1,0:T(8,128)(2,1)} %own_ref.2), channel_id=1, source_target_pairs={{0,1},{1,0},{2,3},{3,2},{4,5},{5,4},{6,7},{7,6},{8,9},{9,8},{10,11... | collective-permute-start | bytes 786440 | tf_op jit(solution)/shard_map/ppermute | solution.py:324
  2.5 0.9 %copy-start.8 = (bf16[128,1024]{1,0:T(8,128)(2,1)S(1)}, bf16[128,1024]{1,0:T(8,128)(2,1)}, u32[]{:S(2)}) copy-start(bf16[128,1024]{1,0:T(8,128)(2,1)} %own_ref.2) | copy-start | bytes 786436
  4.0 16.8 %collective-permute-start.2 = (bf16[272,512]{1,0:T(8,128)(2,1)S(1)}, bf16[272,512]{1,0:T(8,128)(2,1)S(1)}, u32[]{:S(2)}, u32[]{:S(2)}) collective-permute-start(bf16[272,512]{1,0:T(8,128)(2,1)S(1)} %own_block.1.refs_0_), channel_id=1, source_target_pairs={{0,8},{1,3},{2,10},{3,1},{4,12},{5,7},{6,14},{7,5},{8,0},{9,11},{1... | collective-permute-start | bytes 835592 | tf_op jit(solution)/shard_map/ppermute | solution.py:329
  8.1 12.8 %collective-permute-start.3 = (bf16[272,512]{1,0:T(8,128)(2,1)S(1)}, bf16[272,512]{1,0:T(8,128)(2,1)S(1)}, u32[]{:S(2)}, u32[]{:S(2)}) collective-permute-start(bf16[272,512]{1,0:T(8,128)(2,1)S(1)} %own_block.1.refs_0_), channel_id=1, source_target_pairs={{0,4},{1,9},{2,6},{3,11},{4,0},{5,13},{6,2},{7,15},{8,12},{9,1},{1... | collective-permute-start | bytes 835592 | tf_op jit(solution)/shard_map/ppermute | solution.py:329
  9.6 28.0 %collective-permute-start.8 = (bf16[128,3584]{1,0:T(8,128)(2,1)}, bf16[128,3584]{1,0:T(8,128)(2,1)S(1)}, u32[]{:S(2)}, u32[]{:S(2)}) collective-permute-start(bf16[128,3584]{1,0:T(8,128)(2,1)} %own_ref.3), channel_id=1, source_target_pairs={{0,1},{1,0},{2,3},{3,2},{4,5},{5,4},{6,7},{7,6},{8,9},{9,8},{10,11... | collective-permute-start | bytes 2752520 | tf_op jit(solution)/shard_map/ppermute | solution.py:324
  9.6 1.2 %copy-start = (bf16[64,8192]{1,0:T(8,128)(2,1)S(1)}, bf16[64,8192]{1,0:T(8,128)(2,1)}, u32[]{:S(2)}) copy-start(bf16[64,8192]{1,0:T(8,128)(2,1)} %refs_9_.1) | copy-start | bytes 3145732
  10.9 1.0 %copy-start.4 = (bf16[3584,64]{0,1:T(8,128)(2,1)S(1)}, bf16[3584,64]{0,1:T(8,128)(2,1)}, u32[]{:S(2)}) copy-start(bf16[3584,64]{0,1:T(8,128)(2,1)} %param.8) | copy-start | bytes 1376260
  11.9 1.2 %copy-start.6 = (bf16[128,3584]{1,0:T(8,128)(2,1)S(1)}, bf16[128,3584]{1,0:T(8,128)(2,1)}, u32[]{:S(2)}) copy-start(bf16[128,3584]{1,0:T(8,128)(2,1)} %own_ref.3) | copy-start | bytes 2752516
  13.1 11.6 %copy-start.1 = (bf16[64,8192]{1,0:T(8,128)(2,1)S(1)}, bf16[64,8192]{1,0:T(8,128)(2,1)}, u32[]{:S(2)}) copy-start(bf16[64,8192]{1,0:T(8,128)(2,1)} %refs_9_.1) | copy-start | bytes 3145732
  13.1 11.6 %copy-start.5 = (bf16[3584,64]{0,1:T(8,128)(2,1)S(1)}, bf16[3584,64]{0,1:T(8,128)(2,1)}, u32[]{:S(2)}) copy-start(bf16[3584,64]{0,1:T(8,128)(2,1)} %param.8) | copy-start | bytes 1376260
  20.9 16.7 %copy-start.7 = (bf16[128,3584]{1,0:T(8,128)(2,1)S(1)}, bf16[128,3584]{1,0:T(8,128)(2,1)}, u32[]{:S(2)}) copy-start(bf16[128,3584]{1,0:T(8,128)(2,1)} %own_ref.3) | copy-start | bytes 2752516
  21.0 14.7 %collective-permute-start.5 = (bf16[2,272,512]{2,1,0:T(8,128)(2,1)S(1)}, bf16[2,272,512]{2,1,0:T(8,128)(2,1)S(1)}, u32[]{:S(2)}, u32[]{:S(2)}) collective-permute-start(bf16[2,272,512]{2,1,0:T(8,128)(2,1)S(1)} %pad_maximum_fusion), channel_id=1, source_target_pairs={{0,2},{1,5},{2,0},{3,7},{4,6},{5,1},{6,4},{7,3},{8,10},{9,13},{10,... | collective-permute-start | bytes 1671176 | tf_op jit(solution)/shard_map/ppermute | solution.py:329
  22.9 11.0 %collective-permute-start.1 = (bf16[272,512]{1,0:T(8,128)(2,1)S(1)}, bf16[272,512]{1,0:T(8,128)(2,1)S(1)}, u32[]{:S(2)}, u32[]{:S(2)}) collective-permute-start(bf16[272,512]{1,0:T(8,128)(2,1)S(1)} %own_block.1.refs_0_), channel_id=1, source_target_pairs={{0,2},{1,5},{2,0},{3,7},{4,6},{5,1},{6,4},{7,3},{8,10},{9,13},{10,... | collective-permute-start | bytes 835592 | tf_op jit(solution)/shard_map/ppermute | solution.py:329
  23.0 12.6 %collective-permute-start.4 = (bf16[272,512]{1,0:T(8,128)(2,1)S(1)}, bf16[272,512]{1,0:T(8,128)(2,1)S(1)}, u32[]{:S(2)}, u32[]{:S(2)}) collective-permute-start(bf16[272,512]{1,0:T(8,128)(2,1)S(1)} %collective-permute-done.2.refs_1_), channel_id=1, source_target_pairs={{0,4},{1,9},{2,6},{3,11},{4,0},{5,13},{6,2},{7,15},{8,12},{9,1},{1... | collective-permute-start | bytes 835592 | tf_op jit(solution)/shard_map/ppermute | solution.py:329
  33.8 18.4 %copy-start.2 = (bf16[3584,512]{1,0:T(8,128)(2,1)}, bf16[3584,512]{1,0:T(8,128)(2,1)S(1)}, u32[]{:S(2)}) copy-start(bf16[3584,512]{1,0:T(8,128)(2,1)S(1)} %get-tuple-element.90.refs_4_.refs_14_.refs_6_) | copy-start | bytes 11010052
  35.6 7.1 %collective-permute-start.7 = (bf16[272,512]{1,0:T(8,128)(2,1)S(1)}, bf16[272,512]{1,0:T(8,128)(2,1)S(1)}, u32[]{:S(2)}, u32[]{:S(2)}) collective-permute-start(bf16[272,512]{1,0:T(8,128)(2,1)S(1)} %collective-permute-done.4.refs_3_), channel_id=1, source_target_pairs={{0,2},{1,5},{2,0},{3,7},{4,6},{5,1},{6,4},{7,3},{8,10},{9,13},{10,... | collective-permute-start | bytes 835592 | tf_op jit(solution)/shard_map/ppermute | solution.py:329
  36.8 5.9 %collective-permute-start.6 = (f32[24,512]{1,0:T(8,128)S(1)}, f32[24,512]{1,0:T(8,128)S(1)}, u32[]{:S(2)}, u32[]{:S(2)}) collective-permute-start(f32[24,512]{1,0:T(8,128)S(1)} %get-tuple-element.75), channel_id=1, source_target_pairs={{0,2},{1,5},{2,0},{3,7},{4,6},{5,1},{6,4},{7,3},{8,10},{9,13},{10,... | collective-permute-start | bytes 147464 | tf_op jit(solution)/shard_map/ppermute | solution.py:329
  42.7 12.4 %collective-permute-start.11 = (bf16[2,256,512]{2,1,0:T(8,128)(2,1)S(1)}, bf16[2,256,512]{2,1,0:T(8,128)(2,1)S(1)}, u32[]{:S(2)}, u32[]{:S(2)}) collective-permute-start(bf16[2,256,512]{2,1,0:T(8,128)(2,1)S(1)} %get-tuple-element.87), channel_id=1, source_target_pairs={{0,2},{1,5},{2,0},{3,7},{4,6},{5,1},{6,4},{7,3},{8,10},{9,13},{10,... | collective-permute-start | bytes 1572872 | tf_op jit(solution)/shard_map/ppermute | solution.py:329
  43.9 4.2 %collective-permute-start.9 = (f32[24,512]{1,0:T(8,128)S(1)}, f32[24,512]{1,0:T(8,128)S(1)}, u32[]{:S(2)}, u32[]{:S(2)}) collective-permute-start(f32[24,512]{1,0:T(8,128)S(1)} %add.56), channel_id=1, source_target_pairs={{0,4},{1,9},{2,6},{3,11},{4,0},{5,13},{6,2},{7,15},{8,12},{9,1},{1... | collective-permute-start | bytes 147464 | tf_op jit(solution)/shard_map/ppermute | solution.py:329
  48.1 7.0 %collective-permute-start.10 = (f32[24,512]{1,0:T(8,128)S(1)}, f32[24,512]{1,0:T(8,128)S(1)}, u32[]{:S(2)}, u32[]{:S(2)}) collective-permute-start(f32[24,512]{1,0:T(8,128)S(1)} %add.57), channel_id=1, source_target_pairs={{0,8},{1,3},{2,10},{3,1},{4,12},{5,7},{6,14},{7,5},{8,0},{9,11},{1... | collective-permute-start | bytes 147464 | tf_op jit(solution)/shard_map/ppermute | solution.py:329
  51.1 18.8 %collective-permute-start.13 = (bf16[2,256,512]{2,1,0:T(8,128)(2,1)S(1)}, bf16[2,256,512]{2,1,0:T(8,128)(2,1)S(1)}, u32[]{:S(2)}, u32[]{:S(2)}) collective-permute-start(bf16[2,256,512]{2,1,0:T(8,128)(2,1)S(1)} %forward.5), channel_id=1, source_target_pairs={{0,2},{1,5},{2,0},{3,7},{4,6},{5,1},{6,4},{7,3},{8,10},{9,13},{10,... | collective-permute-start | bytes 1572872 | tf_op jit(solution)/shard_map/ppermute | solution.py:329
  55.2 20.3 %collective-permute-start.12 = (bf16[2,256,512]{2,1,0:T(8,128)(2,1)S(1)}, bf16[2,256,512]{2,1,0:T(8,128)(2,1)S(1)}, u32[]{:S(2)}, u32[]{:S(2)}) collective-permute-start(bf16[2,256,512]{2,1,0:T(8,128)(2,1)S(1)} %add_convert_fusion), channel_id=1, source_target_pairs={{0,4},{1,9},{2,6},{3,11},{4,0},{5,13},{6,2},{7,15},{8,12},{9,1},{1... | collective-permute-start | bytes 1572872 | tf_op jit(solution)/shard_map/ppermute | solution.py:329
  57.7 12.3 %collective-permute-start.14 = (f32[16,512]{1,0:T(8,128)S(1)}, f32[16,512]{1,0:T(8,128)S(1)}, u32[]{:S(2)}, u32[]{:S(2)}) collective-permute-start(f32[16,512]{1,0:T(8,128)S(1)} %slice.81), channel_id=1, source_target_pairs={{0,1},{1,0},{2,3},{3,2},{4,5},{5,4},{6,7},{7,6},{8,9},{9,8},{10,11... | collective-permute-start | bytes 98312 | tf_op jit(solution)/shard_map/ppermute | solution.py:324
  61.8 2.7 %copy-start.3 = (bf16[3584,512]{1,0:T(8,128)(2,1)S(1)}, bf16[3584,512]{1,0:T(8,128)(2,1)}, u32[]{:S(2)}) copy-start(bf16[3584,512]{1,0:T(8,128)(2,1)} %copy-done.2) | copy-start | bytes 11010052
  69.9 15.1 %collective-permute-start.16 = (bf16[128,1280]{1,0:T(8,128)(2,1)S(1)}, bf16[128,1280]{1,0:T(8,128)(2,1)S(1)}, u32[]{:S(2)}, u32[]{:S(2)}) collective-permute-start(bf16[128,1280]{1,0:T(8,128)(2,1)S(1)} %get-tuple-element.107), channel_id=1, source_target_pairs={{0,1},{1,0},{2,3},{3,2},{4,5},{5,4},{6,7},{7,6},{8,9},{9,8},{10,11... | collective-permute-start | bytes 983048 | tf_op jit(solution)/shard_map/ppermute | solution.py:324
  75.7 11.4 %collective-permute-start.15 = (bf16[256,512]{1,0:T(8,128)(2,1)S(1)}, bf16[256,512]{1,0:T(8,128)(2,1)S(1)}, u32[]{:S(2)}, u32[]{:S(2)}) collective-permute-start(bf16[256,512]{1,0:T(8,128)(2,1)S(1)} %fusion.2), channel_id=1, source_target_pairs={{0,8},{1,3},{2,10},{3,1},{4,12},{5,7},{6,14},{7,5},{8,0},{9,11},{1... | collective-permute-start | bytes 786440 | tf_op jit(solution)/shard_map/ppermute | solution.py:329
  76.9 8.0 %collective-permute-start.18 = (f32[64,512]{1,0:T(8,128)S(1)}, f32[64,512]{1,0:T(8,128)S(1)}, u32[]{:S(2)}, u32[]{:S(2)}) collective-permute-start(f32[64,512]{1,0:T(8,128)S(1)} %fusion.up_ref), channel_id=1, source_target_pairs={{0,1},{1,0},{2,3},{3,2},{4,5},{5,4},{6,7},{7,6},{8,9},{9,8},{10,11... | collective-permute-start | bytes 393224 | tf_op jit(solution)/shard_map/ppermute | solution.py:324
  77.0 7.9 %collective-permute-start.17 = (f32[256,64]{1,0:T(8,128)S(1)}, f32[256,64]{1,0:T(8,128)S(1)}, u32[]{:S(2)}, u32[]{:S(2)}) collective-permute-start(f32[256,64]{1,0:T(8,128)S(1)} %get-tuple-element.106.refs_1_.proj_ref), channel_id=1, source_target_pairs={{0,1},{1,0},{2,3},{3,2},{4,5},{5,4},{6,7},{7,6},{8,9},{9,8},{10,11... | collective-permute-start | bytes 196616 | tf_op jit(solution)/shard_map/ppermute | solution.py:324
  84.9 2.9 %collective-permute-start.21 = (bf16[128,2304]{1,0:T(8,128)(2,1)S(1)}, bf16[128,2304]{1,0:T(8,128)(2,1)S(1)}, u32[]{:S(2)}, u32[]{:S(2)}) collective-permute-start(bf16[128,2304]{1,0:T(8,128)(2,1)S(1)} %get-tuple-element.121), channel_id=1, source_target_pairs={{0,1},{1,0},{2,3},{3,2},{4,5},{5,4},{6,7},{7,6},{8,9},{9,8},{10,11... | collective-permute-start | bytes 1769480 | tf_op jit(solution)/shard_map/ppermute | solution.py:324
  87.2 2.3 %collective-permute-start.19 = (bf16[128,512]{1,0:T(8,128)(2,1)S(1)}, bf16[128,512]{1,0:T(8,128)(2,1)S(1)}, u32[]{:S(2)}, u32[]{:S(2)}) collective-permute-start(bf16[128,512]{1,0:T(8,128)(2,1)S(1)} %slice.88), channel_id=1, source_target_pairs={{0,1},{1,0},{2,3},{3,2},{4,5},{5,4},{6,7},{7,6},{8,9},{9,8},{10,11... | collective-permute-start | bytes 393224 | tf_op jit(solution)/shard_map/ppermute | solution.py:324
  87.8 1.8 %collective-permute-start.20 = (f32[1,512]{1,0:T(1,128)S(1)}, f32[1,512]{1,0:T(1,128)S(1)}, u32[]{:S(2)}, u32[]{:S(2)}) collective-permute-start(f32[1,512]{1,0:T(1,128)S(1)} %slice_divide_fusion.g_ref), channel_id=1, source_target_pairs={{0,1},{1,0},{2,3},{3,2},{4,5},{5,4},{6,7},{7,6},{8,9},{9,8},{10,11... | collective-permute-start | bytes 6152 | tf_op jit(solution)/shard_map/ppermute | solution.py:324

commit v11 on v10

--- a/solution.py
+++ b/solution.py
@@ -322,7 +322,7 @@
     rows = weight.shape[0]
     me, core = lax.axis_index("tensor"), lax.axis_index("dp")
     swap = lambda x: lax.ppermute(x, "dp", [(0, 1), (1, 0)])
-    orders = [[1, 2, 4], [2, 4, 1]]
+    orders = [[1, 2, 4], [2, 1, 4]]
 
     def send(x, k):
         pairs = [(2 * t + c, 2 * (t ^ orders[c][k]) + c) for t in range(n) for c in range(2)]
@@ -355,14 +355,13 @@
 
     run_load = functools.partial(load, at=at, up=up, weight=weight, half=half)
     block, order = tie((block, order))
-    *far_pair, stats = run_load((0b110, 0b111), order, own=hidden)
-    cots[0b001], cots[0b010], stats = tie((cots[0b001], cots[0b010], stats))
+    *far, stats = run_load(tuple(range(n // 2, n)), order, own=hidden)
+    cots[0b001], cots[0b010], cots[0b100], stats = tie((cots[0b001], cots[0b010], cots[0b100], stats))
     cots[0b011] = send(cots[0b001], 1)
     pair = send(jnp.stack([cots[0b001], cots[0b010]]), 0)
-    *held, stats = run_load(tuple(range(n - 2)), order, before=stats)
-    held = held + far_pair
-    near, far = held[: n // 2], held[n // 2 :]
-    cots[0b100], cots[0b011], pair, stats = tie((cots[0b100], cots[0b011], pair, stats))
+    *near, stats = run_load(tuple(range(n // 2)), order, before=stats)
+    held = near + far
+    cots[0b011], pair, stats = tie((cots[0b011], pair, stats))
     cots[0b101], cots[0b110] = pair[0], pair[1]
     got = send(stats, 0)
     cots[0b111] = send(cots[0b011], 0)

time: 91.1 us -> 82.4 us (0.905)
  starting transfers between devices: 26 us -> 21.8 us
  waiting for transfers between devices: 12.7 us -> 8.5 us
    ppermute x13, waiting for transfers between devices: 12.3 us -> 8.09 us  [send(): return lax.ppermute(x, ('tensor', 'dp'), pairs)]
    ppermute x9, starting transfers between devices: 6.04 us -> 2.4 us  [split_columns(): swap = lambda x: lax.ppermute(x, 'dp', [(0, 1), (1, 0)])]
  transfers between devices with their start and end apart: 22 -> 22, of which waited for: 6 -> 8; matrix products, arithmetic and copies ran while one was open for 2% -> 2% of each run, Pallas kernels for 47% -> 52%
where the time goes in v11:
time: 82.4 us; the launch traced here: 82.1 us
  Pallas kernels  44.5 us (54%)
  starting transfers between devices  21.8 us (26%)
  waiting for transfers between devices  8.5 us (10%)
  local copies, waits for them, and re-layouts  4.68 us (6%)
  other arithmetic  1.33 us (2%)
  between operations  0.95 us (1%)
    ppermute x13, starting transfers between devices, send(): return lax.ppermute(x, ('tensor', 'dp'), pairs)  19.4 us
    pallas_call x2, Pallas kernels, load(): pl.pallas_call(functools.partial(load_kernel, tokens, rank, n, vs, first)...  13.8 us
    pallas_call x2, Pallas kernels, backward(): pl.pallas_call(functools.partial(backward_kernel, tokens, n, start, band,...  12.8 us
    pallas_call x4, Pallas kernels, forward(): pl.pallas_call(functools.partial(forward_kernel, tokens, rank, vs, later...  12.4 us
    ppermute x13, waiting for transfers between devices, send(): return lax.ppermute(x, ('tensor', 'dp'), pairs)  8.09 us
    pallas_call x3, Pallas kernels, finish(): pl.pallas_call(kernel, grid_spec=pltpu.PrefetchScalarGridSpec(num_scalar_...  4.94 us
    unnamed x18, local copies, waits for them, and re-layouts  4.39 us
    ppermute x9, starting transfers between devices, split_columns(): swap = lambda x: lax.ppermute(x, 'dp', [(0, 1), (1, 0)])  2.4 us
  transfers between devices with their start and end apart: 22, of which 8 were waited for; matrix products, arithmetic and copies ran while one was open for 2% of the time, Pallas kernels for 52%

profile of v11, /device:TPU:0, one launch (start us, length us, event | category | flops | bytes accessed | tf_op | source)
XLA Modules:
  0.0 82.1 jit_solution(16821817768396874953)
XLA Ops:
  0.6 0.5 collective-permute-start
  1.1 0.7 reduce-precision_convert_fusion.1
  1.9 0.1 pad.13.clone
  2.0 0.1 stack.88.order_ref
  2.1 0.1 maximum_maximum_fusion.magnitude_ref
  2.1 0.4 collective-permute-done.other_ref
  2.5 0.9 %copy-done.8 = bf16[128,1024]{1,0:T(8,128)(2,1)S(1)} copy-done((bf16[128,1024]{1,0:T(8,128)(2,1)S(1)}, bf16[128,1024]{1,0:T(8,128)(2,1)}, u32[]{:S(2)}) %copy-start.8) | copy-done | bytes 262168
  3.5 0.6 own_block.1.refs_0_
  4.0 4.0 %collective-permute-start.1 = (bf16[272,512]{1,0:T(8,128)(2,1)S(1)}, bf16[272,512]{1,0:T(8,128)(2,1)S(1)}, u32[]{:S(2)}, u32[]{:S(2)}) collective-permute-start(bf16[272,512]{1,0:T(8,128)(2,1)S(1)} %own_block.1.refs_0_), channel_id=1, source_target_pairs={{0,8},{1,9},{2,10},{3,11},{4,12},{5,13},{6,14},{7,15},{8,0},{9,1},... | collective-permute-start | bytes 835592 | tf_op jit(solution)/shard_map/ppermute | solution.py:329
  8.1 1.6 %collective-permute-start.2 = (bf16[272,512]{1,0:T(8,128)(2,1)S(1)}, bf16[272,512]{1,0:T(8,128)(2,1)S(1)}, u32[]{:S(2)}, u32[]{:S(2)}) collective-permute-start(bf16[272,512]{1,0:T(8,128)(2,1)S(1)} %own_block.1.refs_0_), channel_id=1, source_target_pairs={{0,4},{1,3},{2,6},{3,1},{4,0},{5,7},{6,2},{7,5},{8,12},{9,11},{10,... | collective-permute-start | bytes 835592 | tf_op jit(solution)/shard_map/ppermute | solution.py:329
  9.6 1.5 %collective-permute-start.3 = (bf16[272,512]{1,0:T(8,128)(2,1)S(1)}, bf16[272,512]{1,0:T(8,128)(2,1)S(1)}, u32[]{:S(2)}, u32[]{:S(2)}) collective-permute-start(bf16[272,512]{1,0:T(8,128)(2,1)S(1)} %own_block.1.refs_0_), channel_id=1, source_target_pairs={{0,2},{1,5},{2,0},{3,7},{4,6},{5,1},{6,4},{7,3},{8,10},{9,13},{10,... | collective-permute-start | bytes 835592 | tf_op jit(solution)/shard_map/ppermute | solution.py:329
  11.1 0.0 collective-permute-start.8
  11.1 1.2 %copy-done = bf16[64,8192]{1,0:T(8,128)(2,1)S(1)} copy-done((bf16[64,8192]{1,0:T(8,128)(2,1)S(1)}, bf16[64,8192]{1,0:T(8,128)(2,1)}, u32[]{:S(2)}) %copy-start) | copy-done | bytes 1048600
  12.4 1.0 %copy-done.4 = bf16[3584,64]{0,1:T(8,128)(2,1)S(1)} copy-done((bf16[3584,64]{0,1:T(8,128)(2,1)S(1)}, bf16[3584,64]{0,1:T(8,128)(2,1)}, u32[]{:S(2)}) %copy-start.4) | copy-done | bytes 458776
  13.4 1.2 %copy-done.6 = bf16[128,3584]{1,0:T(8,128)(2,1)S(1)} copy-done((bf16[128,3584]{1,0:T(8,128)(2,1)S(1)}, bf16[128,3584]{1,0:T(8,128)(2,1)}, u32[]{:S(2)}) %copy-start.6) | copy-done | bytes 917528
  14.6 6.9 %load.2 = (bf16[3584,512]{1,0:T(8,128)(2,1)S(1)}, bf16[3584,512]{1,0:T(8,128)(2,1)S(1)}, bf16[3584,512]{1,0:T(8,128)(2,1)S(1)}, bf16[3584,512]{1,0:T(8,128)(2,1)S(1)}, f32[24,512]{1,0:T(8,128)S(1)}) custom-call(s32[16]{0:T(128)S(1)} %stack.88.order_ref, bf16[128,3584]{1,0:T(8,128)(2,1)S(1)} %copy-done.6, bf16[64,3584]{1,0:T(8,128)(2,1)S(1)} %bitcast.37, ...), custom_call_target="tpu_custom_call" | custom-call | tf_op jit(solution)/shard_map/load/pallas_call | solution.py:116
  21.4 0.0 collective-permute-done.1.refs_1_
  21.4 0.9 %collective-permute-done.2.refs_2_ = bf16[272,512]{1,0:T(8,128)(2,1)S(1)} collective-permute-done((bf16[272,512]{1,0:T(8,128)(2,1)S(1)}, bf16[272,512]{1,0:T(8,128)(2,1)S(1)}, u32[]{:S(2)}, u32[]{:S(2)}) %collective-permute-start.2) | collective-permute-done | bytes 278560 | tf_op jit(solution)/shard_map/ppermute | solution.py:329
  22.3 0.0 collective-permute-done.3.refs_4_
  22.3 0.1 pad_maximum_fusion
  22.4 0.0 copy-start.7
  22.4 0.8 %collective-permute-start.5 = (bf16[2,272,512]{2,1,0:T(8,128)(2,1)S(1)}, bf16[2,272,512]{2,1,0:T(8,128)(2,1)S(1)}, u32[]{:S(2)}, u32[]{:S(2)}) collective-permute-start(bf16[2,272,512]{2,1,0:T(8,128)(2,1)S(1)} %pad_maximum_fusion), channel_id=1, source_target_pairs={{0,2},{1,5},{2,0},{3,7},{4,6},{5,1},{6,4},{7,3},{8,10},{9,13},{10,... | collective-permute-start | bytes 1671176 | tf_op jit(solution)/shard_map/ppermute | solution.py:329
  23.2 1.2 %collective-permute-start.4 = (bf16[272,512]{1,0:T(8,128)(2,1)S(1)}, bf16[272,512]{1,0:T(8,128)(2,1)S(1)}, u32[]{:S(2)}, u32[]{:S(2)}) collective-permute-start(bf16[272,512]{1,0:T(8,128)(2,1)S(1)} %collective-permute-done.1.refs_1_), channel_id=1, source_target_pairs={{0,4},{1,3},{2,6},{3,1},{4,0},{5,7},{6,2},{7,5},{8,12},{9,11},{10,... | collective-permute-start | bytes 835592 | tf_op jit(solution)/shard_map/ppermute | solution.py:329
  24.4 6.9 %load.3 = (bf16[3584,512]{1,0:T(8,128)(2,1)S(1)}, bf16[3584,512]{1,0:T(8,128)(2,1)S(1)}, bf16[3584,512]{1,0:T(8,128)(2,1)S(1)}, bf16[3584,512]{1,0:T(8,128)(2,1)S(1)}, f32[24,512]{1,0:T(8,128)S(1)}) custom-call(s32[16]{0:T(128)S(1)} %stack.88.order_ref, f32[24,512]{1,0:T(8,128)S(1)} %get-tuple-element.73.before_ref, bf16[64,3584]{1,0:T(8,128)(2,1)S(1)} %bitcast.38, ...), custom_call_target="tpu_custom_call" | custom-call | tf_op jit(solution)/shard_map/load/pallas_call | solution.py:116
  31.4 1.4 %collective-permute-done.4.refs_3_ = bf16[272,512]{1,0:T(8,128)(2,1)S(1)} collective-permute-done((bf16[272,512]{1,0:T(8,128)(2,1)S(1)}, bf16[272,512]{1,0:T(8,128)(2,1)S(1)}, u32[]{:S(2)}, u32[]{:S(2)}) %collective-permute-start.4) | collective-permute-done | bytes 278560 | tf_op jit(solution)/shard_map/ppermute | solution.py:329
  32.8 1.4 %collective-permute-done.5 = bf16[2,272,512]{2,1,0:T(8,128)(2,1)S(1)} collective-permute-done((bf16[2,272,512]{2,1,0:T(8,128)(2,1)S(1)}, bf16[2,272,512]{2,1,0:T(8,128)(2,1)S(1)}, u32[]{:S(2)}, u32[]{:S(2)}) %collective-permute-start.5) | collective-permute-done | bytes 557088 | tf_op jit(solution)/shard_map/ppermute | solution.py:329
  34.2 0.8 collective-permute-start.7
  35.0 1.2 %collective-permute-start.6 = (f32[24,512]{1,0:T(8,128)S(1)}, f32[24,512]{1,0:T(8,128)S(1)}, u32[]{:S(2)}, u32[]{:S(2)}) collective-permute-start(f32[24,512]{1,0:T(8,128)S(1)} %get-tuple-element.75), channel_id=1, source_target_pairs={{0,2},{1,5},{2,0},{3,7},{4,6},{5,1},{6,4},{7,3},{8,10},{9,13},{10,... | collective-permute-start | bytes 147464 | tf_op jit(solution)/shard_map/ppermute | solution.py:329
  36.2 0.0 collective-permute-done.8.refs_1_.other_ref
  36.2 4.1 %forward.4 = (bf16[2,256,512]{2,1,0:T(8,128)(2,1)S(1)}, bf16[256,3584]{1,0:T(8,128)(2,1)S(1)}, bf16[256,128]{1,0:T(8,128)(2,1)S(1)}) custom-call(s32[16]{0:T(128)S(1)} %stack.88.order_ref, bf16[128,3584]{1,0:T(8,128)(2,1)S(1)} %copy-done.7, bf16[128,3584]{1,0:T(8,128)(2,1)S(1)} %collective-permute-done.8.refs_1_.other_ref, bf16[64,3584]{1,0:T(8,128)(2,1)S(1)} %bitcast.39, ...), custom_call_target="tpu_custom_call" | custom-call | tf_op jit(solution)/shard_map/forward/pallas_call | solution.py:158
  40.4 0.9 %collective-permute-done.6 = f32[24,512]{1,0:T(8,128)S(1)} collective-permute-done((f32[24,512]{1,0:T(8,128)S(1)}, f32[24,512]{1,0:T(8,128)S(1)}, u32[]{:S(2)}, u32[]{:S(2)}) %collective-permute-start.6) | collective-permute-done | bytes 49184 | tf_op jit(solution)/shard_map/ppermute | solution.py:329
  41.3 0.8 collective-permute-start.11
  42.1 1.2 %collective-permute-start.9 = (f32[24,512]{1,0:T(8,128)S(1)}, f32[24,512]{1,0:T(8,128)S(1)}, u32[]{:S(2)}, u32[]{:S(2)}) collective-permute-start(f32[24,512]{1,0:T(8,128)S(1)} %add.56), channel_id=1, source_target_pairs={{0,4},{1,3},{2,6},{3,1},{4,0},{5,7},{6,2},{7,5},{8,12},{9,11},{10,... | collective-permute-start | bytes 147464 | tf_op jit(solution)/shard_map/ppermute | solution.py:329
  43.3 2.8 %forward.5 = bf16[2,256,512]{2,1,0:T(8,128)(2,1)S(1)} custom-call(s32[16]{0:T(128)S(1)} %stack.88.order_ref, bf16[256,3584]{1,0:T(8,128)(2,1)S(1)} %get-tuple-element.82.refs_0_, bf16[256,128]{1,0:T(8,128)(2,1)S(1)} %get-tuple-element.83.refs_1_, bf16[64,8192]{1,0:T(8,128)(2,1)S(1)} %copy-done.1, ...), custom_call_target="tpu_custom_call" | custom-call | tf_op jit(solution)/shard_map/forward/pallas_call | solution.py:158
  46.0 0.8 collective-permute-done.9
  46.8 1.9 %collective-permute-start.10 = (f32[24,512]{1,0:T(8,128)S(1)}, f32[24,512]{1,0:T(8,128)S(1)}, u32[]{:S(2)}, u32[]{:S(2)}) collective-permute-start(f32[24,512]{1,0:T(8,128)S(1)} %add.57), channel_id=1, source_target_pairs={{0,8},{1,9},{2,10},{3,11},{4,12},{5,13},{6,14},{7,15},{8,0},{9,1},... | collective-permute-start | bytes 147464 | tf_op jit(solution)/shard_map/ppermute | solution.py:329
  48.7 0.5 collective-permute-start.13
  49.3 2.7 %forward.6 = bf16[2,256,512]{2,1,0:T(8,128)(2,1)S(1)} custom-call(s32[16]{0:T(128)S(1)} %stack.88.order_ref, bf16[256,3584]{1,0:T(8,128)(2,1)S(1)} %get-tuple-element.82.refs_0_, bf16[256,128]{1,0:T(8,128)(2,1)S(1)} %get-tuple-element.83.refs_1_, bf16[64,8192]{1,0:T(8,128)(2,1)S(1)} %copy-done.1, ...), custom_call_target="tpu_custom_call" | custom-call | tf_op jit(solution)/shard_map/forward/pallas_call | solution.py:158
  52.0 0.0 collective-permute-done.10
  52.0 0.0 collective-permute-done.11
  52.0 0.1 add_convert_fusion
  52.2 2.0 %collective-permute-start.12 = (bf16[2,256,512]{2,1,0:T(8,128)(2,1)S(1)}, bf16[2,256,512]{2,1,0:T(8,128)(2,1)S(1)}, u32[]{:S(2)}, u32[]{:S(2)}) collective-permute-start(bf16[2,256,512]{2,1,0:T(8,128)(2,1)S(1)} %add_convert_fusion), channel_id=1, source_target_pairs={{0,4},{1,3},{2,6},{3,1},{4,0},{5,7},{6,2},{7,5},{8,12},{9,11},{10,... | collective-permute-start | bytes 1572872 | tf_op jit(solution)/shard_map/ppermute | solution.py:329
  54.2 0.1 collective-permute-start.14
  54.3 2.8 %forward.7 = bf16[2,256,512]{2,1,0:T(8,128)(2,1)S(1)} custom-call(s32[16]{0:T(128)S(1)} %stack.88.order_ref, bf16[256,3584]{1,0:T(8,128)(2,1)S(1)} %get-tuple-element.82.refs_0_, bf16[256,128]{1,0:T(8,128)(2,1)S(1)} %get-tuple-element.83.refs_1_, bf16[64,8192]{1,0:T(8,128)(2,1)S(1)} %copy-done.1, bf16[3584,512]{1,0:T(8,128)(2,1)S(1)} %get-tuple-element.92.refs_3_.refs_11_, ...), custom_call_target="tpu_custom_call" | custom-call | tf_op jit(solution)/shard_map/forward/pallas_call | solution.py:158
  57.1 5.3 %backward.2 = (f32[128,1280]{1,0:T(8,128)S(1)}, bf16[128,1280]{1,0:T(8,128)(2,1)S(1)}, bf16[256,4096]{1,0:T(8,128)(2,1)S(1)}, f32[256,64]{1,0:T(8,128)S(1)}, f32...) custom-call(s32[16]{0:T(128)S(1)} %stack.88.order_ref, bf16[272,512]{1,0:T(8,128)(2,1)S(1)} %own_block.1.refs_0_, ...), custom_call_target="tpu_custom_call" | custom-call | tf_op jit(solution)/shard_map/backward/pallas_call | solution.py:223
  62.4 0.5 collective-permute-start.16
  63.0 0.0 collective-permute-done.14
  63.0 0.2 collective-permute-done.13
  63.2 0.2 convert_add_fusion
  63.4 1.8 %collective-permute-start.15 = (bf16[256,512]{1,0:T(8,128)(2,1)S(1)}, bf16[256,512]{1,0:T(8,128)(2,1)S(1)}, u32[]{:S(2)}, u32[]{:S(2)}) collective-permute-start(bf16[256,512]{1,0:T(8,128)(2,1)S(1)} %fusion.2), channel_id=1, source_target_pairs={{0,8},{1,9},{2,10},{3,11},{4,12},{5,13},{6,14},{7,15},{8,0},{9,1},... | collective-permute-start | bytes 786440 | tf_op jit(solution)/shard_map/ppermute | solution.py:329
  65.2 0.2 fusion.3
  65.4 0.2 fusion.up_ref
  65.6 0.1 collective-permute-start.18
  65.7 0.5 collective-permute-start.17
  66.2 7.4 %backward.3 = (f32[128,2304]{1,0:T(8,128)S(1)}, bf16[128,2304]{1,0:T(8,128)(2,1)S(1)}) custom-call(s32[16]{0:T(128)S(1)} %stack.88.order_ref, bf16[256,4096]{1,0:T(8,128)(2,1)S(1)} %get-tuple-element.110.refs_0_, f32[256,64]{1,0:T(8,128)S(1)} %get-tuple-element.106.refs_1_.proj_ref, bf16[64,3584]{1,0:T(8,128)(2,1)S(1)} %bitcast.41, ...), custom_call_target="tpu_custom_call" | custom-call | tf_op jit(solution)/shard_map/backward/pallas_call | solution.py:223
  73.7 0.0 collective-permute-done.18.up_other_ref
  73.7 0.1 collective-permute-start.21
  73.9 2.0 %weights.1 = (f32[64,3584]{1,0:T(8,128)}, f32[64,1024]{1,0:T(8,128)}) custom-call(s32[16]{0:T(128)S(1)} %stack.88.order_ref, f32[256,64]{1,0:T(8,128)S(1)} %get-tuple-element.106.refs_1_.proj_ref, f32[256,64]{1,0:T(8,128)S(1)} %collective-permute-done.17.from_ref, bf16[128,3584]{1,0:T(8,128)(2,1)S(1)} %copy-done.7, ...), custom_call_target="tpu_custom_call" | custom-call | tf_op jit(solution)/shard_map/weights/pallas_call | solution.py:280
  75.8 2.5 %collective-permute-done.15 = bf16[256,512]{1,0:T(8,128)(2,1)S(1)} collective-permute-done((bf16[256,512]{1,0:T(8,128)(2,1)S(1)}, bf16[256,512]{1,0:T(8,128)(2,1)S(1)}, u32[]{:S(2)}, u32[]{:S(2)}) %collective-permute-start.15) | collective-permute-done | bytes 262176 | tf_op jit(solution)/shard_map/ppermute | solution.py:329
  78.4 0.1 multiply_reduce_fusion
  78.5 0.1 collective-permute-start.19
  78.6 0.5 collective-permute-start.20
  79.1 1.7 %hidden.1 = bf16[128,3584]{1,0:T(8,128)(2,1)} custom-call(s32[16]{0:T(128)S(1)} %stack.88.order_ref, f32[128,1280]{1,0:T(8,128)S(1)} %get-tuple-element.118.ga_ref, bf16[128,1280]{1,0:T(8,128)(2,1)S(1)} %collective-permute-done.16.ra_ref, f32[128,2304]{1,0:T(8,128)S(1)} %get-tuple-element.120.gb_ref, bf16[128,2304]{1,0:T(8,128)(2,1)S(1)} %collective-permute-done.21.rb_ref), custom_call_target="tpu_custom_call" | custom-call | tf_op jit(solution)/shard_map/hidden/pallas_call | solution.py:280
  80.8 1.3 %mixed.1 = (bf16[128,1024]{1,0:T(8,128)(2,1)}, f32[8,128]{1,0:T(8,128)}) custom-call(s32[16]{0:T(128)S(1)} %stack.88.order_ref, bf16[256,512]{1,0:T(8,128)(2,1)S(1)} %get-tuple-element.130.m_ref, bf16[128,512]{1,0:T(8,128)(2,1)S(1)} %collective-permute-done.19.m_other_ref, f32[1,512]{1,0:T(1,128)S(1)} %slice_divide_fusion.g_ref, ...), custom_call_target="tpu_custom_call" | custom-call | tf_op jit(solution)/shard_map/mixed/pallas_call | solution.py:280
  (35 shorter events, 0.2 us)
Async XLA Ops:
  0.6 1.9 %collective-permute-start = (bf16[128,1024]{1,0:T(8,128)(2,1)}, bf16[128,1024]{1,0:T(8,128)(2,1)S(1)}, u32[]{:S(2)}, u32[]{:S(2)}) collective-permute-start(bf16[128,1024]{1,0:T(8,128)(2,1)} %own_ref.2), channel_id=1, source_target_pairs={{0,1},{1,0},{2,3},{3,2},{4,5},{5,4},{6,7},{7,6},{8,9},{9,8},{10,11... | collective-permute-start | bytes 786440 | tf_op jit(solution)/shard_map/ppermute | solution.py:324
  2.5 0.9 %copy-start.8 = (bf16[128,1024]{1,0:T(8,128)(2,1)S(1)}, bf16[128,1024]{1,0:T(8,128)(2,1)}, u32[]{:S(2)}) copy-start(bf16[128,1024]{1,0:T(8,128)(2,1)} %own_ref.2) | copy-start | bytes 786436
  4.0 17.4 %collective-permute-start.1 = (bf16[272,512]{1,0:T(8,128)(2,1)S(1)}, bf16[272,512]{1,0:T(8,128)(2,1)S(1)}, u32[]{:S(2)}, u32[]{:S(2)}) collective-permute-start(bf16[272,512]{1,0:T(8,128)(2,1)S(1)} %own_block.1.refs_0_), channel_id=1, source_target_pairs={{0,8},{1,9},{2,10},{3,11},{4,12},{5,13},{6,14},{7,15},{8,0},{9,1},... | collective-permute-start | bytes 835592 | tf_op jit(solution)/shard_map/ppermute | solution.py:329
  8.1 14.2 %collective-permute-start.2 = (bf16[272,512]{1,0:T(8,128)(2,1)S(1)}, bf16[272,512]{1,0:T(8,128)(2,1)S(1)}, u32[]{:S(2)}, u32[]{:S(2)}) collective-permute-start(bf16[272,512]{1,0:T(8,128)(2,1)S(1)} %own_block.1.refs_0_), channel_id=1, source_target_pairs={{0,4},{1,3},{2,6},{3,1},{4,0},{5,7},{6,2},{7,5},{8,12},{9,11},{10,... | collective-permute-start | bytes 835592 | tf_op jit(solution)/shard_map/ppermute | solution.py:329
  9.6 12.7 %collective-permute-start.3 = (bf16[272,512]{1,0:T(8,128)(2,1)S(1)}, bf16[272,512]{1,0:T(8,128)(2,1)S(1)}, u32[]{:S(2)}, u32[]{:S(2)}) collective-permute-start(bf16[272,512]{1,0:T(8,128)(2,1)S(1)} %own_block.1.refs_0_), channel_id=1, source_target_pairs={{0,2},{1,5},{2,0},{3,7},{4,6},{5,1},{6,4},{7,3},{8,10},{9,13},{10,... | collective-permute-start | bytes 835592 | tf_op jit(solution)/shard_map/ppermute | solution.py:329
  11.1 25.1 %collective-permute-start.8 = (bf16[128,3584]{1,0:T(8,128)(2,1)}, bf16[128,3584]{1,0:T(8,128)(2,1)S(1)}, u32[]{:S(2)}, u32[]{:S(2)}) collective-permute-start(bf16[128,3584]{1,0:T(8,128)(2,1)} %own_ref.3), channel_id=1, source_target_pairs={{0,1},{1,0},{2,3},{3,2},{4,5},{5,4},{6,7},{7,6},{8,9},{9,8},{10,11... | collective-permute-start | bytes 2752520 | tf_op jit(solution)/shard_map/ppermute | solution.py:324
  11.1 1.2 %copy-start = (bf16[64,8192]{1,0:T(8,128)(2,1)S(1)}, bf16[64,8192]{1,0:T(8,128)(2,1)}, u32[]{:S(2)}) copy-start(bf16[64,8192]{1,0:T(8,128)(2,1)} %refs_9_.1) | copy-start | bytes 3145732
  12.4 1.0 %copy-start.4 = (bf16[3584,64]{0,1:T(8,128)(2,1)S(1)}, bf16[3584,64]{0,1:T(8,128)(2,1)}, u32[]{:S(2)}) copy-start(bf16[3584,64]{0,1:T(8,128)(2,1)} %param.8) | copy-start | bytes 1376260
  13.4 1.2 %copy-start.6 = (bf16[128,3584]{1,0:T(8,128)(2,1)S(1)}, bf16[128,3584]{1,0:T(8,128)(2,1)}, u32[]{:S(2)}) copy-start(bf16[128,3584]{1,0:T(8,128)(2,1)} %own_ref.3) | copy-start | bytes 2752516
  14.6 9.8 %copy-start.1 = (bf16[64,8192]{1,0:T(8,128)(2,1)S(1)}, bf16[64,8192]{1,0:T(8,128)(2,1)}, u32[]{:S(2)}) copy-start(bf16[64,8192]{1,0:T(8,128)(2,1)} %refs_9_.1) | copy-start | bytes 3145732
  14.6 9.8 %copy-start.5 = (bf16[3584,64]{0,1:T(8,128)(2,1)S(1)}, bf16[3584,64]{0,1:T(8,128)(2,1)}, u32[]{:S(2)}) copy-start(bf16[3584,64]{0,1:T(8,128)(2,1)} %param.8) | copy-start | bytes 1376260
  22.4 13.8 %copy-start.7 = (bf16[128,3584]{1,0:T(8,128)(2,1)S(1)}, bf16[128,3584]{1,0:T(8,128)(2,1)}, u32[]{:S(2)}) copy-start(bf16[128,3584]{1,0:T(8,128)(2,1)} %own_ref.3) | copy-start | bytes 2752516
  22.4 11.8 %collective-permute-start.5 = (bf16[2,272,512]{2,1,0:T(8,128)(2,1)S(1)}, bf16[2,272,512]{2,1,0:T(8,128)(2,1)S(1)}, u32[]{:S(2)}, u32[]{:S(2)}) collective-permute-start(bf16[2,272,512]{2,1,0:T(8,128)(2,1)S(1)} %pad_maximum_fusion), channel_id=1, source_target_pairs={{0,2},{1,5},{2,0},{3,7},{4,6},{5,1},{6,4},{7,3},{8,10},{9,13},{10,... | collective-permute-start | bytes 1671176 | tf_op jit(solution)/shard_map/ppermute | solution.py:329
  23.2 9.6 %collective-permute-start.4 = (bf16[272,512]{1,0:T(8,128)(2,1)S(1)}, bf16[272,512]{1,0:T(8,128)(2,1)S(1)}, u32[]{:S(2)}, u32[]{:S(2)}) collective-permute-start(bf16[272,512]{1,0:T(8,128)(2,1)S(1)} %collective-permute-done.1.refs_1_), channel_id=1, source_target_pairs={{0,4},{1,3},{2,6},{3,1},{4,0},{5,7},{6,2},{7,5},{8,12},{9,11},{10,... | collective-permute-start | bytes 835592 | tf_op jit(solution)/shard_map/ppermute | solution.py:329
  31.4 17.9 %copy-start.2 = (bf16[3584,512]{1,0:T(8,128)(2,1)}, bf16[3584,512]{1,0:T(8,128)(2,1)S(1)}, u32[]{:S(2)}) copy-start(bf16[3584,512]{1,0:T(8,128)(2,1)S(1)} %get-tuple-element.89.refs_3_.refs_13_.refs_5_) | copy-start | bytes 11010052
  34.2 7.1 %collective-permute-start.7 = (bf16[272,512]{1,0:T(8,128)(2,1)S(1)}, bf16[272,512]{1,0:T(8,128)(2,1)S(1)}, u32[]{:S(2)}, u32[]{:S(2)}) collective-permute-start(bf16[272,512]{1,0:T(8,128)(2,1)S(1)} %collective-permute-done.4.refs_3_), channel_id=1, source_target_pairs={{0,2},{1,5},{2,0},{3,7},{4,6},{5,1},{6,4},{7,3},{8,10},{9,13},{10,... | collective-permute-start | bytes 835592 | tf_op jit(solution)/shard_map/ppermute | solution.py:329
  35.0 6.3 %collective-permute-start.6 = (f32[24,512]{1,0:T(8,128)S(1)}, f32[24,512]{1,0:T(8,128)S(1)}, u32[]{:S(2)}, u32[]{:S(2)}) collective-permute-start(f32[24,512]{1,0:T(8,128)S(1)} %get-tuple-element.75), channel_id=1, source_target_pairs={{0,2},{1,5},{2,0},{3,7},{4,6},{5,1},{6,4},{7,3},{8,10},{9,13},{10,... | collective-permute-start | bytes 147464 | tf_op jit(solution)/shard_map/ppermute | solution.py:329
  41.3 10.8 %collective-permute-start.11 = (bf16[2,256,512]{2,1,0:T(8,128)(2,1)S(1)}, bf16[2,256,512]{2,1,0:T(8,128)(2,1)S(1)}, u32[]{:S(2)}, u32[]{:S(2)}) collective-permute-start(bf16[2,256,512]{2,1,0:T(8,128)(2,1)S(1)} %get-tuple-element.87), channel_id=1, source_target_pairs={{0,2},{1,5},{2,0},{3,7},{4,6},{5,1},{6,4},{7,3},{8,10},{9,13},{10,... | collective-permute-start | bytes 1572872 | tf_op jit(solution)/shard_map/ppermute | solution.py:329
  42.1 4.7 %collective-permute-start.9 = (f32[24,512]{1,0:T(8,128)S(1)}, f32[24,512]{1,0:T(8,128)S(1)}, u32[]{:S(2)}, u32[]{:S(2)}) collective-permute-start(f32[24,512]{1,0:T(8,128)S(1)} %add.56), channel_id=1, source_target_pairs={{0,4},{1,3},{2,6},{3,1},{4,0},{5,7},{6,2},{7,5},{8,12},{9,11},{10,... | collective-permute-start | bytes 147464 | tf_op jit(solution)/shard_map/ppermute | solution.py:329
  46.8 5.2 %collective-permute-start.10 = (f32[24,512]{1,0:T(8,128)S(1)}, f32[24,512]{1,0:T(8,128)S(1)}, u32[]{:S(2)}, u32[]{:S(2)}) collective-permute-start(f32[24,512]{1,0:T(8,128)S(1)} %add.57), channel_id=1, source_target_pairs={{0,8},{1,9},{2,10},{3,11},{4,12},{5,13},{6,14},{7,15},{8,0},{9,1},... | collective-permute-start | bytes 147464 | tf_op jit(solution)/shard_map/ppermute | solution.py:329
  48.7 14.5 %collective-permute-start.13 = (bf16[2,256,512]{2,1,0:T(8,128)(2,1)S(1)}, bf16[2,256,512]{2,1,0:T(8,128)(2,1)S(1)}, u32[]{:S(2)}, u32[]{:S(2)}) collective-permute-start(bf16[2,256,512]{2,1,0:T(8,128)(2,1)S(1)} %forward.5), channel_id=1, source_target_pairs={{0,2},{1,5},{2,0},{3,7},{4,6},{5,1},{6,4},{7,3},{8,10},{9,13},{10,... | collective-permute-start | bytes 1572872 | tf_op jit(solution)/shard_map/ppermute | solution.py:329
  52.2 11.0 %collective-permute-start.12 = (bf16[2,256,512]{2,1,0:T(8,128)(2,1)S(1)}, bf16[2,256,512]{2,1,0:T(8,128)(2,1)S(1)}, u32[]{:S(2)}, u32[]{:S(2)}) collective-permute-start(bf16[2,256,512]{2,1,0:T(8,128)(2,1)S(1)} %add_convert_fusion), channel_id=1, source_target_pairs={{0,4},{1,3},{2,6},{3,1},{4,0},{5,7},{6,2},{7,5},{8,12},{9,11},{10,... | collective-permute-start | bytes 1572872 | tf_op jit(solution)/shard_map/ppermute | solution.py:329
  54.2 8.7 %collective-permute-start.14 = (f32[16,512]{1,0:T(8,128)S(1)}, f32[16,512]{1,0:T(8,128)S(1)}, u32[]{:S(2)}, u32[]{:S(2)}) collective-permute-start(f32[16,512]{1,0:T(8,128)S(1)} %slice.81), channel_id=1, source_target_pairs={{0,1},{1,0},{2,3},{3,2},{4,5},{5,4},{6,7},{7,6},{8,9},{9,8},{10,11... | collective-permute-start | bytes 98312 | tf_op jit(solution)/shard_map/ppermute | solution.py:324
  54.3 2.8 %copy-start.3 = (bf16[3584,512]{1,0:T(8,128)(2,1)S(1)}, bf16[3584,512]{1,0:T(8,128)(2,1)}, u32[]{:S(2)}) copy-start(bf16[3584,512]{1,0:T(8,128)(2,1)} %copy-done.2) | copy-start | bytes 11010052
  62.4 11.3 %collective-permute-start.16 = (bf16[128,1280]{1,0:T(8,128)(2,1)S(1)}, bf16[128,1280]{1,0:T(8,128)(2,1)S(1)}, u32[]{:S(2)}, u32[]{:S(2)}) collective-permute-start(bf16[128,1280]{1,0:T(8,128)(2,1)S(1)} %get-tuple-element.107), channel_id=1, source_target_pairs={{0,1},{1,0},{2,3},{3,2},{4,5},{5,4},{6,7},{7,6},{8,9},{9,8},{10,11... | collective-permute-start | bytes 983048 | tf_op jit(solution)/shard_map/ppermute | solution.py:324
  63.4 15.0 %collective-permute-start.15 = (bf16[256,512]{1,0:T(8,128)(2,1)S(1)}, bf16[256,512]{1,0:T(8,128)(2,1)S(1)}, u32[]{:S(2)}, u32[]{:S(2)}) collective-permute-start(bf16[256,512]{1,0:T(8,128)(2,1)S(1)} %fusion.2), channel_id=1, source_target_pairs={{0,8},{1,9},{2,10},{3,11},{4,12},{5,13},{6,14},{7,15},{8,0},{9,1},... | collective-permute-start | bytes 786440 | tf_op jit(solution)/shard_map/ppermute | solution.py:329
  65.6 8.1 %collective-permute-start.18 = (f32[64,512]{1,0:T(8,128)S(1)}, f32[64,512]{1,0:T(8,128)S(1)}, u32[]{:S(2)}, u32[]{:S(2)}) collective-permute-start(f32[64,512]{1,0:T(8,128)S(1)} %fusion.up_ref), channel_id=1, source_target_pairs={{0,1},{1,0},{2,3},{3,2},{4,5},{5,4},{6,7},{7,6},{8,9},{9,8},{10,11... | collective-permute-start | bytes 393224 | tf_op jit(solution)/shard_map/ppermute | solution.py:324
  65.7 8.0 %collective-permute-start.17 = (f32[256,64]{1,0:T(8,128)S(1)}, f32[256,64]{1,0:T(8,128)S(1)}, u32[]{:S(2)}, u32[]{:S(2)}) collective-permute-start(f32[256,64]{1,0:T(8,128)S(1)} %get-tuple-element.106.refs_1_.proj_ref), channel_id=1, source_target_pairs={{0,1},{1,0},{2,3},{3,2},{4,5},{5,4},{6,7},{7,6},{8,9},{9,8},{10,11... | collective-permute-start | bytes 196616 | tf_op jit(solution)/shard_map/ppermute | solution.py:324
  73.7 5.4 %collective-permute-start.21 = (bf16[128,2304]{1,0:T(8,128)(2,1)S(1)}, bf16[128,2304]{1,0:T(8,128)(2,1)S(1)}, u32[]{:S(2)}, u32[]{:S(2)}) collective-permute-start(bf16[128,2304]{1,0:T(8,128)(2,1)S(1)} %get-tuple-element.121), channel_id=1, source_target_pairs={{0,1},{1,0},{2,3},{3,2},{4,5},{5,4},{6,7},{7,6},{8,9},{9,8},{10,11... | collective-permute-start | bytes 1769480 | tf_op jit(solution)/shard_map/ppermute | solution.py:324
  78.5 2.3 %collective-permute-start.19 = (bf16[128,512]{1,0:T(8,128)(2,1)S(1)}, bf16[128,512]{1,0:T(8,128)(2,1)S(1)}, u32[]{:S(2)}, u32[]{:S(2)}) collective-permute-start(bf16[128,512]{1,0:T(8,128)(2,1)S(1)} %slice.88), channel_id=1, source_target_pairs={{0,1},{1,0},{2,3},{3,2},{4,5},{5,4},{6,7},{7,6},{8,9},{9,8},{10,11... | collective-permute-start | bytes 393224 | tf_op jit(solution)/shard_map/ppermute | solution.py:324
  78.6 2.2 %collective-permute-start.20 = (f32[1,512]{1,0:T(1,128)S(1)}, f32[1,512]{1,0:T(1,128)S(1)}, u32[]{:S(2)}, u32[]{:S(2)}) collective-permute-start(f32[1,512]{1,0:T(1,128)S(1)} %slice_divide_fusion.g_ref), channel_id=1, source_target_pairs={{0,1},{1,0},{2,3},{3,2},{4,5},{5,4},{6,7},{7,6},{8,9},{9,8},{10,11... | collective-permute-start | bytes 6152 | tf_op jit(solution)/shard_map/ppermute | solution.py:324

commit v12 on v11

--- a/solution.py
+++ b/solution.py
@@ -352,32 +352,32 @@
     block = own_block(order, cotangent, cot_other, magnitude_rows)
 
     cots = {0b000: block, 0b001: send(block, 2), 0b010: send(block, 1), 0b100: send(block, 0)}
+    across = [(2 * t + c, 2 * (t ^ orders[c][0] ^ orders[c][1]) + c) for t in range(n) for c in range(2)]
+    cots[0b110] = lax.ppermute(block, ("tensor", "dp"), across)
 
     run_load = functools.partial(load, at=at, up=up, weight=weight, half=half)
     block, order = tie((block, order))
-    *far, stats = run_load(tuple(range(n // 2, n)), order, own=hidden)
-    cots[0b001], cots[0b010], cots[0b100], stats = tie((cots[0b001], cots[0b010], cots[0b100], stats))
-    cots[0b011] = send(cots[0b001], 1)
-    pair = send(jnp.stack([cots[0b001], cots[0b010]]), 0)
-    *near, stats = run_load(tuple(range(n // 2)), order, before=stats)
-    held = near + far
-    cots[0b011], pair, stats = tie((cots[0b011], pair, stats))
-    cots[0b101], cots[0b110] = pair[0], pair[1]
+    *held, stats = run_load(tuple(range(n)), order, own=hidden)
+    near, far = held[: n // 2], held[n // 2 :]
+    cots[0b001], cots[0b010], cots[0b100], cots[0b110], stats = tie(
+        (cots[0b001], cots[0b010], cots[0b100], cots[0b110], stats)
+    )
+    cots[0b011], cots[0b101] = send(cots[0b001], 1), send(cots[0b001], 0)
     got = send(stats, 0)
-    cots[0b111] = send(cots[0b011], 0)
     far1, lhs, adapter = forward((0b110, 0b111), order, far[2:], up, first=(hidden, hidden_other, at))
     run = lambda order, vs, held: forward(vs, order, held, up, later=(lhs, adapter))[0]
-    got, cots[0b111], far1, order = tie((got, cots[0b111], far1, order))
+    got, cots[0b011], far1, order = tie((got, cots[0b011], far1, order))
+    cots[0b111] = send(cots[0b011], 0)
     stats = stats + got
     got = send(stats, 1)
     from1 = send(far1, 0)
     far0 = run(order, (0b100, 0b101), far[:2])
-    got, far0, order = tie((got, far0, order))
+    got, cots[0b101], far0, order = tie((got, cots[0b101], far0, order))
     stats = stats + got
     got = send(stats, 2)
     from0 = send(far0, 0)
     near1 = run(order, (0b010, 0b011), near[2:])
-    got, from1, near1, order = tie((got, from1, near1, order))
+    got, from1, cots[0b111], near1, order = tie((got, from1, cots[0b111], near1, order))
     stats = stats + got
     arrived = send((near1.astype(f32) + from1.astype(f32)).astype(bf16), 1)
     lowrank_rows = stats[n:]

time: 82.4 us -> 83.4 us (1.012)
  waiting for transfers between devices: 8.5 us -> 13.3 us
  Pallas kernels: 44.5 us -> 41.8 us
  starting transfers between devices: 21.8 us -> 20.7 us
    ppermute x13, waiting for transfers between devices: 8.09 us -> 10.8 us  [send(): return lax.ppermute(x, ('tensor', 'dp'), pairs)]
    pallas_call x2 -> x1, Pallas kernels: 13.8 us -> 11.3 us  [load(): pl.pallas_call(functools.partial(load_kernel, tokens, rank, n, vs, first)...]
    ppermute x0 -> x1, waiting for transfers between devices: none -> 2.14 us  [split_columns(): cots[6] = lax.ppermute(block, ('tensor', 'dp'), across)]
    ppermute x13, starting transfers between devices: 19.4 us -> 17.8 us  [send(): return lax.ppermute(x, ('tensor', 'dp'), pairs)]
  transfers between devices with their start and end apart: 22 -> 23, of which waited for: 8 -> 6; matrix products, arithmetic and copies ran while one was open for 2% -> 2% of each run, Pallas kernels for 52% -> 49%
where the time goes in v12:
time: 83.4 us; the launch traced here: 83.1 us
  Pallas kernels  41.8 us (50%)
  starting transfers between devices  20.7 us (25%)
  waiting for transfers between devices  13.3 us (16%)
  local copies, waits for them, and re-layouts  4.64 us (6%)
  other arithmetic  1.29 us (2%)
  between operations  0.94 us (1%)
    ppermute x13, starting transfers between devices, send(): return lax.ppermute(x, ('tensor', 'dp'), pairs)  17.8 us
    pallas_call x2, Pallas kernels, backward(): pl.pallas_call(functools.partial(backward_kernel, tokens, n, start, band,...  12.7 us
    pallas_call x4, Pallas kernels, forward(): pl.pallas_call(functools.partial(forward_kernel, tokens, rank, vs, later...  12.3 us
    pallas_call x1, Pallas kernels, load(): pl.pallas_call(functools.partial(load_kernel, tokens, rank, n, vs, first)...  11.3 us
    ppermute x13, waiting for transfers between devices, send(): return lax.ppermute(x, ('tensor', 'dp'), pairs)  10.8 us
    pallas_call x3, Pallas kernels, finish(): pl.pallas_call(kernel, grid_spec=pltpu.PrefetchScalarGridSpec(num_scalar_...  4.9 us
    unnamed x18, local copies, waits for them, and re-layouts  4.39 us
    ppermute x9, starting transfers between devices, split_columns(): swap = lambda x: lax.ppermute(x, 'dp', [(0, 1), (1, 0)])  2.46 us
  transfers between devices with their start and end apart: 23, of which 6 were waited for; matrix products, arithmetic and copies ran while one was open for 2% of the time, Pallas kernels for 49%

profile of v12, /device:TPU:0, one launch (start us, length us, event | category | flops | bytes accessed | tf_op | source)
XLA Modules:
  0.0 83.1 jit_solution(9313210057276085298)
XLA Ops:
  0.6 0.5 collective-permute-start
  1.1 0.1 collective-permute-start.7
  1.2 0.7 reduce-precision_convert_fusion.1
  2.0 0.1 pad.11.clone
  2.0 0.1 stack.79.order_ref
  2.1 0.1 maximum_maximum_fusion.magnitude_ref
  2.2 0.3 collective-permute-done.other_ref
  2.5 0.9 %copy-done.8 = bf16[128,1024]{1,0:T(8,128)(2,1)S(1)} copy-done((bf16[128,1024]{1,0:T(8,128)(2,1)S(1)}, bf16[128,1024]{1,0:T(8,128)(2,1)}, u32[]{:S(2)}) %copy-start.8) | copy-done | bytes 262168
  3.5 0.6 own_block.1.refs_0_
  4.0 4.0 %collective-permute-start.1 = (bf16[272,512]{1,0:T(8,128)(2,1)S(1)}, bf16[272,512]{1,0:T(8,128)(2,1)S(1)}, u32[]{:S(2)}, u32[]{:S(2)}) collective-permute-start(bf16[272,512]{1,0:T(8,128)(2,1)S(1)} %own_block.1.refs_0_), channel_id=1, source_target_pairs={{0,8},{1,9},{2,10},{3,11},{4,12},{5,13},{6,14},{7,15},{8,0},{9,1},... | collective-permute-start | bytes 835592 | tf_op jit(solution)/shard_map/ppermute | solution.py:329
  8.1 1.6 %collective-permute-start.2 = (bf16[272,512]{1,0:T(8,128)(2,1)S(1)}, bf16[272,512]{1,0:T(8,128)(2,1)S(1)}, u32[]{:S(2)}, u32[]{:S(2)}) collective-permute-start(bf16[272,512]{1,0:T(8,128)(2,1)S(1)} %own_block.1.refs_0_), channel_id=1, source_target_pairs={{0,4},{1,3},{2,6},{3,1},{4,0},{5,7},{6,2},{7,5},{8,12},{9,11},{10,... | collective-permute-start | bytes 835592 | tf_op jit(solution)/shard_map/ppermute | solution.py:329
  9.6 1.5 %collective-permute-start.3 = (bf16[272,512]{1,0:T(8,128)(2,1)S(1)}, bf16[272,512]{1,0:T(8,128)(2,1)S(1)}, u32[]{:S(2)}, u32[]{:S(2)}) collective-permute-start(bf16[272,512]{1,0:T(8,128)(2,1)S(1)} %own_block.1.refs_0_), channel_id=1, source_target_pairs={{0,2},{1,5},{2,0},{3,7},{4,6},{5,1},{6,4},{7,3},{8,10},{9,13},{10,... | collective-permute-start | bytes 835592 | tf_op jit(solution)/shard_map/ppermute | solution.py:329
  11.1 0.4 collective-permute-start.4
  11.6 1.2 %copy-done = bf16[64,8192]{1,0:T(8,128)(2,1)S(1)} copy-done((bf16[64,8192]{1,0:T(8,128)(2,1)S(1)}, bf16[64,8192]{1,0:T(8,128)(2,1)}, u32[]{:S(2)}) %copy-start) | copy-done | bytes 1048600
  12.8 1.2 %copy-done.4 = bf16[128,3584]{1,0:T(8,128)(2,1)S(1)} copy-done((bf16[128,3584]{1,0:T(8,128)(2,1)S(1)}, bf16[128,3584]{1,0:T(8,128)(2,1)}, u32[]{:S(2)}) %copy-start.4) | copy-done | bytes 917528
  14.0 1.0 %copy-done.6 = bf16[3584,64]{0,1:T(8,128)(2,1)S(1)} copy-done((bf16[3584,64]{0,1:T(8,128)(2,1)S(1)}, bf16[3584,64]{0,1:T(8,128)(2,1)}, u32[]{:S(2)}) %copy-start.6) | copy-done | bytes 458776
  15.0 11.3 %load.1 = (bf16[3584,512]{1,0:T(8,128)(2,1)S(1)}, bf16[3584,512]{1,0:T(8,128)(2,1)S(1)}, bf16[3584,512]{1,0:T(8,128)(2,1)S(1)}, bf16[3584,512]{1,0:T(8,128)(2,1)...) custom-call(s32[16]{0:T(128)S(1)} %stack.79.order_ref, ...), custom_call_target="tpu_custom_call" | custom-call | tf_op jit(solution)/shard_map/load/pallas_call | solution.py:116
  26.3 0.0 collective-permute-done.3.refs_4_
  26.4 2.1 %collective-permute-done.4.refs_6_ = bf16[272,512]{1,0:T(8,128)(2,1)S(1)} collective-permute-done((bf16[272,512]{1,0:T(8,128)(2,1)S(1)}, bf16[272,512]{1,0:T(8,128)(2,1)S(1)}, u32[]{:S(2)}, u32[]{:S(2)}) %collective-permute-start.4) | collective-permute-done | bytes 278560 | tf_op jit(solution)/shard_map/ppermute | solution.py:356
  28.5 1.2 %collective-permute-start.6 = (bf16[272,512]{1,0:T(8,128)(2,1)S(1)}, bf16[272,512]{1,0:T(8,128)(2,1)S(1)}, u32[]{:S(2)}, u32[]{:S(2)}) collective-permute-start(bf16[272,512]{1,0:T(8,128)(2,1)S(1)} %collective-permute-done.1.refs_1_), channel_id=1, source_target_pairs={{0,4},{1,3},{2,6},{3,1},{4,0},{5,7},{6,2},{7,5},{8,12},{9,11},{10,... | collective-permute-start | bytes 835592 | tf_op jit(solution)/shard_map/ppermute | solution.py:329
  29.7 0.5 collective-permute-start.5
  30.2 4.1 %forward.4 = (bf16[2,256,512]{2,1,0:T(8,128)(2,1)S(1)}, bf16[256,3584]{1,0:T(8,128)(2,1)S(1)}, bf16[256,128]{1,0:T(8,128)(2,1)S(1)}) custom-call(s32[16]{0:T(128)S(1)} %stack.79.order_ref, bf16[128,3584]{1,0:T(8,128)(2,1)S(1)} %copy-done.4, bf16[128,3584]{1,0:T(8,128)(2,1)S(1)} %collective-permute-done.7.refs_1_.other_ref, bf16[64,3584]{1,0:T(8,128)(2,1)S(1)} %bitcast.32, ...), custom_call_target="tpu_custom_call" | custom-call | tf_op jit(solution)/shard_map/forward/pallas_call | solution.py:158
  34.3 1.2 %collective-permute-done.6.refs_3_ = bf16[272,512]{1,0:T(8,128)(2,1)S(1)} collective-permute-done((bf16[272,512]{1,0:T(8,128)(2,1)S(1)}, bf16[272,512]{1,0:T(8,128)(2,1)S(1)}, u32[]{:S(2)}, u32[]{:S(2)}) %collective-permute-start.6) | collective-permute-done | bytes 278560 | tf_op jit(solution)/shard_map/ppermute | solution.py:329
  35.6 0.7 collective-permute-start.11
  36.3 1.3 %collective-permute-start.9 = (bf16[272,512]{1,0:T(8,128)(2,1)S(1)}, bf16[272,512]{1,0:T(8,128)(2,1)S(1)}, u32[]{:S(2)}, u32[]{:S(2)}) collective-permute-start(bf16[272,512]{1,0:T(8,128)(2,1)S(1)} %collective-permute-done.1.refs_1_), channel_id=1, source_target_pairs={{0,2},{1,5},{2,0},{3,7},{4,6},{5,1},{6,4},{7,3},{8,10},{9,13},{10,... | collective-permute-start | bytes 835592 | tf_op jit(solution)/shard_map/ppermute | solution.py:329
  37.6 0.7 collective-permute-start.12
  38.3 0.6 collective-permute-start.8
  38.9 2.8 %forward.5 = bf16[2,256,512]{2,1,0:T(8,128)(2,1)S(1)} custom-call(s32[16]{0:T(128)S(1)} %stack.79.order_ref, bf16[256,3584]{1,0:T(8,128)(2,1)S(1)} %get-tuple-element.77.refs_0_, bf16[256,128]{1,0:T(8,128)(2,1)S(1)} %get-tuple-element.78.refs_1_, bf16[64,8192]{1,0:T(8,128)(2,1)S(1)} %copy-done.1, ...), custom_call_target="tpu_custom_call" | custom-call | tf_op jit(solution)/shard_map/forward/pallas_call | solution.py:158
  41.7 6.5 %collective-permute-done.9.refs_5_ = bf16[272,512]{1,0:T(8,128)(2,1)S(1)} collective-permute-done((bf16[272,512]{1,0:T(8,128)(2,1)S(1)}, bf16[272,512]{1,0:T(8,128)(2,1)S(1)}, u32[]{:S(2)}, u32[]{:S(2)}) %collective-permute-start.9) | collective-permute-done | bytes 278560 | tf_op jit(solution)/shard_map/ppermute | solution.py:329
  48.3 0.0 collective-permute-done.8
  48.3 1.5 %collective-permute-start.10 = (f32[24,512]{1,0:T(8,128)S(1)}, f32[24,512]{1,0:T(8,128)S(1)}, u32[]{:S(2)}, u32[]{:S(2)}) collective-permute-start(f32[24,512]{1,0:T(8,128)S(1)} %add.57), channel_id=1, source_target_pairs={{0,8},{1,9},{2,10},{3,11},{4,12},{5,13},{6,14},{7,15},{8,0},{9,1},... | collective-permute-start | bytes 147464 | tf_op jit(solution)/shard_map/ppermute | solution.py:329
  49.8 0.8 collective-permute-start.14
  50.5 2.7 %forward.6 = bf16[2,256,512]{2,1,0:T(8,128)(2,1)S(1)} custom-call(s32[16]{0:T(128)S(1)} %stack.79.order_ref, bf16[256,3584]{1,0:T(8,128)(2,1)S(1)} %get-tuple-element.77.refs_0_, bf16[256,128]{1,0:T(8,128)(2,1)S(1)} %get-tuple-element.78.refs_1_, bf16[64,8192]{1,0:T(8,128)(2,1)S(1)} %copy-done.1, ...), custom_call_target="tpu_custom_call" | custom-call | tf_op jit(solution)/shard_map/forward/pallas_call | solution.py:158
  53.3 0.4 collective-permute-done.10
  53.7 0.1 add_convert_fusion
  53.8 1.2 %collective-permute-start.13 = (bf16[2,256,512]{2,1,0:T(8,128)(2,1)S(1)}, bf16[2,256,512]{2,1,0:T(8,128)(2,1)S(1)}, u32[]{:S(2)}, u32[]{:S(2)}) collective-permute-start(bf16[2,256,512]{2,1,0:T(8,128)(2,1)S(1)} %add_convert_fusion), channel_id=1, source_target_pairs={{0,4},{1,3},{2,6},{3,1},{4,0},{5,7},{6,2},{7,5},{8,12},{9,11},{10,... | collective-permute-start | bytes 1572872 | tf_op jit(solution)/shard_map/ppermute | solution.py:329
  55.1 0.1 collective-permute-start.15
  55.2 0.0 copy-start.7
  55.2 2.7 %forward.7 = bf16[2,256,512]{2,1,0:T(8,128)(2,1)S(1)} custom-call(s32[16]{0:T(128)S(1)} %stack.79.order_ref, bf16[256,3584]{1,0:T(8,128)(2,1)S(1)} %get-tuple-element.77.refs_0_, bf16[256,128]{1,0:T(8,128)(2,1)S(1)} %get-tuple-element.78.refs_1_, bf16[64,8192]{1,0:T(8,128)(2,1)S(1)} %copy-done.1, bf16[3584,512]{1,0:T(8,128)(2,1)S(1)} %get-tuple-element.88.refs_3_.refs_11_, ...), custom_call_target="tpu_custom_call" | custom-call | tf_op jit(solution)/shard_map/forward/pallas_call | solution.py:158
  58.0 5.3 %backward.2 = (f32[128,1280]{1,0:T(8,128)S(1)}, bf16[128,1280]{1,0:T(8,128)(2,1)S(1)}, bf16[256,4096]{1,0:T(8,128)(2,1)S(1)}, f32[256,64]{1,0:T(8,128)S(1)}, f32...) custom-call(s32[16]{0:T(128)S(1)} %stack.79.order_ref, bf16[272,512]{1,0:T(8,128)(2,1)S(1)} %own_block.1.refs_0_, ...), custom_call_target="tpu_custom_call" | custom-call | tf_op jit(solution)/shard_map/backward/pallas_call | solution.py:223
  63.3 0.5 collective-permute-start.17
  63.8 0.0 collective-permute-done.15
  63.8 0.0 collective-permute-done.14
  63.8 0.0 collective-permute-done.13
  63.8 0.2 convert_add_fusion
  64.1 2.2 %collective-permute-start.16 = (bf16[256,512]{1,0:T(8,128)(2,1)S(1)}, bf16[256,512]{1,0:T(8,128)(2,1)S(1)}, u32[]{:S(2)}, u32[]{:S(2)}) collective-permute-start(bf16[256,512]{1,0:T(8,128)(2,1)S(1)} %fusion.2), channel_id=1, source_target_pairs={{0,8},{1,9},{2,10},{3,11},{4,12},{5,13},{6,14},{7,15},{8,0},{9,1},... | collective-permute-start | bytes 786440 | tf_op jit(solution)/shard_map/ppermute | solution.py:329
  66.2 0.2 fusion.3
  66.4 0.2 fusion.up_ref
  66.6 0.1 collective-permute-start.19
  66.7 0.5 collective-permute-start.18
  67.2 7.4 %backward.3 = (f32[128,2304]{1,0:T(8,128)S(1)}, bf16[128,2304]{1,0:T(8,128)(2,1)S(1)}) custom-call(s32[16]{0:T(128)S(1)} %stack.79.order_ref, bf16[256,4096]{1,0:T(8,128)(2,1)S(1)} %get-tuple-element.108.refs_0_, f32[256,64]{1,0:T(8,128)S(1)} %get-tuple-element.104.refs_1_.proj_ref, bf16[64,3584]{1,0:T(8,128)(2,1)S(1)} %bitcast.34, ...), custom_call_target="tpu_custom_call" | custom-call | tf_op jit(solution)/shard_map/backward/pallas_call | solution.py:223
  74.6 0.0 collective-permute-done.17.ra_ref
  74.7 0.0 collective-permute-done.19.up_other_ref
  74.7 0.1 collective-permute-start.22
  74.8 2.0 %weights.1 = (f32[64,3584]{1,0:T(8,128)}, f32[64,1024]{1,0:T(8,128)}) custom-call(s32[16]{0:T(128)S(1)} %stack.79.order_ref, f32[256,64]{1,0:T(8,128)S(1)} %get-tuple-element.104.refs_1_.proj_ref, f32[256,64]{1,0:T(8,128)S(1)} %collective-permute-done.18.from_ref, bf16[128,3584]{1,0:T(8,128)(2,1)S(1)} %copy-done.5, ...), custom_call_target="tpu_custom_call" | custom-call | tf_op jit(solution)/shard_map/weights/pallas_call | solution.py:280
  76.8 2.6 %collective-permute-done.16 = bf16[256,512]{1,0:T(8,128)(2,1)S(1)} collective-permute-done((bf16[256,512]{1,0:T(8,128)(2,1)S(1)}, bf16[256,512]{1,0:T(8,128)(2,1)S(1)}, u32[]{:S(2)}, u32[]{:S(2)}) %collective-permute-start.16) | collective-permute-done | bytes 262176 | tf_op jit(solution)/shard_map/ppermute | solution.py:329
  79.4 0.2 multiply_reduce_fusion
  79.6 0.1 collective-permute-start.20
  79.7 0.5 collective-permute-start.21
  80.2 0.0 collective-permute-done.22.rb_ref
  80.2 1.6 %hidden.1 = bf16[128,3584]{1,0:T(8,128)(2,1)} custom-call(s32[16]{0:T(128)S(1)} %stack.79.order_ref, f32[128,1280]{1,0:T(8,128)S(1)} %get-tuple-element.116.ga_ref, bf16[128,1280]{1,0:T(8,128)(2,1)S(1)} %collective-permute-done.17.ra_ref, f32[128,2304]{1,0:T(8,128)S(1)} %get-tuple-element.118.gb_ref, bf16[128,2304]{1,0:T(8,128)(2,1)S(1)} %collective-permute-done.22.rb_ref), custom_call_target="tpu_custom_call" | custom-call | tf_op jit(solution)/shard_map/hidden/pallas_call | solution.py:280
  81.8 0.0 collective-permute-done.21.g_other_ref
  81.8 0.0 collective-permute-done.20.m_other_ref
  81.8 1.3 %mixed.1 = (bf16[128,1024]{1,0:T(8,128)(2,1)}, f32[8,128]{1,0:T(8,128)}) custom-call(s32[16]{0:T(128)S(1)} %stack.79.order_ref, bf16[256,512]{1,0:T(8,128)(2,1)S(1)} %get-tuple-element.128.m_ref, bf16[128,512]{1,0:T(8,128)(2,1)S(1)} %collective-permute-done.20.m_other_ref, f32[1,512]{1,0:T(1,128)S(1)} %slice_divide_fusion.g_ref, ...), custom_call_target="tpu_custom_call" | custom-call | tf_op jit(solution)/shard_map/mixed/pallas_call | solution.py:280
  (34 shorter events, 0.2 us)
Async XLA Ops:
  0.6 1.9 %collective-permute-start = (bf16[128,1024]{1,0:T(8,128)(2,1)}, bf16[128,1024]{1,0:T(8,128)(2,1)S(1)}, u32[]{:S(2)}, u32[]{:S(2)}) collective-permute-start(bf16[128,1024]{1,0:T(8,128)(2,1)} %own_ref.2), channel_id=1, source_target_pairs={{0,1},{1,0},{2,3},{3,2},{4,5},{5,4},{6,7},{7,6},{8,9},{9,8},{10,11... | collective-permute-start | bytes 786440 | tf_op jit(solution)/shard_map/ppermute | solution.py:324
  1.1 29.1 %collective-permute-start.7 = (bf16[128,3584]{1,0:T(8,128)(2,1)}, bf16[128,3584]{1,0:T(8,128)(2,1)S(1)}, u32[]{:S(2)}, u32[]{:S(2)}) collective-permute-start(bf16[128,3584]{1,0:T(8,128)(2,1)} %own_ref.3), channel_id=1, source_target_pairs={{0,1},{1,0},{2,3},{3,2},{4,5},{5,4},{6,7},{7,6},{8,9},{9,8},{10,11... | collective-permute-start | bytes 2752520 | tf_op jit(solution)/shard_map/ppermute | solution.py:324
  2.5 0.9 %copy-start.8 = (bf16[128,1024]{1,0:T(8,128)(2,1)S(1)}, bf16[128,1024]{1,0:T(8,128)(2,1)}, u32[]{:S(2)}) copy-start(bf16[128,1024]{1,0:T(8,128)(2,1)} %own_ref.2) | copy-start | bytes 786436
  4.0 22.3 %collective-permute-start.1 = (bf16[272,512]{1,0:T(8,128)(2,1)S(1)}, bf16[272,512]{1,0:T(8,128)(2,1)S(1)}, u32[]{:S(2)}, u32[]{:S(2)}) collective-permute-start(bf16[272,512]{1,0:T(8,128)(2,1)S(1)} %own_block.1.refs_0_), channel_id=1, source_target_pairs={{0,8},{1,9},{2,10},{3,11},{4,12},{5,13},{6,14},{7,15},{8,0},{9,1},... | collective-permute-start | bytes 835592 | tf_op jit(solution)/shard_map/ppermute | solution.py:329
  8.1 18.3 %collective-permute-start.2 = (bf16[272,512]{1,0:T(8,128)(2,1)S(1)}, bf16[272,512]{1,0:T(8,128)(2,1)S(1)}, u32[]{:S(2)}, u32[]{:S(2)}) collective-permute-start(bf16[272,512]{1,0:T(8,128)(2,1)S(1)} %own_block.1.refs_0_), channel_id=1, source_target_pairs={{0,4},{1,3},{2,6},{3,1},{4,0},{5,7},{6,2},{7,5},{8,12},{9,11},{10,... | collective-permute-start | bytes 835592 | tf_op jit(solution)/shard_map/ppermute | solution.py:329
  9.6 16.7 %collective-permute-start.3 = (bf16[272,512]{1,0:T(8,128)(2,1)S(1)}, bf16[272,512]{1,0:T(8,128)(2,1)S(1)}, u32[]{:S(2)}, u32[]{:S(2)}) collective-permute-start(bf16[272,512]{1,0:T(8,128)(2,1)S(1)} %own_block.1.refs_0_), channel_id=1, source_target_pairs={{0,2},{1,5},{2,0},{3,7},{4,6},{5,1},{6,4},{7,3},{8,10},{9,13},{10,... | collective-permute-start | bytes 835592 | tf_op jit(solution)/shard_map/ppermute | solution.py:329
  11.1 17.4 %collective-permute-start.4 = (bf16[272,512]{1,0:T(8,128)(2,1)S(1)}, bf16[272,512]{1,0:T(8,128)(2,1)S(1)}, u32[]{:S(2)}, u32[]{:S(2)}) collective-permute-start(bf16[272,512]{1,0:T(8,128)(2,1)S(1)} %own_block.1.refs_0_), channel_id=1, source_target_pairs={{0,6},{1,7},{2,4},{3,5},{4,2},{5,3},{6,0},{7,1},{8,14},{9,15},{10,... | collective-permute-start | bytes 835592 | tf_op jit(solution)/shard_map/ppermute | solution.py:356
  11.6 1.2 %copy-start = (bf16[64,8192]{1,0:T(8,128)(2,1)S(1)}, bf16[64,8192]{1,0:T(8,128)(2,1)}, u32[]{:S(2)}) copy-start(bf16[64,8192]{1,0:T(8,128)(2,1)} %refs_9_.1) | copy-start | bytes 3145732
  12.8 1.2 %copy-start.4 = (bf16[128,3584]{1,0:T(8,128)(2,1)S(1)}, bf16[128,3584]{1,0:T(8,128)(2,1)}, u32[]{:S(2)}) copy-start(bf16[128,3584]{1,0:T(8,128)(2,1)} %own_ref.3) | copy-start | bytes 2752516
  14.0 1.0 %copy-start.6 = (bf16[3584,64]{0,1:T(8,128)(2,1)S(1)}, bf16[3584,64]{0,1:T(8,128)(2,1)}, u32[]{:S(2)}) copy-start(bf16[3584,64]{0,1:T(8,128)(2,1)} %param.8) | copy-start | bytes 1376260
  26.3 12.6 %copy-start.2 = (bf16[3584,512]{1,0:T(8,128)(2,1)}, bf16[3584,512]{1,0:T(8,128)(2,1)S(1)}, u32[]{:S(2)}) copy-start(bf16[3584,512]{1,0:T(8,128)(2,1)S(1)} %get-tuple-element.79.refs_3_.refs_15_.refs_7_) | copy-start | bytes 11010052
  28.5 7.1 %collective-permute-start.6 = (bf16[272,512]{1,0:T(8,128)(2,1)S(1)}, bf16[272,512]{1,0:T(8,128)(2,1)S(1)}, u32[]{:S(2)}, u32[]{:S(2)}) collective-permute-start(bf16[272,512]{1,0:T(8,128)(2,1)S(1)} %collective-permute-done.1.refs_1_), channel_id=1, source_target_pairs={{0,4},{1,3},{2,6},{3,1},{4,0},{5,7},{6,2},{7,5},{8,12},{9,11},{10,... | collective-permute-start | bytes 835592 | tf_op jit(solution)/shard_map/ppermute | solution.py:329
  29.7 4.6 %collective-permute-start.5 = (f32[24,512]{1,0:T(8,128)S(1)}, f32[24,512]{1,0:T(8,128)S(1)}, u32[]{:S(2)}, u32[]{:S(2)}) collective-permute-start(f32[24,512]{1,0:T(8,128)S(1)} %get-tuple-element.70), channel_id=1, source_target_pairs={{0,2},{1,5},{2,0},{3,7},{4,6},{5,1},{6,4},{7,3},{8,10},{9,13},{10,... | collective-permute-start | bytes 147464 | tf_op jit(solution)/shard_map/ppermute | solution.py:329
  30.2 8.7 %copy-start.1 = (bf16[64,8192]{1,0:T(8,128)(2,1)S(1)}, bf16[64,8192]{1,0:T(8,128)(2,1)}, u32[]{:S(2)}) copy-start(bf16[64,8192]{1,0:T(8,128)(2,1)} %refs_9_.1) | copy-start | bytes 3145732
  35.6 18.1 %collective-permute-start.11 = (bf16[2,256,512]{2,1,0:T(8,128)(2,1)S(1)}, bf16[2,256,512]{2,1,0:T(8,128)(2,1)S(1)}, u32[]{:S(2)}, u32[]{:S(2)}) collective-permute-start(bf16[2,256,512]{2,1,0:T(8,128)(2,1)S(1)} %get-tuple-element.82), channel_id=1, source_target_pairs={{0,2},{1,5},{2,0},{3,7},{4,6},{5,1},{6,4},{7,3},{8,10},{9,13},{10,... | collective-permute-start | bytes 1572872 | tf_op jit(solution)/shard_map/ppermute | solution.py:329
  36.3 12.0 %collective-permute-start.9 = (bf16[272,512]{1,0:T(8,128)(2,1)S(1)}, bf16[272,512]{1,0:T(8,128)(2,1)S(1)}, u32[]{:S(2)}, u32[]{:S(2)}) collective-permute-start(bf16[272,512]{1,0:T(8,128)(2,1)S(1)} %collective-permute-done.1.refs_1_), channel_id=1, source_target_pairs={{0,2},{1,5},{2,0},{3,7},{4,6},{5,1},{6,4},{7,3},{8,10},{9,13},{10,... | collective-permute-start | bytes 835592 | tf_op jit(solution)/shard_map/ppermute | solution.py:329
  37.6 16.1 %collective-permute-start.12 = (bf16[272,512]{1,0:T(8,128)(2,1)S(1)}, bf16[272,512]{1,0:T(8,128)(2,1)S(1)}, u32[]{:S(2)}, u32[]{:S(2)}) collective-permute-start(bf16[272,512]{1,0:T(8,128)(2,1)S(1)} %collective-permute-done.6.refs_3_), channel_id=1, source_target_pairs={{0,2},{1,5},{2,0},{3,7},{4,6},{5,1},{6,4},{7,3},{8,10},{9,13},{10,... | collective-permute-start | bytes 835592 | tf_op jit(solution)/shard_map/ppermute | solution.py:329
  38.3 9.9 %collective-permute-start.8 = (f32[24,512]{1,0:T(8,128)S(1)}, f32[24,512]{1,0:T(8,128)S(1)}, u32[]{:S(2)}, u32[]{:S(2)}) collective-permute-start(f32[24,512]{1,0:T(8,128)S(1)} %add.56), channel_id=1, source_target_pairs={{0,4},{1,3},{2,6},{3,1},{4,0},{5,7},{6,2},{7,5},{8,12},{9,11},{10,... | collective-permute-start | bytes 147464 | tf_op jit(solution)/shard_map/ppermute | solution.py:329
  48.3 5.4 %collective-permute-start.10 = (f32[24,512]{1,0:T(8,128)S(1)}, f32[24,512]{1,0:T(8,128)S(1)}, u32[]{:S(2)}, u32[]{:S(2)}) collective-permute-start(f32[24,512]{1,0:T(8,128)S(1)} %add.57), channel_id=1, source_target_pairs={{0,8},{1,9},{2,10},{3,11},{4,12},{5,13},{6,14},{7,15},{8,0},{9,1},... | collective-permute-start | bytes 147464 | tf_op jit(solution)/shard_map/ppermute | solution.py:329
  49.8 14.1 %collective-permute-start.14 = (bf16[2,256,512]{2,1,0:T(8,128)(2,1)S(1)}, bf16[2,256,512]{2,1,0:T(8,128)(2,1)S(1)}, u32[]{:S(2)}, u32[]{:S(2)}) collective-permute-start(bf16[2,256,512]{2,1,0:T(8,128)(2,1)S(1)} %forward.5), channel_id=1, source_target_pairs={{0,2},{1,5},{2,0},{3,7},{4,6},{5,1},{6,4},{7,3},{8,10},{9,13},{10,... | collective-permute-start | bytes 1572872 | tf_op jit(solution)/shard_map/ppermute | solution.py:329
  53.8 10.0 %collective-permute-start.13 = (bf16[2,256,512]{2,1,0:T(8,128)(2,1)S(1)}, bf16[2,256,512]{2,1,0:T(8,128)(2,1)S(1)}, u32[]{:S(2)}, u32[]{:S(2)}) collective-permute-start(bf16[2,256,512]{2,1,0:T(8,128)(2,1)S(1)} %add_convert_fusion), channel_id=1, source_target_pairs={{0,4},{1,3},{2,6},{3,1},{4,0},{5,7},{6,2},{7,5},{8,12},{9,11},{10,... | collective-permute-start | bytes 1572872 | tf_op jit(solution)/shard_map/ppermute | solution.py:329
  55.1 8.7 %collective-permute-start.15 = (f32[16,512]{1,0:T(8,128)S(1)}, f32[16,512]{1,0:T(8,128)S(1)}, u32[]{:S(2)}, u32[]{:S(2)}) collective-permute-start(f32[16,512]{1,0:T(8,128)S(1)} %slice.73), channel_id=1, source_target_pairs={{0,1},{1,0},{2,3},{3,2},{4,5},{5,4},{6,7},{7,6},{8,9},{9,8},{10,11... | collective-permute-start | bytes 98312 | tf_op jit(solution)/shard_map/ppermute | solution.py:324
  55.2 2.8 %copy-start.3 = (bf16[3584,512]{1,0:T(8,128)(2,1)S(1)}, bf16[3584,512]{1,0:T(8,128)(2,1)}, u32[]{:S(2)}) copy-start(bf16[3584,512]{1,0:T(8,128)(2,1)} %copy-done.2) | copy-start | bytes 11010052
  55.2 2.8 %copy-start.7 = (bf16[3584,64]{0,1:T(8,128)(2,1)S(1)}, bf16[3584,64]{0,1:T(8,128)(2,1)}, u32[]{:S(2)}) copy-start(bf16[3584,64]{0,1:T(8,128)(2,1)} %param.8) | copy-start | bytes 1376260
  63.3 11.4 %collective-permute-start.17 = (bf16[128,1280]{1,0:T(8,128)(2,1)S(1)}, bf16[128,1280]{1,0:T(8,128)(2,1)S(1)}, u32[]{:S(2)}, u32[]{:S(2)}) collective-permute-start(bf16[128,1280]{1,0:T(8,128)(2,1)S(1)} %get-tuple-element.105), channel_id=1, source_target_pairs={{0,1},{1,0},{2,3},{3,2},{4,5},{5,4},{6,7},{7,6},{8,9},{9,8},{10,11... | collective-permute-start | bytes 983048 | tf_op jit(solution)/shard_map/ppermute | solution.py:324
  64.1 15.3 %collective-permute-start.16 = (bf16[256,512]{1,0:T(8,128)(2,1)S(1)}, bf16[256,512]{1,0:T(8,128)(2,1)S(1)}, u32[]{:S(2)}, u32[]{:S(2)}) collective-permute-start(bf16[256,512]{1,0:T(8,128)(2,1)S(1)} %fusion.2), channel_id=1, source_target_pairs={{0,8},{1,9},{2,10},{3,11},{4,12},{5,13},{6,14},{7,15},{8,0},{9,1},... | collective-permute-start | bytes 786440 | tf_op jit(solution)/shard_map/ppermute | solution.py:329
  66.6 8.0 %collective-permute-start.19 = (f32[64,512]{1,0:T(8,128)S(1)}, f32[64,512]{1,0:T(8,128)S(1)}, u32[]{:S(2)}, u32[]{:S(2)}) collective-permute-start(f32[64,512]{1,0:T(8,128)S(1)} %fusion.up_ref), channel_id=1, source_target_pairs={{0,1},{1,0},{2,3},{3,2},{4,5},{5,4},{6,7},{7,6},{8,9},{9,8},{10,11... | collective-permute-start | bytes 393224 | tf_op jit(solution)/shard_map/ppermute | solution.py:324
  66.7 7.9 %collective-permute-start.18 = (f32[256,64]{1,0:T(8,128)S(1)}, f32[256,64]{1,0:T(8,128)S(1)}, u32[]{:S(2)}, u32[]{:S(2)}) collective-permute-start(f32[256,64]{1,0:T(8,128)S(1)} %get-tuple-element.104.refs_1_.proj_ref), channel_id=1, source_target_pairs={{0,1},{1,0},{2,3},{3,2},{4,5},{5,4},{6,7},{7,6},{8,9},{9,8},{10,11... | collective-permute-start | bytes 196616 | tf_op jit(solution)/shard_map/ppermute | solution.py:324
  67.2 7.6 %copy-start.5 = (bf16[128,3584]{1,0:T(8,128)(2,1)S(1)}, bf16[128,3584]{1,0:T(8,128)(2,1)}, u32[]{:S(2)}) copy-start(bf16[128,3584]{1,0:T(8,128)(2,1)} %own_ref.3) | copy-start | bytes 2752516
  74.7 5.5 %collective-permute-start.22 = (bf16[128,2304]{1,0:T(8,128)(2,1)S(1)}, bf16[128,2304]{1,0:T(8,128)(2,1)S(1)}, u32[]{:S(2)}, u32[]{:S(2)}) collective-permute-start(bf16[128,2304]{1,0:T(8,128)(2,1)S(1)} %get-tuple-element.119), channel_id=1, source_target_pairs={{0,1},{1,0},{2,3},{3,2},{4,5},{5,4},{6,7},{7,6},{8,9},{9,8},{10,11... | collective-permute-start | bytes 1769480 | tf_op jit(solution)/shard_map/ppermute | solution.py:324
  79.6 2.2 %collective-permute-start.20 = (bf16[128,512]{1,0:T(8,128)(2,1)S(1)}, bf16[128,512]{1,0:T(8,128)(2,1)S(1)}, u32[]{:S(2)}, u32[]{:S(2)}) collective-permute-start(bf16[128,512]{1,0:T(8,128)(2,1)S(1)} %slice.80), channel_id=1, source_target_pairs={{0,1},{1,0},{2,3},{3,2},{4,5},{5,4},{6,7},{7,6},{8,9},{9,8},{10,11... | collective-permute-start | bytes 393224 | tf_op jit(solution)/shard_map/ppermute | solution.py:324
  79.7 2.1 %collective-permute-start.21 = (f32[1,512]{1,0:T(1,128)S(1)}, f32[1,512]{1,0:T(1,128)S(1)}, u32[]{:S(2)}, u32[]{:S(2)}) collective-permute-start(f32[1,512]{1,0:T(1,128)S(1)} %slice_divide_fusion.g_ref), channel_id=1, source_target_pairs={{0,1},{1,0},{2,3},{3,2},{4,5},{5,4},{6,7},{7,6},{8,9},{9,8},{10,11... | collective-permute-start | bytes 6152 | tf_op jit(solution)/shard_map/ppermute | solution.py:324

commit v13 on v12

--- a/solution.py
+++ b/solution.py
@@ -372,12 +372,12 @@
     got = send(stats, 1)
     from1 = send(far1, 0)
     far0 = run(order, (0b100, 0b101), far[:2])
-    got, cots[0b101], far0, order = tie((got, cots[0b101], far0, order))
+    got, far0, order = tie((got, far0, order))
     stats = stats + got
     got = send(stats, 2)
     from0 = send(far0, 0)
     near1 = run(order, (0b010, 0b011), near[2:])
-    got, from1, cots[0b111], near1, order = tie((got, from1, cots[0b111], near1, order))
+    got, from1, cots[0b101], cots[0b111], near1, order = tie((got, from1, cots[0b101], cots[0b111], near1, order))
     stats = stats + got
     arrived = send((near1.astype(f32) + from1.astype(f32)).astype(bf16), 1)
     lowrank_rows = stats[n:]

time: 83.4 us -> 81 us (0.971)
  waiting for transfers between devices: 13.3 us -> 10.7 us
    ppermute x13, waiting for transfers between devices: 10.8 us -> 8.18 us  [send(): return lax.ppermute(x, ('tensor', 'dp'), pairs)]
  transfers between devices with their start and end apart: 23 -> 23, of which waited for: 6 -> 7; matrix products, arithmetic and copies ran while one was open for 2% -> 2% of each run, Pallas kernels for 49% -> 50%
where the time goes in v13:
time: 81 us; the launch traced here: 80.7 us
  Pallas kernels  41.8 us (52%)
  starting transfers between devices  21 us (26%)
  waiting for transfers between devices  10.7 us (13%)
  local copies, waits for them, and re-layouts  4.64 us (6%)
  other arithmetic  1.28 us (2%)
  between operations  0.94 us (1%)
    ppermute x13, starting transfers between devices, send(): return lax.ppermute(x, ('tensor', 'dp'), pairs)  18.1 us
    pallas_call x2, Pallas kernels, backward(): pl.pallas_call(functools.partial(backward_kernel, tokens, n, start, band,...  12.7 us
    pallas_call x4, Pallas kernels, forward(): pl.pallas_call(functools.partial(forward_kernel, tokens, rank, vs, later...  12.3 us
    pallas_call x1, Pallas kernels, load(): pl.pallas_call(functools.partial(load_kernel, tokens, rank, n, vs, first)...  11.3 us
    ppermute x13, waiting for transfers between devices, send(): return lax.ppermute(x, ('tensor', 'dp'), pairs)  8.18 us
    pallas_call x3, Pallas kernels, finish(): pl.pallas_call(kernel, grid_spec=pltpu.PrefetchScalarGridSpec(num_scalar_...  4.91 us
    unnamed x18, local copies, waits for them, and re-layouts  4.39 us
    ppermute x9, starting transfers between devices, split_columns(): swap = lambda x: lax.ppermute(x, 'dp', [(0, 1), (1, 0)])  2.48 us
  transfers between devices with their start and end apart: 23, of which 7 were waited for; matrix products, arithmetic and copies ran while one was open for 2% of the time, Pallas kernels for 50%

profile of v13, /device:TPU:0, one launch (start us, length us, event | category | flops | bytes accessed | tf_op | source)
XLA Modules:
  0.0 80.7 jit_solution(14310953353245934637)
XLA Ops:
  0.6 0.5 collective-permute-start
  1.1 0.1 collective-permute-start.7
  1.2 0.7 reduce-precision_convert_fusion.1
  2.0 0.1 pad.11.clone
  2.0 0.1 stack.79.order_ref
  2.1 0.1 maximum_maximum_fusion.magnitude_ref
  2.2 0.3 collective-permute-done.other_ref
  2.5 0.9 %copy-done.8 = bf16[128,1024]{1,0:T(8,128)(2,1)S(1)} copy-done((bf16[128,1024]{1,0:T(8,128)(2,1)S(1)}, bf16[128,1024]{1,0:T(8,128)(2,1)}, u32[]{:S(2)}) %copy-start.8) | copy-done | bytes 262168
  3.5 0.6 own_block.1.refs_0_
  4.0 4.0 %collective-permute-start.1 = (bf16[272,512]{1,0:T(8,128)(2,1)S(1)}, bf16[272,512]{1,0:T(8,128)(2,1)S(1)}, u32[]{:S(2)}, u32[]{:S(2)}) collective-permute-start(bf16[272,512]{1,0:T(8,128)(2,1)S(1)} %own_block.1.refs_0_), channel_id=1, source_target_pairs={{0,8},{1,9},{2,10},{3,11},{4,12},{5,13},{6,14},{7,15},{8,0},{9,1},... | collective-permute-start | bytes 835592 | tf_op jit(solution)/shard_map/ppermute | solution.py:329
  8.1 1.6 %collective-permute-start.2 = (bf16[272,512]{1,0:T(8,128)(2,1)S(1)}, bf16[272,512]{1,0:T(8,128)(2,1)S(1)}, u32[]{:S(2)}, u32[]{:S(2)}) collective-permute-start(bf16[272,512]{1,0:T(8,128)(2,1)S(1)} %own_block.1.refs_0_), channel_id=1, source_target_pairs={{0,4},{1,3},{2,6},{3,1},{4,0},{5,7},{6,2},{7,5},{8,12},{9,11},{10,... | collective-permute-start | bytes 835592 | tf_op jit(solution)/shard_map/ppermute | solution.py:329
  9.6 1.5 %collective-permute-start.3 = (bf16[272,512]{1,0:T(8,128)(2,1)S(1)}, bf16[272,512]{1,0:T(8,128)(2,1)S(1)}, u32[]{:S(2)}, u32[]{:S(2)}) collective-permute-start(bf16[272,512]{1,0:T(8,128)(2,1)S(1)} %own_block.1.refs_0_), channel_id=1, source_target_pairs={{0,2},{1,5},{2,0},{3,7},{4,6},{5,1},{6,4},{7,3},{8,10},{9,13},{10,... | collective-permute-start | bytes 835592 | tf_op jit(solution)/shard_map/ppermute | solution.py:329
  11.1 0.4 collective-permute-start.4
  11.6 1.2 %copy-done = bf16[64,8192]{1,0:T(8,128)(2,1)S(1)} copy-done((bf16[64,8192]{1,0:T(8,128)(2,1)S(1)}, bf16[64,8192]{1,0:T(8,128)(2,1)}, u32[]{:S(2)}) %copy-start) | copy-done | bytes 1048600
  12.8 1.2 %copy-done.4 = bf16[128,3584]{1,0:T(8,128)(2,1)S(1)} copy-done((bf16[128,3584]{1,0:T(8,128)(2,1)S(1)}, bf16[128,3584]{1,0:T(8,128)(2,1)}, u32[]{:S(2)}) %copy-start.4) | copy-done | bytes 917528
  14.0 1.0 %copy-done.6 = bf16[3584,64]{0,1:T(8,128)(2,1)S(1)} copy-done((bf16[3584,64]{0,1:T(8,128)(2,1)S(1)}, bf16[3584,64]{0,1:T(8,128)(2,1)}, u32[]{:S(2)}) %copy-start.6) | copy-done | bytes 458776
  15.0 11.3 %load.1 = (bf16[3584,512]{1,0:T(8,128)(2,1)S(1)}, bf16[3584,512]{1,0:T(8,128)(2,1)S(1)}, bf16[3584,512]{1,0:T(8,128)(2,1)S(1)}, bf16[3584,512]{1,0:T(8,128)(2,1)...) custom-call(s32[16]{0:T(128)S(1)} %stack.79.order_ref, ...), custom_call_target="tpu_custom_call" | custom-call | tf_op jit(solution)/shard_map/load/pallas_call | solution.py:116
  26.3 0.0 collective-permute-done.1.refs_1_
  26.3 0.0 collective-permute-done.2.refs_2_
  26.4 2.1 %collective-permute-done.4.refs_6_ = bf16[272,512]{1,0:T(8,128)(2,1)S(1)} collective-permute-done((bf16[272,512]{1,0:T(8,128)(2,1)S(1)}, bf16[272,512]{1,0:T(8,128)(2,1)S(1)}, u32[]{:S(2)}, u32[]{:S(2)}) %collective-permute-start.4) | collective-permute-done | bytes 278560 | tf_op jit(solution)/shard_map/ppermute | solution.py:356
  28.5 1.2 %collective-permute-start.6 = (bf16[272,512]{1,0:T(8,128)(2,1)S(1)}, bf16[272,512]{1,0:T(8,128)(2,1)S(1)}, u32[]{:S(2)}, u32[]{:S(2)}) collective-permute-start(bf16[272,512]{1,0:T(8,128)(2,1)S(1)} %collective-permute-done.1.refs_1_), channel_id=1, source_target_pairs={{0,4},{1,3},{2,6},{3,1},{4,0},{5,7},{6,2},{7,5},{8,12},{9,11},{10,... | collective-permute-start | bytes 835592 | tf_op jit(solution)/shard_map/ppermute | solution.py:329
  29.7 0.5 collective-permute-start.5
  30.2 0.0 collective-permute-done.7.refs_1_.other_ref
  30.2 4.1 %forward.4 = (bf16[2,256,512]{2,1,0:T(8,128)(2,1)S(1)}, bf16[256,3584]{1,0:T(8,128)(2,1)S(1)}, bf16[256,128]{1,0:T(8,128)(2,1)S(1)}) custom-call(s32[16]{0:T(128)S(1)} %stack.79.order_ref, bf16[128,3584]{1,0:T(8,128)(2,1)S(1)} %copy-done.4, bf16[128,3584]{1,0:T(8,128)(2,1)S(1)} %collective-permute-done.7.refs_1_.other_ref, bf16[64,3584]{1,0:T(8,128)(2,1)S(1)} %bitcast.32, ...), custom_call_target="tpu_custom_call" | custom-call | tf_op jit(solution)/shard_map/forward/pallas_call | solution.py:158
  34.3 0.0 collective-permute-done.5
  34.3 1.2 %collective-permute-done.6.refs_3_ = bf16[272,512]{1,0:T(8,128)(2,1)S(1)} collective-permute-done((bf16[272,512]{1,0:T(8,128)(2,1)S(1)}, bf16[272,512]{1,0:T(8,128)(2,1)S(1)}, u32[]{:S(2)}, u32[]{:S(2)}) %collective-permute-start.6) | collective-permute-done | bytes 278560 | tf_op jit(solution)/shard_map/ppermute | solution.py:329
  35.6 0.7 collective-permute-start.10
  36.3 1.3 %collective-permute-start.11 = (bf16[272,512]{1,0:T(8,128)(2,1)S(1)}, bf16[272,512]{1,0:T(8,128)(2,1)S(1)}, u32[]{:S(2)}, u32[]{:S(2)}) collective-permute-start(bf16[272,512]{1,0:T(8,128)(2,1)S(1)} %collective-permute-done.1.refs_1_), channel_id=1, source_target_pairs={{0,2},{1,5},{2,0},{3,7},{4,6},{5,1},{6,4},{7,3},{8,10},{9,13},{10,... | collective-permute-start | bytes 835592 | tf_op jit(solution)/shard_map/ppermute | solution.py:329
  37.6 0.7 collective-permute-start.12
  38.3 0.6 collective-permute-start.8
  38.9 2.8 %forward.5 = bf16[2,256,512]{2,1,0:T(8,128)(2,1)S(1)} custom-call(s32[16]{0:T(128)S(1)} %stack.79.order_ref, bf16[256,3584]{1,0:T(8,128)(2,1)S(1)} %get-tuple-element.77.refs_0_, bf16[256,128]{1,0:T(8,128)(2,1)S(1)} %get-tuple-element.78.refs_1_, bf16[64,8192]{1,0:T(8,128)(2,1)S(1)} %copy-done.1, ...), custom_call_target="tpu_custom_call" | custom-call | tf_op jit(solution)/shard_map/forward/pallas_call | solution.py:158
  41.7 1.4 %collective-permute-done.8 = f32[24,512]{1,0:T(8,128)S(1)} collective-permute-done((f32[24,512]{1,0:T(8,128)S(1)}, f32[24,512]{1,0:T(8,128)S(1)}, u32[]{:S(2)}, u32[]{:S(2)}) %collective-permute-start.8) | collective-permute-done | bytes 49184 | tf_op jit(solution)/shard_map/ppermute | solution.py:329
  43.1 1.5 %collective-permute-start.9 = (f32[24,512]{1,0:T(8,128)S(1)}, f32[24,512]{1,0:T(8,128)S(1)}, u32[]{:S(2)}, u32[]{:S(2)}) collective-permute-start(f32[24,512]{1,0:T(8,128)S(1)} %add.57), channel_id=1, source_target_pairs={{0,8},{1,9},{2,10},{3,11},{4,12},{5,13},{6,14},{7,15},{8,0},{9,1},... | collective-permute-start | bytes 147464 | tf_op jit(solution)/shard_map/ppermute | solution.py:329
  44.6 1.2 %collective-permute-start.14 = (bf16[2,256,512]{2,1,0:T(8,128)(2,1)S(1)}, bf16[2,256,512]{2,1,0:T(8,128)(2,1)S(1)}, u32[]{:S(2)}, u32[]{:S(2)}) collective-permute-start(bf16[2,256,512]{2,1,0:T(8,128)(2,1)S(1)} %forward.5), channel_id=1, source_target_pairs={{0,2},{1,5},{2,0},{3,7},{4,6},{5,1},{6,4},{7,3},{8,10},{9,13},{10,... | collective-permute-start | bytes 1572872 | tf_op jit(solution)/shard_map/ppermute | solution.py:329
  45.9 2.7 %forward.6 = bf16[2,256,512]{2,1,0:T(8,128)(2,1)S(1)} custom-call(s32[16]{0:T(128)S(1)} %stack.79.order_ref, bf16[256,3584]{1,0:T(8,128)(2,1)S(1)} %get-tuple-element.77.refs_0_, bf16[256,128]{1,0:T(8,128)(2,1)S(1)} %get-tuple-element.78.refs_1_, bf16[64,8192]{1,0:T(8,128)(2,1)S(1)} %copy-done.1, ...), custom_call_target="tpu_custom_call" | custom-call | tf_op jit(solution)/shard_map/forward/pallas_call | solution.py:158
  48.6 2.6 %collective-permute-done.12.refs_7_ = bf16[272,512]{1,0:T(8,128)(2,1)S(1)} collective-permute-done((bf16[272,512]{1,0:T(8,128)(2,1)S(1)}, bf16[272,512]{1,0:T(8,128)(2,1)S(1)}, u32[]{:S(2)}, u32[]{:S(2)}) %collective-permute-start.12) | collective-permute-done | bytes 278560 | tf_op jit(solution)/shard_map/ppermute | solution.py:329
  51.2 0.0 collective-permute-done.10
  51.2 0.1 add_convert_fusion
  51.4 0.7 collective-permute-start.13
  52.1 0.1 collective-permute-start.15
  52.2 0.0 copy-start.7
  52.2 2.7 %forward.7 = bf16[2,256,512]{2,1,0:T(8,128)(2,1)S(1)} custom-call(s32[16]{0:T(128)S(1)} %stack.79.order_ref, bf16[256,3584]{1,0:T(8,128)(2,1)S(1)} %get-tuple-element.77.refs_0_, bf16[256,128]{1,0:T(8,128)(2,1)S(1)} %get-tuple-element.78.refs_1_, bf16[64,8192]{1,0:T(8,128)(2,1)S(1)} %copy-done.1, bf16[3584,512]{1,0:T(8,128)(2,1)S(1)} %get-tuple-element.88.refs_3_.refs_11_, ...), custom_call_target="tpu_custom_call" | custom-call | tf_op jit(solution)/shard_map/forward/pallas_call | solution.py:158
  55.0 5.3 %backward.2 = (f32[128,1280]{1,0:T(8,128)S(1)}, bf16[128,1280]{1,0:T(8,128)(2,1)S(1)}, bf16[256,4096]{1,0:T(8,128)(2,1)S(1)}, f32[256,64]{1,0:T(8,128)S(1)}, f32...) custom-call(s32[16]{0:T(128)S(1)} %stack.79.order_ref, bf16[272,512]{1,0:T(8,128)(2,1)S(1)} %own_block.1.refs_0_, ...), custom_call_target="tpu_custom_call" | custom-call | tf_op jit(solution)/shard_map/backward/pallas_call | solution.py:223
  60.3 0.5 collective-permute-start.17
  60.8 0.0 collective-permute-done.15
  60.8 0.3 collective-permute-done.13
  61.2 0.2 convert_add_fusion
  61.4 2.4 %collective-permute-start.16 = (bf16[256,512]{1,0:T(8,128)(2,1)S(1)}, bf16[256,512]{1,0:T(8,128)(2,1)S(1)}, u32[]{:S(2)}, u32[]{:S(2)}) collective-permute-start(bf16[256,512]{1,0:T(8,128)(2,1)S(1)} %fusion.2), channel_id=1, source_target_pairs={{0,8},{1,9},{2,10},{3,11},{4,12},{5,13},{6,14},{7,15},{8,0},{9,1},... | collective-permute-start | bytes 786440 | tf_op jit(solution)/shard_map/ppermute | solution.py:329
  63.8 0.2 fusion.3
  64.0 0.2 fusion.up_ref
  64.2 0.1 collective-permute-start.19
  64.3 0.5 collective-permute-start.18
  64.8 7.4 %backward.3 = (f32[128,2304]{1,0:T(8,128)S(1)}, bf16[128,2304]{1,0:T(8,128)(2,1)S(1)}) custom-call(s32[16]{0:T(128)S(1)} %stack.79.order_ref, bf16[256,4096]{1,0:T(8,128)(2,1)S(1)} %get-tuple-element.108.refs_0_, f32[256,64]{1,0:T(8,128)S(1)} %get-tuple-element.104.refs_1_.proj_ref, bf16[64,3584]{1,0:T(8,128)(2,1)S(1)} %bitcast.34, ...), custom_call_target="tpu_custom_call" | custom-call | tf_op jit(solution)/shard_map/backward/pallas_call | solution.py:223
  72.2 0.0 collective-permute-done.18.from_ref
  72.3 0.0 collective-permute-done.17.ra_ref
  72.3 0.1 collective-permute-start.22
  72.4 2.0 %weights.1 = (f32[64,3584]{1,0:T(8,128)}, f32[64,1024]{1,0:T(8,128)}) custom-call(s32[16]{0:T(128)S(1)} %stack.79.order_ref, f32[256,64]{1,0:T(8,128)S(1)} %get-tuple-element.104.refs_1_.proj_ref, f32[256,64]{1,0:T(8,128)S(1)} %collective-permute-done.18.from_ref, bf16[128,3584]{1,0:T(8,128)(2,1)S(1)} %copy-done.5, ...), custom_call_target="tpu_custom_call" | custom-call | tf_op jit(solution)/shard_map/weights/pallas_call | solution.py:280
  74.4 2.6 %collective-permute-done.16 = bf16[256,512]{1,0:T(8,128)(2,1)S(1)} collective-permute-done((bf16[256,512]{1,0:T(8,128)(2,1)S(1)}, bf16[256,512]{1,0:T(8,128)(2,1)S(1)}, u32[]{:S(2)}, u32[]{:S(2)}) %collective-permute-start.16) | collective-permute-done | bytes 262176 | tf_op jit(solution)/shard_map/ppermute | solution.py:329
  77.0 0.2 multiply_reduce_fusion
  77.2 0.2 collective-permute-start.20
  77.4 0.4 collective-permute-start.21
  77.8 0.0 collective-permute-done.22.rb_ref
  77.8 1.6 %hidden.1 = bf16[128,3584]{1,0:T(8,128)(2,1)} custom-call(s32[16]{0:T(128)S(1)} %stack.79.order_ref, f32[128,1280]{1,0:T(8,128)S(1)} %get-tuple-element.116.ga_ref, bf16[128,1280]{1,0:T(8,128)(2,1)S(1)} %collective-permute-done.17.ra_ref, f32[128,2304]{1,0:T(8,128)S(1)} %get-tuple-element.118.gb_ref, bf16[128,2304]{1,0:T(8,128)(2,1)S(1)} %collective-permute-done.22.rb_ref), custom_call_target="tpu_custom_call" | custom-call | tf_op jit(solution)/shard_map/hidden/pallas_call | solution.py:280
  79.4 1.3 %mixed.1 = (bf16[128,1024]{1,0:T(8,128)(2,1)}, f32[8,128]{1,0:T(8,128)}) custom-call(s32[16]{0:T(128)S(1)} %stack.79.order_ref, bf16[256,512]{1,0:T(8,128)(2,1)S(1)} %get-tuple-element.128.m_ref, bf16[128,512]{1,0:T(8,128)(2,1)S(1)} %collective-permute-done.20.m_other_ref, f32[1,512]{1,0:T(1,128)S(1)} %slice_divide_fusion.g_ref, ...), custom_call_target="tpu_custom_call" | custom-call | tf_op jit(solution)/shard_map/mixed/pallas_call | solution.py:280
  (34 shorter events, 0.2 us)
Async XLA Ops:
  0.6 1.9 %collective-permute-start = (bf16[128,1024]{1,0:T(8,128)(2,1)}, bf16[128,1024]{1,0:T(8,128)(2,1)S(1)}, u32[]{:S(2)}, u32[]{:S(2)}) collective-permute-start(bf16[128,1024]{1,0:T(8,128)(2,1)} %own_ref.2), channel_id=1, source_target_pairs={{0,1},{1,0},{2,3},{3,2},{4,5},{5,4},{6,7},{7,6},{8,9},{9,8},{10,11... | collective-permute-start | bytes 786440 | tf_op jit(solution)/shard_map/ppermute | solution.py:324
  1.1 29.1 %collective-permute-start.7 = (bf16[128,3584]{1,0:T(8,128)(2,1)}, bf16[128,3584]{1,0:T(8,128)(2,1)S(1)}, u32[]{:S(2)}, u32[]{:S(2)}) collective-permute-start(bf16[128,3584]{1,0:T(8,128)(2,1)} %own_ref.3), channel_id=1, source_target_pairs={{0,1},{1,0},{2,3},{3,2},{4,5},{5,4},{6,7},{7,6},{8,9},{9,8},{10,11... | collective-permute-start | bytes 2752520 | tf_op jit(solution)/shard_map/ppermute | solution.py:324
  2.5 0.9 %copy-start.8 = (bf16[128,1024]{1,0:T(8,128)(2,1)S(1)}, bf16[128,1024]{1,0:T(8,128)(2,1)}, u32[]{:S(2)}) copy-start(bf16[128,1024]{1,0:T(8,128)(2,1)} %own_ref.2) | copy-start | bytes 786436
  4.0 22.3 %collective-permute-start.1 = (bf16[272,512]{1,0:T(8,128)(2,1)S(1)}, bf16[272,512]{1,0:T(8,128)(2,1)S(1)}, u32[]{:S(2)}, u32[]{:S(2)}) collective-permute-start(bf16[272,512]{1,0:T(8,128)(2,1)S(1)} %own_block.1.refs_0_), channel_id=1, source_target_pairs={{0,8},{1,9},{2,10},{3,11},{4,12},{5,13},{6,14},{7,15},{8,0},{9,1},... | collective-permute-start | bytes 835592 | tf_op jit(solution)/shard_map/ppermute | solution.py:329
  8.1 18.3 %collective-permute-start.2 = (bf16[272,512]{1,0:T(8,128)(2,1)S(1)}, bf16[272,512]{1,0:T(8,128)(2,1)S(1)}, u32[]{:S(2)}, u32[]{:S(2)}) collective-permute-start(bf16[272,512]{1,0:T(8,128)(2,1)S(1)} %own_block.1.refs_0_), channel_id=1, source_target_pairs={{0,4},{1,3},{2,6},{3,1},{4,0},{5,7},{6,2},{7,5},{8,12},{9,11},{10,... | collective-permute-start | bytes 835592 | tf_op jit(solution)/shard_map/ppermute | solution.py:329
  9.6 16.7 %collective-permute-start.3 = (bf16[272,512]{1,0:T(8,128)(2,1)S(1)}, bf16[272,512]{1,0:T(8,128)(2,1)S(1)}, u32[]{:S(2)}, u32[]{:S(2)}) collective-permute-start(bf16[272,512]{1,0:T(8,128)(2,1)S(1)} %own_block.1.refs_0_), channel_id=1, source_target_pairs={{0,2},{1,5},{2,0},{3,7},{4,6},{5,1},{6,4},{7,3},{8,10},{9,13},{10,... | collective-permute-start | bytes 835592 | tf_op jit(solution)/shard_map/ppermute | solution.py:329
  11.1 17.4 %collective-permute-start.4 = (bf16[272,512]{1,0:T(8,128)(2,1)S(1)}, bf16[272,512]{1,0:T(8,128)(2,1)S(1)}, u32[]{:S(2)}, u32[]{:S(2)}) collective-permute-start(bf16[272,512]{1,0:T(8,128)(2,1)S(1)} %own_block.1.refs_0_), channel_id=1, source_target_pairs={{0,6},{1,7},{2,4},{3,5},{4,2},{5,3},{6,0},{7,1},{8,14},{9,15},{10,... | collective-permute-start | bytes 835592 | tf_op jit(solution)/shard_map/ppermute | solution.py:356
  11.6 1.2 %copy-start = (bf16[64,8192]{1,0:T(8,128)(2,1)S(1)}, bf16[64,8192]{1,0:T(8,128)(2,1)}, u32[]{:S(2)}) copy-start(bf16[64,8192]{1,0:T(8,128)(2,1)} %refs_9_.1) | copy-start | bytes 3145732
  12.8 1.2 %copy-start.4 = (bf16[128,3584]{1,0:T(8,128)(2,1)S(1)}, bf16[128,3584]{1,0:T(8,128)(2,1)}, u32[]{:S(2)}) copy-start(bf16[128,3584]{1,0:T(8,128)(2,1)} %own_ref.3) | copy-start | bytes 2752516
  14.0 1.0 %copy-start.6 = (bf16[3584,64]{0,1:T(8,128)(2,1)S(1)}, bf16[3584,64]{0,1:T(8,128)(2,1)}, u32[]{:S(2)}) copy-start(bf16[3584,64]{0,1:T(8,128)(2,1)} %param.8) | copy-start | bytes 1376260
  26.3 12.6 %copy-start.2 = (bf16[3584,512]{1,0:T(8,128)(2,1)}, bf16[3584,512]{1,0:T(8,128)(2,1)S(1)}, u32[]{:S(2)}) copy-start(bf16[3584,512]{1,0:T(8,128)(2,1)S(1)} %get-tuple-element.79.refs_3_.refs_15_.refs_7_) | copy-start | bytes 11010052
  28.5 7.1 %collective-permute-start.6 = (bf16[272,512]{1,0:T(8,128)(2,1)S(1)}, bf16[272,512]{1,0:T(8,128)(2,1)S(1)}, u32[]{:S(2)}, u32[]{:S(2)}) collective-permute-start(bf16[272,512]{1,0:T(8,128)(2,1)S(1)} %collective-permute-done.1.refs_1_), channel_id=1, source_target_pairs={{0,4},{1,3},{2,6},{3,1},{4,0},{5,7},{6,2},{7,5},{8,12},{9,11},{10,... | collective-permute-start | bytes 835592 | tf_op jit(solution)/shard_map/ppermute | solution.py:329
  29.7 4.6 %collective-permute-start.5 = (f32[24,512]{1,0:T(8,128)S(1)}, f32[24,512]{1,0:T(8,128)S(1)}, u32[]{:S(2)}, u32[]{:S(2)}) collective-permute-start(f32[24,512]{1,0:T(8,128)S(1)} %get-tuple-element.70), channel_id=1, source_target_pairs={{0,2},{1,5},{2,0},{3,7},{4,6},{5,1},{6,4},{7,3},{8,10},{9,13},{10,... | collective-permute-start | bytes 147464 | tf_op jit(solution)/shard_map/ppermute | solution.py:329
  30.2 8.7 %copy-start.1 = (bf16[64,8192]{1,0:T(8,128)(2,1)S(1)}, bf16[64,8192]{1,0:T(8,128)(2,1)}, u32[]{:S(2)}) copy-start(bf16[64,8192]{1,0:T(8,128)(2,1)} %refs_9_.1) | copy-start | bytes 3145732
  35.6 15.7 %collective-permute-start.10 = (bf16[2,256,512]{2,1,0:T(8,128)(2,1)S(1)}, bf16[2,256,512]{2,1,0:T(8,128)(2,1)S(1)}, u32[]{:S(2)}, u32[]{:S(2)}) collective-permute-start(bf16[2,256,512]{2,1,0:T(8,128)(2,1)S(1)} %get-tuple-element.82), channel_id=1, source_target_pairs={{0,2},{1,5},{2,0},{3,7},{4,6},{5,1},{6,4},{7,3},{8,10},{9,13},{10,... | collective-permute-start | bytes 1572872 | tf_op jit(solution)/shard_map/ppermute | solution.py:329
  36.3 12.3 %collective-permute-start.11 = (bf16[272,512]{1,0:T(8,128)(2,1)S(1)}, bf16[272,512]{1,0:T(8,128)(2,1)S(1)}, u32[]{:S(2)}, u32[]{:S(2)}) collective-permute-start(bf16[272,512]{1,0:T(8,128)(2,1)S(1)} %collective-permute-done.1.refs_1_), channel_id=1, source_target_pairs={{0,2},{1,5},{2,0},{3,7},{4,6},{5,1},{6,4},{7,3},{8,10},{9,13},{10,... | collective-permute-start | bytes 835592 | tf_op jit(solution)/shard_map/ppermute | solution.py:329
  37.6 13.6 %collective-permute-start.12 = (bf16[272,512]{1,0:T(8,128)(2,1)S(1)}, bf16[272,512]{1,0:T(8,128)(2,1)S(1)}, u32[]{:S(2)}, u32[]{:S(2)}) collective-permute-start(bf16[272,512]{1,0:T(8,128)(2,1)S(1)} %collective-permute-done.6.refs_3_), channel_id=1, source_target_pairs={{0,2},{1,5},{2,0},{3,7},{4,6},{5,1},{6,4},{7,3},{8,10},{9,13},{10,... | collective-permute-start | bytes 835592 | tf_op jit(solution)/shard_map/ppermute | solution.py:329
  38.3 4.7 %collective-permute-start.8 = (f32[24,512]{1,0:T(8,128)S(1)}, f32[24,512]{1,0:T(8,128)S(1)}, u32[]{:S(2)}, u32[]{:S(2)}) collective-permute-start(f32[24,512]{1,0:T(8,128)S(1)} %add.56), channel_id=1, source_target_pairs={{0,4},{1,3},{2,6},{3,1},{4,0},{5,7},{6,2},{7,5},{8,12},{9,11},{10,... | collective-permute-start | bytes 147464 | tf_op jit(solution)/shard_map/ppermute | solution.py:329
  43.1 5.5 %collective-permute-start.9 = (f32[24,512]{1,0:T(8,128)S(1)}, f32[24,512]{1,0:T(8,128)S(1)}, u32[]{:S(2)}, u32[]{:S(2)}) collective-permute-start(f32[24,512]{1,0:T(8,128)S(1)} %add.57), channel_id=1, source_target_pairs={{0,8},{1,9},{2,10},{3,11},{4,12},{5,13},{6,14},{7,15},{8,0},{9,1},... | collective-permute-start | bytes 147464 | tf_op jit(solution)/shard_map/ppermute | solution.py:329
  44.6 16.2 %collective-permute-start.14 = (bf16[2,256,512]{2,1,0:T(8,128)(2,1)S(1)}, bf16[2,256,512]{2,1,0:T(8,128)(2,1)S(1)}, u32[]{:S(2)}, u32[]{:S(2)}) collective-permute-start(bf16[2,256,512]{2,1,0:T(8,128)(2,1)S(1)} %forward.5), channel_id=1, source_target_pairs={{0,2},{1,5},{2,0},{3,7},{4,6},{5,1},{6,4},{7,3},{8,10},{9,13},{10,... | collective-permute-start | bytes 1572872 | tf_op jit(solution)/shard_map/ppermute | solution.py:329
  51.4 9.8 %collective-permute-start.13 = (bf16[2,256,512]{2,1,0:T(8,128)(2,1)S(1)}, bf16[2,256,512]{2,1,0:T(8,128)(2,1)S(1)}, u32[]{:S(2)}, u32[]{:S(2)}) collective-permute-start(bf16[2,256,512]{2,1,0:T(8,128)(2,1)S(1)} %add_convert_fusion), channel_id=1, source_target_pairs={{0,4},{1,3},{2,6},{3,1},{4,0},{5,7},{6,2},{7,5},{8,12},{9,11},{10,... | collective-permute-start | bytes 1572872 | tf_op jit(solution)/shard_map/ppermute | solution.py:329
  52.1 8.7 %collective-permute-start.15 = (f32[16,512]{1,0:T(8,128)S(1)}, f32[16,512]{1,0:T(8,128)S(1)}, u32[]{:S(2)}, u32[]{:S(2)}) collective-permute-start(f32[16,512]{1,0:T(8,128)S(1)} %slice.73), channel_id=1, source_target_pairs={{0,1},{1,0},{2,3},{3,2},{4,5},{5,4},{6,7},{7,6},{8,9},{9,8},{10,11... | collective-permute-start | bytes 98312 | tf_op jit(solution)/shard_map/ppermute | solution.py:324
  52.2 2.8 %copy-start.3 = (bf16[3584,512]{1,0:T(8,128)(2,1)S(1)}, bf16[3584,512]{1,0:T(8,128)(2,1)}, u32[]{:S(2)}) copy-start(bf16[3584,512]{1,0:T(8,128)(2,1)} %copy-done.2) | copy-start | bytes 11010052
  52.2 2.8 %copy-start.7 = (bf16[3584,64]{0,1:T(8,128)(2,1)S(1)}, bf16[3584,64]{0,1:T(8,128)(2,1)}, u32[]{:S(2)}) copy-start(bf16[3584,64]{0,1:T(8,128)(2,1)} %param.8) | copy-start | bytes 1376260
  60.3 11.9 %collective-permute-start.17 = (bf16[128,1280]{1,0:T(8,128)(2,1)S(1)}, bf16[128,1280]{1,0:T(8,128)(2,1)S(1)}, u32[]{:S(2)}, u32[]{:S(2)}) collective-permute-start(bf16[128,1280]{1,0:T(8,128)(2,1)S(1)} %get-tuple-element.105), channel_id=1, source_target_pairs={{0,1},{1,0},{2,3},{3,2},{4,5},{5,4},{6,7},{7,6},{8,9},{9,8},{10,11... | collective-permute-start | bytes 983048 | tf_op jit(solution)/shard_map/ppermute | solution.py:324
  61.4 15.6 %collective-permute-start.16 = (bf16[256,512]{1,0:T(8,128)(2,1)S(1)}, bf16[256,512]{1,0:T(8,128)(2,1)S(1)}, u32[]{:S(2)}, u32[]{:S(2)}) collective-permute-start(bf16[256,512]{1,0:T(8,128)(2,1)S(1)} %fusion.2), channel_id=1, source_target_pairs={{0,8},{1,9},{2,10},{3,11},{4,12},{5,13},{6,14},{7,15},{8,0},{9,1},... | collective-permute-start | bytes 786440 | tf_op jit(solution)/shard_map/ppermute | solution.py:329
  64.2 8.0 %collective-permute-start.19 = (f32[64,512]{1,0:T(8,128)S(1)}, f32[64,512]{1,0:T(8,128)S(1)}, u32[]{:S(2)}, u32[]{:S(2)}) collective-permute-start(f32[64,512]{1,0:T(8,128)S(1)} %fusion.up_ref), channel_id=1, source_target_pairs={{0,1},{1,0},{2,3},{3,2},{4,5},{5,4},{6,7},{7,6},{8,9},{9,8},{10,11... | collective-permute-start | bytes 393224 | tf_op jit(solution)/shard_map/ppermute | solution.py:324
  64.3 7.9 %collective-permute-start.18 = (f32[256,64]{1,0:T(8,128)S(1)}, f32[256,64]{1,0:T(8,128)S(1)}, u32[]{:S(2)}, u32[]{:S(2)}) collective-permute-start(f32[256,64]{1,0:T(8,128)S(1)} %get-tuple-element.104.refs_1_.proj_ref), channel_id=1, source_target_pairs={{0,1},{1,0},{2,3},{3,2},{4,5},{5,4},{6,7},{7,6},{8,9},{9,8},{10,11... | collective-permute-start | bytes 196616 | tf_op jit(solution)/shard_map/ppermute | solution.py:324
  64.8 7.6 %copy-start.5 = (bf16[128,3584]{1,0:T(8,128)(2,1)S(1)}, bf16[128,3584]{1,0:T(8,128)(2,1)}, u32[]{:S(2)}) copy-start(bf16[128,3584]{1,0:T(8,128)(2,1)} %own_ref.3) | copy-start | bytes 2752516
  72.3 5.5 %collective-permute-start.22 = (bf16[128,2304]{1,0:T(8,128)(2,1)S(1)}, bf16[128,2304]{1,0:T(8,128)(2,1)S(1)}, u32[]{:S(2)}, u32[]{:S(2)}) collective-permute-start(bf16[128,2304]{1,0:T(8,128)(2,1)S(1)} %get-tuple-element.119), channel_id=1, source_target_pairs={{0,1},{1,0},{2,3},{3,2},{4,5},{5,4},{6,7},{7,6},{8,9},{9,8},{10,11... | collective-permute-start | bytes 1769480 | tf_op jit(solution)/shard_map/ppermute | solution.py:324
  77.2 2.2 %collective-permute-start.20 = (bf16[128,512]{1,0:T(8,128)(2,1)S(1)}, bf16[128,512]{1,0:T(8,128)(2,1)S(1)}, u32[]{:S(2)}, u32[]{:S(2)}) collective-permute-start(bf16[128,512]{1,0:T(8,128)(2,1)S(1)} %slice.80), channel_id=1, source_target_pairs={{0,1},{1,0},{2,3},{3,2},{4,5},{5,4},{6,7},{7,6},{8,9},{9,8},{10,11... | collective-permute-start | bytes 393224 | tf_op jit(solution)/shard_map/ppermute | solution.py:324
  77.4 2.0 %collective-permute-start.21 = (f32[1,512]{1,0:T(1,128)S(1)}, f32[1,512]{1,0:T(1,128)S(1)}, u32[]{:S(2)}, u32[]{:S(2)}) collective-permute-start(f32[1,512]{1,0:T(1,128)S(1)} %slice_divide_fusion.g_ref), channel_id=1, source_target_pairs={{0,1},{1,0},{2,3},{3,2},{4,5},{5,4},{6,7},{7,6},{8,9},{9,8},{10,11... | collective-permute-start | bytes 6152 | tf_op jit(solution)/shard_map/ppermute | solution.py:324

commit v14 on v13

--- a/solution.py
+++ b/solution.py
@@ -375,11 +375,12 @@
     got, far0, order = tie((got, far0, order))
     stats = stats + got
     got = send(stats, 2)
-    from0 = send(far0, 0)
+    from0_high, from0_low = send(far0[1], 0), send(far0[0], 0)
     near1 = run(order, (0b010, 0b011), near[2:])
     got, from1, cots[0b101], cots[0b111], near1, order = tie((got, from1, cots[0b101], cots[0b111], near1, order))
     stats = stats + got
-    arrived = send((near1.astype(f32) + from1.astype(f32)).astype(bf16), 1)
+    total = (near1.astype(f32) + from1.astype(f32)).astype(bf16)
+    high, low = send(total[1], 1), send(total[0], 1)
     lowrank_rows = stats[n:]
     lowrank_other = swap(lowrank_rows)
     near0 = run(order, (0b000, 0b001), near[:2])
@@ -387,14 +388,12 @@
 
     band = 256
     bands = rows // band
-    many = max(bands * 5 // 14, 1)
+    many = max(bands * 3 // 14, 1)
     run = functools.partial(backward, order, band=band, at=at, held=held)
     grad_a, other_a, scaled, proj, scales, scaled_own = run(0, many, first=([cots[v] for v in range(n)], stats, up))
-    got_a = swap(other_a)
     from_sibling = swap(proj)
-    arrived, from0, lowrank_other, scaled_own = tie((arrived, from0, lowrank_other, scaled_own))
-    kept = near0.astype(f32) + from0.astype(f32) + arrived.astype(f32)
-    last = send(kept[1].astype(bf16), 2)
+    high, from0_high, lowrank_other, scaled_own = tie((high, from0_high, lowrank_other, scaled_own))
+    last = send((near0[1].astype(f32) + from0_high.astype(f32) + high.astype(f32)).astype(bf16), 2)
     scaled_own = scaled_own.astype(f32)
 
     def turned(part):
@@ -407,15 +406,15 @@
     )
     up_other = swap(up_half)
     grad_b, other_b = backward(order, many, bands - many, band, at, held, later=(scaled, proj))
-    got_a, from_sibling, up_other, other_b = tie((got_a, from_sibling, up_other, other_b))
-    got_b = swap(other_b)
+    other_a, from_sibling, up_other, other_b = tie((other_a, from_sibling, up_other, other_b))
+    got_a, got_b = swap(other_a), swap(other_b)
 
     down_weight_gradient, up_weight_gradient = finish_weights(
         order, proj, from_sibling, hidden, hidden_other, up_half, up_other
     )
 
-    last, down_weight_gradient = tie((last, down_weight_gradient))
-    unscaled = kept[0] + last.astype(f32)
+    last, low, from0_low, down_weight_gradient = tie((last, low, from0_low, down_weight_gradient))
+    unscaled = near0[0].astype(f32) + from0_low.astype(f32) + low.astype(f32) + last.astype(f32)
     mixed = (unscaled * scales[1]).astype(bf16)
     magnitude_half = jnp.sum(block[: 2 * tokens].astype(f32) * unscaled, axis=0, keepdims=True) / scales[0:1]
     mixed_other, magnitude_other = swap(mixed[tokens:]), swap(magnitude_half)

time: 81 us -> 80.5 us (level)
  waiting for transfers between devices: 10.7 us -> 7.18 us
  starting transfers between devices: 21 us -> 24 us
    ppermute x13 -> x15, waiting for transfers between devices: 8.18 us -> 4.71 us  [send(): return lax.ppermute(x, ('tensor', 'dp'), pairs)]
    ppermute x13 -> x15, starting transfers between devices: 18.1 us -> 21.1 us  [send(): return lax.ppermute(x, ('tensor', 'dp'), pairs)]
  transfers between devices with their start and end apart: 23 -> 25, of which waited for: 7 -> 5; matrix products, arithmetic and copies ran while one was open for 2% -> 2% of each run, Pallas kernels for 50% -> 51%
where the time goes in v14:
time: 80.5 us; the launch traced here: 80.2 us
  Pallas kernels  41.8 us (52%)
  starting transfers between devices  24 us (30%)
  waiting for transfers between devices  7.18 us (9%)
  local copies, waits for them, and re-layouts  4.68 us (6%)
  other arithmetic  1.26 us (2%)
  between operations  0.95 us (1%)
    ppermute x15, starting transfers between devices, send(): return lax.ppermute(x, ('tensor', 'dp'), pairs)  21.1 us
    pallas_call x2, Pallas kernels, backward(): pl.pallas_call(functools.partial(backward_kernel, tokens, n, start, band,...  12.7 us
    pallas_call x4, Pallas kernels, forward(): pl.pallas_call(functools.partial(forward_kernel, tokens, rank, vs, later...  12.4 us
    pallas_call x1, Pallas kernels, load(): pl.pallas_call(functools.partial(load_kernel, tokens, rank, n, vs, first)...  11.3 us
    pallas_call x3, Pallas kernels, finish(): pl.pallas_call(kernel, grid_spec=pltpu.PrefetchScalarGridSpec(num_scalar_...  4.89 us
    ppermute x15, waiting for transfers between devices, send(): return lax.ppermute(x, ('tensor', 'dp'), pairs)  4.71 us
    unnamed x18, local copies, waits for them, and re-layouts  4.39 us
    ppermute x9, starting transfers between devices, split_columns(): swap = lambda x: lax.ppermute(x, 'dp', [(0, 1), (1, 0)])  2.45 us
  transfers between devices with their start and end apart: 25, of which 5 were waited for; matrix products, arithmetic and copies ran while one was open for 2% of the time, Pallas kernels for 51%

profile of v14, /device:TPU:0, one launch (start us, length us, event | category | flops | bytes accessed | tf_op | source)
XLA Modules:
  0.0 80.2 jit_solution(12014098640690570658)
XLA Ops:
  0.6 0.5 collective-permute-start
  1.1 0.1 collective-permute-start.7
  1.2 0.7 reduce-precision_convert_fusion.1
  2.0 0.1 pad.11.clone
  2.0 0.1 stack.79.order_ref
  2.1 0.1 maximum_maximum_fusion.magnitude_ref
  2.2 0.3 collective-permute-done.other_ref
  2.5 0.9 %copy-done.8 = bf16[128,1024]{1,0:T(8,128)(2,1)S(1)} copy-done((bf16[128,1024]{1,0:T(8,128)(2,1)S(1)}, bf16[128,1024]{1,0:T(8,128)(2,1)}, u32[]{:S(2)}) %copy-start.8) | copy-done | bytes 262168
  3.5 0.6 own_block.1.refs_0_
  4.0 4.0 %collective-permute-start.1 = (bf16[272,512]{1,0:T(8,128)(2,1)S(1)}, bf16[272,512]{1,0:T(8,128)(2,1)S(1)}, u32[]{:S(2)}, u32[]{:S(2)}) collective-permute-start(bf16[272,512]{1,0:T(8,128)(2,1)S(1)} %own_block.1.refs_0_), channel_id=1, source_target_pairs={{0,8},{1,9},{2,10},{3,11},{4,12},{5,13},{6,14},{7,15},{8,0},{9,1},... | collective-permute-start | bytes 835592 | tf_op jit(solution)/shard_map/ppermute | solution.py:329
  8.1 1.6 %collective-permute-start.2 = (bf16[272,512]{1,0:T(8,128)(2,1)S(1)}, bf16[272,512]{1,0:T(8,128)(2,1)S(1)}, u32[]{:S(2)}, u32[]{:S(2)}) collective-permute-start(bf16[272,512]{1,0:T(8,128)(2,1)S(1)} %own_block.1.refs_0_), channel_id=1, source_target_pairs={{0,4},{1,3},{2,6},{3,1},{4,0},{5,7},{6,2},{7,5},{8,12},{9,11},{10,... | collective-permute-start | bytes 835592 | tf_op jit(solution)/shard_map/ppermute | solution.py:329
  9.6 1.5 %collective-permute-start.3 = (bf16[272,512]{1,0:T(8,128)(2,1)S(1)}, bf16[272,512]{1,0:T(8,128)(2,1)S(1)}, u32[]{:S(2)}, u32[]{:S(2)}) collective-permute-start(bf16[272,512]{1,0:T(8,128)(2,1)S(1)} %own_block.1.refs_0_), channel_id=1, source_target_pairs={{0,2},{1,5},{2,0},{3,7},{4,6},{5,1},{6,4},{7,3},{8,10},{9,13},{10,... | collective-permute-start | bytes 835592 | tf_op jit(solution)/shard_map/ppermute | solution.py:329
  11.1 0.4 collective-permute-start.4
  11.6 1.2 %copy-done = bf16[64,8192]{1,0:T(8,128)(2,1)S(1)} copy-done((bf16[64,8192]{1,0:T(8,128)(2,1)S(1)}, bf16[64,8192]{1,0:T(8,128)(2,1)}, u32[]{:S(2)}) %copy-start) | copy-done | bytes 1048600
  12.8 1.2 %copy-done.4 = bf16[128,3584]{1,0:T(8,128)(2,1)S(1)} copy-done((bf16[128,3584]{1,0:T(8,128)(2,1)S(1)}, bf16[128,3584]{1,0:T(8,128)(2,1)}, u32[]{:S(2)}) %copy-start.4) | copy-done | bytes 917528
  14.0 1.0 %copy-done.6 = bf16[3584,64]{0,1:T(8,128)(2,1)S(1)} copy-done((bf16[3584,64]{0,1:T(8,128)(2,1)S(1)}, bf16[3584,64]{0,1:T(8,128)(2,1)}, u32[]{:S(2)}) %copy-start.6) | copy-done | bytes 458776
  15.0 11.3 %load.1 = (bf16[3584,512]{1,0:T(8,128)(2,1)S(1)}, bf16[3584,512]{1,0:T(8,128)(2,1)S(1)}, bf16[3584,512]{1,0:T(8,128)(2,1)S(1)}, bf16[3584,512]{1,0:T(8,128)(2,1)...) custom-call(s32[16]{0:T(128)S(1)} %stack.79.order_ref, ...), custom_call_target="tpu_custom_call" | custom-call | tf_op jit(solution)/shard_map/load/pallas_call | solution.py:116
  26.3 0.0 collective-permute-done.1.refs_1_
  26.3 0.0 collective-permute-done.2.refs_2_
  26.3 0.0 collective-permute-done.3.refs_4_
  26.4 2.1 %collective-permute-done.4.refs_6_ = bf16[272,512]{1,0:T(8,128)(2,1)S(1)} collective-permute-done((bf16[272,512]{1,0:T(8,128)(2,1)S(1)}, bf16[272,512]{1,0:T(8,128)(2,1)S(1)}, u32[]{:S(2)}, u32[]{:S(2)}) %collective-permute-start.4) | collective-permute-done | bytes 278560 | tf_op jit(solution)/shard_map/ppermute | solution.py:356
  28.5 1.2 %collective-permute-start.6 = (bf16[272,512]{1,0:T(8,128)(2,1)S(1)}, bf16[272,512]{1,0:T(8,128)(2,1)S(1)}, u32[]{:S(2)}, u32[]{:S(2)}) collective-permute-start(bf16[272,512]{1,0:T(8,128)(2,1)S(1)} %collective-permute-done.1.refs_1_), channel_id=1, source_target_pairs={{0,4},{1,3},{2,6},{3,1},{4,0},{5,7},{6,2},{7,5},{8,12},{9,11},{10,... | collective-permute-start | bytes 835592 | tf_op jit(solution)/shard_map/ppermute | solution.py:329
  29.7 0.5 collective-permute-start.5
  30.2 0.0 collective-permute-done.7.refs_1_.other_ref
  30.2 4.1 %forward.4 = (bf16[2,256,512]{2,1,0:T(8,128)(2,1)S(1)}, bf16[256,3584]{1,0:T(8,128)(2,1)S(1)}, bf16[256,128]{1,0:T(8,128)(2,1)S(1)}) custom-call(s32[16]{0:T(128)S(1)} %stack.79.order_ref, bf16[128,3584]{1,0:T(8,128)(2,1)S(1)} %copy-done.4, bf16[128,3584]{1,0:T(8,128)(2,1)S(1)} %collective-permute-done.7.refs_1_.other_ref, bf16[64,3584]{1,0:T(8,128)(2,1)S(1)} %bitcast.40, ...), custom_call_target="tpu_custom_call" | custom-call | tf_op jit(solution)/shard_map/forward/pallas_call | solution.py:158
  34.4 0.0 collective-permute-done.5
  34.4 1.2 %collective-permute-done.6.refs_3_ = bf16[272,512]{1,0:T(8,128)(2,1)S(1)} collective-permute-done((bf16[272,512]{1,0:T(8,128)(2,1)S(1)}, bf16[272,512]{1,0:T(8,128)(2,1)S(1)}, u32[]{:S(2)}, u32[]{:S(2)}) %collective-permute-start.6) | collective-permute-done | bytes 278560 | tf_op jit(solution)/shard_map/ppermute | solution.py:329
  35.6 0.7 collective-permute-start.10
  36.3 0.6 collective-permute-start.8
  36.9 1.4 %collective-permute-start.11 = (bf16[272,512]{1,0:T(8,128)(2,1)S(1)}, bf16[272,512]{1,0:T(8,128)(2,1)S(1)}, u32[]{:S(2)}, u32[]{:S(2)}) collective-permute-start(bf16[272,512]{1,0:T(8,128)(2,1)S(1)} %collective-permute-done.1.refs_1_), channel_id=1, source_target_pairs={{0,2},{1,5},{2,0},{3,7},{4,6},{5,1},{6,4},{7,3},{8,10},{9,13},{10,... | collective-permute-start | bytes 835592 | tf_op jit(solution)/shard_map/ppermute | solution.py:329
  38.3 0.6 collective-permute-start.12
  38.9 2.7 %forward.5 = bf16[2,256,512]{2,1,0:T(8,128)(2,1)S(1)} custom-call(s32[16]{0:T(128)S(1)} %stack.79.order_ref, bf16[256,3584]{1,0:T(8,128)(2,1)S(1)} %get-tuple-element.79.refs_0_, bf16[256,128]{1,0:T(8,128)(2,1)S(1)} %get-tuple-element.80.refs_1_, bf16[64,8192]{1,0:T(8,128)(2,1)S(1)} %copy-done.1, ...), custom_call_target="tpu_custom_call" | custom-call | tf_op jit(solution)/shard_map/forward/pallas_call | solution.py:158
  41.7 2.6 %collective-permute-start.9 = (f32[24,512]{1,0:T(8,128)S(1)}, f32[24,512]{1,0:T(8,128)S(1)}, u32[]{:S(2)}, u32[]{:S(2)}) collective-permute-start(f32[24,512]{1,0:T(8,128)S(1)} %add.63), channel_id=1, source_target_pairs={{0,8},{1,9},{2,10},{3,11},{4,12},{5,13},{6,14},{7,15},{8,0},{9,1},... | collective-permute-start | bytes 147464 | tf_op jit(solution)/shard_map/ppermute | solution.py:329
  44.3 1.4 %collective-permute-start.14 = (bf16[256,512]{1,0:T(8,128)(2,1)S(1)}, bf16[256,512]{1,0:T(8,128)(2,1)S(1)}, u32[]{:S(2)}, u32[]{:S(2)}) collective-permute-start(bf16[256,512]{1,0:T(8,128)(2,1)S(1)} %get-tuple-element.134), channel_id=1, source_target_pairs={{0,2},{1,5},{2,0},{3,7},{4,6},{5,1},{6,4},{7,3},{8,10},{9,13},{10,... | collective-permute-start | bytes 786440 | tf_op jit(solution)/shard_map/ppermute | solution.py:329
  45.7 2.8 %forward.6 = bf16[2,256,512]{2,1,0:T(8,128)(2,1)S(1)} custom-call(s32[16]{0:T(128)S(1)} %stack.79.order_ref, bf16[256,3584]{1,0:T(8,128)(2,1)S(1)} %get-tuple-element.79.refs_0_, bf16[256,128]{1,0:T(8,128)(2,1)S(1)} %get-tuple-element.80.refs_1_, bf16[64,8192]{1,0:T(8,128)(2,1)S(1)} %copy-done.1, ...), custom_call_target="tpu_custom_call" | custom-call | tf_op jit(solution)/shard_map/forward/pallas_call | solution.py:158
  48.5 2.2 %collective-permute-done.12.refs_7_ = bf16[272,512]{1,0:T(8,128)(2,1)S(1)} collective-permute-done((bf16[272,512]{1,0:T(8,128)(2,1)S(1)}, bf16[272,512]{1,0:T(8,128)(2,1)S(1)}, u32[]{:S(2)}, u32[]{:S(2)}) %collective-permute-start.12) | collective-permute-done | bytes 278560 | tf_op jit(solution)/shard_map/ppermute | solution.py:329
  50.7 0.0 collective-permute-done.10
  50.7 0.1 add_convert_fusion
  50.9 0.7 collective-permute-start.13
  51.6 1.1 %collective-permute-start.18 = (bf16[256,512]{1,0:T(8,128)(2,1)S(1)}, bf16[256,512]{1,0:T(8,128)(2,1)S(1)}, u32[]{:S(2)}, u32[]{:S(2)}) collective-permute-start(bf16[256,512]{1,0:T(8,128)(2,1)S(1)} %get-tuple-element.133), channel_id=1, source_target_pairs={{0,2},{1,5},{2,0},{3,7},{4,6},{5,1},{6,4},{7,3},{8,10},{9,13},{10,... | collective-permute-start | bytes 786440 | tf_op jit(solution)/shard_map/ppermute | solution.py:329
  52.8 0.1 collective-permute-start.15
  52.9 0.0 copy-start.7
  52.9 2.7 %forward.7 = bf16[2,256,512]{2,1,0:T(8,128)(2,1)S(1)} custom-call(s32[16]{0:T(128)S(1)} %stack.79.order_ref, bf16[256,3584]{1,0:T(8,128)(2,1)S(1)} %get-tuple-element.79.refs_0_, bf16[256,128]{1,0:T(8,128)(2,1)S(1)} %get-tuple-element.80.refs_1_, bf16[64,8192]{1,0:T(8,128)(2,1)S(1)} %copy-done.1, bf16[3584,512]{1,0:T(8,128)(2,1)S(1)} %get-tuple-element.90.refs_3_.refs_11_, ...), custom_call_target="tpu_custom_call" | custom-call | tf_op jit(solution)/shard_map/forward/pallas_call | solution.py:158
  55.7 1.0 %collective-permute-start.17 = (bf16[256,512]{1,0:T(8,128)(2,1)S(1)}, bf16[256,512]{1,0:T(8,128)(2,1)S(1)}, u32[]{:S(2)}, u32[]{:S(2)}) collective-permute-start(bf16[256,512]{1,0:T(8,128)(2,1)S(1)} %get-tuple-element.135), channel_id=1, source_target_pairs={{0,4},{1,3},{2,6},{3,1},{4,0},{5,7},{6,2},{7,5},{8,12},{9,11},{10,... | collective-permute-start | bytes 786440 | tf_op jit(solution)/shard_map/ppermute | solution.py:329
  56.7 3.7 %backward.2 = (f32[128,768]{1,0:T(8,128)S(1)}, bf16[128,768]{1,0:T(8,128)(2,1)S(1)}, bf16[256,4096]{1,0:T(8,128)(2,1)S(1)}, f32[256,64]{1,0:T(8,128)S(1)}, f32[2...) custom-call(s32[16]{0:T(128)S(1)} %stack.79.order_ref, bf16[272,512]{1,0:T(8,128)(2,1)S(1)} %own_block.1.refs_0_, ...), custom_call_target="tpu_custom_call" | custom-call | tf_op jit(solution)/shard_map/backward/pallas_call | solution.py:223
  60.4 0.0 collective-permute-done.14
  60.4 0.2 collective-permute-start.19
  60.6 0.0 collective-permute-done.13
  60.6 0.2 fusion.5
  60.8 0.2 fusion.up_ref
  61.0 0.5 collective-permute-start.20
  61.5 0.1 fusion.2
  61.6 2.1 %collective-permute-start.16 = (bf16[256,512]{1,0:T(8,128)(2,1)S(1)}, bf16[256,512]{1,0:T(8,128)(2,1)S(1)}, u32[]{:S(2)}, u32[]{:S(2)}) collective-permute-start(bf16[256,512]{1,0:T(8,128)(2,1)S(1)} %fusion.2), channel_id=1, source_target_pairs={{0,8},{1,9},{2,10},{3,11},{4,12},{5,13},{6,14},{7,15},{8,0},{9,1},... | collective-permute-start | bytes 786440 | tf_op jit(solution)/shard_map/ppermute | solution.py:329
  63.7 9.0 %backward.3 = (f32[128,2816]{1,0:T(8,128)S(1)}, bf16[128,2816]{1,0:T(8,128)(2,1)S(1)}) custom-call(s32[16]{0:T(128)S(1)} %stack.79.order_ref, bf16[256,4096]{1,0:T(8,128)(2,1)S(1)} %get-tuple-element.110.refs_0_, f32[256,64]{1,0:T(8,128)S(1)} %get-tuple-element.106.refs_1_.proj_ref, bf16[64,3584]{1,0:T(8,128)(2,1)S(1)} %bitcast.42, ...), custom_call_target="tpu_custom_call" | custom-call | tf_op jit(solution)/shard_map/backward/pallas_call | solution.py:223
  72.7 0.0 collective-permute-done.20.up_other_ref
  72.7 0.3 collective-permute-start.24
  72.9 0.3 collective-permute-start.23
  73.3 2.0 %weights.1 = (f32[64,3584]{1,0:T(8,128)}, f32[64,1024]{1,0:T(8,128)}) custom-call(s32[16]{0:T(128)S(1)} %stack.79.order_ref, f32[256,64]{1,0:T(8,128)S(1)} %get-tuple-element.106.refs_1_.proj_ref, f32[256,64]{1,0:T(8,128)S(1)} %collective-permute-done.19.from_ref, bf16[128,3584]{1,0:T(8,128)(2,1)S(1)} %copy-done.5, ...), custom_call_target="tpu_custom_call" | custom-call | tf_op jit(solution)/shard_map/weights/pallas_call | solution.py:280
  75.3 1.2 %collective-permute-done.16 = bf16[256,512]{1,0:T(8,128)(2,1)S(1)} collective-permute-done((bf16[256,512]{1,0:T(8,128)(2,1)S(1)}, bf16[256,512]{1,0:T(8,128)(2,1)S(1)}, u32[]{:S(2)}, u32[]{:S(2)}) %collective-permute-start.16) | collective-permute-done | bytes 262176 | tf_op jit(solution)/shard_map/ppermute | solution.py:329
  76.5 0.2 multiply_reduce_fusion
  76.7 0.1 collective-permute-start.21
  76.8 0.5 collective-permute-start.22
  77.3 1.6 %hidden.1 = bf16[128,3584]{1,0:T(8,128)(2,1)} custom-call(s32[16]{0:T(128)S(1)} %stack.79.order_ref, f32[128,768]{1,0:T(8,128)S(1)} %get-tuple-element.120.ga_ref, bf16[128,768]{1,0:T(8,128)(2,1)S(1)} %collective-permute-done.23.ra_ref, f32[128,2816]{1,0:T(8,128)S(1)} %get-tuple-element.122.gb_ref, bf16[128,2816]{1,0:T(8,128)(2,1)S(1)} %collective-permute-done.24.rb_ref), custom_call_target="tpu_custom_call" | custom-call | tf_op jit(solution)/shard_map/hidden/pallas_call | solution.py:280
  78.9 1.3 %mixed.1 = (bf16[128,1024]{1,0:T(8,128)(2,1)}, f32[8,128]{1,0:T(8,128)}) custom-call(s32[16]{0:T(128)S(1)} %stack.79.order_ref, bf16[256,512]{1,0:T(8,128)(2,1)S(1)} %get-tuple-element.132.m_ref, bf16[128,512]{1,0:T(8,128)(2,1)S(1)} %collective-permute-done.21.m_other_ref, f32[1,512]{1,0:T(1,128)S(1)} %slice_divide_fusion.g_ref, ...), custom_call_target="tpu_custom_call" | custom-call | tf_op jit(solution)/shard_map/mixed/pallas_call | solution.py:280
  (39 shorter events, 0.2 us)
Async XLA Ops:
  0.6 1.9 %collective-permute-start = (bf16[128,1024]{1,0:T(8,128)(2,1)}, bf16[128,1024]{1,0:T(8,128)(2,1)S(1)}, u32[]{:S(2)}, u32[]{:S(2)}) collective-permute-start(bf16[128,1024]{1,0:T(8,128)(2,1)} %own_ref.2), channel_id=1, source_target_pairs={{0,1},{1,0},{2,3},{3,2},{4,5},{5,4},{6,7},{7,6},{8,9},{9,8},{10,11... | collective-permute-start | bytes 786440 | tf_op jit(solution)/shard_map/ppermute | solution.py:324
  1.1 29.1 %collective-permute-start.7 = (bf16[128,3584]{1,0:T(8,128)(2,1)}, bf16[128,3584]{1,0:T(8,128)(2,1)S(1)}, u32[]{:S(2)}, u32[]{:S(2)}) collective-permute-start(bf16[128,3584]{1,0:T(8,128)(2,1)} %own_ref.3), channel_id=1, source_target_pairs={{0,1},{1,0},{2,3},{3,2},{4,5},{5,4},{6,7},{7,6},{8,9},{9,8},{10,11... | collective-permute-start | bytes 2752520 | tf_op jit(solution)/shard_map/ppermute | solution.py:324
  2.5 0.9 %copy-start.8 = (bf16[128,1024]{1,0:T(8,128)(2,1)S(1)}, bf16[128,1024]{1,0:T(8,128)(2,1)}, u32[]{:S(2)}) copy-start(bf16[128,1024]{1,0:T(8,128)(2,1)} %own_ref.2) | copy-start | bytes 786436
  4.0 22.3 %collective-permute-start.1 = (bf16[272,512]{1,0:T(8,128)(2,1)S(1)}, bf16[272,512]{1,0:T(8,128)(2,1)S(1)}, u32[]{:S(2)}, u32[]{:S(2)}) collective-permute-start(bf16[272,512]{1,0:T(8,128)(2,1)S(1)} %own_block.1.refs_0_), channel_id=1, source_target_pairs={{0,8},{1,9},{2,10},{3,11},{4,12},{5,13},{6,14},{7,15},{8,0},{9,1},... | collective-permute-start | bytes 835592 | tf_op jit(solution)/shard_map/ppermute | solution.py:329
  8.1 18.3 %collective-permute-start.2 = (bf16[272,512]{1,0:T(8,128)(2,1)S(1)}, bf16[272,512]{1,0:T(8,128)(2,1)S(1)}, u32[]{:S(2)}, u32[]{:S(2)}) collective-permute-start(bf16[272,512]{1,0:T(8,128)(2,1)S(1)} %own_block.1.refs_0_), channel_id=1, source_target_pairs={{0,4},{1,3},{2,6},{3,1},{4,0},{5,7},{6,2},{7,5},{8,12},{9,11},{10,... | collective-permute-start | bytes 835592 | tf_op jit(solution)/shard_map/ppermute | solution.py:329
  9.6 16.7 %collective-permute-start.3 = (bf16[272,512]{1,0:T(8,128)(2,1)S(1)}, bf16[272,512]{1,0:T(8,128)(2,1)S(1)}, u32[]{:S(2)}, u32[]{:S(2)}) collective-permute-start(bf16[272,512]{1,0:T(8,128)(2,1)S(1)} %own_block.1.refs_0_), channel_id=1, source_target_pairs={{0,2},{1,5},{2,0},{3,7},{4,6},{5,1},{6,4},{7,3},{8,10},{9,13},{10,... | collective-permute-start | bytes 835592 | tf_op jit(solution)/shard_map/ppermute | solution.py:329
  11.1 17.4 %collective-permute-start.4 = (bf16[272,512]{1,0:T(8,128)(2,1)S(1)}, bf16[272,512]{1,0:T(8,128)(2,1)S(1)}, u32[]{:S(2)}, u32[]{:S(2)}) collective-permute-start(bf16[272,512]{1,0:T(8,128)(2,1)S(1)} %own_block.1.refs_0_), channel_id=1, source_target_pairs={{0,6},{1,7},{2,4},{3,5},{4,2},{5,3},{6,0},{7,1},{8,14},{9,15},{10,... | collective-permute-start | bytes 835592 | tf_op jit(solution)/shard_map/ppermute | solution.py:356
  11.6 1.2 %copy-start = (bf16[64,8192]{1,0:T(8,128)(2,1)S(1)}, bf16[64,8192]{1,0:T(8,128)(2,1)}, u32[]{:S(2)}) copy-start(bf16[64,8192]{1,0:T(8,128)(2,1)} %refs_9_.1) | copy-start | bytes 3145732
  12.8 1.2 %copy-start.4 = (bf16[128,3584]{1,0:T(8,128)(2,1)S(1)}, bf16[128,3584]{1,0:T(8,128)(2,1)}, u32[]{:S(2)}) copy-start(bf16[128,3584]{1,0:T(8,128)(2,1)} %own_ref.3) | copy-start | bytes 2752516
  14.0 1.0 %copy-start.6 = (bf16[3584,64]{0,1:T(8,128)(2,1)S(1)}, bf16[3584,64]{0,1:T(8,128)(2,1)}, u32[]{:S(2)}) copy-start(bf16[3584,64]{0,1:T(8,128)(2,1)} %param.8) | copy-start | bytes 1376260
  26.3 12.6 %copy-start.2 = (bf16[3584,512]{1,0:T(8,128)(2,1)}, bf16[3584,512]{1,0:T(8,128)(2,1)S(1)}, u32[]{:S(2)}) copy-start(bf16[3584,512]{1,0:T(8,128)(2,1)S(1)} %get-tuple-element.81.refs_3_.refs_15_.refs_7_) | copy-start | bytes 11010052
  28.5 7.1 %collective-permute-start.6 = (bf16[272,512]{1,0:T(8,128)(2,1)S(1)}, bf16[272,512]{1,0:T(8,128)(2,1)S(1)}, u32[]{:S(2)}, u32[]{:S(2)}) collective-permute-start(bf16[272,512]{1,0:T(8,128)(2,1)S(1)} %collective-permute-done.1.refs_1_), channel_id=1, source_target_pairs={{0,4},{1,3},{2,6},{3,1},{4,0},{5,7},{6,2},{7,5},{8,12},{9,11},{10,... | collective-permute-start | bytes 835592 | tf_op jit(solution)/shard_map/ppermute | solution.py:329
  29.7 4.7 %collective-permute-start.5 = (f32[24,512]{1,0:T(8,128)S(1)}, f32[24,512]{1,0:T(8,128)S(1)}, u32[]{:S(2)}, u32[]{:S(2)}) collective-permute-start(f32[24,512]{1,0:T(8,128)S(1)} %get-tuple-element.72), channel_id=1, source_target_pairs={{0,2},{1,5},{2,0},{3,7},{4,6},{5,1},{6,4},{7,3},{8,10},{9,13},{10,... | collective-permute-start | bytes 147464 | tf_op jit(solution)/shard_map/ppermute | solution.py:329
  30.2 8.7 %copy-start.1 = (bf16[64,8192]{1,0:T(8,128)(2,1)S(1)}, bf16[64,8192]{1,0:T(8,128)(2,1)}, u32[]{:S(2)}) copy-start(bf16[64,8192]{1,0:T(8,128)(2,1)} %refs_9_.1) | copy-start | bytes 3145732
  35.6 15.2 %collective-permute-start.10 = (bf16[2,256,512]{2,1,0:T(8,128)(2,1)S(1)}, bf16[2,256,512]{2,1,0:T(8,128)(2,1)S(1)}, u32[]{:S(2)}, u32[]{:S(2)}) collective-permute-start(bf16[2,256,512]{2,1,0:T(8,128)(2,1)S(1)} %get-tuple-element.84), channel_id=1, source_target_pairs={{0,2},{1,5},{2,0},{3,7},{4,6},{5,1},{6,4},{7,3},{8,10},{9,13},{10,... | collective-permute-start | bytes 1572872 | tf_op jit(solution)/shard_map/ppermute | solution.py:329
  36.3 5.4 %collective-permute-start.8 = (f32[24,512]{1,0:T(8,128)S(1)}, f32[24,512]{1,0:T(8,128)S(1)}, u32[]{:S(2)}, u32[]{:S(2)}) collective-permute-start(f32[24,512]{1,0:T(8,128)S(1)} %add.62), channel_id=1, source_target_pairs={{0,4},{1,3},{2,6},{3,1},{4,0},{5,7},{6,2},{7,5},{8,12},{9,11},{10,... | collective-permute-start | bytes 147464 | tf_op jit(solution)/shard_map/ppermute | solution.py:329
  36.9 11.5 %collective-permute-start.11 = (bf16[272,512]{1,0:T(8,128)(2,1)S(1)}, bf16[272,512]{1,0:T(8,128)(2,1)S(1)}, u32[]{:S(2)}, u32[]{:S(2)}) collective-permute-start(bf16[272,512]{1,0:T(8,128)(2,1)S(1)} %collective-permute-done.1.refs_1_), channel_id=1, source_target_pairs={{0,2},{1,5},{2,0},{3,7},{4,6},{5,1},{6,4},{7,3},{8,10},{9,13},{10,... | collective-permute-start | bytes 835592 | tf_op jit(solution)/shard_map/ppermute | solution.py:329
  38.3 12.4 %collective-permute-start.12 = (bf16[272,512]{1,0:T(8,128)(2,1)S(1)}, bf16[272,512]{1,0:T(8,128)(2,1)S(1)}, u32[]{:S(2)}, u32[]{:S(2)}) collective-permute-start(bf16[272,512]{1,0:T(8,128)(2,1)S(1)} %collective-permute-done.6.refs_3_), channel_id=1, source_target_pairs={{0,2},{1,5},{2,0},{3,7},{4,6},{5,1},{6,4},{7,3},{8,10},{9,13},{10,... | collective-permute-start | bytes 835592 | tf_op jit(solution)/shard_map/ppermute | solution.py:329
  41.7 6.8 %collective-permute-start.9 = (f32[24,512]{1,0:T(8,128)S(1)}, f32[24,512]{1,0:T(8,128)S(1)}, u32[]{:S(2)}, u32[]{:S(2)}) collective-permute-start(f32[24,512]{1,0:T(8,128)S(1)} %add.63), channel_id=1, source_target_pairs={{0,8},{1,9},{2,10},{3,11},{4,12},{5,13},{6,14},{7,15},{8,0},{9,1},... | collective-permute-start | bytes 147464 | tf_op jit(solution)/shard_map/ppermute | solution.py:329
  44.3 16.1 %collective-permute-start.14 = (bf16[256,512]{1,0:T(8,128)(2,1)S(1)}, bf16[256,512]{1,0:T(8,128)(2,1)S(1)}, u32[]{:S(2)}, u32[]{:S(2)}) collective-permute-start(bf16[256,512]{1,0:T(8,128)(2,1)S(1)} %get-tuple-element.134), channel_id=1, source_target_pairs={{0,2},{1,5},{2,0},{3,7},{4,6},{5,1},{6,4},{7,3},{8,10},{9,13},{10,... | collective-permute-start | bytes 786440 | tf_op jit(solution)/shard_map/ppermute | solution.py:329
  50.9 9.7 %collective-permute-start.13 = (bf16[256,512]{1,0:T(8,128)(2,1)S(1)}, bf16[256,512]{1,0:T(8,128)(2,1)S(1)}, u32[]{:S(2)}, u32[]{:S(2)}) collective-permute-start(bf16[256,512]{1,0:T(8,128)(2,1)S(1)} %get-tuple-element.136), channel_id=1, source_target_pairs={{0,4},{1,3},{2,6},{3,1},{4,0},{5,7},{6,2},{7,5},{8,12},{9,11},{10,... | collective-permute-start | bytes 786440 | tf_op jit(solution)/shard_map/ppermute | solution.py:329
  51.6 23.6 %collective-permute-start.18 = (bf16[256,512]{1,0:T(8,128)(2,1)S(1)}, bf16[256,512]{1,0:T(8,128)(2,1)S(1)}, u32[]{:S(2)}, u32[]{:S(2)}) collective-permute-start(bf16[256,512]{1,0:T(8,128)(2,1)S(1)} %get-tuple-element.133), channel_id=1, source_target_pairs={{0,2},{1,5},{2,0},{3,7},{4,6},{5,1},{6,4},{7,3},{8,10},{9,13},{10,... | collective-permute-start | bytes 786440 | tf_op jit(solution)/shard_map/ppermute | solution.py:329
  52.8 7.8 %collective-permute-start.15 = (f32[16,512]{1,0:T(8,128)S(1)}, f32[16,512]{1,0:T(8,128)S(1)}, u32[]{:S(2)}, u32[]{:S(2)}) collective-permute-start(f32[16,512]{1,0:T(8,128)S(1)} %slice.89), channel_id=1, source_target_pairs={{0,1},{1,0},{2,3},{3,2},{4,5},{5,4},{6,7},{7,6},{8,9},{9,8},{10,11... | collective-permute-start | bytes 98312 | tf_op jit(solution)/shard_map/ppermute | solution.py:324
  52.9 3.8 %copy-start.3 = (bf16[3584,512]{1,0:T(8,128)(2,1)S(1)}, bf16[3584,512]{1,0:T(8,128)(2,1)}, u32[]{:S(2)}) copy-start(bf16[3584,512]{1,0:T(8,128)(2,1)} %copy-done.2) | copy-start | bytes 11010052
  52.9 3.8 %copy-start.7 = (bf16[3584,64]{0,1:T(8,128)(2,1)S(1)}, bf16[3584,64]{0,1:T(8,128)(2,1)}, u32[]{:S(2)}) copy-start(bf16[3584,64]{0,1:T(8,128)(2,1)} %param.8) | copy-start | bytes 1376260
  55.7 19.6 %collective-permute-start.17 = (bf16[256,512]{1,0:T(8,128)(2,1)S(1)}, bf16[256,512]{1,0:T(8,128)(2,1)S(1)}, u32[]{:S(2)}, u32[]{:S(2)}) collective-permute-start(bf16[256,512]{1,0:T(8,128)(2,1)S(1)} %get-tuple-element.135), channel_id=1, source_target_pairs={{0,4},{1,3},{2,6},{3,1},{4,0},{5,7},{6,2},{7,5},{8,12},{9,11},{10,... | collective-permute-start | bytes 786440 | tf_op jit(solution)/shard_map/ppermute | solution.py:329
  60.4 12.2 %collective-permute-start.19 = (f32[256,64]{1,0:T(8,128)S(1)}, f32[256,64]{1,0:T(8,128)S(1)}, u32[]{:S(2)}, u32[]{:S(2)}) collective-permute-start(f32[256,64]{1,0:T(8,128)S(1)} %get-tuple-element.106.refs_1_.proj_ref), channel_id=1, source_target_pairs={{0,1},{1,0},{2,3},{3,2},{4,5},{5,4},{6,7},{7,6},{8,9},{9,8},{10,11... | collective-permute-start | bytes 196616 | tf_op jit(solution)/shard_map/ppermute | solution.py:324
  61.0 11.6 %collective-permute-start.20 = (f32[64,512]{1,0:T(8,128)S(1)}, f32[64,512]{1,0:T(8,128)S(1)}, u32[]{:S(2)}, u32[]{:S(2)}) collective-permute-start(f32[64,512]{1,0:T(8,128)S(1)} %fusion.up_ref), channel_id=1, source_target_pairs={{0,1},{1,0},{2,3},{3,2},{4,5},{5,4},{6,7},{7,6},{8,9},{9,8},{10,11... | collective-permute-start | bytes 393224 | tf_op jit(solution)/shard_map/ppermute | solution.py:324
  61.6 14.9 %collective-permute-start.16 = (bf16[256,512]{1,0:T(8,128)(2,1)S(1)}, bf16[256,512]{1,0:T(8,128)(2,1)S(1)}, u32[]{:S(2)}, u32[]{:S(2)}) collective-permute-start(bf16[256,512]{1,0:T(8,128)(2,1)S(1)} %fusion.2), channel_id=1, source_target_pairs={{0,8},{1,9},{2,10},{3,11},{4,12},{5,13},{6,14},{7,15},{8,0},{9,1},... | collective-permute-start | bytes 786440 | tf_op jit(solution)/shard_map/ppermute | solution.py:329
  63.7 9.6 %copy-start.5 = (bf16[128,3584]{1,0:T(8,128)(2,1)S(1)}, bf16[128,3584]{1,0:T(8,128)(2,1)}, u32[]{:S(2)}) copy-start(bf16[128,3584]{1,0:T(8,128)(2,1)} %own_ref.3) | copy-start | bytes 2752516
  72.7 4.6 %collective-permute-start.24 = (bf16[128,2816]{1,0:T(8,128)(2,1)S(1)}, bf16[128,2816]{1,0:T(8,128)(2,1)S(1)}, u32[]{:S(2)}, u32[]{:S(2)}) collective-permute-start(bf16[128,2816]{1,0:T(8,128)(2,1)S(1)} %get-tuple-element.123), channel_id=1, source_target_pairs={{0,1},{1,0},{2,3},{3,2},{4,5},{5,4},{6,7},{7,6},{8,9},{9,8},{10,11... | collective-permute-start | bytes 2162696 | tf_op jit(solution)/shard_map/ppermute | solution.py:324
  72.9 4.4 %collective-permute-start.23 = (bf16[128,768]{1,0:T(8,128)(2,1)S(1)}, bf16[128,768]{1,0:T(8,128)(2,1)S(1)}, u32[]{:S(2)}, u32[]{:S(2)}) collective-permute-start(bf16[128,768]{1,0:T(8,128)(2,1)S(1)} %get-tuple-element.121), channel_id=1, source_target_pairs={{0,1},{1,0},{2,3},{3,2},{4,5},{5,4},{6,7},{7,6},{8,9},{9,8},{10,11... | collective-permute-start | bytes 589832 | tf_op jit(solution)/shard_map/ppermute | solution.py:324
  76.7 2.2 %collective-permute-start.21 = (bf16[128,512]{1,0:T(8,128)(2,1)S(1)}, bf16[128,512]{1,0:T(8,128)(2,1)S(1)}, u32[]{:S(2)}, u32[]{:S(2)}) collective-permute-start(bf16[128,512]{1,0:T(8,128)(2,1)S(1)} %slice.95), channel_id=1, source_target_pairs={{0,1},{1,0},{2,3},{3,2},{4,5},{5,4},{6,7},{7,6},{8,9},{9,8},{10,11... | collective-permute-start | bytes 393224 | tf_op jit(solution)/shard_map/ppermute | solution.py:324
  76.8 2.1 %collective-permute-start.22 = (f32[1,512]{1,0:T(1,128)S(1)}, f32[1,512]{1,0:T(1,128)S(1)}, u32[]{:S(2)}, u32[]{:S(2)}) collective-permute-start(f32[1,512]{1,0:T(1,128)S(1)} %slice_divide_fusion.g_ref), channel_id=1, source_target_pairs={{0,1},{1,0},{2,3},{3,2},{4,5},{5,4},{6,7},{7,6},{8,9},{9,8},{10,11... | collective-permute-start | bytes 6152 | tf_op jit(solution)/shard_map/ppermute | solution.py:324

commit v15 on v14

--- a/solution.py
+++ b/solution.py
@@ -359,14 +359,12 @@
     block, order = tie((block, order))
     *held, stats = run_load(tuple(range(n)), order, own=hidden)
     near, far = held[: n // 2], held[n // 2 :]
-    cots[0b001], cots[0b010], cots[0b100], cots[0b110], stats = tie(
-        (cots[0b001], cots[0b010], cots[0b100], cots[0b110], stats)
-    )
+    cots[0b001], cots[0b010], cots[0b100], stats = tie((cots[0b001], cots[0b010], cots[0b100], stats))
     cots[0b011], cots[0b101] = send(cots[0b001], 1), send(cots[0b001], 0)
     got = send(stats, 0)
     far1, lhs, adapter = forward((0b110, 0b111), order, far[2:], up, first=(hidden, hidden_other, at))
     run = lambda order, vs, held: forward(vs, order, held, up, later=(lhs, adapter))[0]
-    got, cots[0b011], far1, order = tie((got, cots[0b011], far1, order))
+    got, cots[0b011], cots[0b110], far1, order = tie((got, cots[0b011], cots[0b110], far1, order))
     cots[0b111] = send(cots[0b011], 0)
     stats = stats + got
     got = send(stats, 1)
@@ -388,7 +386,7 @@
 
     band = 256
     bands = rows // band
-    many = max(bands * 3 // 14, 1)
+    many = max(bands * 2 // 14, 1)
     run = functools.partial(backward, order, band=band, at=at, held=held)
     grad_a, other_a, scaled, proj, scales, scaled_own = run(0, many, first=([cots[v] for v in range(n)], stats, up))
     from_sibling = swap(proj)

time: 80.5 us -> 88.1 us (1.094)
  waiting for transfers between devices: 7.18 us -> 16.5 us
  starting transfers between devices: 24 us -> 22.2 us
    ppermute x15, waiting for transfers between devices: 4.71 us -> 16.1 us  [send(): return lax.ppermute(x, ('tensor', 'dp'), pairs)]
    ppermute x1, waiting for transfers between devices: 2.14 us -> 0.01 us  [split_columns(): cots[6] = lax.ppermute(block, ('tensor', 'dp'), across)]
    ppermute x15, starting transfers between devices: 21.1 us -> 19.7 us  [send(): return lax.ppermute(x, ('tensor', 'dp'), pairs)]
  transfers between devices with their start and end apart: 25 -> 25, of which waited for: 5 -> 5; matrix products, arithmetic and copies ran while one was open for 2% -> 2% of each run, Pallas kernels for 51% -> 46%
where the time goes in v15:
time: 88.1 us; the launch traced here: 87.8 us
  Pallas kernels  41.8 us (47%)
  starting transfers between devices  22.2 us (25%)
  waiting for transfers between devices  16.5 us (19%)
  local copies, waits for them, and re-layouts  4.68 us (5%)
  other arithmetic  1.26 us (1%)
  between operations  1 us (1%)
    ppermute x15, starting transfers between devices, send(): return lax.ppermute(x, ('tensor', 'dp'), pairs)  19.7 us
    ppermute x15, waiting for transfers between devices, send(): return lax.ppermute(x, ('tensor', 'dp'), pairs)  16.1 us
    pallas_call x2, Pallas kernels, backward(): pl.pallas_call(functools.partial(backward_kernel, tokens, n, start, band,...  12.7 us
    pallas_call x4, Pallas kernels, forward(): pl.pallas_call(functools.partial(forward_kernel, tokens, rank, vs, later...  12.3 us
    pallas_call x1, Pallas kernels, load(): pl.pallas_call(functools.partial(load_kernel, tokens, rank, n, vs, first)...  11.3 us
    pallas_call x3, Pallas kernels, finish(): pl.pallas_call(kernel, grid_spec=pltpu.PrefetchScalarGridSpec(num_scalar_...  4.9 us
    unnamed x18, local copies, waits for them, and re-layouts  4.39 us
    ppermute x9, starting transfers between devices, split_columns(): swap = lambda x: lax.ppermute(x, 'dp', [(0, 1), (1, 0)])  2.12 us
  transfers between devices with their start and end apart: 25, of which 5 were waited for; matrix products, arithmetic and copies ran while one was open for 2% of the time, Pallas kernels for 46%

profile of v15, /device:TPU:0, one launch (start us, length us, event | category | flops | bytes accessed | tf_op | source)
XLA Modules:
  0.0 87.8 jit_solution(14732296383667890393)
XLA Ops:
  0.6 0.5 collective-permute-start
  1.1 0.1 collective-permute-start.7
  1.2 0.7 reduce-precision_convert_fusion.1
  2.0 0.1 pad.11.clone
  2.0 0.1 stack.79.order_ref
  2.1 0.1 maximum_maximum_fusion.magnitude_ref
  2.2 0.3 collective-permute-done.other_ref
  2.5 0.9 %copy-done.8 = bf16[128,1024]{1,0:T(8,128)(2,1)S(1)} copy-done((bf16[128,1024]{1,0:T(8,128)(2,1)S(1)}, bf16[128,1024]{1,0:T(8,128)(2,1)}, u32[]{:S(2)}) %copy-start.8) | copy-done | bytes 262168
  3.5 0.6 own_block.1.refs_0_
  4.0 4.0 %collective-permute-start.1 = (bf16[272,512]{1,0:T(8,128)(2,1)S(1)}, bf16[272,512]{1,0:T(8,128)(2,1)S(1)}, u32[]{:S(2)}, u32[]{:S(2)}) collective-permute-start(bf16[272,512]{1,0:T(8,128)(2,1)S(1)} %own_block.1.refs_0_), channel_id=1, source_target_pairs={{0,8},{1,9},{2,10},{3,11},{4,12},{5,13},{6,14},{7,15},{8,0},{9,1},... | collective-permute-start | bytes 835592 | tf_op jit(solution)/shard_map/ppermute | solution.py:329
  8.1 1.6 %collective-permute-start.2 = (bf16[272,512]{1,0:T(8,128)(2,1)S(1)}, bf16[272,512]{1,0:T(8,128)(2,1)S(1)}, u32[]{:S(2)}, u32[]{:S(2)}) collective-permute-start(bf16[272,512]{1,0:T(8,128)(2,1)S(1)} %own_block.1.refs_0_), channel_id=1, source_target_pairs={{0,4},{1,3},{2,6},{3,1},{4,0},{5,7},{6,2},{7,5},{8,12},{9,11},{10,... | collective-permute-start | bytes 835592 | tf_op jit(solution)/shard_map/ppermute | solution.py:329
  9.6 1.5 %collective-permute-start.3 = (bf16[272,512]{1,0:T(8,128)(2,1)S(1)}, bf16[272,512]{1,0:T(8,128)(2,1)S(1)}, u32[]{:S(2)}, u32[]{:S(2)}) collective-permute-start(bf16[272,512]{1,0:T(8,128)(2,1)S(1)} %own_block.1.refs_0_), channel_id=1, source_target_pairs={{0,2},{1,5},{2,0},{3,7},{4,6},{5,1},{6,4},{7,3},{8,10},{9,13},{10,... | collective-permute-start | bytes 835592 | tf_op jit(solution)/shard_map/ppermute | solution.py:329
  11.1 0.4 collective-permute-start.6
  11.6 1.2 %copy-done = bf16[64,8192]{1,0:T(8,128)(2,1)S(1)} copy-done((bf16[64,8192]{1,0:T(8,128)(2,1)S(1)}, bf16[64,8192]{1,0:T(8,128)(2,1)}, u32[]{:S(2)}) %copy-start) | copy-done | bytes 1048600
  12.8 1.2 %copy-done.4 = bf16[128,3584]{1,0:T(8,128)(2,1)S(1)} copy-done((bf16[128,3584]{1,0:T(8,128)(2,1)S(1)}, bf16[128,3584]{1,0:T(8,128)(2,1)}, u32[]{:S(2)}) %copy-start.4) | copy-done | bytes 917528
  14.0 1.0 %copy-done.6 = bf16[3584,64]{0,1:T(8,128)(2,1)S(1)} copy-done((bf16[3584,64]{0,1:T(8,128)(2,1)S(1)}, bf16[3584,64]{0,1:T(8,128)(2,1)}, u32[]{:S(2)}) %copy-start.6) | copy-done | bytes 458776
  15.0 11.3 %load.1 = (bf16[3584,512]{1,0:T(8,128)(2,1)S(1)}, bf16[3584,512]{1,0:T(8,128)(2,1)S(1)}, bf16[3584,512]{1,0:T(8,128)(2,1)S(1)}, bf16[3584,512]{1,0:T(8,128)(2,1)...) custom-call(s32[16]{0:T(128)S(1)} %stack.79.order_ref, ...), custom_call_target="tpu_custom_call" | custom-call | tf_op jit(solution)/shard_map/load/pallas_call | solution.py:116
  26.3 0.0 collective-permute-done.2.refs_2_
  26.3 0.0 collective-permute-done.3.refs_4_
  26.4 1.6 %collective-permute-start.5 = (bf16[272,512]{1,0:T(8,128)(2,1)S(1)}, bf16[272,512]{1,0:T(8,128)(2,1)S(1)}, u32[]{:S(2)}, u32[]{:S(2)}) collective-permute-start(bf16[272,512]{1,0:T(8,128)(2,1)S(1)} %collective-permute-done.1.refs_1_), channel_id=1, source_target_pairs={{0,4},{1,3},{2,6},{3,1},{4,0},{5,7},{6,2},{7,5},{8,12},{9,11},{10,... | collective-permute-start | bytes 835592 | tf_op jit(solution)/shard_map/ppermute | solution.py:329
  28.0 1.5 %collective-permute-start.4 = (f32[24,512]{1,0:T(8,128)S(1)}, f32[24,512]{1,0:T(8,128)S(1)}, u32[]{:S(2)}, u32[]{:S(2)}) collective-permute-start(f32[24,512]{1,0:T(8,128)S(1)} %get-tuple-element.72), channel_id=1, source_target_pairs={{0,2},{1,5},{2,0},{3,7},{4,6},{5,1},{6,4},{7,3},{8,10},{9,13},{10,... | collective-permute-start | bytes 147464 | tf_op jit(solution)/shard_map/ppermute | solution.py:329
  29.5 0.0 collective-permute-done.7.refs_1_.other_ref
  29.5 4.1 %forward.4 = (bf16[2,256,512]{2,1,0:T(8,128)(2,1)S(1)}, bf16[256,3584]{1,0:T(8,128)(2,1)S(1)}, bf16[256,128]{1,0:T(8,128)(2,1)S(1)}) custom-call(s32[16]{0:T(128)S(1)} %stack.79.order_ref, bf16[128,3584]{1,0:T(8,128)(2,1)S(1)} %copy-done.4, bf16[128,3584]{1,0:T(8,128)(2,1)S(1)} %collective-permute-done.7.refs_1_.other_ref, bf16[64,3584]{1,0:T(8,128)(2,1)S(1)} %bitcast.40, ...), custom_call_target="tpu_custom_call" | custom-call | tf_op jit(solution)/shard_map/forward/pallas_call | solution.py:158
  33.6 0.0 collective-permute-done.6.refs_6_
  33.6 0.0 collective-permute-done.5.refs_3_
  33.6 0.8 collective-permute-start.10
  34.5 1.6 %collective-permute-start.8 = (f32[24,512]{1,0:T(8,128)S(1)}, f32[24,512]{1,0:T(8,128)S(1)}, u32[]{:S(2)}, u32[]{:S(2)}) collective-permute-start(f32[24,512]{1,0:T(8,128)S(1)} %add.62), channel_id=1, source_target_pairs={{0,4},{1,3},{2,6},{3,1},{4,0},{5,7},{6,2},{7,5},{8,12},{9,11},{10,... | collective-permute-start | bytes 147464 | tf_op jit(solution)/shard_map/ppermute | solution.py:329
  36.1 0.5 collective-permute-start.11
  36.6 1.5 %collective-permute-start.12 = (bf16[272,512]{1,0:T(8,128)(2,1)S(1)}, bf16[272,512]{1,0:T(8,128)(2,1)S(1)}, u32[]{:S(2)}, u32[]{:S(2)}) collective-permute-start(bf16[272,512]{1,0:T(8,128)(2,1)S(1)} %collective-permute-done.5.refs_3_), channel_id=1, source_target_pairs={{0,2},{1,5},{2,0},{3,7},{4,6},{5,1},{6,4},{7,3},{8,10},{9,13},{10,... | collective-permute-start | bytes 835592 | tf_op jit(solution)/shard_map/ppermute | solution.py:329
  38.1 2.8 %forward.5 = bf16[2,256,512]{2,1,0:T(8,128)(2,1)S(1)} custom-call(s32[16]{0:T(128)S(1)} %stack.79.order_ref, bf16[256,3584]{1,0:T(8,128)(2,1)S(1)} %get-tuple-element.79.refs_0_, bf16[256,128]{1,0:T(8,128)(2,1)S(1)} %get-tuple-element.80.refs_1_, bf16[64,8192]{1,0:T(8,128)(2,1)S(1)} %copy-done.1, ...), custom_call_target="tpu_custom_call" | custom-call | tf_op jit(solution)/shard_map/forward/pallas_call | solution.py:158
  40.9 0.0 collective-permute-done.8
  40.9 0.4 collective-permute-start.9
  41.4 0.7 collective-permute-start.14
  42.1 2.7 %forward.6 = bf16[2,256,512]{2,1,0:T(8,128)(2,1)S(1)} custom-call(s32[16]{0:T(128)S(1)} %stack.79.order_ref, bf16[256,3584]{1,0:T(8,128)(2,1)S(1)} %get-tuple-element.79.refs_0_, bf16[256,128]{1,0:T(8,128)(2,1)S(1)} %get-tuple-element.80.refs_1_, bf16[64,8192]{1,0:T(8,128)(2,1)S(1)} %copy-done.1, ...), custom_call_target="tpu_custom_call" | custom-call | tf_op jit(solution)/shard_map/forward/pallas_call | solution.py:158
  44.8 1.1 %collective-permute-done.11.refs_5_ = bf16[272,512]{1,0:T(8,128)(2,1)S(1)} collective-permute-done((bf16[272,512]{1,0:T(8,128)(2,1)S(1)}, bf16[272,512]{1,0:T(8,128)(2,1)S(1)}, u32[]{:S(2)}, u32[]{:S(2)}) %collective-permute-start.11) | collective-permute-done | bytes 278560 | tf_op jit(solution)/shard_map/ppermute | solution.py:329
  45.9 0.7 collective-permute-done.9
  46.6 2.2 %collective-permute-done.12.refs_7_ = bf16[272,512]{1,0:T(8,128)(2,1)S(1)} collective-permute-done((bf16[272,512]{1,0:T(8,128)(2,1)S(1)}, bf16[272,512]{1,0:T(8,128)(2,1)S(1)}, u32[]{:S(2)}, u32[]{:S(2)}) %collective-permute-start.12) | collective-permute-done | bytes 278560 | tf_op jit(solution)/shard_map/ppermute | solution.py:329
  48.8 0.1 add_convert_fusion
  49.0 0.9 %collective-permute-start.13 = (bf16[256,512]{1,0:T(8,128)(2,1)S(1)}, bf16[256,512]{1,0:T(8,128)(2,1)S(1)}, u32[]{:S(2)}, u32[]{:S(2)}) collective-permute-start(bf16[256,512]{1,0:T(8,128)(2,1)S(1)} %get-tuple-element.136), channel_id=1, source_target_pairs={{0,4},{1,3},{2,6},{3,1},{4,0},{5,7},{6,2},{7,5},{8,12},{9,11},{10,... | collective-permute-start | bytes 786440 | tf_op jit(solution)/shard_map/ppermute | solution.py:329
  50.0 0.1 collective-permute-start.15
  50.1 0.0 copy-start.7
  50.1 2.7 %forward.7 = bf16[2,256,512]{2,1,0:T(8,128)(2,1)S(1)} custom-call(s32[16]{0:T(128)S(1)} %stack.79.order_ref, bf16[256,3584]{1,0:T(8,128)(2,1)S(1)} %get-tuple-element.79.refs_0_, bf16[256,128]{1,0:T(8,128)(2,1)S(1)} %get-tuple-element.80.refs_1_, bf16[64,8192]{1,0:T(8,128)(2,1)S(1)} %copy-done.1, bf16[3584,512]{1,0:T(8,128)(2,1)S(1)} %get-tuple-element.90.refs_3_.refs_11_, ...), custom_call_target="tpu_custom_call" | custom-call | tf_op jit(solution)/shard_map/forward/pallas_call | solution.py:158
  52.8 3.0 %backward.2 = (f32[128,512]{1,0:T(8,128)S(1)}, bf16[128,512]{1,0:T(8,128)(2,1)S(1)}, bf16[256,4096]{1,0:T(8,128)(2,1)S(1)}, f32[256,64]{1,0:T(8,128)S(1)}, f32[2...) custom-call(s32[16]{0:T(128)S(1)} %stack.79.order_ref, bf16[272,512]{1,0:T(8,128)(2,1)S(1)} %own_block.1.refs_0_, ...), custom_call_target="tpu_custom_call" | custom-call | tf_op jit(solution)/shard_map/backward/pallas_call | solution.py:223
  55.8 0.0 collective-permute-done.14
  55.8 0.0 collective-permute-done.13
  55.9 0.2 fusion.5
  56.1 0.2 fusion.up_ref
  56.3 0.5 collective-permute-start.20
  56.8 0.1 collective-permute-start.19
  56.9 1.5 %collective-permute-start.18 = (bf16[256,512]{1,0:T(8,128)(2,1)S(1)}, bf16[256,512]{1,0:T(8,128)(2,1)S(1)}, u32[]{:S(2)}, u32[]{:S(2)}) collective-permute-start(bf16[256,512]{1,0:T(8,128)(2,1)S(1)} %get-tuple-element.133), channel_id=1, source_target_pairs={{0,2},{1,5},{2,0},{3,7},{4,6},{5,1},{6,4},{7,3},{8,10},{9,13},{10,... | collective-permute-start | bytes 786440 | tf_op jit(solution)/shard_map/ppermute | solution.py:329
  58.4 0.5 collective-permute-start.17
  58.8 9.7 %backward.3 = (f32[128,3072]{1,0:T(8,128)S(1)}, bf16[128,3072]{1,0:T(8,128)(2,1)S(1)}) custom-call(s32[16]{0:T(128)S(1)} %stack.79.order_ref, bf16[256,4096]{1,0:T(8,128)(2,1)S(1)} %get-tuple-element.110.refs_0_, f32[256,64]{1,0:T(8,128)S(1)} %get-tuple-element.106.refs_1_.proj_ref, bf16[64,3584]{1,0:T(8,128)(2,1)S(1)} %bitcast.42, ...), custom_call_target="tpu_custom_call" | custom-call | tf_op jit(solution)/shard_map/backward/pallas_call | solution.py:223
  68.6 0.0 collective-permute-done.19.from_ref
  68.6 0.1 collective-permute-start.24
  68.7 0.1 fusion.2
  68.8 1.0 %collective-permute-start.16 = (bf16[256,512]{1,0:T(8,128)(2,1)S(1)}, bf16[256,512]{1,0:T(8,128)(2,1)S(1)}, u32[]{:S(2)}, u32[]{:S(2)}) collective-permute-start(bf16[256,512]{1,0:T(8,128)(2,1)S(1)} %fusion.2), channel_id=1, source_target_pairs={{0,8},{1,9},{2,10},{3,11},{4,12},{5,13},{6,14},{7,15},{8,0},{9,1},... | collective-permute-start | bytes 786440 | tf_op jit(solution)/shard_map/ppermute | solution.py:329
  69.8 0.2 collective-permute-start.23
  70.0 2.0 %weights.1 = (f32[64,3584]{1,0:T(8,128)}, f32[64,1024]{1,0:T(8,128)}) custom-call(s32[16]{0:T(128)S(1)} %stack.79.order_ref, f32[256,64]{1,0:T(8,128)S(1)} %get-tuple-element.106.refs_1_.proj_ref, f32[256,64]{1,0:T(8,128)S(1)} %collective-permute-done.19.from_ref, bf16[128,3584]{1,0:T(8,128)(2,1)S(1)} %copy-done.5, ...), custom_call_target="tpu_custom_call" | custom-call | tf_op jit(solution)/shard_map/weights/pallas_call | solution.py:280
  72.0 12.0 %collective-permute-done.16 = bf16[256,512]{1,0:T(8,128)(2,1)S(1)} collective-permute-done((bf16[256,512]{1,0:T(8,128)(2,1)S(1)}, bf16[256,512]{1,0:T(8,128)(2,1)S(1)}, u32[]{:S(2)}, u32[]{:S(2)}) %collective-permute-start.16) | collective-permute-done | bytes 262176 | tf_op jit(solution)/shard_map/ppermute | solution.py:329
  84.1 0.2 multiply_reduce_fusion
  84.3 0.1 collective-permute-start.21
  84.4 0.5 collective-permute-start.22
  84.9 1.6 %hidden.1 = bf16[128,3584]{1,0:T(8,128)(2,1)} custom-call(s32[16]{0:T(128)S(1)} %stack.79.order_ref, f32[128,512]{1,0:T(8,128)S(1)} %get-tuple-element.120.ga_ref, bf16[128,512]{1,0:T(8,128)(2,1)S(1)} %collective-permute-done.23.ra_ref, f32[128,3072]{1,0:T(8,128)S(1)} %get-tuple-element.122.gb_ref, bf16[128,3072]{1,0:T(8,128)(2,1)S(1)} %collective-permute-done.24.rb_ref), custom_call_target="tpu_custom_call" | custom-call | tf_op jit(solution)/shard_map/hidden/pallas_call | solution.py:280
  86.5 1.3 %mixed.1 = (bf16[128,1024]{1,0:T(8,128)(2,1)}, f32[8,128]{1,0:T(8,128)}) custom-call(s32[16]{0:T(128)S(1)} %stack.79.order_ref, bf16[256,512]{1,0:T(8,128)(2,1)S(1)} %get-tuple-element.132.m_ref, bf16[128,512]{1,0:T(8,128)(2,1)S(1)} %collective-permute-done.21.m_other_ref, f32[1,512]{1,0:T(1,128)S(1)} %slice_divide_fusion.g_ref, ...), custom_call_target="tpu_custom_call" | custom-call | tf_op jit(solution)/shard_map/mixed/pallas_call | solution.py:280
  (39 shorter events, 0.2 us)
Async XLA Ops:
  0.6 1.9 %collective-permute-start = (bf16[128,1024]{1,0:T(8,128)(2,1)}, bf16[128,1024]{1,0:T(8,128)(2,1)S(1)}, u32[]{:S(2)}, u32[]{:S(2)}) collective-permute-start(bf16[128,1024]{1,0:T(8,128)(2,1)} %own_ref.2), channel_id=1, source_target_pairs={{0,1},{1,0},{2,3},{3,2},{4,5},{5,4},{6,7},{7,6},{8,9},{9,8},{10,11... | collective-permute-start | bytes 786440 | tf_op jit(solution)/shard_map/ppermute | solution.py:324
  1.1 28.3 %collective-permute-start.7 = (bf16[128,3584]{1,0:T(8,128)(2,1)}, bf16[128,3584]{1,0:T(8,128)(2,1)S(1)}, u32[]{:S(2)}, u32[]{:S(2)}) collective-permute-start(bf16[128,3584]{1,0:T(8,128)(2,1)} %own_ref.3), channel_id=1, source_target_pairs={{0,1},{1,0},{2,3},{3,2},{4,5},{5,4},{6,7},{7,6},{8,9},{9,8},{10,11... | collective-permute-start | bytes 2752520 | tf_op jit(solution)/shard_map/ppermute | solution.py:324
  2.5 0.9 %copy-start.8 = (bf16[128,1024]{1,0:T(8,128)(2,1)S(1)}, bf16[128,1024]{1,0:T(8,128)(2,1)}, u32[]{:S(2)}) copy-start(bf16[128,1024]{1,0:T(8,128)(2,1)} %own_ref.2) | copy-start | bytes 786436
  4.0 22.3 %collective-permute-start.1 = (bf16[272,512]{1,0:T(8,128)(2,1)S(1)}, bf16[272,512]{1,0:T(8,128)(2,1)S(1)}, u32[]{:S(2)}, u32[]{:S(2)}) collective-permute-start(bf16[272,512]{1,0:T(8,128)(2,1)S(1)} %own_block.1.refs_0_), channel_id=1, source_target_pairs={{0,8},{1,9},{2,10},{3,11},{4,12},{5,13},{6,14},{7,15},{8,0},{9,1},... | collective-permute-start | bytes 835592 | tf_op jit(solution)/shard_map/ppermute | solution.py:329
  8.1 18.3 %collective-permute-start.2 = (bf16[272,512]{1,0:T(8,128)(2,1)S(1)}, bf16[272,512]{1,0:T(8,128)(2,1)S(1)}, u32[]{:S(2)}, u32[]{:S(2)}) collective-permute-start(bf16[272,512]{1,0:T(8,128)(2,1)S(1)} %own_block.1.refs_0_), channel_id=1, source_target_pairs={{0,4},{1,3},{2,6},{3,1},{4,0},{5,7},{6,2},{7,5},{8,12},{9,11},{10,... | collective-permute-start | bytes 835592 | tf_op jit(solution)/shard_map/ppermute | solution.py:329
  9.6 16.7 %collective-permute-start.3 = (bf16[272,512]{1,0:T(8,128)(2,1)S(1)}, bf16[272,512]{1,0:T(8,128)(2,1)S(1)}, u32[]{:S(2)}, u32[]{:S(2)}) collective-permute-start(bf16[272,512]{1,0:T(8,128)(2,1)S(1)} %own_block.1.refs_0_), channel_id=1, source_target_pairs={{0,2},{1,5},{2,0},{3,7},{4,6},{5,1},{6,4},{7,3},{8,10},{9,13},{10,... | collective-permute-start | bytes 835592 | tf_op jit(solution)/shard_map/ppermute | solution.py:329
  11.1 22.5 %collective-permute-start.6 = (bf16[272,512]{1,0:T(8,128)(2,1)S(1)}, bf16[272,512]{1,0:T(8,128)(2,1)S(1)}, u32[]{:S(2)}, u32[]{:S(2)}) collective-permute-start(bf16[272,512]{1,0:T(8,128)(2,1)S(1)} %own_block.1.refs_0_), channel_id=1, source_target_pairs={{0,6},{1,7},{2,4},{3,5},{4,2},{5,3},{6,0},{7,1},{8,14},{9,15},{10,... | collective-permute-start | bytes 835592 | tf_op jit(solution)/shard_map/ppermute | solution.py:356
  11.6 1.2 %copy-start = (bf16[64,8192]{1,0:T(8,128)(2,1)S(1)}, bf16[64,8192]{1,0:T(8,128)(2,1)}, u32[]{:S(2)}) copy-start(bf16[64,8192]{1,0:T(8,128)(2,1)} %refs_9_.1) | copy-start | bytes 3145732
  12.8 1.2 %copy-start.4 = (bf16[128,3584]{1,0:T(8,128)(2,1)S(1)}, bf16[128,3584]{1,0:T(8,128)(2,1)}, u32[]{:S(2)}) copy-start(bf16[128,3584]{1,0:T(8,128)(2,1)} %own_ref.3) | copy-start | bytes 2752516
  14.0 1.0 %copy-start.6 = (bf16[3584,64]{0,1:T(8,128)(2,1)S(1)}, bf16[3584,64]{0,1:T(8,128)(2,1)}, u32[]{:S(2)}) copy-start(bf16[3584,64]{0,1:T(8,128)(2,1)} %param.8) | copy-start | bytes 1376260
  26.3 11.8 %copy-start.2 = (bf16[3584,512]{1,0:T(8,128)(2,1)}, bf16[3584,512]{1,0:T(8,128)(2,1)S(1)}, u32[]{:S(2)}) copy-start(bf16[3584,512]{1,0:T(8,128)(2,1)S(1)} %get-tuple-element.81.refs_3_.refs_15_.refs_7_) | copy-start | bytes 11010052
  26.4 7.3 %collective-permute-start.5 = (bf16[272,512]{1,0:T(8,128)(2,1)S(1)}, bf16[272,512]{1,0:T(8,128)(2,1)S(1)}, u32[]{:S(2)}, u32[]{:S(2)}) collective-permute-start(bf16[272,512]{1,0:T(8,128)(2,1)S(1)} %collective-permute-done.1.refs_1_), channel_id=1, source_target_pairs={{0,4},{1,3},{2,6},{3,1},{4,0},{5,7},{6,2},{7,5},{8,12},{9,11},{10,... | collective-permute-start | bytes 835592 | tf_op jit(solution)/shard_map/ppermute | solution.py:329
  28.0 5.6 %collective-permute-start.4 = (f32[24,512]{1,0:T(8,128)S(1)}, f32[24,512]{1,0:T(8,128)S(1)}, u32[]{:S(2)}, u32[]{:S(2)}) collective-permute-start(f32[24,512]{1,0:T(8,128)S(1)} %get-tuple-element.72), channel_id=1, source_target_pairs={{0,2},{1,5},{2,0},{3,7},{4,6},{5,1},{6,4},{7,3},{8,10},{9,13},{10,... | collective-permute-start | bytes 147464 | tf_op jit(solution)/shard_map/ppermute | solution.py:329
  29.5 8.7 %copy-start.1 = (bf16[64,8192]{1,0:T(8,128)(2,1)S(1)}, bf16[64,8192]{1,0:T(8,128)(2,1)}, u32[]{:S(2)}) copy-start(bf16[64,8192]{1,0:T(8,128)(2,1)} %refs_9_.1) | copy-start | bytes 3145732
  33.6 15.2 %collective-permute-start.10 = (bf16[2,256,512]{2,1,0:T(8,128)(2,1)S(1)}, bf16[2,256,512]{2,1,0:T(8,128)(2,1)S(1)}, u32[]{:S(2)}, u32[]{:S(2)}) collective-permute-start(bf16[2,256,512]{2,1,0:T(8,128)(2,1)S(1)} %get-tuple-element.84), channel_id=1, source_target_pairs={{0,2},{1,5},{2,0},{3,7},{4,6},{5,1},{6,4},{7,3},{8,10},{9,13},{10,... | collective-permute-start | bytes 1572872 | tf_op jit(solution)/shard_map/ppermute | solution.py:329
  34.5 6.5 %collective-permute-start.8 = (f32[24,512]{1,0:T(8,128)S(1)}, f32[24,512]{1,0:T(8,128)S(1)}, u32[]{:S(2)}, u32[]{:S(2)}) collective-permute-start(f32[24,512]{1,0:T(8,128)S(1)} %add.62), channel_id=1, source_target_pairs={{0,4},{1,3},{2,6},{3,1},{4,0},{5,7},{6,2},{7,5},{8,12},{9,11},{10,... | collective-permute-start | bytes 147464 | tf_op jit(solution)/shard_map/ppermute | solution.py:329
  36.1 9.7 %collective-permute-start.11 = (bf16[272,512]{1,0:T(8,128)(2,1)S(1)}, bf16[272,512]{1,0:T(8,128)(2,1)S(1)}, u32[]{:S(2)}, u32[]{:S(2)}) collective-permute-start(bf16[272,512]{1,0:T(8,128)(2,1)S(1)} %collective-permute-done.1.refs_1_), channel_id=1, source_target_pairs={{0,2},{1,5},{2,0},{3,7},{4,6},{5,1},{6,4},{7,3},{8,10},{9,13},{10,... | collective-permute-start | bytes 835592 | tf_op jit(solution)/shard_map/ppermute | solution.py:329
  36.6 12.2 %collective-permute-start.12 = (bf16[272,512]{1,0:T(8,128)(2,1)S(1)}, bf16[272,512]{1,0:T(8,128)(2,1)S(1)}, u32[]{:S(2)}, u32[]{:S(2)}) collective-permute-start(bf16[272,512]{1,0:T(8,128)(2,1)S(1)} %collective-permute-done.5.refs_3_), channel_id=1, source_target_pairs={{0,2},{1,5},{2,0},{3,7},{4,6},{5,1},{6,4},{7,3},{8,10},{9,13},{10,... | collective-permute-start | bytes 835592 | tf_op jit(solution)/shard_map/ppermute | solution.py:329
  40.9 5.7 %collective-permute-start.9 = (f32[24,512]{1,0:T(8,128)S(1)}, f32[24,512]{1,0:T(8,128)S(1)}, u32[]{:S(2)}, u32[]{:S(2)}) collective-permute-start(f32[24,512]{1,0:T(8,128)S(1)} %add.63), channel_id=1, source_target_pairs={{0,8},{1,9},{2,10},{3,11},{4,12},{5,13},{6,14},{7,15},{8,0},{9,1},... | collective-permute-start | bytes 147464 | tf_op jit(solution)/shard_map/ppermute | solution.py:329
  41.4 14.4 %collective-permute-start.14 = (bf16[256,512]{1,0:T(8,128)(2,1)S(1)}, bf16[256,512]{1,0:T(8,128)(2,1)S(1)}, u32[]{:S(2)}, u32[]{:S(2)}) collective-permute-start(bf16[256,512]{1,0:T(8,128)(2,1)S(1)} %get-tuple-element.134), channel_id=1, source_target_pairs={{0,2},{1,5},{2,0},{3,7},{4,6},{5,1},{6,4},{7,3},{8,10},{9,13},{10,... | collective-permute-start | bytes 786440 | tf_op jit(solution)/shard_map/ppermute | solution.py:329
  49.0 6.8 %collective-permute-start.13 = (bf16[256,512]{1,0:T(8,128)(2,1)S(1)}, bf16[256,512]{1,0:T(8,128)(2,1)S(1)}, u32[]{:S(2)}, u32[]{:S(2)}) collective-permute-start(bf16[256,512]{1,0:T(8,128)(2,1)S(1)} %get-tuple-element.136), channel_id=1, source_target_pairs={{0,4},{1,3},{2,6},{3,1},{4,0},{5,7},{6,2},{7,5},{8,12},{9,11},{10,... | collective-permute-start | bytes 786440 | tf_op jit(solution)/shard_map/ppermute | solution.py:329
  50.0 5.9 %collective-permute-start.15 = (f32[16,512]{1,0:T(8,128)S(1)}, f32[16,512]{1,0:T(8,128)S(1)}, u32[]{:S(2)}, u32[]{:S(2)}) collective-permute-start(f32[16,512]{1,0:T(8,128)S(1)} %slice.89), channel_id=1, source_target_pairs={{0,1},{1,0},{2,3},{3,2},{4,5},{5,4},{6,7},{7,6},{8,9},{9,8},{10,11... | collective-permute-start | bytes 98312 | tf_op jit(solution)/shard_map/ppermute | solution.py:324
  50.1 2.8 %copy-start.3 = (bf16[3584,512]{1,0:T(8,128)(2,1)S(1)}, bf16[3584,512]{1,0:T(8,128)(2,1)}, u32[]{:S(2)}) copy-start(bf16[3584,512]{1,0:T(8,128)(2,1)} %copy-done.2) | copy-start | bytes 11010052
  50.1 2.8 %copy-start.7 = (bf16[3584,64]{0,1:T(8,128)(2,1)S(1)}, bf16[3584,64]{0,1:T(8,128)(2,1)}, u32[]{:S(2)}) copy-start(bf16[3584,64]{0,1:T(8,128)(2,1)} %param.8) | copy-start | bytes 1376260
  56.3 12.3 %collective-permute-start.20 = (f32[64,512]{1,0:T(8,128)S(1)}, f32[64,512]{1,0:T(8,128)S(1)}, u32[]{:S(2)}, u32[]{:S(2)}) collective-permute-start(f32[64,512]{1,0:T(8,128)S(1)} %fusion.up_ref), channel_id=1, source_target_pairs={{0,1},{1,0},{2,3},{3,2},{4,5},{5,4},{6,7},{7,6},{8,9},{9,8},{10,11... | collective-permute-start | bytes 393224 | tf_op jit(solution)/shard_map/ppermute | solution.py:324
  56.8 11.8 %collective-permute-start.19 = (f32[256,64]{1,0:T(8,128)S(1)}, f32[256,64]{1,0:T(8,128)S(1)}, u32[]{:S(2)}, u32[]{:S(2)}) collective-permute-start(f32[256,64]{1,0:T(8,128)S(1)} %get-tuple-element.106.refs_1_.proj_ref), channel_id=1, source_target_pairs={{0,1},{1,0},{2,3},{3,2},{4,5},{5,4},{6,7},{7,6},{8,9},{9,8},{10,11... | collective-permute-start | bytes 196616 | tf_op jit(solution)/shard_map/ppermute | solution.py:324
  56.9 15.1 %collective-permute-start.18 = (bf16[256,512]{1,0:T(8,128)(2,1)S(1)}, bf16[256,512]{1,0:T(8,128)(2,1)S(1)}, u32[]{:S(2)}, u32[]{:S(2)}) collective-permute-start(bf16[256,512]{1,0:T(8,128)(2,1)S(1)} %get-tuple-element.133), channel_id=1, source_target_pairs={{0,2},{1,5},{2,0},{3,7},{4,6},{5,1},{6,4},{7,3},{8,10},{9,13},{10,... | collective-permute-start | bytes 786440 | tf_op jit(solution)/shard_map/ppermute | solution.py:329
  58.4 13.7 %collective-permute-start.17 = (bf16[256,512]{1,0:T(8,128)(2,1)S(1)}, bf16[256,512]{1,0:T(8,128)(2,1)S(1)}, u32[]{:S(2)}, u32[]{:S(2)}) collective-permute-start(bf16[256,512]{1,0:T(8,128)(2,1)S(1)} %get-tuple-element.135), channel_id=1, source_target_pairs={{0,4},{1,3},{2,6},{3,1},{4,0},{5,7},{6,2},{7,5},{8,12},{9,11},{10,... | collective-permute-start | bytes 786440 | tf_op jit(solution)/shard_map/ppermute | solution.py:329
  58.8 11.2 %copy-start.5 = (bf16[128,3584]{1,0:T(8,128)(2,1)S(1)}, bf16[128,3584]{1,0:T(8,128)(2,1)}, u32[]{:S(2)}) copy-start(bf16[128,3584]{1,0:T(8,128)(2,1)} %own_ref.3) | copy-start | bytes 2752516
  68.6 16.3 %collective-permute-start.24 = (bf16[128,3072]{1,0:T(8,128)(2,1)S(1)}, bf16[128,3072]{1,0:T(8,128)(2,1)S(1)}, u32[]{:S(2)}, u32[]{:S(2)}) collective-permute-start(bf16[128,3072]{1,0:T(8,128)(2,1)S(1)} %get-tuple-element.123), channel_id=1, source_target_pairs={{0,1},{1,0},{2,3},{3,2},{4,5},{5,4},{6,7},{7,6},{8,9},{9,8},{10,11... | collective-permute-start | bytes 2359304 | tf_op jit(solution)/shard_map/ppermute | solution.py:324
  68.8 15.3 %collective-permute-start.16 = (bf16[256,512]{1,0:T(8,128)(2,1)S(1)}, bf16[256,512]{1,0:T(8,128)(2,1)S(1)}, u32[]{:S(2)}, u32[]{:S(2)}) collective-permute-start(bf16[256,512]{1,0:T(8,128)(2,1)S(1)} %fusion.2), channel_id=1, source_target_pairs={{0,8},{1,9},{2,10},{3,11},{4,12},{5,13},{6,14},{7,15},{8,0},{9,1},... | collective-permute-start | bytes 786440 | tf_op jit(solution)/shard_map/ppermute | solution.py:329
  69.8 15.1 %collective-permute-start.23 = (bf16[128,512]{1,0:T(8,128)(2,1)S(1)}, bf16[128,512]{1,0:T(8,128)(2,1)S(1)}, u32[]{:S(2)}, u32[]{:S(2)}) collective-permute-start(bf16[128,512]{1,0:T(8,128)(2,1)S(1)} %get-tuple-element.121), channel_id=1, source_target_pairs={{0,1},{1,0},{2,3},{3,2},{4,5},{5,4},{6,7},{7,6},{8,9},{9,8},{10,11... | collective-permute-start | bytes 393224 | tf_op jit(solution)/shard_map/ppermute | solution.py:324
  84.3 2.2 %collective-permute-start.21 = (bf16[128,512]{1,0:T(8,128)(2,1)S(1)}, bf16[128,512]{1,0:T(8,128)(2,1)S(1)}, u32[]{:S(2)}, u32[]{:S(2)}) collective-permute-start(bf16[128,512]{1,0:T(8,128)(2,1)S(1)} %slice.95), channel_id=1, source_target_pairs={{0,1},{1,0},{2,3},{3,2},{4,5},{5,4},{6,7},{7,6},{8,9},{9,8},{10,11... | collective-permute-start | bytes 393224 | tf_op jit(solution)/shard_map/ppermute | solution.py:324
  84.4 2.1 %collective-permute-start.22 = (f32[1,512]{1,0:T(1,128)S(1)}, f32[1,512]{1,0:T(1,128)S(1)}, u32[]{:S(2)}, u32[]{:S(2)}) collective-permute-start(f32[1,512]{1,0:T(1,128)S(1)} %slice_divide_fusion.g_ref), channel_id=1, source_target_pairs={{0,1},{1,0},{2,3},{3,2},{4,5},{5,4},{6,7},{7,6},{8,9},{9,8},{10,11... | collective-permute-start | bytes 6152 | tf_op jit(solution)/shard_map/ppermute | solution.py:324

commit v16 on v15

--- a/solution.py
+++ b/solution.py
@@ -386,11 +386,10 @@
 
     band = 256
     bands = rows // band
-    many = max(bands * 2 // 14, 1)
+    many = max(bands * 3 // 14, 1)
     run = functools.partial(backward, order, band=band, at=at, held=held)
     grad_a, other_a, scaled, proj, scales, scaled_own = run(0, many, first=([cots[v] for v in range(n)], stats, up))
-    from_sibling = swap(proj)
-    high, from0_high, lowrank_other, scaled_own = tie((high, from0_high, lowrank_other, scaled_own))
+    high, from0_high, lowrank_other, scaled_own, scaled = tie((high, from0_high, lowrank_other, scaled_own, scaled))
     last = send((near0[1].astype(f32) + from0_high.astype(f32) + high.astype(f32)).astype(bf16), 2)
     scaled_own = scaled_own.astype(f32)
 
@@ -402,9 +401,9 @@
         jnp.dot(turned(lowrank_rows), scaled_own[:tokens], precision=lax.Precision.HIGHEST)
         + jnp.dot(turned(lowrank_other), scaled_own[tokens:], precision=lax.Precision.HIGHEST)
     )
-    up_other = swap(up_half)
     grad_b, other_b = backward(order, many, bands - many, band, at, held, later=(scaled, proj))
-    other_a, from_sibling, up_other, other_b = tie((other_a, from_sibling, up_other, other_b))
+    other_a, proj, up_half, other_b = tie((other_a, proj, up_half, other_b))
+    from_sibling, up_other = swap(proj), swap(up_half)
     got_a, got_b = swap(other_a), swap(other_b)
 
     down_weight_gradient, up_weight_gradient = finish_weights(

time: 88.1 us -> 79.1 us (0.90)
  waiting for transfers between devices: 16.5 us -> 7.54 us
    ppermute x15, waiting for transfers between devices: 16.1 us -> 4.14 us  [send(): return lax.ppermute(x, ('tensor', 'dp'), pairs)]
    ppermute x9, waiting for transfers between devices: 0.33 us -> 3.4 us  [split_columns(): swap = lambda x: lax.ppermute(x, 'dp', [(0, 1), (1, 0)])]
  transfers between devices with their start and end apart: 25 -> 25, of which waited for: 5 -> 6; matrix products, arithmetic and copies ran while one was open for 2% -> 2% of each run, Pallas kernels for 46% -> 51%
where the time goes in v16:
time: 79.1 us; the launch traced here: 78.8 us
  Pallas kernels  41.8 us (53%)
  starting transfers between devices  22.1 us (28%)
  waiting for transfers between devices  7.54 us (10%)
  local copies, waits for them, and re-layouts  4.68 us (6%)
  other arithmetic  1.26 us (2%)
  between operations  0.96 us (1%)
    ppermute x15, starting transfers between devices, send(): return lax.ppermute(x, ('tensor', 'dp'), pairs)  19.5 us
    pallas_call x2, Pallas kernels, backward(): pl.pallas_call(functools.partial(backward_kernel, tokens, n, start, band,...  12.7 us
    pallas_call x4, Pallas kernels, forward(): pl.pallas_call(functools.partial(forward_kernel, tokens, rank, vs, later...  12.4 us
    pallas_call x1, Pallas kernels, load(): pl.pallas_call(functools.partial(load_kernel, tokens, rank, n, vs, first)...  11.3 us
    pallas_call x3, Pallas kernels, finish(): pl.pallas_call(kernel, grid_spec=pltpu.PrefetchScalarGridSpec(num_scalar_...  4.88 us
    unnamed x18, local copies, waits for them, and re-layouts  4.39 us
    ppermute x15, waiting for transfers between devices, send(): return lax.ppermute(x, ('tensor', 'dp'), pairs)  4.14 us
    ppermute x9, waiting for transfers between devices, split_columns(): swap = lambda x: lax.ppermute(x, 'dp', [(0, 1), (1, 0)])  3.4 us
  transfers between devices with their start and end apart: 25, of which 6 were waited for; matrix products, arithmetic and copies ran while one was open for 2% of the time, Pallas kernels for 51%

profile of v16, /device:TPU:0, one launch (start us, length us, event | category | flops | bytes accessed | tf_op | source)
XLA Modules:
  0.0 78.8 jit_solution(3975047734812681730)
XLA Ops:
  0.6 0.5 collective-permute-start
  1.1 0.1 collective-permute-start.7
  1.2 0.7 reduce-precision_convert_fusion.1
  2.0 0.1 pad.11.clone
  2.0 0.1 stack.79.order_ref
  2.1 0.1 maximum_maximum_fusion.magnitude_ref
  2.2 0.3 collective-permute-done.other_ref
  2.5 0.9 %copy-done.8 = bf16[128,1024]{1,0:T(8,128)(2,1)S(1)} copy-done((bf16[128,1024]{1,0:T(8,128)(2,1)S(1)}, bf16[128,1024]{1,0:T(8,128)(2,1)}, u32[]{:S(2)}) %copy-start.8) | copy-done | bytes 262168
  3.5 0.6 own_block.1.refs_0_
  4.0 4.0 %collective-permute-start.1 = (bf16[272,512]{1,0:T(8,128)(2,1)S(1)}, bf16[272,512]{1,0:T(8,128)(2,1)S(1)}, u32[]{:S(2)}, u32[]{:S(2)}) collective-permute-start(bf16[272,512]{1,0:T(8,128)(2,1)S(1)} %own_block.1.refs_0_), channel_id=1, source_target_pairs={{0,8},{1,9},{2,10},{3,11},{4,12},{5,13},{6,14},{7,15},{8,0},{9,1},... | collective-permute-start | bytes 835592 | tf_op jit(solution)/shard_map/ppermute | solution.py:329
  8.1 1.6 %collective-permute-start.2 = (bf16[272,512]{1,0:T(8,128)(2,1)S(1)}, bf16[272,512]{1,0:T(8,128)(2,1)S(1)}, u32[]{:S(2)}, u32[]{:S(2)}) collective-permute-start(bf16[272,512]{1,0:T(8,128)(2,1)S(1)} %own_block.1.refs_0_), channel_id=1, source_target_pairs={{0,4},{1,3},{2,6},{3,1},{4,0},{5,7},{6,2},{7,5},{8,12},{9,11},{10,... | collective-permute-start | bytes 835592 | tf_op jit(solution)/shard_map/ppermute | solution.py:329
  9.6 1.5 %collective-permute-start.3 = (bf16[272,512]{1,0:T(8,128)(2,1)S(1)}, bf16[272,512]{1,0:T(8,128)(2,1)S(1)}, u32[]{:S(2)}, u32[]{:S(2)}) collective-permute-start(bf16[272,512]{1,0:T(8,128)(2,1)S(1)} %own_block.1.refs_0_), channel_id=1, source_target_pairs={{0,2},{1,5},{2,0},{3,7},{4,6},{5,1},{6,4},{7,3},{8,10},{9,13},{10,... | collective-permute-start | bytes 835592 | tf_op jit(solution)/shard_map/ppermute | solution.py:329
  11.1 0.4 collective-permute-start.6
  11.6 1.2 %copy-done = bf16[64,8192]{1,0:T(8,128)(2,1)S(1)} copy-done((bf16[64,8192]{1,0:T(8,128)(2,1)S(1)}, bf16[64,8192]{1,0:T(8,128)(2,1)}, u32[]{:S(2)}) %copy-start) | copy-done | bytes 1048600
  12.8 1.2 %copy-done.4 = bf16[128,3584]{1,0:T(8,128)(2,1)S(1)} copy-done((bf16[128,3584]{1,0:T(8,128)(2,1)S(1)}, bf16[128,3584]{1,0:T(8,128)(2,1)}, u32[]{:S(2)}) %copy-start.4) | copy-done | bytes 917528
  14.0 1.0 %copy-done.6 = bf16[3584,64]{0,1:T(8,128)(2,1)S(1)} copy-done((bf16[3584,64]{0,1:T(8,128)(2,1)S(1)}, bf16[3584,64]{0,1:T(8,128)(2,1)}, u32[]{:S(2)}) %copy-start.6) | copy-done | bytes 458776
  15.0 11.3 %load.1 = (bf16[3584,512]{1,0:T(8,128)(2,1)S(1)}, bf16[3584,512]{1,0:T(8,128)(2,1)S(1)}, bf16[3584,512]{1,0:T(8,128)(2,1)S(1)}, bf16[3584,512]{1,0:T(8,128)(2,1)...) custom-call(s32[16]{0:T(128)S(1)} %stack.79.order_ref, ...), custom_call_target="tpu_custom_call" | custom-call | tf_op jit(solution)/shard_map/load/pallas_call | solution.py:116
  26.3 0.0 collective-permute-done.1.refs_1_
  26.3 0.0 collective-permute-done.2.refs_2_
  26.4 1.6 %collective-permute-start.5 = (bf16[272,512]{1,0:T(8,128)(2,1)S(1)}, bf16[272,512]{1,0:T(8,128)(2,1)S(1)}, u32[]{:S(2)}, u32[]{:S(2)}) collective-permute-start(bf16[272,512]{1,0:T(8,128)(2,1)S(1)} %collective-permute-done.1.refs_1_), channel_id=1, source_target_pairs={{0,4},{1,3},{2,6},{3,1},{4,0},{5,7},{6,2},{7,5},{8,12},{9,11},{10,... | collective-permute-start | bytes 835592 | tf_op jit(solution)/shard_map/ppermute | solution.py:329
  28.0 1.5 %collective-permute-start.4 = (f32[24,512]{1,0:T(8,128)S(1)}, f32[24,512]{1,0:T(8,128)S(1)}, u32[]{:S(2)}, u32[]{:S(2)}) collective-permute-start(f32[24,512]{1,0:T(8,128)S(1)} %get-tuple-element.73), channel_id=1, source_target_pairs={{0,2},{1,5},{2,0},{3,7},{4,6},{5,1},{6,4},{7,3},{8,10},{9,13},{10,... | collective-permute-start | bytes 147464 | tf_op jit(solution)/shard_map/ppermute | solution.py:329
  29.5 4.1 %forward.4 = (bf16[2,256,512]{2,1,0:T(8,128)(2,1)S(1)}, bf16[256,3584]{1,0:T(8,128)(2,1)S(1)}, bf16[256,128]{1,0:T(8,128)(2,1)S(1)}) custom-call(s32[16]{0:T(128)S(1)} %stack.79.order_ref, bf16[128,3584]{1,0:T(8,128)(2,1)S(1)} %copy-done.4, bf16[128,3584]{1,0:T(8,128)(2,1)S(1)} %collective-permute-done.7.refs_1_.other_ref, bf16[64,3584]{1,0:T(8,128)(2,1)S(1)} %bitcast.40, ...), custom_call_target="tpu_custom_call" | custom-call | tf_op jit(solution)/shard_map/forward/pallas_call | solution.py:158
  33.6 0.0 collective-permute-done.6.refs_6_
  33.7 0.8 collective-permute-start.10
  34.5 1.6 %collective-permute-start.8 = (f32[24,512]{1,0:T(8,128)S(1)}, f32[24,512]{1,0:T(8,128)S(1)}, u32[]{:S(2)}, u32[]{:S(2)}) collective-permute-start(f32[24,512]{1,0:T(8,128)S(1)} %add.62), channel_id=1, source_target_pairs={{0,4},{1,3},{2,6},{3,1},{4,0},{5,7},{6,2},{7,5},{8,12},{9,11},{10,... | collective-permute-start | bytes 147464 | tf_op jit(solution)/shard_map/ppermute | solution.py:329
  36.1 0.5 collective-permute-start.11
  36.6 1.5 %collective-permute-start.12 = (bf16[272,512]{1,0:T(8,128)(2,1)S(1)}, bf16[272,512]{1,0:T(8,128)(2,1)S(1)}, u32[]{:S(2)}, u32[]{:S(2)}) collective-permute-start(bf16[272,512]{1,0:T(8,128)(2,1)S(1)} %collective-permute-done.5.refs_3_), channel_id=1, source_target_pairs={{0,2},{1,5},{2,0},{3,7},{4,6},{5,1},{6,4},{7,3},{8,10},{9,13},{10,... | collective-permute-start | bytes 835592 | tf_op jit(solution)/shard_map/ppermute | solution.py:329
  38.1 2.7 %forward.5 = bf16[2,256,512]{2,1,0:T(8,128)(2,1)S(1)} custom-call(s32[16]{0:T(128)S(1)} %stack.79.order_ref, bf16[256,3584]{1,0:T(8,128)(2,1)S(1)} %get-tuple-element.80.refs_0_, bf16[256,128]{1,0:T(8,128)(2,1)S(1)} %get-tuple-element.81.refs_1_, bf16[64,8192]{1,0:T(8,128)(2,1)S(1)} %copy-done.1, ...), custom_call_target="tpu_custom_call" | custom-call | tf_op jit(solution)/shard_map/forward/pallas_call | solution.py:158
  40.9 0.4 collective-permute-start.9
  41.4 0.7 collective-permute-start.14
  42.0 2.8 %forward.6 = bf16[2,256,512]{2,1,0:T(8,128)(2,1)S(1)} custom-call(s32[16]{0:T(128)S(1)} %stack.79.order_ref, bf16[256,3584]{1,0:T(8,128)(2,1)S(1)} %get-tuple-element.80.refs_0_, bf16[256,128]{1,0:T(8,128)(2,1)S(1)} %get-tuple-element.81.refs_1_, bf16[64,8192]{1,0:T(8,128)(2,1)S(1)} %copy-done.1, ...), custom_call_target="tpu_custom_call" | custom-call | tf_op jit(solution)/shard_map/forward/pallas_call | solution.py:158
  44.8 1.1 %collective-permute-done.11.refs_5_ = bf16[272,512]{1,0:T(8,128)(2,1)S(1)} collective-permute-done((bf16[272,512]{1,0:T(8,128)(2,1)S(1)}, bf16[272,512]{1,0:T(8,128)(2,1)S(1)}, u32[]{:S(2)}, u32[]{:S(2)}) %collective-permute-start.11) | collective-permute-done | bytes 278560 | tf_op jit(solution)/shard_map/ppermute | solution.py:329
  45.9 0.7 collective-permute-done.9
  46.6 2.3 %collective-permute-done.12.refs_7_ = bf16[272,512]{1,0:T(8,128)(2,1)S(1)} collective-permute-done((bf16[272,512]{1,0:T(8,128)(2,1)S(1)}, bf16[272,512]{1,0:T(8,128)(2,1)S(1)}, u32[]{:S(2)}, u32[]{:S(2)}) %collective-permute-start.12) | collective-permute-done | bytes 278560 | tf_op jit(solution)/shard_map/ppermute | solution.py:329
  48.9 0.1 add_convert_fusion
  49.1 0.9 %collective-permute-start.13 = (bf16[256,512]{1,0:T(8,128)(2,1)S(1)}, bf16[256,512]{1,0:T(8,128)(2,1)S(1)}, u32[]{:S(2)}, u32[]{:S(2)}) collective-permute-start(bf16[256,512]{1,0:T(8,128)(2,1)S(1)} %get-tuple-element.138), channel_id=1, source_target_pairs={{0,4},{1,3},{2,6},{3,1},{4,0},{5,7},{6,2},{7,5},{8,12},{9,11},{10,... | collective-permute-start | bytes 786440 | tf_op jit(solution)/shard_map/ppermute | solution.py:329
  50.0 1.5 %collective-permute-start.18 = (bf16[256,512]{1,0:T(8,128)(2,1)S(1)}, bf16[256,512]{1,0:T(8,128)(2,1)S(1)}, u32[]{:S(2)}, u32[]{:S(2)}) collective-permute-start(bf16[256,512]{1,0:T(8,128)(2,1)S(1)} %get-tuple-element.135), channel_id=1, source_target_pairs={{0,2},{1,5},{2,0},{3,7},{4,6},{5,1},{6,4},{7,3},{8,10},{9,13},{10,... | collective-permute-start | bytes 786440 | tf_op jit(solution)/shard_map/ppermute | solution.py:329
  51.5 0.1 collective-permute-start.15
  51.6 0.0 copy-start.7
  51.6 2.7 %forward.7 = bf16[2,256,512]{2,1,0:T(8,128)(2,1)S(1)} custom-call(s32[16]{0:T(128)S(1)} %stack.79.order_ref, bf16[256,3584]{1,0:T(8,128)(2,1)S(1)} %get-tuple-element.80.refs_0_, bf16[256,128]{1,0:T(8,128)(2,1)S(1)} %get-tuple-element.81.refs_1_, bf16[64,8192]{1,0:T(8,128)(2,1)S(1)} %copy-done.1, bf16[3584,512]{1,0:T(8,128)(2,1)S(1)} %get-tuple-element.91.refs_3_.refs_11_, ...), custom_call_target="tpu_custom_call" | custom-call | tf_op jit(solution)/shard_map/forward/pallas_call | solution.py:158
  54.3 0.5 collective-permute-start.17
  54.9 3.7 %backward.2 = (f32[128,768]{1,0:T(8,128)S(1)}, bf16[128,768]{1,0:T(8,128)(2,1)S(1)}, bf16[256,4096]{1,0:T(8,128)(2,1)S(1)}, f32[256,64]{1,0:T(8,128)S(1)}, f32[2...) custom-call(s32[16]{0:T(128)S(1)} %stack.79.order_ref, bf16[272,512]{1,0:T(8,128)(2,1)S(1)} %own_block.1.refs_0_, ...), custom_call_target="tpu_custom_call" | custom-call | tf_op jit(solution)/shard_map/backward/pallas_call | solution.py:223
  58.6 0.0 collective-permute-done.15
  58.6 0.0 collective-permute-done.13
  58.6 0.1 fusion.2
  58.7 0.9 %collective-permute-start.16 = (bf16[256,512]{1,0:T(8,128)(2,1)S(1)}, bf16[256,512]{1,0:T(8,128)(2,1)S(1)}, u32[]{:S(2)}, u32[]{:S(2)}) collective-permute-start(bf16[256,512]{1,0:T(8,128)(2,1)S(1)} %fusion.2), channel_id=1, source_target_pairs={{0,8},{1,9},{2,10},{3,11},{4,12},{5,13},{6,14},{7,15},{8,0},{9,1},... | collective-permute-start | bytes 786440 | tf_op jit(solution)/shard_map/ppermute | solution.py:329
  59.7 0.2 fusion.5
  59.9 0.2 fusion.up_ref
  60.1 0.0 copy-start.5
  60.1 9.0 %backward.3 = (f32[128,2816]{1,0:T(8,128)S(1)}, bf16[128,2816]{1,0:T(8,128)(2,1)S(1)}) custom-call(s32[16]{0:T(128)S(1)} %stack.79.order_ref, bf16[256,4096]{1,0:T(8,128)(2,1)S(1)} %get-tuple-element.112.refs_0_, f32[256,64]{1,0:T(8,128)S(1)} %get-tuple-element.114.refs_1_.proj_ref, bf16[64,3584]{1,0:T(8,128)(2,1)S(1)} %bitcast.42, ...), custom_call_target="tpu_custom_call" | custom-call | tf_op jit(solution)/shard_map/backward/pallas_call | solution.py:223
  69.1 0.1 collective-permute-start.24
  69.1 0.5 collective-permute-start.19
  69.6 1.9 %collective-permute-done.19.from_ref = f32[256,64]{1,0:T(8,128)S(1)} collective-permute-done((f32[256,64]{1,0:T(8,128)S(1)}, f32[256,64]{1,0:T(8,128)S(1)}, u32[]{:S(2)}, u32[]{:S(2)}) %collective-permute-start.19) | collective-permute-done | bytes 65568 | tf_op jit(solution)/shard_map/ppermute | solution.py:324
  71.5 0.1 collective-permute-start.20
  71.7 1.2 %collective-permute-done.20.up_other_ref = f32[64,512]{1,0:T(8,128)S(1)} collective-permute-done((f32[64,512]{1,0:T(8,128)S(1)}, f32[64,512]{1,0:T(8,128)S(1)}, u32[]{:S(2)}, u32[]{:S(2)}) %collective-permute-start.20) | collective-permute-done | bytes 131104 | tf_op jit(solution)/shard_map/ppermute | solution.py:324
  72.9 0.1 collective-permute-start.23
  73.0 2.0 %weights.1 = (f32[64,3584]{1,0:T(8,128)}, f32[64,1024]{1,0:T(8,128)}) custom-call(s32[16]{0:T(128)S(1)} %stack.79.order_ref, f32[256,64]{1,0:T(8,128)S(1)} %get-tuple-element.114.refs_1_.proj_ref, f32[256,64]{1,0:T(8,128)S(1)} %collective-permute-done.19.from_ref, bf16[128,3584]{1,0:T(8,128)(2,1)S(1)} %copy-done.5, ...), custom_call_target="tpu_custom_call" | custom-call | tf_op jit(solution)/shard_map/weights/pallas_call | solution.py:280
  75.0 0.0 collective-permute-done.17
  75.0 0.0 collective-permute-done.16
  75.0 0.2 multiply_reduce_fusion
  75.2 0.4 collective-permute-start.21
  75.7 0.2 collective-permute-start.22
  75.9 1.6 %hidden.1 = bf16[128,3584]{1,0:T(8,128)(2,1)} custom-call(s32[16]{0:T(128)S(1)} %stack.79.order_ref, f32[128,768]{1,0:T(8,128)S(1)} %get-tuple-element.122.ga_ref, bf16[128,768]{1,0:T(8,128)(2,1)S(1)} %collective-permute-done.23.ra_ref, f32[128,2816]{1,0:T(8,128)S(1)} %get-tuple-element.124.gb_ref, bf16[128,2816]{1,0:T(8,128)(2,1)S(1)} %collective-permute-done.24.rb_ref), custom_call_target="tpu_custom_call" | custom-call | tf_op jit(solution)/shard_map/hidden/pallas_call | solution.py:280
  77.5 1.3 %mixed.1 = (bf16[128,1024]{1,0:T(8,128)(2,1)}, f32[8,128]{1,0:T(8,128)}) custom-call(s32[16]{0:T(128)S(1)} %stack.79.order_ref, bf16[256,512]{1,0:T(8,128)(2,1)S(1)} %get-tuple-element.134.m_ref, bf16[128,512]{1,0:T(8,128)(2,1)S(1)} %collective-permute-done.21.m_other_ref, f32[1,512]{1,0:T(1,128)S(1)} %slice_divide_fusion.g_ref, ...), custom_call_target="tpu_custom_call" | custom-call | tf_op jit(solution)/shard_map/mixed/pallas_call | solution.py:280
  (39 shorter events, 0.2 us)
Async XLA Ops:
  0.6 1.9 %collective-permute-start = (bf16[128,1024]{1,0:T(8,128)(2,1)}, bf16[128,1024]{1,0:T(8,128)(2,1)S(1)}, u32[]{:S(2)}, u32[]{:S(2)}) collective-permute-start(bf16[128,1024]{1,0:T(8,128)(2,1)} %own_ref.2), channel_id=1, source_target_pairs={{0,1},{1,0},{2,3},{3,2},{4,5},{5,4},{6,7},{7,6},{8,9},{9,8},{10,11... | collective-permute-start | bytes 786440 | tf_op jit(solution)/shard_map/ppermute | solution.py:324
  1.1 28.3 %collective-permute-start.7 = (bf16[128,3584]{1,0:T(8,128)(2,1)}, bf16[128,3584]{1,0:T(8,128)(2,1)S(1)}, u32[]{:S(2)}, u32[]{:S(2)}) collective-permute-start(bf16[128,3584]{1,0:T(8,128)(2,1)} %own_ref.3), channel_id=1, source_target_pairs={{0,1},{1,0},{2,3},{3,2},{4,5},{5,4},{6,7},{7,6},{8,9},{9,8},{10,11... | collective-permute-start | bytes 2752520 | tf_op jit(solution)/shard_map/ppermute | solution.py:324
  2.5 0.9 %copy-start.8 = (bf16[128,1024]{1,0:T(8,128)(2,1)S(1)}, bf16[128,1024]{1,0:T(8,128)(2,1)}, u32[]{:S(2)}) copy-start(bf16[128,1024]{1,0:T(8,128)(2,1)} %own_ref.2) | copy-start | bytes 786436
  4.0 22.3 %collective-permute-start.1 = (bf16[272,512]{1,0:T(8,128)(2,1)S(1)}, bf16[272,512]{1,0:T(8,128)(2,1)S(1)}, u32[]{:S(2)}, u32[]{:S(2)}) collective-permute-start(bf16[272,512]{1,0:T(8,128)(2,1)S(1)} %own_block.1.refs_0_), channel_id=1, source_target_pairs={{0,8},{1,9},{2,10},{3,11},{4,12},{5,13},{6,14},{7,15},{8,0},{9,1},... | collective-permute-start | bytes 835592 | tf_op jit(solution)/shard_map/ppermute | solution.py:329
  8.1 18.3 %collective-permute-start.2 = (bf16[272,512]{1,0:T(8,128)(2,1)S(1)}, bf16[272,512]{1,0:T(8,128)(2,1)S(1)}, u32[]{:S(2)}, u32[]{:S(2)}) collective-permute-start(bf16[272,512]{1,0:T(8,128)(2,1)S(1)} %own_block.1.refs_0_), channel_id=1, source_target_pairs={{0,4},{1,3},{2,6},{3,1},{4,0},{5,7},{6,2},{7,5},{8,12},{9,11},{10,... | collective-permute-start | bytes 835592 | tf_op jit(solution)/shard_map/ppermute | solution.py:329
  9.6 16.7 %collective-permute-start.3 = (bf16[272,512]{1,0:T(8,128)(2,1)S(1)}, bf16[272,512]{1,0:T(8,128)(2,1)S(1)}, u32[]{:S(2)}, u32[]{:S(2)}) collective-permute-start(bf16[272,512]{1,0:T(8,128)(2,1)S(1)} %own_block.1.refs_0_), channel_id=1, source_target_pairs={{0,2},{1,5},{2,0},{3,7},{4,6},{5,1},{6,4},{7,3},{8,10},{9,13},{10,... | collective-permute-start | bytes 835592 | tf_op jit(solution)/shard_map/ppermute | solution.py:329
  11.1 22.5 %collective-permute-start.6 = (bf16[272,512]{1,0:T(8,128)(2,1)S(1)}, bf16[272,512]{1,0:T(8,128)(2,1)S(1)}, u32[]{:S(2)}, u32[]{:S(2)}) collective-permute-start(bf16[272,512]{1,0:T(8,128)(2,1)S(1)} %own_block.1.refs_0_), channel_id=1, source_target_pairs={{0,6},{1,7},{2,4},{3,5},{4,2},{5,3},{6,0},{7,1},{8,14},{9,15},{10,... | collective-permute-start | bytes 835592 | tf_op jit(solution)/shard_map/ppermute | solution.py:356
  11.6 1.2 %copy-start = (bf16[64,8192]{1,0:T(8,128)(2,1)S(1)}, bf16[64,8192]{1,0:T(8,128)(2,1)}, u32[]{:S(2)}) copy-start(bf16[64,8192]{1,0:T(8,128)(2,1)} %refs_9_.1) | copy-start | bytes 3145732
  12.8 1.2 %copy-start.4 = (bf16[128,3584]{1,0:T(8,128)(2,1)S(1)}, bf16[128,3584]{1,0:T(8,128)(2,1)}, u32[]{:S(2)}) copy-start(bf16[128,3584]{1,0:T(8,128)(2,1)} %own_ref.3) | copy-start | bytes 2752516
  14.0 1.0 %copy-start.6 = (bf16[3584,64]{0,1:T(8,128)(2,1)S(1)}, bf16[3584,64]{0,1:T(8,128)(2,1)}, u32[]{:S(2)}) copy-start(bf16[3584,64]{0,1:T(8,128)(2,1)} %param.8) | copy-start | bytes 1376260
  26.3 11.8 %copy-start.2 = (bf16[3584,512]{1,0:T(8,128)(2,1)}, bf16[3584,512]{1,0:T(8,128)(2,1)S(1)}, u32[]{:S(2)}) copy-start(bf16[3584,512]{1,0:T(8,128)(2,1)S(1)} %get-tuple-element.82.refs_3_.refs_15_.refs_7_) | copy-start | bytes 11010052
  26.4 7.3 %collective-permute-start.5 = (bf16[272,512]{1,0:T(8,128)(2,1)S(1)}, bf16[272,512]{1,0:T(8,128)(2,1)S(1)}, u32[]{:S(2)}, u32[]{:S(2)}) collective-permute-start(bf16[272,512]{1,0:T(8,128)(2,1)S(1)} %collective-permute-done.1.refs_1_), channel_id=1, source_target_pairs={{0,4},{1,3},{2,6},{3,1},{4,0},{5,7},{6,2},{7,5},{8,12},{9,11},{10,... | collective-permute-start | bytes 835592 | tf_op jit(solution)/shard_map/ppermute | solution.py:329
  28.0 5.7 %collective-permute-start.4 = (f32[24,512]{1,0:T(8,128)S(1)}, f32[24,512]{1,0:T(8,128)S(1)}, u32[]{:S(2)}, u32[]{:S(2)}) collective-permute-start(f32[24,512]{1,0:T(8,128)S(1)} %get-tuple-element.73), channel_id=1, source_target_pairs={{0,2},{1,5},{2,0},{3,7},{4,6},{5,1},{6,4},{7,3},{8,10},{9,13},{10,... | collective-permute-start | bytes 147464 | tf_op jit(solution)/shard_map/ppermute | solution.py:329
  29.5 8.7 %copy-start.1 = (bf16[64,8192]{1,0:T(8,128)(2,1)S(1)}, bf16[64,8192]{1,0:T(8,128)(2,1)}, u32[]{:S(2)}) copy-start(bf16[64,8192]{1,0:T(8,128)(2,1)} %refs_9_.1) | copy-start | bytes 3145732
  33.7 15.2 %collective-permute-start.10 = (bf16[2,256,512]{2,1,0:T(8,128)(2,1)S(1)}, bf16[2,256,512]{2,1,0:T(8,128)(2,1)S(1)}, u32[]{:S(2)}, u32[]{:S(2)}) collective-permute-start(bf16[2,256,512]{2,1,0:T(8,128)(2,1)S(1)} %get-tuple-element.85), channel_id=1, source_target_pairs={{0,2},{1,5},{2,0},{3,7},{4,6},{5,1},{6,4},{7,3},{8,10},{9,13},{10,... | collective-permute-start | bytes 1572872 | tf_op jit(solution)/shard_map/ppermute | solution.py:329
  34.5 6.4 %collective-permute-start.8 = (f32[24,512]{1,0:T(8,128)S(1)}, f32[24,512]{1,0:T(8,128)S(1)}, u32[]{:S(2)}, u32[]{:S(2)}) collective-permute-start(f32[24,512]{1,0:T(8,128)S(1)} %add.62), channel_id=1, source_target_pairs={{0,4},{1,3},{2,6},{3,1},{4,0},{5,7},{6,2},{7,5},{8,12},{9,11},{10,... | collective-permute-start | bytes 147464 | tf_op jit(solution)/shard_map/ppermute | solution.py:329
  36.1 9.8 %collective-permute-start.11 = (bf16[272,512]{1,0:T(8,128)(2,1)S(1)}, bf16[272,512]{1,0:T(8,128)(2,1)S(1)}, u32[]{:S(2)}, u32[]{:S(2)}) collective-permute-start(bf16[272,512]{1,0:T(8,128)(2,1)S(1)} %collective-permute-done.1.refs_1_), channel_id=1, source_target_pairs={{0,2},{1,5},{2,0},{3,7},{4,6},{5,1},{6,4},{7,3},{8,10},{9,13},{10,... | collective-permute-start | bytes 835592 | tf_op jit(solution)/shard_map/ppermute | solution.py:329
  36.6 12.2 %collective-permute-start.12 = (bf16[272,512]{1,0:T(8,128)(2,1)S(1)}, bf16[272,512]{1,0:T(8,128)(2,1)S(1)}, u32[]{:S(2)}, u32[]{:S(2)}) collective-permute-start(bf16[272,512]{1,0:T(8,128)(2,1)S(1)} %collective-permute-done.5.refs_3_), channel_id=1, source_target_pairs={{0,2},{1,5},{2,0},{3,7},{4,6},{5,1},{6,4},{7,3},{8,10},{9,13},{10,... | collective-permute-start | bytes 835592 | tf_op jit(solution)/shard_map/ppermute | solution.py:329
  40.9 5.7 %collective-permute-start.9 = (f32[24,512]{1,0:T(8,128)S(1)}, f32[24,512]{1,0:T(8,128)S(1)}, u32[]{:S(2)}, u32[]{:S(2)}) collective-permute-start(f32[24,512]{1,0:T(8,128)S(1)} %add.63), channel_id=1, source_target_pairs={{0,8},{1,9},{2,10},{3,11},{4,12},{5,13},{6,14},{7,15},{8,0},{9,1},... | collective-permute-start | bytes 147464 | tf_op jit(solution)/shard_map/ppermute | solution.py:329
  41.4 17.2 %collective-permute-start.14 = (bf16[256,512]{1,0:T(8,128)(2,1)S(1)}, bf16[256,512]{1,0:T(8,128)(2,1)S(1)}, u32[]{:S(2)}, u32[]{:S(2)}) collective-permute-start(bf16[256,512]{1,0:T(8,128)(2,1)S(1)} %get-tuple-element.136), channel_id=1, source_target_pairs={{0,2},{1,5},{2,0},{3,7},{4,6},{5,1},{6,4},{7,3},{8,10},{9,13},{10,... | collective-permute-start | bytes 786440 | tf_op jit(solution)/shard_map/ppermute | solution.py:329
  49.1 9.5 %collective-permute-start.13 = (bf16[256,512]{1,0:T(8,128)(2,1)S(1)}, bf16[256,512]{1,0:T(8,128)(2,1)S(1)}, u32[]{:S(2)}, u32[]{:S(2)}) collective-permute-start(bf16[256,512]{1,0:T(8,128)(2,1)S(1)} %get-tuple-element.138), channel_id=1, source_target_pairs={{0,4},{1,3},{2,6},{3,1},{4,0},{5,7},{6,2},{7,5},{8,12},{9,11},{10,... | collective-permute-start | bytes 786440 | tf_op jit(solution)/shard_map/ppermute | solution.py:329
  50.0 25.0 %collective-permute-start.18 = (bf16[256,512]{1,0:T(8,128)(2,1)S(1)}, bf16[256,512]{1,0:T(8,128)(2,1)S(1)}, u32[]{:S(2)}, u32[]{:S(2)}) collective-permute-start(bf16[256,512]{1,0:T(8,128)(2,1)S(1)} %get-tuple-element.135), channel_id=1, source_target_pairs={{0,2},{1,5},{2,0},{3,7},{4,6},{5,1},{6,4},{7,3},{8,10},{9,13},{10,... | collective-permute-start | bytes 786440 | tf_op jit(solution)/shard_map/ppermute | solution.py:329
  51.5 7.1 %collective-permute-start.15 = (f32[16,512]{1,0:T(8,128)S(1)}, f32[16,512]{1,0:T(8,128)S(1)}, u32[]{:S(2)}, u32[]{:S(2)}) collective-permute-start(f32[16,512]{1,0:T(8,128)S(1)} %slice.89), channel_id=1, source_target_pairs={{0,1},{1,0},{2,3},{3,2},{4,5},{5,4},{6,7},{7,6},{8,9},{9,8},{10,11... | collective-permute-start | bytes 98312 | tf_op jit(solution)/shard_map/ppermute | solution.py:324
  51.6 3.3 %copy-start.3 = (bf16[3584,512]{1,0:T(8,128)(2,1)S(1)}, bf16[3584,512]{1,0:T(8,128)(2,1)}, u32[]{:S(2)}) copy-start(bf16[3584,512]{1,0:T(8,128)(2,1)} %copy-done.2) | copy-start | bytes 11010052
  51.6 3.3 %copy-start.7 = (bf16[3584,64]{0,1:T(8,128)(2,1)S(1)}, bf16[3584,64]{0,1:T(8,128)(2,1)}, u32[]{:S(2)}) copy-start(bf16[3584,64]{0,1:T(8,128)(2,1)} %param.8) | copy-start | bytes 1376260
  54.3 20.7 %collective-permute-start.17 = (bf16[256,512]{1,0:T(8,128)(2,1)S(1)}, bf16[256,512]{1,0:T(8,128)(2,1)S(1)}, u32[]{:S(2)}, u32[]{:S(2)}) collective-permute-start(bf16[256,512]{1,0:T(8,128)(2,1)S(1)} %get-tuple-element.137), channel_id=1, source_target_pairs={{0,4},{1,3},{2,6},{3,1},{4,0},{5,7},{6,2},{7,5},{8,12},{9,11},{10,... | collective-permute-start | bytes 786440 | tf_op jit(solution)/shard_map/ppermute | solution.py:329
  58.7 16.3 %collective-permute-start.16 = (bf16[256,512]{1,0:T(8,128)(2,1)S(1)}, bf16[256,512]{1,0:T(8,128)(2,1)S(1)}, u32[]{:S(2)}, u32[]{:S(2)}) collective-permute-start(bf16[256,512]{1,0:T(8,128)(2,1)S(1)} %fusion.2), channel_id=1, source_target_pairs={{0,8},{1,9},{2,10},{3,11},{4,12},{5,13},{6,14},{7,15},{8,0},{9,1},... | collective-permute-start | bytes 786440 | tf_op jit(solution)/shard_map/ppermute | solution.py:329
  60.1 12.9 %copy-start.5 = (bf16[128,3584]{1,0:T(8,128)(2,1)S(1)}, bf16[128,3584]{1,0:T(8,128)(2,1)}, u32[]{:S(2)}) copy-start(bf16[128,3584]{1,0:T(8,128)(2,1)} %own_ref.3) | copy-start | bytes 2752516
  69.1 6.8 %collective-permute-start.24 = (bf16[128,2816]{1,0:T(8,128)(2,1)S(1)}, bf16[128,2816]{1,0:T(8,128)(2,1)S(1)}, u32[]{:S(2)}, u32[]{:S(2)}) collective-permute-start(bf16[128,2816]{1,0:T(8,128)(2,1)S(1)} %get-tuple-element.125), channel_id=1, source_target_pairs={{0,1},{1,0},{2,3},{3,2},{4,5},{5,4},{6,7},{7,6},{8,9},{9,8},{10,11... | collective-permute-start | bytes 2162696 | tf_op jit(solution)/shard_map/ppermute | solution.py:324
  69.1 2.4 %collective-permute-start.19 = (f32[256,64]{1,0:T(8,128)S(1)}, f32[256,64]{1,0:T(8,128)S(1)}, u32[]{:S(2)}, u32[]{:S(2)}) collective-permute-start(f32[256,64]{1,0:T(8,128)S(1)} %get-tuple-element.114.refs_1_.proj_ref), channel_id=1, source_target_pairs={{0,1},{1,0},{2,3},{3,2},{4,5},{5,4},{6,7},{7,6},{8,9},{9,8},{10,11... | collective-permute-start | bytes 196616 | tf_op jit(solution)/shard_map/ppermute | solution.py:324
  71.5 1.3 %collective-permute-start.20 = (f32[64,512]{1,0:T(8,128)S(1)}, f32[64,512]{1,0:T(8,128)S(1)}, u32[]{:S(2)}, u32[]{:S(2)}) collective-permute-start(f32[64,512]{1,0:T(8,128)S(1)} %fusion.up_ref), channel_id=1, source_target_pairs={{0,1},{1,0},{2,3},{3,2},{4,5},{5,4},{6,7},{7,6},{8,9},{9,8},{10,11... | collective-permute-start | bytes 393224 | tf_op jit(solution)/shard_map/ppermute | solution.py:324
  72.9 3.0 %collective-permute-start.23 = (bf16[128,768]{1,0:T(8,128)(2,1)S(1)}, bf16[128,768]{1,0:T(8,128)(2,1)S(1)}, u32[]{:S(2)}, u32[]{:S(2)}) collective-permute-start(bf16[128,768]{1,0:T(8,128)(2,1)S(1)} %get-tuple-element.123), channel_id=1, source_target_pairs={{0,1},{1,0},{2,3},{3,2},{4,5},{5,4},{6,7},{7,6},{8,9},{9,8},{10,11... | collective-permute-start | bytes 589832 | tf_op jit(solution)/shard_map/ppermute | solution.py:324
  75.2 2.2 %collective-permute-start.21 = (bf16[128,512]{1,0:T(8,128)(2,1)S(1)}, bf16[128,512]{1,0:T(8,128)(2,1)S(1)}, u32[]{:S(2)}, u32[]{:S(2)}) collective-permute-start(bf16[128,512]{1,0:T(8,128)(2,1)S(1)} %slice.95), channel_id=1, source_target_pairs={{0,1},{1,0},{2,3},{3,2},{4,5},{5,4},{6,7},{7,6},{8,9},{9,8},{10,11... | collective-permute-start | bytes 393224 | tf_op jit(solution)/shard_map/ppermute | solution.py:324
  75.7 1.8 %collective-permute-start.22 = (f32[1,512]{1,0:T(1,128)S(1)}, f32[1,512]{1,0:T(1,128)S(1)}, u32[]{:S(2)}, u32[]{:S(2)}) collective-permute-start(f32[1,512]{1,0:T(1,128)S(1)} %slice_divide_fusion.g_ref), channel_id=1, source_target_pairs={{0,1},{1,0},{2,3},{3,2},{4,5},{5,4},{6,7},{7,6},{8,9},{9,8},{10,11... | collective-permute-start | bytes 6152 | tf_op jit(solution)/shard_map/ppermute | solution.py:324
